TPU v7x, 128 devices: a whole 4x4x4 slice. The times are simulated.
128 devices in a mesh: dp: 16 (over z_hi, x, core), space: 8 (over y, z_lo).
Axes of the slice: x: 4, y: 4, z: 4 (z_hi: 2, z_lo: 2; z = z_hi * 2 + z_lo), core: 2. Of those that a mesh axis runs over, the one named last changes fastest.
Arguments:
- inputs: bfloat16 [16, 8, 4, 8, 8, 128], P('dp', 'space'), may hold values from -6 to 6
- pre_act: bfloat16 [16, 8, 16, 8, 8, 128], P('dp', 'space'), may hold values from -6 to 6
- out_grad: bfloat16 [16, 8, 32, 16, 512], P('dp', 'space'), may hold values from -6 to 6
- conv1_weight: bfloat16 [27, 4, 16], replicated, may hold values from -0.3125 to 0.3125
- conv2_weight: bfloat16 [27, 16, 32], replicated, may hold values from -0.21875 to 0.21875
Outputs:
- input_grad: bfloat16 [16, 8, 4, 8, 8, 128], P('dp', 'space')
- conv1_grad: float32 [27, 4, 16], replicated
- conv2_grad: float32 [27, 16, 32], replicated
All inputs are finite; a program needn't handle non-finite values.
Results may differ from a plain program's by a relative error of at most 0.0049.
Values may be sent and summed in bfloat16 or wider, within the bound.
No kernel may reach another device: no remote copies, remote signals or barrier semaphores. Data moves between devices by JAX's collectives and lax.ppermute only.
A program may use at most 64 MiB of HBM per device.

v0:
```python
import jax
import jax.numpy as jnp
from jax import lax
from jax.sharding import PartitionSpec as P

leak = 0.3
numbers = ("NCDHW", "OIDHW", "NCDHW")


def shifted(x, axis, by):
    length = lax.axis_size(axis)
    pairs = [(i, i + by) for i in range(length) if 0 <= i + by < length]
    return lax.ppermute(x, axis, pairs)


def swapped(block, axis, bit):
    count = lax.axis_size(axis)
    route = []
    for low in range(count):
        high = low | 1 << bit
        if high != low and high < count:
            route += [(low, high), (high, low)]
    return lax.ppermute(block, axis, route)


def flipped(weights):
    ins, outs = (weights.shape[1], weights.shape[2])
    return weights[::-1].reshape(3, 3, 3, ins, outs).transpose(3, 4, 0, 1, 2)


def correlate(field, kernel):
    result = lax.conv_general_dilated(
        field[None],
        kernel,
        (1, 1, 1),
        "VALID",
        dimension_numbers=numbers,
        preferred_element_type=jnp.float32,
    )
    return result[0]


def patch_grad(padded_in, grads):
    result = lax.conv_general_dilated(
        padded_in[:, None],
        grads[:, None],
        (1, 1, 1),
        "VALID",
        dimension_numbers=numbers,
        preferred_element_type=jnp.float32,
    )
    ins, outs = (padded_in.shape[0], grads.shape[0])
    return result.transpose(2, 3, 4, 0, 1).reshape(27, ins, outs)


def extend(stack):
    tile_cols = lax.axis_size("space") // 2
    column = lax.axis_index("space") // 2
    tile_row = lax.axis_index("space") % 2
    from_left = shifted(stack[..., -1:], "space", 2)
    from_right = shifted(stack[..., :1], "space", -2)
    from_left = jnp.where(column == 0, jnp.zeros_like(from_left), from_left)
    from_right = jnp.where(column == tile_cols - 1, jnp.zeros_like(from_right), from_right)
    widened = jnp.concatenate([from_left, stack, from_right], axis=-1)
    outgoing = jnp.where(tile_row == 0, widened[..., -1:, :], widened[..., :1, :])
    across = swapped(outgoing, "space", 0)
    from_above = jnp.where(tile_row == 1, across, jnp.zeros_like(across))
    from_below = jnp.where(tile_row == 0, across, jnp.zeros_like(across))
    grown = jnp.concatenate([from_above, widened, from_below], axis=-2)
    return jnp.pad(grown, ((0, 0), (1, 1), (0, 0), (0, 0)))


def to_tiles(slab):
    tile_cols = lax.axis_size("space") // 2
    planes, chans, rows, width = slab.shape
    tile_rows = rows // 2
    tile_width = width // tile_cols
    shaped = slab.reshape(planes, chans, 2, tile_rows, tile_cols, tile_width)
    shaped = shaped.transpose(4, 2, 1, 0, 3, 5).reshape(
        2 * tile_cols, chans, planes, tile_rows, tile_width
    )
    return lax.all_to_all(shaped, "space", split_axis=0, concat_axis=2, tiled=True)[0]


def body(inputs, pre_act, out_grad, conv1_weight, conv2_weight):
    input_tile = inputs[0, 0]
    act_tile = pre_act[0, 0].astype(jnp.float32)
    hidden = jnp.where(act_tile > 0, act_tile, leak * act_tile).astype(jnp.bfloat16)
    slab = out_grad[0]
    grad_chans = slab.shape[1]
    act_chans = hidden.shape[0]
    grad_tile = to_tiles(slab)
    joined = extend(jnp.concatenate([grad_tile, hidden], axis=0))
    grad_pad = joined[:grad_chans]
    hidden_pad = joined[grad_chans:]
    hidden_grad = correlate(grad_pad, flipped(conv2_weight))
    act_grad = (hidden_grad * jnp.where(act_tile > 0, 1.0, leak)).astype(jnp.bfloat16)
    second = patch_grad(hidden_pad, grad_pad[:, 1:-1, 1:-1, 1:-1])
    joined_late = extend(jnp.concatenate([act_grad, input_tile], axis=0))
    act_pad = joined_late[:act_chans]
    input_pad = joined_late[act_chans:]
    first = patch_grad(input_pad, act_grad)
    input_grad = correlate(act_pad, flipped(conv1_weight)).astype(jnp.bfloat16)
    cells = (
        lax.axis_size("dp")
        * lax.axis_size("space")
        * input_tile.shape[1]
        * input_tile.shape[2]
        * input_tile.shape[3]
    )
    scale = 1.0 / jnp.sqrt(jnp.float32(cells))
    first = first * scale
    second = second * scale
    first, second = lax.psum((first, second), ("dp", "space"))
    return (input_grad[None, None], first, second)


def solution(mesh):
    placed = (
        P("dp", "space", None, None, None, None),
        P("dp", "space", None, None, None, None),
        P("dp", "space", None, None, None),
        P(),
        P(),
    )
    return jax.shard_map(
        body,
        mesh=mesh,
        in_specs=placed,
        out_specs=(P("dp", "space", None, None, None, None), P(), P()),
        check_vma=False,
    )
```

profile of v0, /device:TPU:1, one launch (start us, length us, event | category | flops | bytes accessed | tf_op | source)
XLA Modules:
  0.0 455.1 jit_solution(192490400127302727)
XLA Ops:
  0.6 2.2 copy.78
  2.8 6.4 %all-to-all-start = ((bf16[8,32,1,8,128]{4,1,3,2,0:T(8,128)(2,1)}), bf16[8,32,1,8,128]{4,1,3,2,0:T(8,128)(2,1)S(1)}, u32[]{:S(2)}, u32[]{:S(2)}) async-start(bf16[8,32,1,8,128]{4,1,3,2,0:T(8,128)(2,1)} %bitcast.2), calls=%async_computation | async-start | bytes 1048576 | tf_op jit(solution)/shard_map/all_to_all | solution.py:82
  9.2 1.2 fusion.38
  10.3 7.5 %all-to-all-done = bf16[8,32,1,8,128]{4,1,3,2,0:T(8,128)(2,1)S(1)} async-done(((bf16[8,32,1,8,128]{4,1,3,2,0:T(8,128)(2,1)}), bf16[8,32,1,8,128]{4,1,3,2,0:T(8,128)(2,1)S(1)}, u32[]{:S(2)}, u32[]{:S(2)}) %all-to-all-start) | async-done | bytes 524320 | tf_op jit(solution)/shard_map/all_to_all | solution.py:82
  17.9 0.3 slice_maximum_fusion
  18.2 0.0 copy-start.12
  18.2 0.0 copy-start.10
  18.2 0.0 copy-start.9
  18.2 0.5 copy.81
  18.7 1.3 collective-permute-start.1
  20.0 0.5 copy.80
  20.5 4.0 collective-permute-start
  24.5 0.0 collective-permute-done.1
  24.5 0.5 copy.83
  25.0 0.3 collective-permute-done
  25.3 0.5 copy.82
  25.8 0.3 fusion.40
  26.1 0.8 collective-permute-start.2
  26.9 0.1 rev.7
  27.0 0.7 copy.90
  27.8 0.1 copy.110
  27.8 0.0 copy-start.6
  27.8 0.7 rev.6
  28.5 7.6 %copy.98 = bf16[32,1,8,8,128]{0,1,4,3,2:T(2,128)(2,1)} copy(bf16[32,1,8,8,128]{4,0,3,2,1:T(8,128)(2,1)S(1)} %bitcast.86) | data formatting | bytes 1048576 | tf_op jit(solution)/shard_map/broadcast_in_dim | solution.py:46
  36.1 1.7 select_maximum_fusion
  37.9 0.2 slice_bitcast_fusion
  38.1 1.0 slice_bitcast_fusion.1
  39.1 0.5 pad.10
  39.6 6.0 %reshape.76 = bf16[32,10,10,1,8,17]{5,4,0,2,1,3:T(8,128)(2,1)} reshape(bf16[32,10,10,1,136]{4,0,2,1,3:T(8,128)(2,1)S(1)} %pad.10) | data formatting | bytes 1740800 | tf_op jit(solution)/shard_map/conv_general_dilated | solution.py:32
  45.6 9.4 %copy.85 = bf16[32,10,10,1,8,17]{0,4,5,2,1,3:T(8,128)(2,1)S(1)} copy(bf16[32,10,10,1,8,17]{5,4,0,2,1,3:T(8,128)(2,1)} %reshape.76) | data formatting | bytes 1740800 | tf_op jit(solution)/shard_map/conv_general_dilated | solution.py:32
  54.9 0.1 slice.60
  55.1 10.7 %broadcast_select_fusion = f32[8,8,8,17,16]{4,2,3,1,0:T(8,128)} fusion(pred[8,17]{0,1:T(8,128)(4,1)S(1)} %copy-done.14, bf16[3,3,3,16,32]{4,3,2,1,0:T(8,128)(2,1)} %bitcast.94, bf16[32,10,10,1,7,2]{0,4,5,2,1,3:T(8,128)(2,1)S(1)} %slice.60, bf16[32,10,10,1,8,17]{0,4,5,2,1,3:T(8,128)(2,1)S(1)} %copy.85), kind=kOutput, calls=%fused_computation.31 | convolution fusion | flops 243705856 | bytes 1544840 | tf_op jit(solution)/shard_map/conv_general_dilated | solution.py:32
  65.7 6.4 %copy.86 = f32[8,8,8,17,16]{3,2,4,1,0:T(8,128)} copy(f32[8,8,8,17,16]{4,2,3,1,0:T(8,128)} %broadcast_select_fusion) | data formatting | bytes 1114112 | tf_op jit(solution)/shard_map/conv_general_dilated | solution.py:32
  72.1 3.4 reshape.80
  75.6 0.2 fusion.37
  75.8 0.8 copy-done.1
  76.6 1.1 slice_maximum_fusion.1
  77.7 1.3 collective-permute-start.4
  79.0 5.2 %collective-permute-start.3 = (bf16[20,8,8,1]{3,0,2,1:T(8,128)(2,1)}, bf16[20,8,8,1]{3,0,2,1:T(8,128)(2,1)}, u32[]{:S(2)}, u32[]{:S(2)}) collective-permute-start(bf16[20,8,8,1]{3,0,2,1:T(8,128)(2,1)} %get-tuple-element.19), channel_id=1, source_target_pairs={{0,2},{1,3},{2,4},{3,5},{4,6},{5,7},{8,10},{9,11},{10,12},{11,13},... | collective-permute-start | bytes 7688 | tf_op jit(solution)/shard_map/ppermute | solution.py:13
  84.1 10.9 %copy.97 = bf16[16,1,10,10,130]{0,1,4,3,2:T(2,128)(2,1)} copy(bf16[16,1,10,10,130]{4,0,3,2,1:T(8,128)(2,1)S(1)} %copy-done.3) | data formatting | bytes 832000 | tf_op jit(solution)/shard_map/broadcast_in_dim | solution.py:45
  95.0 51.0 %convolution_multiply_fusion = f32[3,3,3,16,32]{4,3,2,1,0:T(8,128)} fusion(bf16[16,1,10,10,130]{0,1,4,3,2:T(2,128)(2,1)} %copy.97, bf16[32,1,8,8,128]{0,1,4,3,2:T(2,128)(2,1)} %copy.98), kind=kOutput, calls=%fused_computation.44 | convolution fusion | flops 226506240 | bytes 995584 | tf_op jit(solution)/shard_map/transpose | solution.py:53
  146.0 1.0 broadcast_select_fusion.1
  147.1 0.2 fusion.41
  147.3 1.2 collective-permute-start.5
  148.5 1.3 fusion.39
  149.8 7.2 %copy.94 = bf16[16,1,8,8,128]{0,1,4,3,2:T(2,128)(2,1)} copy(bf16[16,1,8,8,128]{4,0,3,2,1:T(8,128)(2,1)S(1)} %fusion.39) | data formatting | bytes 524288 | tf_op jit(solution)/shard_map/convert_element_type | solution.py:97
  156.9 0.5 select_maximum_fusion.2
  157.4 0.1 slice_bitcast_fusion.2
  157.5 0.1 slice_bitcast_fusion.3
  157.6 1.1 pad.12
  158.6 3.8 reshape.83
  162.5 0.0 copy-start.11
  162.5 6.4 %copy.89 = bf16[16,10,10,1,8,17]{0,4,5,2,1,3:T(8,128)(2,1)} copy(bf16[16,10,10,1,8,17]{5,4,0,2,1,3:T(8,128)(2,1)S(1)} %reshape.83) | data formatting | bytes 870400 | tf_op jit(solution)/shard_map/conv_general_dilated | solution.py:32
  168.8 1.1 slice.65
  170.0 0.0 copy-start.13
  170.0 148.3 %fusion.5 = bf16[8,8,8,17,4]{2,4,3,1,0:T(4,128)(2,1)S(1)} fusion(bf16[3,3,3,4,16]{4,3,2,1,0:T(4,128)(2,1)S(1)} %bitcast.96, bf16[16,10,10,1,7,2]{0,4,5,2,1,3:T(8,128)(2,1)S(1)} %slice.65, bf16[16,10,10,1,8,17]{0,4,5,2,1,3:T(8,128)(2,1)} %copy.89), kind=kOutput, calls=%fused_computation.9 | convolution fusion | flops 31540224 | bytes 553088 | tf_op jit(solution)/shard_map/conv_general_dilated | solution.py:32
  318.3 1.8 copy.91
  320.1 0.1 select_convert_fusion
  320.2 0.4 reshape.99
  320.6 0.6 copy.99
  321.3 11.1 %copy.93 = bf16[4,1,10,10,130]{0,1,4,3,2:T(2,128)(2,1)} copy(bf16[4,1,10,10,130]{4,0,3,2,1:T(4,128)(2,1)S(1)} %slice_bitcast_fusion.3) | data formatting | bytes 208000 | tf_op jit(solution)/shard_map/broadcast_in_dim | solution.py:45
  332.4 50.2 %convolution_multiply_fusion.1 = f32[3,3,3,4,16]{4,3,2,1,0:T(4,128)S(1)} fusion(bf16[4,1,10,10,130]{0,1,4,3,2:T(2,128)(2,1)} %copy.93, bf16[16,1,8,8,128]{0,1,4,3,2:T(2,128)(2,1)} %copy.94), kind=kOutput, calls=%fused_computation.45 | convolution fusion | flops 28313280 | bytes 373056 | tf_op jit(solution)/shard_map/transpose | solution.py:53
  382.6 0.1 copy.95
  382.7 72.2 %all-reduce.2 = (f32[27,4,16]{0,2,1:T(8,128)}, f32[27,16,32]{2,1,0:T(8,128)}) all-reduce(f32[27,4,16]{0,2,1:T(8,128)S(1)} %copy.95, f32[27,16,32]{2,1,0:T(8,128)S(1)} %bitcast.93), channel_id=1, replica_groups=mesh['dp'=16,'space'=8] {'dp','space'}, use_global_device_ids=true, to_apply=%region_0.1 | all-reduce | flops 15552 | bytes 124416 | tf_op jit(solution)/shard_map/psum | solution.py:114
  (34 shorter events, 0.2 us)
Async XLA Ops:
  2.8 15.1 %all-to-all-start = ((bf16[8,32,1,8,128]{4,1,3,2,0:T(8,128)(2,1)}), bf16[8,32,1,8,128]{4,1,3,2,0:T(8,128)(2,1)S(1)}, u32[]{:S(2)}, u32[]{:S(2)}) async-start(bf16[8,32,1,8,128]{4,1,3,2,0:T(8,128)(2,1)} %bitcast.2), calls=%async_computation | async-start | bytes 1048576 | tf_op jit(solution)/shard_map/all_to_all | solution.py:82
  18.2 8.7 %copy-start.12 = (bf16[27,4,16]{0,2,1:T(8,128)(2,1)S(1)}, bf16[27,4,16]{0,2,1:T(8,128)(2,1)}, u32[]{:S(2)}) copy-start(bf16[27,4,16]{0,2,1:T(8,128)(2,1)} %param.8) | copy-start | bytes 10372
  18.2 9.5 %copy-start.10 = (bf16[1,1,4,8,8,128]{5,4,3,2,1,0:T(8,128)(2,1)S(1)}, bf16[1,1,4,8,8,128]{5,4,3,2,1,0:T(8,128)(2,1)}, u32[]{:S(2)}) copy-start(bf16[1,1,4,8,8,128]{5,4,3,2,1,0:T(8,128)(2,1)} %param.5) | copy-start | bytes 196612
  18.2 9.6 %copy-start.9 = (bf16[27,16,32]{2,1,0:T(8,128)(2,1)S(1)}, bf16[27,16,32]{2,1,0:T(8,128)(2,1)}, u32[]{:S(2)}) copy-start(bf16[27,16,32]{2,1,0:T(8,128)(2,1)} %param.9) | copy-start | bytes 82948
  18.7 5.8 %collective-permute-start.1 = (bf16[48,8,8,1]{0,2,3,1:T(8,128)(2,1)S(1)}, bf16[48,8,8,1]{0,2,3,1:T(8,128)(2,1)S(1)}, u32[]{:S(2)}, u32[]{:S(2)}) collective-permute-start(bf16[48,8,8,1]{0,2,3,1:T(8,128)(2,1)S(1)} %copy.81), channel_id=1, source_target_pairs={{2,0},{3,1},{4,2},{5,3},{6,4},{7,5},{10,8},{11,9},{12,10},{13,11},... | collective-permute-start | bytes 18440 | tf_op jit(solution)/shard_map/ppermute | solution.py:13
  20.5 4.8 %collective-permute-start = (bf16[48,8,8,1]{0,2,3,1:T(8,128)(2,1)S(1)}, bf16[48,8,8,1]{0,2,3,1:T(8,128)(2,1)S(1)}, u32[]{:S(2)}, u32[]{:S(2)}) collective-permute-start(bf16[48,8,8,1]{0,2,3,1:T(8,128)(2,1)S(1)} %copy.80), channel_id=1, source_target_pairs={{0,2},{1,3},{2,4},{3,5},{4,6},{5,7},{8,10},{9,11},{10,12},{11,13},... | collective-permute-start | bytes 18440 | tf_op jit(solution)/shard_map/ppermute | solution.py:13
  26.1 10.0 %collective-permute-start.2 = (bf16[48,8,1,130]{3,0,2,1:T(8,128)(2,1)S(1)}, bf16[48,8,1,130]{3,0,2,1:T(8,128)(2,1)S(1)}, u32[]{:S(2)}, u32[]{:S(2)}) collective-permute-start(bf16[48,8,1,130]{3,0,2,1:T(8,128)(2,1)S(1)} %fusion.40), channel_id=1, source_target_pairs={{0,1},{1,0},{2,3},{3,2},{4,5},{5,4},{6,7},{7,6},{8,9},{9,8},{10,11... | collective-permute-start | bytes 299528 | tf_op jit(solution)/shard_map/ppermute | solution.py:23
  27.8 48.0 %copy-start.6 = (bf16[1,1,4,8,8,128]{5,2,4,3,1,0:T(4,128)(2,1)}, bf16[1,1,4,8,8,128]{5,2,4,3,1,0:T(4,128)(2,1)S(1)}, u32[]{:S(2)}) copy-start(bf16[1,1,4,8,8,128]{5,2,4,3,1,0:T(4,128)(2,1)S(1)} %copy.110) | copy-start | bytes 196612
  45.6 9.5 %copy-start.14 = (pred[8,17]{0,1:T(8,128)(4,1)S(1)}, pred[8,17]{0,1:T(8,128)(4,1)}, u32[]{:S(2)}) copy-start(pred[8,17]{0,1:T(8,128)(4,1)} %constant.69) | copy-start | bytes 412
  72.1 3.4 copy-start.4
  72.1 12.0 %copy-start.3 = (bf16[16,1,10,10,130]{4,0,3,2,1:T(8,128)(2,1)S(1)}, bf16[16,1,10,10,130]{4,0,3,2,1:T(8,128)(2,1)}, u32[]{:S(2)}) copy-start(bf16[16,1,10,10,130]{4,0,3,2,1:T(8,128)(2,1)} %slice_bitcast_fusion.1) | copy-start | bytes 1248004
  75.5 19.5 %copy-start = (f32[8,8,1,136,16]{3,4,1,0,2:T(8,128)}, f32[8,8,1,136,16]{3,4,1,0,2:T(8,128)S(1)}, u32[]{:S(2)}) copy-start(f32[8,8,1,136,16]{3,4,1,0,2:T(8,128)S(1)} %reshape.80) | copy-start | bytes 1671172
  75.8 0.8 copy-start.1
  77.7 68.4 %collective-permute-start.4 = (bf16[20,8,8,1]{3,0,2,1:T(8,128)(2,1)}, bf16[20,8,8,1]{3,0,2,1:T(8,128)(2,1)}, u32[]{:S(2)}, u32[]{:S(2)}) collective-permute-start(bf16[20,8,8,1]{3,0,2,1:T(8,128)(2,1)} %get-tuple-element.20), channel_id=1, source_target_pairs={{2,0},{3,1},{4,2},{5,3},{6,4},{7,5},{10,8},{11,9},{12,10},{13,11},... | collective-permute-start | bytes 7688 | tf_op jit(solution)/shard_map/ppermute | solution.py:13
  79.0 68.1 %collective-permute-start.3 = (bf16[20,8,8,1]{3,0,2,1:T(8,128)(2,1)}, bf16[20,8,8,1]{3,0,2,1:T(8,128)(2,1)}, u32[]{:S(2)}, u32[]{:S(2)}) collective-permute-start(bf16[20,8,8,1]{3,0,2,1:T(8,128)(2,1)} %get-tuple-element.19), channel_id=1, source_target_pairs={{0,2},{1,3},{2,4},{3,5},{4,6},{5,7},{8,10},{9,11},{10,12},{11,13},... | collective-permute-start | bytes 7688 | tf_op jit(solution)/shard_map/ppermute | solution.py:13
  95.0 52.1 %copy-start.2 = (bf16[16,8,8,128]{3,0,2,1:T(8,128)(2,1)S(1)}, bf16[16,8,8,128]{3,0,2,1:T(8,128)(2,1)}, u32[]{:S(2)}) copy-start(bf16[16,8,8,128]{3,0,2,1:T(8,128)(2,1)} %copy-done.1) | copy-start | bytes 786436
  95.0 52.1 %copy-start.7 = (bf16[1,1,4,8,8,128]{5,2,4,3,1,0:T(4,128)(2,1)S(1)}, bf16[1,1,4,8,8,128]{5,2,4,3,1,0:T(4,128)(2,1)}, u32[]{:S(2)}) copy-start(bf16[1,1,4,8,8,128]{5,2,4,3,1,0:T(4,128)(2,1)} %copy-done.6) | copy-start | bytes 196612
  95.0 53.5 %copy-start.5 = (bf16[1,1,16,8,8,128]{5,4,3,2,1,0:T(8,128)(2,1)S(1)}, bf16[1,1,16,8,8,128]{5,4,3,2,1,0:T(8,128)(2,1)}, u32[]{:S(2)}) copy-start(bf16[1,1,16,8,8,128]{5,4,3,2,1,0:T(8,128)(2,1)} %param.6) | copy-start | bytes 786436
  147.3 9.6 %collective-permute-start.5 = (bf16[20,8,1,130]{3,0,2,1:T(8,128)(2,1)S(1)}, bf16[20,8,1,130]{3,0,2,1:T(8,128)(2,1)S(1)}, u32[]{:S(2)}, u32[]{:S(2)}) collective-permute-start(bf16[20,8,1,130]{3,0,2,1:T(8,128)(2,1)S(1)} %fusion.41), channel_id=1, source_target_pairs={{0,1},{1,0},{2,3},{3,2},{4,5},{5,4},{6,7},{7,6},{8,9},{9,8},{10,11... | collective-permute-start | bytes 124808 | tf_op jit(solution)/shard_map/ppermute | solution.py:23
  162.5 7.5 %copy-start.11 = (bf16[27,4,16]{2,1,0:T(4,128)(2,1)S(1)}, bf16[27,4,16]{2,1,0:T(4,128)(2,1)}, u32[]{:S(2)}) copy-start(bf16[27,4,16]{2,1,0:T(4,128)(2,1)} %copy.90) | copy-start | bytes 10372
  170.0 150.1 %copy-start.13 = (pred[8,17]{1,0:T(8,128)(4,1)S(1)}, pred[8,17]{1,0:T(8,128)(4,1)}, u32[]{:S(2)}) copy-start(pred[8,17]{1,0:T(8,128)(4,1)} %constant.67) | copy-start | bytes 412
  332.4 50.3 %copy-start.8 = (f32[3,3,3,16,32]{4,3,2,1,0:T(8,128)S(1)}, f32[3,3,3,16,32]{4,3,2,1,0:T(8,128)}, u32[]{:S(2)}) copy-start(f32[3,3,3,16,32]{4,3,2,1,0:T(8,128)} %convolution_multiply_fusion) | copy-start | bytes 165892
where the time goes:
time: 459 us; the launch traced here: 455 us
  matrix products  260 us (57%)
  local copies, waits for them, and re-layouts  85.6 us (19%)
  blocking collectives  72.2 us (16%)
  starting transfers between devices  20.1 us (4%)
  other arithmetic  7.89 us (2%)
  waiting for transfers between devices  7.88 us (2%)
    conv_general_dilated x2, matrix products, correlate(): lax.conv_general_dilated(field[None], kernel, (1, 1, 1), 'VALID', dimensi...  159 us
    transpose x2, matrix products, patch_grad(): return result.transpose(2, 3, 4, 0, 1).reshape(27, ins, outs)  101 us
    psum x1, blocking collectives, body(): first, second = lax.psum((first, second), ('dp', 'space'))  72.2 us
    conv_general_dilated x9, local copies, waits for them, and re-layouts, correlate(): lax.conv_general_dilated(field[None], kernel, (1, 1, 1), 'VALID', dimensi...  38.3 us
    broadcast_in_dim x4, local copies, waits for them, and re-layouts, patch_grad(): padded_in[:, None]  23 us
    ppermute x4, starting transfers between devices, shifted(): return lax.ppermute(x, axis, pairs)  11.7 us
  transfers between devices with their start and end apart: 7, of which 2 were waited for; matrix products, arithmetic and copies ran while one was open for 18% of the time, Pallas kernels for 0%

commit v1 on v0

v1 whole, which is shorter than its diff:
```python
import itertools

import jax
import jax.numpy as jnp
from jax import lax
from jax.experimental import pallas as pl
from jax.experimental.pallas import tpu as pltpu
from jax.sharding import PartitionSpec as P

LEAK = 0.3
STRIP = 64
WIDE = 72
PAD = 80
ROWS = 8 * PAD
ALL = ("dp", "space")
F32 = jnp.float32
BF16 = jnp.bfloat16


def iota(shape, dim):
    return lax.broadcasted_iota(jnp.int32, shape, dim)


def one_hot(flags):
    return jnp.where(flags, 1.0, 0.0).astype(BF16)


def dot(a, b):
    return jnp.dot(a, b, preferred_element_type=F32)


def dot_t(a, b):
    return lax.dot_general(a, b, (((1,), (1,)), ((), ())), preferred_element_type=F32)


def call(kernel, name, outs, scratch, args, flops=1e8, size=4e6):
    return pl.pallas_call(
        kernel,
        name=name,
        out_shape=outs,
        in_specs=[pl.BlockSpec(memory_space=pltpu.VMEM)] * len(args),
        out_specs=jax.tree.map(lambda _: pl.BlockSpec(memory_space=pltpu.VMEM), outs),
        scratch_shapes=scratch,
        compiler_params=pltpu.CompilerParams(vmem_limit_bytes=40 << 20),
        cost_estimate=pl.CostEstimate(flops=int(flops), bytes_accessed=int(size), transcendentals=0),
    )(*args)


def cut_kernel(slab_ref, out_ref, wide_ref, turned_ref):
    for b in range(4):
        wide_ref[b] = slab_ref[:, :, 128 * b : 128 * b + 128].astype(F32).reshape(512, 128)
    for y in range(16):
        for b in range(4):
            turned_ref[32 * y : 32 * y + 32, 128 * b : 128 * b + 128] = wide_ref[
                b, pl.ds(y, 32, stride=16), :
            ].astype(BF16)
    p, x = iota((WIDE, 512), 0), iota((WIDE, 512), 1)
    gap = jnp.where(p < STRIP + 4, x - p, -9999)
    pick = jnp.concatenate([jnp.where(gap == STRIP * t - 2, 1.0, 0.0) for t in range(8)], axis=0)
    cut = dot_t(pick.astype(BF16), turned_ref[...])
    for t in range(8):
        out_ref[t] = cut[WIDE * t : WIDE * t + WIDE].astype(BF16)


def turn_kernel(pre_ref, in_ref, keep_ref, send_ref, edge_ref):
    r = lax.rem(lax.axis_index("space"), 2)
    a, x = iota((WIDE, 128), 0), iota((WIDE, 128), 1)
    gap = jnp.where(a < STRIP + 2, x - a, -9999)
    first, x1 = iota((8, 128), 0) == 0, iota((8, 128), 1)
    pick = jnp.concatenate(
        [
            jnp.where(gap == STRIP * r - 1, 1.0, 0.0),
            jnp.where(gap == STRIP * (1 - r) - 1, 1.0, 0.0),
            jnp.where(first & (x1 == 127 * (1 - r)), 1.0, 0.0),
            jnp.where(first & (x1 == 127 * r), 1.0, 0.0),
        ],
        axis=0,
    ).astype(BF16)
    src, dst = iota((128, 128), 0), iota((128, 128), 1)
    order = one_hot((src // 8 == dst % 16) & (src % 8 == dst // 16))
    for z in range(8):
        rows = pre_ref[:, z].astype(F32).reshape(128, 128).astype(BF16)
        got = dot(dot_t(pick, rows).astype(BF16), order).astype(BF16).astype(F32)
        keep_ref[z] = got[:WIDE].astype(BF16)
        send_ref[z] = got[WIDE : 2 * WIDE].astype(BF16)
        edge_ref[0, z] = got[2 * WIDE : 2 * WIDE + 8].astype(BF16)
        edge_ref[1, z] = got[2 * WIDE + 8 :].astype(BF16)
    gap = jnp.where(a < STRIP, x - a, -9999)
    pick = jnp.concatenate(
        [jnp.where(gap == STRIP * r, 1.0, 0.0), jnp.where(gap == STRIP * (1 - r), 1.0, 0.0)], axis=0
    ).astype(BF16)
    src, dst = iota((256, 256), 0), iota((256, 256), 1)
    same = (src // 64 == dst // 8 % 4) & (src // 8 % 8 == dst // 32) & (src % 8 == dst % 8)
    rows = in_ref[...].astype(F32).reshape(256, 128).astype(BF16)
    got = dot(dot_t(pick, rows).astype(BF16), one_hot(same))
    for half in range(2):
        keep_ref[8 + half] = got[:WIDE, 128 * half : 128 * half + 128].astype(BF16)
        send_ref[8 + half] = got[WIDE:, 128 * half : 128 * half + 128].astype(BF16)


def join_kernel(keep_ref, recv_ref, near_ref, far_ref, pre_ref, hid_ref, ins_ref, wide_ref, thin_ref):
    r = lax.rem(lax.axis_index("space"), 2)
    left = r == 0
    row = iota((WIDE, 128), 0)
    edge = row == jnp.where(left, 0, STRIP + 1)
    lane = iota((PAD, 128), 1)
    tail = jnp.zeros((PAD - WIDE, 128), F32)
    own = (iota((PAD, 128), 0) >= 1) & (iota((PAD, 128), 0) <= STRIP)
    for z in range(8):
        mine = jnp.where(edge, near_ref[z].astype(F32)[:1], keep_ref[z].astype(F32))
        other = jnp.where(edge, far_ref[z].astype(F32)[:1], recv_ref[z].astype(F32))
        mine = jnp.concatenate([mine, tail], axis=0)
        other = jnp.concatenate([other, tail], axis=0)
        for part in range(2):
            value = jnp.where(left, mine, other) if part == 0 else jnp.where(left, other, mine)
            pre_ref[z, :, 128 * part : 128 * part + 128] = value.astype(BF16)
            hidden = jnp.where(value > 0, value, LEAK * value)
            wide_ref[PAD * z : PAD * z + PAD, 128 * part : 128 * part + 128] = jnp.where(own, hidden, 0.0)
        mine = jnp.concatenate([keep_ref[8 + z // 4].astype(F32), tail], axis=0)
        other = jnp.concatenate([recv_ref[8 + z // 4].astype(F32), tail], axis=0)
        low, high = jnp.where(left, mine, other), jnp.where(left, other, mine)
        low = pltpu.roll(low, (128 - 32 * (z % 4)) % 128, 1)
        high = pltpu.roll(high, (160 - 32 * (z % 4)) % 128, 1)
        value = jnp.where(lane < 32, low, jnp.where(lane < 64, high, 0.0))
        thin_ref[PAD * z : PAD * z + PAD, :] = value
    for part in range(2):
        turned = wide_ref[:, 128 * part : 128 * part + 128].T
        for kx in range(3):
            shifted = pltpu.roll(turned, 2 - kx, 1) if kx < 2 else turned
            hid_ref[256 * kx + 128 * part : 256 * kx + 128 * part + 128, :] = shifted.astype(BF16)
    turned = thin_ref[...].T[:64]
    for kx in range(3):
        shifted = pltpu.roll(turned, 2 - kx, 1) if kx < 2 else turned
        ins_ref[64 * kx : 64 * kx + 64, :] = shifted.astype(BF16)


def band_kernel(two_ref, one_ref, wide_ref, thin_ref):
    spread = one_hot(iota((16, 256), 1) % 16 == iota((16, 256), 0))
    two = dot(two_ref[...], spread)
    group = iota((32, 256), 1) // 16
    for kz in range(3):
        for kx in range(3):
            terms = [two[32 * (9 * kz + 3 * ky + kx) :][:32] for ky in range(3)]
            for y in range(16):
                block = jnp.zeros((32, 256), F32)
                for ky in range(3):
                    block = jnp.where(group == y + ky - 1, terms[ky], block)
                wide_ref[512 * kz + 32 * y : 512 * kz + 32 * y + 32, 256 * kx : 256 * kx + 256] = block.astype(BF16)
    lane = iota((4, 128), 1)
    spread = one_hot((lane < 64) & (lane // 8 % 4 == iota((4, 128), 0)))
    one = dot(one_ref[...], spread)
    lane = iota((16, 128), 1)
    group = 8 * (lane // 32) + lane % 8
    for kz in range(3):
        for kx in range(3):
            terms = [one[16 * (9 * kz + 3 * ky + kx) :][:16] for ky in range(3)]
            for y in range(16):
                block = jnp.zeros((16, 128), F32)
                for ky in range(3):
                    block = jnp.where(group == y + ky - 1, terms[ky], block)
                thin_ref[256 * kz + 16 * y : 256 * kz + 16 * y + 16, 128 * kx : 128 * kx + 128] = block.astype(BF16)


def planes(ref, kz):
    return ref[(2 - kz) * PAD : (2 - kz) * PAD + ROWS, :]


def grads_kernel(
    grad_ref, pre_ref, hid_ref, ins_ref, wide_ref, thin_ref,
    own_ref, give_ref, mine_ref, rest_ref, grad_s, act_s, out_s, terms_s,
):
    space = lax.axis_index("space")
    left = lax.rem(space, 2) == 0
    for block in (0, 9):
        grad_s[PAD * block : PAD * block + PAD, :] = jnp.zeros((PAD, 512), BF16)
        act_s[PAD * block : PAD * block + PAD, :] = jnp.zeros((PAD, 256), BF16)
    for z in range(8):
        plane = jnp.concatenate([grad_ref[z].astype(F32), jnp.zeros((PAD - WIDE, 512), F32)], axis=0)
        grad_s[PAD * (z + 1) : PAD * (z + 2), :] = plane.astype(BF16)

    lane = iota((16, 128), 1)
    taps = [None] * 28
    for kz in range(3):
        terms_s[...] = dot(hid_ref[...], planes(grad_s, kz))
        for kx in range(3):
            for ky in range(3):
                total = jnp.zeros((16, 128), F32)
                for y in range(16):
                    at = y + ky - 1
                    if 0 <= at < 16:
                        piece = terms_s[256 * kx + 16 * at : 256 * kx + 16 * at + 16, 128 * (y // 4) : 128 * (y // 4) + 128]
                        total = total + jnp.where(lane // 32 == y % 4, piece, 0.0)
                total = total + pltpu.roll(total, 64, 1)
                taps[9 * kz + 3 * ky + kx] = total + pltpu.roll(total, 32, 1)

    left_side = jnp.concatenate([planes(grad_s, kz) for kz in range(3)], axis=1)
    sums = dot(left_side, wide_ref[...])
    act = sums[:, 512:] + pltpu.roll(sums[:, 256:512], ROWS - 1, 0) + pltpu.roll(sums[:, :256], ROWS - 2, 0)
    act = act.reshape(8, PAD, 256)
    at = STRIP * space - 1 + iota((8, PAD, 256), 1)
    inside = (iota((8, PAD, 256), 1) < STRIP + 2) & (at >= 0) & (at < 512)
    act = act * jnp.where(pre_ref[...].astype(F32) > 0, 1.0, LEAK)
    act_s[PAD : PAD + ROWS, :] = jnp.where(inside, act, 0.0).reshape(ROWS, 256).astype(BF16)

    left_side = jnp.concatenate([planes(act_s, kz) for kz in range(3)], axis=1)
    sums = dot(left_side, thin_ref[...])
    out_s[...] = sums[:, 256:] + pltpu.roll(sums[:, 128:256], ROWS - 1, 0) + pltpu.roll(sums[:, :128], ROWS - 2, 0)
    for z in range(4):
        pair = jnp.concatenate([out_s[PAD * z : PAD * z + STRIP], out_s[PAD * (z + 4) : PAD * (z + 4) + STRIP]], axis=0).T
        own_ref[z] = jnp.where(left, pair[:32], pair[32:64]).astype(BF16)
        give_ref[z] = jnp.where(left, pair[32:64], pair[:32]).astype(BF16)

    row, col = iota((64, 256), 0), iota((64, 256), 1)
    gap = 8 * (row // 32) + row % 8 - col // 16
    packed = jnp.zeros((12, 128), F32)
    for kz in range(3):
        terms = dot(ins_ref[...], planes(act_s, kz)).reshape(3, 64, 256)
        for ky in range(3):
            part = jnp.where((gap == ky - 1)[None], terms, 0.0)
            part = (part[:, :, :128] + part[:, :, 128:]).reshape(3, 2, 4, 8, 128)
            part = jnp.sum(part[:, 0] + part[:, 1], axis=2).reshape(12, 128)
            for by in (64, 32, 16):
                part = part + pltpu.roll(part, by, 1)
            if 3 * kz + ky < 8:
                packed = jnp.where(iota((12, 128), 1) // 16 == 3 * kz + ky, part, packed)
            else:
                last = part
    filler = jnp.zeros((4, 128), F32)
    taps[27] = jnp.concatenate([last, filler], axis=0)
    blocks = []
    for q in range(7):
        block = taps[4 * q]
        for g in range(1, 4):
            block = jnp.where(lane // 32 == g, taps[4 * q + g], block)
        blocks.append(block)
    blocks.append(jnp.concatenate([packed, filler], axis=0))
    first = lax.rem(lax.axis_index("dp"), 2) == 0
    cells = 16 * 8 * 16 * 512
    scale = cells**-0.5
    for q in range(4):
        low, high = blocks[q] * scale, blocks[q + 4] * scale
        mine_ref[16 * q : 16 * q + 16, :] = jnp.where(first, low, high)
        rest_ref[16 * q : 16 * q + 16, :] = jnp.where(first, high, low)


def tile_kernel(own_ref, recv_ref, out_ref):
    left = lax.rem(lax.axis_index("space"), 2) == 0
    low_lanes = iota((32, 128), 1) < STRIP
    for z in range(4):
        own, recv = own_ref[z].astype(F32), recv_ref[z].astype(F32)
        a, b = jnp.where(left, own, recv), jnp.where(left, recv, own)
        near = jnp.where(low_lanes, a, pltpu.roll(b, STRIP, 1))
        far = jnp.where(low_lanes, pltpu.roll(a, STRIP, 1), b)
        out_ref[:, z] = near.reshape(4, 8, 128).astype(BF16)
        out_ref[:, z + 4] = far.reshape(4, 8, 128).astype(BF16)


def unpack_kernel(mine_ref, rest_ref, one_ref, two_ref):
    first = lax.rem(lax.axis_index("dp"), 2) == 0
    mine, rest = mine_ref[...], rest_ref[...]
    low, high = jnp.where(first, mine, rest), jnp.where(first, rest, mine)
    blocks = [low[16 * q : 16 * q + 16] for q in range(4)] + [high[16 * q : 16 * q + 16] for q in range(4)]
    for k in range(27):
        two_ref[k] = blocks[k // 4][:, 32 * (k % 4) : 32 * (k % 4) + 32]
    for pair in range(9):
        for kx in range(3):
            source, lane = (blocks[7], 16 * pair) if pair < 8 else (blocks[6], 96)
            one_ref[3 * pair + kx] = source[4 * kx : 4 * kx + 4, lane : lane + 16]


def routes():
    def number(zh, x, core, y, zl):
        return ((zh * 4 + x) * 2 + core) * 8 + y * 2 + zl

    every = list(itertools.product(range(2), range(4), range(2), range(4), range(2)))
    cores = [(number(*d), number(d[0], d[1], 1 - d[2], d[3], d[4])) for d in every]
    along_x = [[(number(*d), number(d[0], (d[1] + j) % 4, *d[2:])) for d in every] for j in (1, 3, 2)]
    along_y = [[(number(*d), number(*d[:3], (d[3] + j) % 4, d[4])) for d in every] for j in (1, 3, 2)]
    along_z = []
    for j in (1, 3, 2):
        pairs = []
        for d in every:
            z = (2 * d[0] + d[4] + j) % 4
            pairs.append((number(*d), number(z // 2, d[1], d[2], d[3], z % 2)))
        along_z.append(pairs)
    return cores, [along_x, along_y, along_z]


def body(inputs, pre_act, out_grad, conv1_weight, conv2_weight):
    shape = jax.ShapeDtypeStruct
    cores, stages = routes()
    strips = call(
        cut_kernel, "cut", shape((8, WIDE, 512), BF16),
        [pltpu.VMEM((4, 512, 128), F32), pltpu.VMEM((512, 512), BF16)], [out_grad[0, 0]], 3e8, 1.2e6,
    )
    strips = lax.all_to_all(strips, "space", 0, 0, tiled=True)
    keep, send, edges = call(
        turn_kernel, "turn",
        [shape((10, WIDE, 128), BF16), shape((10, WIDE, 128), BF16), shape((2, 8, 8, 128), BF16)],
        [], [pre_act[0, 0], inputs[0, 0]], 1e8, 1e6,
    )
    swap = [(i, i ^ 1) for i in range(8)]
    recv = lax.ppermute(send, "space", swap)
    near = [(i, i + 2) for i in (0, 2, 4)] + [(i, i - 2) for i in (3, 5, 7)]
    far = [(i, i + 1) for i in (1, 3, 5)] + [(i, i - 1) for i in (2, 4, 6)]
    near = lax.ppermute(edges[0], "space", near)
    far = lax.ppermute(edges[1], "space", far)
    pre, hid, ins = call(
        join_kernel, "join",
        [shape((8, PAD, 256), BF16), shape((768, ROWS), BF16), shape((192, ROWS), BF16)],
        [pltpu.VMEM((ROWS, 256), F32), pltpu.VMEM((ROWS, 128), F32)], [keep, recv, near, far], 1e7, 2e6,
    )
    wide, thin = call(
        band_kernel, "band", [shape((1536, 768), BF16), shape((768, 384), BF16)], [],
        [conv2_weight.transpose(0, 2, 1).reshape(864, 16), conv1_weight.transpose(0, 2, 1).reshape(432, 4)], 1e7, 3e6,
    )
    own, give, mine, rest = call(
        grads_kernel, "grads",
        [shape((4, 32, 128), BF16), shape((4, 32, 128), BF16), shape((64, 128), F32), shape((64, 128), F32)],
        [
            pltpu.VMEM((10 * PAD, 512), BF16), pltpu.VMEM((10 * PAD, 256), BF16),
            pltpu.VMEM((ROWS, 128), F32), pltpu.VMEM((768, 512), F32),
        ],
        [strips, pre, hid, ins, wide, thin], 3e9, 4e6,
    )
    total = mine + lax.ppermute(rest, ALL, cores)
    got = lax.ppermute(give, "space", swap)
    for stage in stages:
        parts = [lax.ppermute(total, ALL, pairs) for pairs in stage]
        total = (total + parts[2]) + (parts[0] + parts[1])
    other = lax.ppermute(total, ALL, cores)
    input_grad = call(tile_kernel, "tile", shape((4, 8, 8, 128), BF16), [], [own, got], 1e6, 2e5)
    first, second = call(
        unpack_kernel, "unpack", [shape((27, 4, 16), F32), shape((27, 16, 32), F32)], [], [total, other], 1e6, 2e5
    )
    return input_grad[None, None], first, second


def solution(mesh):
    placed = (
        P("dp", "space", None, None, None, None),
        P("dp", "space", None, None, None, None),
        P("dp", "space", None, None, None),
        P(),
        P(),
    )
    return jax.shard_map(
        body,
        mesh=mesh,
        in_specs=placed,
        out_specs=(P("dp", "space", None, None, None, None), P(), P()),
        check_vma=False,
    )
```

time: 459 us -> 62.2 us (0.14)
  matrix products: 260 us -> 0 us
  local copies, waits for them, and re-layouts: 85.6 us -> 7.01 us
  blocking collectives: 72.2 us -> 0 us
  starting transfers between devices: 20.1 us -> 34.1 us
  Pallas kernels: 0 us -> 11.7 us
  other arithmetic: 7.89 us -> 0.03 us
    conv_general_dilated x2 -> x0, matrix products: 159 us -> none  [correlate(): lax.conv_general_dilated(field[None], kernel, (1, 1, 1), 'VALID', dimensi...]
    transpose x2 -> x0, matrix products: 101 us -> none  [patch_grad(): return result.transpose(2, 3, 4, 0, 1).reshape(27, ins, outs)]
    psum x1 -> x0, blocking collectives: 72.2 us -> none  [body(): first, second = lax.psum((first, second), ('dp', 'space'))]
    conv_general_dilated x9 -> x0, local copies, waits for them, and re-layouts: 38.3 us -> none  [correlate(): lax.conv_general_dilated(field[None], kernel, (1, 1, 1), 'VALID', dimensi...]
    broadcast_in_dim x9 -> x0, local copies, waits for them, and re-layouts: 32.4 us -> none  [the longest x4 23 us: patch_grad(): padded_in[:, None]]
    ppermute x6 -> x15, starting transfers between devices: 13.8 us -> 27.7 us  [the longest x9 14 us: body(): parts = [lax.ppermute(total, ALL, pairs) for pairs in stage]]
    pallas_call x0 -> x7, Pallas kernels: none -> 11.7 us  [call(): pl.pallas_call(kernel, name=name, out_shape=outs, in_specs=[pl.BlockSpec(...]
    ppermute x6 -> x15, waiting for transfers between devices: 0.34 us -> 8.26 us  [the longest x9 5.97 us: body(): parts = [lax.ppermute(total, ALL, pairs) for pairs in stage]]
  transfers between devices with their start and end apart: 7 -> 16, of which waited for: 2 -> 9; matrix products, arithmetic and copies ran while one was open for 18% -> 1% of each run, Pallas kernels for 0% -> 6%
where the time goes in v1:
time: 62.2 us; the launch traced here: 61.9 us
  starting transfers between devices  34.1 us (55%)
  Pallas kernels  11.7 us (19%)
  waiting for transfers between devices  8.26 us (13%)
  local copies, waits for them, and re-layouts  7.01 us (11%)
  between operations  0.76 us (1%)
    ppermute x9, starting transfers between devices, body(): parts = [lax.ppermute(total, ALL, pairs) for pairs in stage]  14 us
    pallas_call x7, Pallas kernels, call(): pl.pallas_call(kernel, name=name, out_shape=outs, in_specs=[pl.BlockSpec(...  11.7 us
    unnamed x15, local copies, waits for them, and re-layouts  6.62 us
    all_to_all x1, starting transfers between devices, body(): strips = lax.all_to_all(strips, 'space', 0, 0, tiled=True)  6.37 us
    ppermute x9, waiting for transfers between devices, body(): parts = [lax.ppermute(total, ALL, pairs) for pairs in stage]  5.97 us
    ppermute x1, starting transfers between devices, body(): other = lax.ppermute(total, ALL, cores)  4.58 us
    ppermute x1, starting transfers between devices, body(): near = lax.ppermute(edges[0], 'space', near)  4.37 us
    ppermute x1, starting transfers between devices, body(): got = lax.ppermute(give, 'space', swap)  1.99 us
  transfers between devices with their start and end apart: 16, of which 9 were waited for; matrix products, arithmetic and copies ran while one was open for 1% of the time, Pallas kernels for 6%

profile of v1, /device:TPU:1, one launch (start us, length us, event | category | flops | bytes accessed | tf_op | source)
XLA Modules:
  0.0 61.9 jit_solution(9993474476595601793)
XLA Ops:
  0.6 0.0 copy-start
  0.6 1.0 %copy-done = bf16[1,1,32,16,512]{4,3,2,1,0:T(8,128)(2,1)S(1)} copy-done((bf16[1,1,32,16,512]{4,3,2,1,0:T(8,128)(2,1)S(1)}, bf16[1,1,32,16,512]{4,3,2,1,0:T(8,128)(2,1)}, u32[]{:S(2)}) %copy-start) | copy-done | bytes 524312
  1.7 0.0 copy-start.6
  1.7 0.0 copy-start.5
  1.7 1.6 %cut.1 = bf16[8,72,512]{2,1,0:T(8,128)(2,1)} custom-call(bf16[32,16,512]{2,1,0:T(8,128)(2,1)S(1)} %bitcast.13), custom_call_target="tpu_custom_call" | custom-call | flops 300000000 | bytes 1200000 | tf_op jit(solution)/shard_map/cut/pallas_call | solution.py:37
  3.3 6.4 %all-to-all-start = ((bf16[8,72,512]{2,1,0:T(8,128)(2,1)}), bf16[8,72,512]{2,1,0:T(8,128)(2,1)S(1)}, u32[]{:S(2)}, u32[]{:S(2)}) async-start(bf16[8,72,512]{2,1,0:T(8,128)(2,1)} %cut.1), calls=%async_computation | async-start | bytes 1179648 | tf_op jit(solution)/shard_map/all_to_all | solution.py:296
  9.7 0.0 copy-start.3
  9.7 0.9 %copy-done.3 = bf16[1,1,16,8,8,128]{5,4,3,2,1,0:T(8,128)(2,1)S(1)} copy-done((bf16[1,1,16,8,8,128]{5,4,3,2,1,0:T(8,128)(2,1)S(1)}, bf16[1,1,16,8,8,128]{5,4,3,2,1,0:T(8,128)(2,1)}, u32[]{:S(2)}) %copy-start.3) | copy-done | bytes 262168
  10.6 0.0 copy-start.4
  10.6 0.8 %copy-done.4 = bf16[1,1,4,8,8,128]{5,4,3,2,1,0:T(8,128)(2,1)S(1)} copy-done((bf16[1,1,4,8,8,128]{5,4,3,2,1,0:T(8,128)(2,1)S(1)}, bf16[1,1,4,8,8,128]{5,4,3,2,1,0:T(8,128)(2,1)}, u32[]{:S(2)}) %copy-start.4) | copy-done | bytes 65560
  11.5 1.4 %turn.1 = (bf16[10,72,128]{2,1,0:T(8,128)(2,1)S(1)}, bf16[10,72,128]{2,1,0:T(8,128)(2,1)S(1)}, bf16[2,8,8,128]{3,2,1,0:T(8,128)(2,1)S(1)}) custom-call(bf16[16,8,8,128]{3,2,1,0:T(8,128)(2,1)S(1)} %bitcast.15, bf16[4,8,8,128]{3,2,1,0:T(8,128)(2,1)S(1)} %bitcast.16), custom_call_target="tpu_custom_call" | custom-call | flops 100000000 | bytes 1000000 | tf_op jit(solution)/shard_map/turn/pallas_call | solution.py:37
  12.9 1.5 %collective-permute-start = (bf16[10,72,128]{2,1,0:T(8,128)(2,1)S(1)}, bf16[10,72,128]{2,1,0:T(8,128)(2,1)S(1)}, u32[]{:S(2)}, u32[]{:S(2)}) collective-permute-start(bf16[10,72,128]{2,1,0:T(8,128)(2,1)S(1)} %get-tuple-element.18), channel_id=1, source_target_pairs={{0,1},{1,0},{2,3},{3,2},{4,5},{5,4},{6,7},{7,6},{8,9},{9,8},{10,11... | collective-permute-start | bytes 552968 | tf_op jit(solution)/shard_map/ppermute | solution.py:303
  14.4 0.7 %collective-permute-start.2 = (bf16[8,8,128]{2,1,0:T(8,128)(2,1)S(1)}, bf16[8,8,128]{2,1,0:T(8,128)(2,1)S(1)}, u32[]{:S(2)}, u32[]{:S(2)}) collective-permute-start(bf16[8,8,128]{2,1,0:T(8,128)(2,1)S(1)} %get-tuple-element.34), channel_id=1, source_target_pairs={{1,2},{3,4},{5,6},{2,1},{4,3},{6,5},{9,10},{11,12},{13,14},{10,9},... | collective-permute-start | bytes 49160 | tf_op jit(solution)/shard_map/ppermute | solution.py:307
  15.1 4.4 %collective-permute-start.1 = (bf16[8,8,128]{2,1,0:T(8,128)(2,1)S(1)}, bf16[8,8,128]{2,1,0:T(8,128)(2,1)S(1)}, u32[]{:S(2)}, u32[]{:S(2)}) collective-permute-start(bf16[8,8,128]{2,1,0:T(8,128)(2,1)S(1)} %get-tuple-element.35), channel_id=1, source_target_pairs={{0,2},{2,4},{4,6},{3,1},{5,3},{7,5},{8,10},{10,12},{12,14},{11,9},... | collective-permute-start | bytes 49160 | tf_op jit(solution)/shard_map/ppermute | solution.py:306
  19.5 0.0 copy-done.6
  19.5 0.2 copy.9
  19.7 0.0 copy-done.5
  19.7 0.2 copy.8
  19.9 1.1 %band.1 = (bf16[1536,768]{1,0:T(8,128)(2,1)S(1)}, bf16[768,384]{1,0:T(8,128)(2,1)S(1)}) custom-call(bf16[864,16]{1,0:T(8,128)(2,1)S(1)} %bitcast.12, bf16[432,4]{1,0:T(8,128)(2,1)S(1)} %bitcast.14), custom_call_target="tpu_custom_call" | custom-call | flops 10000000 | bytes 3000000 | tf_op jit(solution)/shard_map/band/pallas_call | solution.py:37
  21.0 0.0 copy-start.1
  21.0 1.4 %copy-done.1 = bf16[1536,768]{1,0:T(8,128)(2,1)} copy-done((bf16[1536,768]{1,0:T(8,128)(2,1)}, bf16[1536,768]{1,0:T(8,128)(2,1)S(1)}, u32[]{:S(2)}) %copy-start.1) | copy-done | bytes 2359320
  22.4 0.0 collective-permute-done.2.far_ref
  22.4 0.0 collective-permute-done.1.near_ref
  22.4 1.3 %collective-permute-done.recv_ref = bf16[10,72,128]{2,1,0:T(8,128)(2,1)S(1)} collective-permute-done((bf16[10,72,128]{2,1,0:T(8,128)(2,1)S(1)}, bf16[10,72,128]{2,1,0:T(8,128)(2,1)S(1)}, u32[]{:S(2)}, u32[]{:S(2)}) %collective-permute-start) | collective-permute-done | bytes 184352 | tf_op jit(solution)/shard_map/ppermute | solution.py:303
  23.7 0.6 join.1
  24.3 0.0 all-to-all-done.grad_ref
  24.3 0.0 copy-start.2
  24.3 1.7 %copy-done.2 = bf16[1536,768]{1,0:T(8,128)(2,1)S(1)} copy-done((bf16[1536,768]{1,0:T(8,128)(2,1)S(1)}, bf16[1536,768]{1,0:T(8,128)(2,1)}, u32[]{:S(2)}) %copy-start.2) | copy-done | bytes 2359320
  26.0 5.4 %grads.1 = (bf16[4,32,128]{2,1,0:T(8,128)(2,1)S(1)}, bf16[4,32,128]{2,1,0:T(8,128)(2,1)S(1)}, f32[64,128]{1,0:T(8,128)S(1)}, f32[64,128]{1,0:T(8,128)S(1)}) custom-call(bf16[8,72,512]{2,1,0:T(8,128)(2,1)S(1)} %all-to-all-done.grad_ref, bf16[8,80,256]{2,1,0:T(8,128)(2,1)S(1)} %get-tuple-element.20.pre_ref, bf16[768,640]{1,0:T(8,128)(2,1)S(1)} %get-tuple-element.21.hid_ref, ...), custom_call_target="tpu_custom_call" | custom-call | flops 3000000000 | bytes 4000000 | tf_op jit(solution)/shard_map/grads/pallas_call | solution.py:37
  31.4 0.6 collective-permute-start.4
  32.0 0.9 %collective-permute-done.4 = f32[64,128]{1,0:T(8,128)S(1)} collective-permute-done((f32[64,128]{1,0:T(8,128)S(1)}, f32[64,128]{1,0:T(8,128)S(1)}, u32[]{:S(2)}, u32[]{:S(2)}) %collective-permute-start.4) | collective-permute-done | bytes 32800 | tf_op jit(solution)/shard_map/ppermute | solution.py:326
  32.9 2.5 %collective-permute-start.7 = (f32[64,128]{1,0:T(8,128)S(1)}, f32[64,128]{1,0:T(8,128)S(1)}, u32[]{:S(2)}, u32[]{:S(2)}) collective-permute-start(f32[64,128]{1,0:T(8,128)S(1)} %add.30), channel_id=1, source_target_pairs={{0,48},{1,49},{2,50},{3,51},{4,52},{5,53},{6,54},{7,55},{8,56},{9,... | collective-permute-start | bytes 98312 | tf_op jit(solution)/shard_map/ppermute | solution.py:329
  35.4 0.0 collective-permute-start.6
  35.4 1.7 %collective-permute-start.5 = (f32[64,128]{1,0:T(8,128)S(1)}, f32[64,128]{1,0:T(8,128)S(1)}, u32[]{:S(2)}, u32[]{:S(2)}) collective-permute-start(f32[64,128]{1,0:T(8,128)S(1)} %add.30), channel_id=1, source_target_pairs={{0,32},{1,33},{2,34},{3,35},{4,36},{5,37},{6,38},{7,39},{8,40},{9,... | collective-permute-start | bytes 98312 | tf_op jit(solution)/shard_map/ppermute | solution.py:329
  37.1 0.0 collective-permute-done.7
  37.1 2.3 %collective-permute-done.6 = f32[64,128]{1,0:T(8,128)S(1)} collective-permute-done((f32[64,128]{1,0:T(8,128)S(1)}, f32[64,128]{1,0:T(8,128)S(1)}, u32[]{:S(2)}, u32[]{:S(2)}) %collective-permute-start.6) | collective-permute-done | bytes 32800 | tf_op jit(solution)/shard_map/ppermute | solution.py:329
  39.4 0.4 collective-permute-done.5
  39.9 2.6 %collective-permute-start.10 = (f32[64,128]{1,0:T(8,128)S(1)}, f32[64,128]{1,0:T(8,128)S(1)}, u32[]{:S(2)}, u32[]{:S(2)}) collective-permute-start(f32[64,128]{1,0:T(8,128)S(1)} %add_add_fusion.2), channel_id=1, source_target_pairs={{0,6},{1,7},{2,0},{3,1},{4,2},{5,3},{6,4},{7,5},{8,14},{9,15},{10,... | collective-permute-start | bytes 98312 | tf_op jit(solution)/shard_map/ppermute | solution.py:329
  42.5 0.0 collective-permute-start.9
  42.5 2.2 %collective-permute-start.8 = (f32[64,128]{1,0:T(8,128)S(1)}, f32[64,128]{1,0:T(8,128)S(1)}, u32[]{:S(2)}, u32[]{:S(2)}) collective-permute-start(f32[64,128]{1,0:T(8,128)S(1)} %add_add_fusion.2), channel_id=1, source_target_pairs={{0,4},{1,5},{2,6},{3,7},{4,0},{5,1},{6,2},{7,3},{8,12},{9,13},{10,... | collective-permute-start | bytes 98312 | tf_op jit(solution)/shard_map/ppermute | solution.py:329
  44.6 0.0 collective-permute-done.10
  44.6 1.8 %collective-permute-done.9 = f32[64,128]{1,0:T(8,128)S(1)} collective-permute-done((f32[64,128]{1,0:T(8,128)S(1)}, f32[64,128]{1,0:T(8,128)S(1)}, u32[]{:S(2)}, u32[]{:S(2)}) %collective-permute-start.9) | collective-permute-done | bytes 32800 | tf_op jit(solution)/shard_map/ppermute | solution.py:329
  46.4 0.3 collective-permute-done.8
  46.8 3.8 %collective-permute-start.13 = (f32[64,128]{1,0:T(8,128)S(1)}, f32[64,128]{1,0:T(8,128)S(1)}, u32[]{:S(2)}, u32[]{:S(2)}) collective-permute-start(f32[64,128]{1,0:T(8,128)S(1)} %add_add_fusion.1), channel_id=1, source_target_pairs={{0,65},{1,0},{2,67},{3,2},{4,69},{5,4},{6,71},{7,6},{8,73},{9,8},{... | collective-permute-start | bytes 98312 | tf_op jit(solution)/shard_map/ppermute | solution.py:329
  50.6 0.0 collective-permute-start.12
  50.6 1.3 %collective-permute-start.11 = (f32[64,128]{1,0:T(8,128)S(1)}, f32[64,128]{1,0:T(8,128)S(1)}, u32[]{:S(2)}, u32[]{:S(2)}) collective-permute-start(f32[64,128]{1,0:T(8,128)S(1)} %add_add_fusion.1), channel_id=1, source_target_pairs={{0,64},{1,65},{2,66},{3,67},{4,68},{5,69},{6,70},{7,71},{8,72},{9,... | collective-permute-start | bytes 98312 | tf_op jit(solution)/shard_map/ppermute | solution.py:329
  51.8 2.0 %collective-permute-start.3 = (bf16[4,32,128]{2,1,0:T(8,128)(2,1)S(1)}, bf16[4,32,128]{2,1,0:T(8,128)(2,1)S(1)}, u32[]{:S(2)}, u32[]{:S(2)}) collective-permute-start(bf16[4,32,128]{2,1,0:T(8,128)(2,1)S(1)} %get-tuple-element.26), channel_id=1, source_target_pairs={{0,1},{1,0},{2,3},{3,2},{4,5},{5,4},{6,7},{7,6},{8,9},{9,8},{10,11... | collective-permute-start | bytes 98312 | tf_op jit(solution)/shard_map/ppermute | solution.py:327
  53.8 0.0 collective-permute-done.13
  53.8 0.7 %collective-permute-done.12 = f32[64,128]{1,0:T(8,128)S(1)} collective-permute-done((f32[64,128]{1,0:T(8,128)S(1)}, f32[64,128]{1,0:T(8,128)S(1)}, u32[]{:S(2)}, u32[]{:S(2)}) %collective-permute-start.12) | collective-permute-done | bytes 32800 | tf_op jit(solution)/shard_map/ppermute | solution.py:329
  54.5 0.3 collective-permute-done.11
  54.9 4.6 %collective-permute-start.14 = (f32[64,128]{1,0:T(8,128)S(1)}, f32[64,128]{1,0:T(8,128)S(1)}, u32[]{:S(2)}, u32[]{:S(2)}) collective-permute-start(f32[64,128]{1,0:T(8,128)S(1)} %add_add_fusion.mine_ref), channel_id=1, source_target_pairs={{0,8},{1,9},{2,10},{3,11},{4,12},{5,13},{6,14},{7,15},{8,0},{9,1},... | collective-permute-start | bytes 98312 | tf_op jit(solution)/shard_map/ppermute | solution.py:331
  59.5 0.0 collective-permute-done.3.recv_ref
  59.5 0.7 %tile.1 = bf16[4,8,8,128]{3,2,1,0:T(8,128)(2,1)} custom-call(bf16[4,32,128]{2,1,0:T(8,128)(2,1)S(1)} %get-tuple-element.25.own_ref, bf16[4,32,128]{2,1,0:T(8,128)(2,1)S(1)} %collective-permute-done.3.recv_ref), custom_call_target="tpu_custom_call" | custom-call | flops 1000000 | bytes 200000 | tf_op jit(solution)/shard_map/tile/pallas_call | solution.py:37
  60.2 0.1 collective-permute-done.14.rest_ref
  60.3 0.8 %unpack.1 = (f32[27,4,16]{2,1,0:T(4,128)S(1)}, f32[27,16,32]{2,1,0:T(8,128)}) custom-call(f32[64,128]{1,0:T(8,128)S(1)} %add_add_fusion.mine_ref, f32[64,128]{1,0:T(8,128)S(1)} %collective-permute-done.14.rest_ref), custom_call_target="tpu_custom_call" | custom-call | flops 1000000 | bytes 200000 | tf_op jit(solution)/shard_map/unpack/pallas_call | solution.py:37
  61.1 0.7 %copy.10 = f32[27,4,16]{0,2,1:T(8,128)} copy(f32[27,4,16]{2,1,0:T(4,128)S(1)} %get-tuple-element.32) | data formatting | bytes 13824
  (5 shorter events, 0.0 us)
Async XLA Ops:
  0.6 1.0 %copy-start = (bf16[1,1,32,16,512]{4,3,2,1,0:T(8,128)(2,1)S(1)}, bf16[1,1,32,16,512]{4,3,2,1,0:T(8,128)(2,1)}, u32[]{:S(2)}) copy-start(bf16[1,1,32,16,512]{4,3,2,1,0:T(8,128)(2,1)} %param.7) | copy-start | bytes 1572868
  1.7 17.8 %copy-start.6 = (bf16[27,4,16]{0,2,1:T(8,128)(2,1)S(1)}, bf16[27,4,16]{0,2,1:T(8,128)(2,1)}, u32[]{:S(2)}) copy-start(bf16[27,4,16]{0,2,1:T(8,128)(2,1)} %param.8) | copy-start | bytes 10372
  1.7 18.0 %copy-start.5 = (bf16[27,16,32]{2,1,0:T(8,128)(2,1)S(1)}, bf16[27,16,32]{2,1,0:T(8,128)(2,1)}, u32[]{:S(2)}) copy-start(bf16[27,16,32]{2,1,0:T(8,128)(2,1)} %param.9) | copy-start | bytes 82948
  3.3 21.0 %all-to-all-start = ((bf16[8,72,512]{2,1,0:T(8,128)(2,1)}), bf16[8,72,512]{2,1,0:T(8,128)(2,1)S(1)}, u32[]{:S(2)}, u32[]{:S(2)}) async-start(bf16[8,72,512]{2,1,0:T(8,128)(2,1)} %cut.1), calls=%async_computation | async-start | bytes 1179648 | tf_op jit(solution)/shard_map/all_to_all | solution.py:296
  9.7 0.9 %copy-start.3 = (bf16[1,1,16,8,8,128]{5,4,3,2,1,0:T(8,128)(2,1)S(1)}, bf16[1,1,16,8,8,128]{5,4,3,2,1,0:T(8,128)(2,1)}, u32[]{:S(2)}) copy-start(bf16[1,1,16,8,8,128]{5,4,3,2,1,0:T(8,128)(2,1)} %param.6) | copy-start | bytes 786436
  10.6 0.8 %copy-start.4 = (bf16[1,1,4,8,8,128]{5,4,3,2,1,0:T(8,128)(2,1)S(1)}, bf16[1,1,4,8,8,128]{5,4,3,2,1,0:T(8,128)(2,1)}, u32[]{:S(2)}) copy-start(bf16[1,1,4,8,8,128]{5,4,3,2,1,0:T(8,128)(2,1)} %param.5) | copy-start | bytes 196612
  12.9 10.8 %collective-permute-start = (bf16[10,72,128]{2,1,0:T(8,128)(2,1)S(1)}, bf16[10,72,128]{2,1,0:T(8,128)(2,1)S(1)}, u32[]{:S(2)}, u32[]{:S(2)}) collective-permute-start(bf16[10,72,128]{2,1,0:T(8,128)(2,1)S(1)} %get-tuple-element.18), channel_id=1, source_target_pairs={{0,1},{1,0},{2,3},{3,2},{4,5},{5,4},{6,7},{7,6},{8,9},{9,8},{10,11... | collective-permute-start | bytes 552968 | tf_op jit(solution)/shard_map/ppermute | solution.py:303
  14.4 8.0 %collective-permute-start.2 = (bf16[8,8,128]{2,1,0:T(8,128)(2,1)S(1)}, bf16[8,8,128]{2,1,0:T(8,128)(2,1)S(1)}, u32[]{:S(2)}, u32[]{:S(2)}) collective-permute-start(bf16[8,8,128]{2,1,0:T(8,128)(2,1)S(1)} %get-tuple-element.34), channel_id=1, source_target_pairs={{1,2},{3,4},{5,6},{2,1},{4,3},{6,5},{9,10},{11,12},{13,14},{10,9},... | collective-permute-start | bytes 49160 | tf_op jit(solution)/shard_map/ppermute | solution.py:307
  15.1 7.3 %collective-permute-start.1 = (bf16[8,8,128]{2,1,0:T(8,128)(2,1)S(1)}, bf16[8,8,128]{2,1,0:T(8,128)(2,1)S(1)}, u32[]{:S(2)}, u32[]{:S(2)}) collective-permute-start(bf16[8,8,128]{2,1,0:T(8,128)(2,1)S(1)} %get-tuple-element.35), channel_id=1, source_target_pairs={{0,2},{2,4},{4,6},{3,1},{5,3},{7,5},{8,10},{10,12},{12,14},{11,9},... | collective-permute-start | bytes 49160 | tf_op jit(solution)/shard_map/ppermute | solution.py:306
  21.0 1.4 %copy-start.1 = (bf16[1536,768]{1,0:T(8,128)(2,1)}, bf16[1536,768]{1,0:T(8,128)(2,1)S(1)}, u32[]{:S(2)}) copy-start(bf16[1536,768]{1,0:T(8,128)(2,1)S(1)} %get-tuple-element.23.wide_ref) | copy-start | bytes 7077892
  24.3 1.7 %copy-start.2 = (bf16[1536,768]{1,0:T(8,128)(2,1)S(1)}, bf16[1536,768]{1,0:T(8,128)(2,1)}, u32[]{:S(2)}) copy-start(bf16[1536,768]{1,0:T(8,128)(2,1)} %copy-done.1) | copy-start | bytes 7077892
  31.4 1.4 %collective-permute-start.4 = (f32[64,128]{1,0:T(8,128)S(1)}, f32[64,128]{1,0:T(8,128)S(1)}, u32[]{:S(2)}, u32[]{:S(2)}) collective-permute-start(f32[64,128]{1,0:T(8,128)S(1)} %get-tuple-element.28), channel_id=1, source_target_pairs={{0,8},{1,9},{2,10},{3,11},{4,12},{5,13},{6,14},{7,15},{8,0},{9,1},... | collective-permute-start | bytes 98312 | tf_op jit(solution)/shard_map/ppermute | solution.py:326
  32.9 4.2 %collective-permute-start.7 = (f32[64,128]{1,0:T(8,128)S(1)}, f32[64,128]{1,0:T(8,128)S(1)}, u32[]{:S(2)}, u32[]{:S(2)}) collective-permute-start(f32[64,128]{1,0:T(8,128)S(1)} %add.30), channel_id=1, source_target_pairs={{0,48},{1,49},{2,50},{3,51},{4,52},{5,53},{6,54},{7,55},{8,56},{9,... | collective-permute-start | bytes 98312 | tf_op jit(solution)/shard_map/ppermute | solution.py:329
  35.4 4.0 %collective-permute-start.6 = (f32[64,128]{1,0:T(8,128)S(1)}, f32[64,128]{1,0:T(8,128)S(1)}, u32[]{:S(2)}, u32[]{:S(2)}) collective-permute-start(f32[64,128]{1,0:T(8,128)S(1)} %add.30), channel_id=1, source_target_pairs={{0,16},{1,17},{2,18},{3,19},{4,20},{5,21},{6,22},{7,23},{8,24},{9,... | collective-permute-start | bytes 98312 | tf_op jit(solution)/shard_map/ppermute | solution.py:329
  35.4 4.5 %collective-permute-start.5 = (f32[64,128]{1,0:T(8,128)S(1)}, f32[64,128]{1,0:T(8,128)S(1)}, u32[]{:S(2)}, u32[]{:S(2)}) collective-permute-start(f32[64,128]{1,0:T(8,128)S(1)} %add.30), channel_id=1, source_target_pairs={{0,32},{1,33},{2,34},{3,35},{4,36},{5,37},{6,38},{7,39},{8,40},{9,... | collective-permute-start | bytes 98312 | tf_op jit(solution)/shard_map/ppermute | solution.py:329
  39.9 4.8 %collective-permute-start.10 = (f32[64,128]{1,0:T(8,128)S(1)}, f32[64,128]{1,0:T(8,128)S(1)}, u32[]{:S(2)}, u32[]{:S(2)}) collective-permute-start(f32[64,128]{1,0:T(8,128)S(1)} %add_add_fusion.2), channel_id=1, source_target_pairs={{0,6},{1,7},{2,0},{3,1},{4,2},{5,3},{6,4},{7,5},{8,14},{9,15},{10,... | collective-permute-start | bytes 98312 | tf_op jit(solution)/shard_map/ppermute | solution.py:329
  42.5 4.0 %collective-permute-start.9 = (f32[64,128]{1,0:T(8,128)S(1)}, f32[64,128]{1,0:T(8,128)S(1)}, u32[]{:S(2)}, u32[]{:S(2)}) collective-permute-start(f32[64,128]{1,0:T(8,128)S(1)} %add_add_fusion.2), channel_id=1, source_target_pairs={{0,2},{1,3},{2,4},{3,5},{4,6},{5,7},{6,0},{7,1},{8,10},{9,11},{10,... | collective-permute-start | bytes 98312 | tf_op jit(solution)/shard_map/ppermute | solution.py:329
  42.5 4.3 %collective-permute-start.8 = (f32[64,128]{1,0:T(8,128)S(1)}, f32[64,128]{1,0:T(8,128)S(1)}, u32[]{:S(2)}, u32[]{:S(2)}) collective-permute-start(f32[64,128]{1,0:T(8,128)S(1)} %add_add_fusion.2), channel_id=1, source_target_pairs={{0,4},{1,5},{2,6},{3,7},{4,0},{5,1},{6,2},{7,3},{8,12},{9,13},{10,... | collective-permute-start | bytes 98312 | tf_op jit(solution)/shard_map/ppermute | solution.py:329
  46.8 7.0 %collective-permute-start.13 = (f32[64,128]{1,0:T(8,128)S(1)}, f32[64,128]{1,0:T(8,128)S(1)}, u32[]{:S(2)}, u32[]{:S(2)}) collective-permute-start(f32[64,128]{1,0:T(8,128)S(1)} %add_add_fusion.1), channel_id=1, source_target_pairs={{0,65},{1,0},{2,67},{3,2},{4,69},{5,4},{6,71},{7,6},{8,73},{9,8},{... | collective-permute-start | bytes 98312 | tf_op jit(solution)/shard_map/ppermute | solution.py:329
  50.6 4.0 %collective-permute-start.12 = (f32[64,128]{1,0:T(8,128)S(1)}, f32[64,128]{1,0:T(8,128)S(1)}, u32[]{:S(2)}, u32[]{:S(2)}) collective-permute-start(f32[64,128]{1,0:T(8,128)S(1)} %add_add_fusion.1), channel_id=1, source_target_pairs={{0,1},{1,64},{2,3},{3,66},{4,5},{5,68},{6,7},{7,70},{8,9},{9,72},{... | collective-permute-start | bytes 98312 | tf_op jit(solution)/shard_map/ppermute | solution.py:329
  50.6 4.3 %collective-permute-start.11 = (f32[64,128]{1,0:T(8,128)S(1)}, f32[64,128]{1,0:T(8,128)S(1)}, u32[]{:S(2)}, u32[]{:S(2)}) collective-permute-start(f32[64,128]{1,0:T(8,128)S(1)} %add_add_fusion.1), channel_id=1, source_target_pairs={{0,64},{1,65},{2,66},{3,67},{4,68},{5,69},{6,70},{7,71},{8,72},{9,... | collective-permute-start | bytes 98312 | tf_op jit(solution)/shard_map/ppermute | solution.py:329
  51.8 7.7 %collective-permute-start.3 = (bf16[4,32,128]{2,1,0:T(8,128)(2,1)S(1)}, bf16[4,32,128]{2,1,0:T(8,128)(2,1)S(1)}, u32[]{:S(2)}, u32[]{:S(2)}) collective-permute-start(bf16[4,32,128]{2,1,0:T(8,128)(2,1)S(1)} %get-tuple-element.26), channel_id=1, source_target_pairs={{0,1},{1,0},{2,3},{3,2},{4,5},{5,4},{6,7},{7,6},{8,9},{9,8},{10,11... | collective-permute-start | bytes 98312 | tf_op jit(solution)/shard_map/ppermute | solution.py:327
  54.9 5.4 %collective-permute-start.14 = (f32[64,128]{1,0:T(8,128)S(1)}, f32[64,128]{1,0:T(8,128)S(1)}, u32[]{:S(2)}, u32[]{:S(2)}) collective-permute-start(f32[64,128]{1,0:T(8,128)S(1)} %add_add_fusion.mine_ref), channel_id=1, source_target_pairs={{0,8},{1,9},{2,10},{3,11},{4,12},{5,13},{6,14},{7,15},{8,0},{9,1},... | collective-permute-start | bytes 98312 | tf_op jit(solution)/shard_map/ppermute | solution.py:331

commit v2 on v1

--- a/solution.py
+++ b/solution.py
@@ -33,58 +33,87 @@
     return lax.dot_general(a, b, (((1,), (1,)), ((), ())), preferred_element_type=F32)
 
 
-def call(kernel, name, outs, scratch, args, flops=1e8, size=4e6):
+def call(kernel, name, outs, scratch, args, flops=1e8, size=4e6, space=pltpu.VMEM, limit=10):
     return pl.pallas_call(
         kernel,
         name=name,
         out_shape=outs,
-        in_specs=[pl.BlockSpec(memory_space=pltpu.VMEM)] * len(args),
+        in_specs=[pl.BlockSpec(memory_space=space)] * len(args),
         out_specs=jax.tree.map(lambda _: pl.BlockSpec(memory_space=pltpu.VMEM), outs),
         scratch_shapes=scratch,
-        compiler_params=pltpu.CompilerParams(vmem_limit_bytes=40 << 20),
+        compiler_params=pltpu.CompilerParams(vmem_limit_bytes=limit << 20),
         cost_estimate=pl.CostEstimate(flops=int(flops), bytes_accessed=int(size), transcendentals=0),
     )(*args)
 
 
-def cut_kernel(slab_ref, out_ref, wide_ref, turned_ref):
+def plane_rows(ref, z):
+    return ref[:, z].astype(F32).reshape(128, 128).astype(BF16)
+
+
+def row_major():
+    src, dst = iota((128, 128), 0), iota((128, 128), 1)
+    return one_hot((src // 8 == dst % 16) & (src % 8 == dst // 16))
+
+
+def cut_kernel(slab_hbm, pre_hbm, out_ref, slab_ref, pre_ref, wide_ref, turned_ref, sems):
+    copies = [
+        pltpu.make_async_copy(slab_hbm.at[:, :, pl.ds(128 * b, 128)], slab_ref.at[b], sems.at[b]) for b in range(4)
+    ]
+    copies.append(pltpu.make_async_copy(pre_hbm, pre_ref, sems.at[4]))
+    for copy in copies:
+        copy.start()
+    p, x = iota((WIDE, 512), 0), iota((WIDE, 512), 1)
+    gap = jnp.where(p < STRIP + 4, x - p, -9999)
+    pick = jnp.concatenate([jnp.where(gap == STRIP * t - 2, 1.0, 0.0) for t in range(8)], axis=0).astype(BF16)
     for b in range(4):
-        wide_ref[b] = slab_ref[:, :, 128 * b : 128 * b + 128].astype(F32).reshape(512, 128)
-    for y in range(16):
-        for b in range(4):
+        copies[b].wait()
+        wide_ref[b] = slab_ref[b].astype(F32).reshape(512, 128)
+        for y in range(16):
             turned_ref[32 * y : 32 * y + 32, 128 * b : 128 * b + 128] = wide_ref[
                 b, pl.ds(y, 32, stride=16), :
             ].astype(BF16)
-    p, x = iota((WIDE, 512), 0), iota((WIDE, 512), 1)
-    gap = jnp.where(p < STRIP + 4, x - p, -9999)
-    pick = jnp.concatenate([jnp.where(gap == STRIP * t - 2, 1.0, 0.0) for t in range(8)], axis=0)
-    cut = dot_t(pick.astype(BF16), turned_ref[...])
+    copies[4].wait()
+    row, lane = iota((16, 1024), 0), iota((16, 1024), 1)
+    ends = one_hot((lane // 128 == row % 8) & (lane % 128 == jnp.where(row < 8, 127, 0)))
+    edges = dot_t(ends, jnp.concatenate([plane_rows(pre_ref, z) for z in range(8)], axis=1))
+    edges = dot(edges.astype(BF16), row_major())
+    cut = dot_t(pick, turned_ref[...])
+    late = iota((8, 128), 0) >= 4
     for t in range(8):
-        out_ref[t] = cut[WIDE * t : WIDE * t + WIDE].astype(BF16)
-
-
-def turn_kernel(pre_ref, in_ref, keep_ref, send_ref, edge_ref):
+        out_ref[t, :STRIP] = cut[WIDE * t : WIDE * t + STRIP].astype(BF16)
+        last = cut[WIDE * t + STRIP : WIDE * t + WIDE]
+        edge = edges[:8] if t % 2 == 0 else edges[8:]
+        last = jnp.concatenate(
+            [
+                jnp.where(late, pltpu.roll(edge, 4, 0), last[:, :128]),
+                jnp.where(late, edge, last[:, 128:256]),
+                last[:, 256:],
+            ],
+            axis=1,
+        )
+        out_ref[t, STRIP:] = last.astype(BF16)
+
+
+def turn_kernel(pre_hbm, in_hbm, keep_ref, send_ref, pre_ref, in_ref, sems):
+    copies = [
+        pltpu.make_async_copy(pre_hbm, pre_ref, sems.at[0]),
+        pltpu.make_async_copy(in_hbm, in_ref, sems.at[1]),
+    ]
+    for copy in copies:
+        copy.start()
     r = lax.rem(lax.axis_index("space"), 2)
     a, x = iota((WIDE, 128), 0), iota((WIDE, 128), 1)
     gap = jnp.where(a < STRIP + 2, x - a, -9999)
-    first, x1 = iota((8, 128), 0) == 0, iota((8, 128), 1)
     pick = jnp.concatenate(
-        [
-            jnp.where(gap == STRIP * r - 1, 1.0, 0.0),
-            jnp.where(gap == STRIP * (1 - r) - 1, 1.0, 0.0),
-            jnp.where(first & (x1 == 127 * (1 - r)), 1.0, 0.0),
-            jnp.where(first & (x1 == 127 * r), 1.0, 0.0),
-        ],
-        axis=0,
+        [jnp.where(gap == STRIP * r - 1, 1.0, 0.0), jnp.where(gap == STRIP * (1 - r) - 1, 1.0, 0.0)], axis=0
     ).astype(BF16)
-    src, dst = iota((128, 128), 0), iota((128, 128), 1)
-    order = one_hot((src // 8 == dst % 16) & (src % 8 == dst // 16))
+    order = row_major()
+    for copy in copies:
+        copy.wait()
     for z in range(8):
-        rows = pre_ref[:, z].astype(F32).reshape(128, 128).astype(BF16)
-        got = dot(dot_t(pick, rows).astype(BF16), order).astype(BF16).astype(F32)
+        got = dot(dot_t(pick, plane_rows(pre_ref, z)).astype(BF16), order)
         keep_ref[z] = got[:WIDE].astype(BF16)
-        send_ref[z] = got[WIDE : 2 * WIDE].astype(BF16)
-        edge_ref[0, z] = got[2 * WIDE : 2 * WIDE + 8].astype(BF16)
-        edge_ref[1, z] = got[2 * WIDE + 8 :].astype(BF16)
+        send_ref[z] = got[WIDE:].astype(BF16)
     gap = jnp.where(a < STRIP, x - a, -9999)
     pick = jnp.concatenate(
         [jnp.where(gap == STRIP * r, 1.0, 0.0), jnp.where(gap == STRIP * (1 - r), 1.0, 0.0)], axis=0
@@ -98,19 +127,15 @@
         send_ref[8 + half] = got[WIDE:, 128 * half : 128 * half + 128].astype(BF16)
 
 
-def join_kernel(keep_ref, recv_ref, near_ref, far_ref, pre_ref, hid_ref, ins_ref, wide_ref, thin_ref):
+def join_kernel(keep_ref, recv_ref, pre_ref, hid_ref, ins_ref, wide_ref, thin_ref):
     r = lax.rem(lax.axis_index("space"), 2)
     left = r == 0
-    row = iota((WIDE, 128), 0)
-    edge = row == jnp.where(left, 0, STRIP + 1)
     lane = iota((PAD, 128), 1)
     tail = jnp.zeros((PAD - WIDE, 128), F32)
     own = (iota((PAD, 128), 0) >= 1) & (iota((PAD, 128), 0) <= STRIP)
     for z in range(8):
-        mine = jnp.where(edge, near_ref[z].astype(F32)[:1], keep_ref[z].astype(F32))
-        other = jnp.where(edge, far_ref[z].astype(F32)[:1], recv_ref[z].astype(F32))
-        mine = jnp.concatenate([mine, tail], axis=0)
-        other = jnp.concatenate([other, tail], axis=0)
+        mine = jnp.concatenate([keep_ref[z].astype(F32), tail], axis=0)
+        other = jnp.concatenate([recv_ref[z].astype(F32), tail], axis=0)
         for part in range(2):
             value = jnp.where(left, mine, other) if part == 0 else jnp.where(left, other, mine)
             pre_ref[z, :, 128 * part : 128 * part + 128] = value.astype(BF16)
@@ -127,7 +152,9 @@
         turned = wide_ref[:, 128 * part : 128 * part + 128].T
         for kx in range(3):
             shifted = pltpu.roll(turned, 2 - kx, 1) if kx < 2 else turned
-            hid_ref[256 * kx + 128 * part : 256 * kx + 128 * part + 128, :] = shifted.astype(BF16)
+            for y in range(8):
+                at = 48 * (8 * part + y) + 16 * kx
+                hid_ref[at : at + 16, :] = shifted[16 * y : 16 * y + 16].astype(BF16)
     turned = thin_ref[...].T[:64]
     for kx in range(3):
         shifted = pltpu.roll(turned, 2 - kx, 1) if kx < 2 else turned
@@ -181,14 +208,21 @@
     lane = iota((16, 128), 1)
     taps = [None] * 28
     for kz in range(3):
-        terms_s[...] = dot(hid_ref[...], planes(grad_s, kz))
+        for half in range(2):
+            low = 7 * half
+            terms_s[half] = dot(
+                hid_ref[48 * low : 48 * low + 432, :],
+                grad_s[(2 - kz) * PAD : (2 - kz) * PAD + ROWS, 256 * half : 256 * half + 256],
+            )
         for kx in range(3):
             for ky in range(3):
                 total = jnp.zeros((16, 128), F32)
                 for y in range(16):
                     at = y + ky - 1
                     if 0 <= at < 16:
-                        piece = terms_s[256 * kx + 16 * at : 256 * kx + 16 * at + 16, 128 * (y // 4) : 128 * (y // 4) + 128]
+                        half = y // 8
+                        row, col = 48 * (at - 7 * half) + 16 * kx, 128 * (y % 8 // 4)
+                        piece = terms_s[half, row : row + 16, col : col + 128]
                         total = total + jnp.where(lane // 32 == y % 4, piece, 0.0)
                 total = total + pltpu.roll(total, 64, 1)
                 taps[9 * kz + 3 * ky + kx] = total + pltpu.roll(total, 32, 1)
@@ -196,11 +230,17 @@
     left_side = jnp.concatenate([planes(grad_s, kz) for kz in range(3)], axis=1)
     sums = dot(left_side, wide_ref[...])
     act = sums[:, 512:] + pltpu.roll(sums[:, 256:512], ROWS - 1, 0) + pltpu.roll(sums[:, :256], ROWS - 2, 0)
-    act = act.reshape(8, PAD, 256)
-    at = STRIP * space - 1 + iota((8, PAD, 256), 1)
-    inside = (iota((8, PAD, 256), 1) < STRIP + 2) & (at >= 0) & (at < 512)
-    act = act * jnp.where(pre_ref[...].astype(F32) > 0, 1.0, LEAK)
-    act_s[PAD : PAD + ROWS, :] = jnp.where(inside, act, 0.0).reshape(ROWS, 256).astype(BF16)
+    row = iota((PAD, 256), 0)
+    at = STRIP * space - 1 + row
+    inside = (row < STRIP + 2) & (at >= 0) & (at < 512)
+    edge_row = row == jnp.where(left, 0, STRIP + 1)
+    side = jnp.clip(space // 2 * 2 + jnp.where(left, -2, 2), 0, 6)
+    edges = [grad_ref[side + r, STRIP:, :256].astype(F32) for r in range(2)]
+    for z in range(8):
+        beside = [edges[r][4 + z % 4 : 5 + z % 4, 128 * (z // 4) : 128 * (z // 4) + 128] for r in range(2)]
+        pre = jnp.where(edge_row, jnp.concatenate(beside, axis=1), pre_ref[z].astype(F32))
+        value = act[PAD * z : PAD * z + PAD] * jnp.where(pre > 0, 1.0, LEAK)
+        act_s[PAD * (z + 1) : PAD * (z + 2), :] = jnp.where(inside, value, 0.0).astype(BF16)
 
     left_side = jnp.concatenate([planes(act_s, kz) for kz in range(3)], axis=1)
     sums = dot(left_side, thin_ref[...])
@@ -255,17 +295,21 @@
         out_ref[:, z + 4] = far.reshape(4, 8, 128).astype(BF16)
 
 
-def unpack_kernel(mine_ref, rest_ref, one_ref, two_ref):
+def unpack_kernel(mine_ref, rest_ref, one_ref, two_ref, flat_ref):
     first = lax.rem(lax.axis_index("dp"), 2) == 0
     mine, rest = mine_ref[...], rest_ref[...]
     low, high = jnp.where(first, mine, rest), jnp.where(first, rest, mine)
     blocks = [low[16 * q : 16 * q + 16] for q in range(4)] + [high[16 * q : 16 * q + 16] for q in range(4)]
+    for pair in range(9):
+        source, lane = (blocks[7], 16 * pair) if pair < 8 else (blocks[6], 96)
+        source = pltpu.roll(source, 128 - lane, 1) if lane else source
+        for kx in range(3):
+            flat_ref[pl.ds(3 * pair + kx, 4, stride=32), :] = source[4 * kx : 4 * kx + 4]
     for k in range(27):
         two_ref[k] = blocks[k // 4][:, 32 * (k % 4) : 32 * (k % 4) + 32]
-    for pair in range(9):
-        for kx in range(3):
-            source, lane = (blocks[7], 16 * pair) if pair < 8 else (blocks[6], 96)
-            one_ref[3 * pair + kx] = source[4 * kx : 4 * kx + 4, lane : lane + 16]
+    turned = flat_ref[...].T
+    for c in range(4):
+        one_ref[c] = turned[:16, 32 * c : 32 * c + 27]
 
 
 def routes():
@@ -274,13 +318,13 @@
 
     every = list(itertools.product(range(2), range(4), range(2), range(4), range(2)))
     cores = [(number(*d), number(d[0], d[1], 1 - d[2], d[3], d[4])) for d in every]
-    along_x = [[(number(*d), number(d[0], (d[1] + j) % 4, *d[2:])) for d in every] for j in (1, 3, 2)]
-    along_y = [[(number(*d), number(*d[:3], (d[3] + j) % 4, d[4])) for d in every] for j in (1, 3, 2)]
+    along_x = [[(number(*d), number(d[0], d[1] ^ j, *d[2:])) for d in every] for j in (1, 3, 2)]
+    along_y = [[(number(*d), number(*d[:3], d[3] ^ j, d[4])) for d in every] for j in (1, 3, 2)]
     along_z = []
     for j in (1, 3, 2):
         pairs = []
         for d in every:
-            z = (2 * d[0] + d[4] + j) % 4
+            z = (2 * d[0] + d[4]) ^ j
             pairs.append((number(*d), number(z // 2, d[1], d[2], d[3], z % 2)))
         along_z.append(pairs)
     return cores, [along_x, along_y, along_z]
@@ -291,24 +335,24 @@
     cores, stages = routes()
     strips = call(
         cut_kernel, "cut", shape((8, WIDE, 512), BF16),
-        [pltpu.VMEM((4, 512, 128), F32), pltpu.VMEM((512, 512), BF16)], [out_grad[0, 0]], 3e8, 1.2e6,
+        [
+            pltpu.VMEM((4, 32, 16, 128), BF16), pltpu.VMEM((16, 8, 8, 128), BF16), pltpu.VMEM((4, 512, 128), F32),
+            pltpu.VMEM((512, 512), BF16), pltpu.SemaphoreType.DMA((5,)),
+        ],
+        [out_grad[0, 0], pre_act[0, 0]], 3e8, 1.2e6, pl.ANY,
     )
     strips = lax.all_to_all(strips, "space", 0, 0, tiled=True)
-    keep, send, edges = call(
-        turn_kernel, "turn",
-        [shape((10, WIDE, 128), BF16), shape((10, WIDE, 128), BF16), shape((2, 8, 8, 128), BF16)],
-        [], [pre_act[0, 0], inputs[0, 0]], 1e8, 1e6,
+    keep, send = call(
+        turn_kernel, "turn", [shape((10, WIDE, 128), BF16), shape((10, WIDE, 128), BF16)],
+        [pltpu.VMEM((16, 8, 8, 128), BF16), pltpu.VMEM((4, 8, 8, 128), BF16), pltpu.SemaphoreType.DMA((2,))],
+        [pre_act[0, 0], inputs[0, 0]], 1e8, 1e6, pl.ANY,
     )
     swap = [(i, i ^ 1) for i in range(8)]
     recv = lax.ppermute(send, "space", swap)
-    near = [(i, i + 2) for i in (0, 2, 4)] + [(i, i - 2) for i in (3, 5, 7)]
-    far = [(i, i + 1) for i in (1, 3, 5)] + [(i, i - 1) for i in (2, 4, 6)]
-    near = lax.ppermute(edges[0], "space", near)
-    far = lax.ppermute(edges[1], "space", far)
     pre, hid, ins = call(
         join_kernel, "join",
         [shape((8, PAD, 256), BF16), shape((768, ROWS), BF16), shape((192, ROWS), BF16)],
-        [pltpu.VMEM((ROWS, 256), F32), pltpu.VMEM((ROWS, 128), F32)], [keep, recv, near, far], 1e7, 2e6,
+        [pltpu.VMEM((ROWS, 256), F32), pltpu.VMEM((ROWS, 128), F32)], [keep, recv], 1e7, 2e6,
     )
     wide, thin = call(
         band_kernel, "band", [shape((1536, 768), BF16), shape((768, 384), BF16)], [],
@@ -319,21 +363,22 @@
         [shape((4, 32, 128), BF16), shape((4, 32, 128), BF16), shape((64, 128), F32), shape((64, 128), F32)],
         [
             pltpu.VMEM((10 * PAD, 512), BF16), pltpu.VMEM((10 * PAD, 256), BF16),
-            pltpu.VMEM((ROWS, 128), F32), pltpu.VMEM((768, 512), F32),
+            pltpu.VMEM((ROWS, 128), F32), pltpu.VMEM((2, 432, 256), F32),
         ],
-        [strips, pre, hid, ins, wide, thin], 3e9, 4e6,
+        [strips, pre, hid, ins, wide, thin], 3e9, 4e6, limit=20,
     )
     total = mine + lax.ppermute(rest, ALL, cores)
     got = lax.ppermute(give, "space", swap)
     for stage in stages:
         parts = [lax.ppermute(total, ALL, pairs) for pairs in stage]
-        total = (total + parts[2]) + (parts[0] + parts[1])
+        total = (total + parts[0]) + (parts[1] + parts[2])
     other = lax.ppermute(total, ALL, cores)
     input_grad = call(tile_kernel, "tile", shape((4, 8, 8, 128), BF16), [], [own, got], 1e6, 2e5)
     first, second = call(
-        unpack_kernel, "unpack", [shape((27, 4, 16), F32), shape((27, 16, 32), F32)], [], [total, other], 1e6, 2e5
-    )
-    return input_grad[None, None], first, second
+        unpack_kernel, "unpack", [shape((4, 16, 27), F32), shape((27, 16, 32), F32)], [pltpu.VMEM((128, 128), F32)],
+        [total, other], 1e6, 2e5,
+    )
+    return input_grad[None, None], first.transpose(2, 0, 1), second
 
 
 def solution(mesh):

time: 62.2 us -> 60.5 us (0.973)
  waiting for transfers between devices: 8.26 us -> 16 us
  starting transfers between devices: 34.1 us -> 27 us
  local copies, waits for them, and re-layouts: 7.01 us -> 5.48 us
  Pallas kernels: 11.7 us -> 11 us
    ppermute x1, waiting for transfers between devices: 1.29 us -> 6.34 us  [body(): recv = lax.ppermute(send, 'space', swap)]
    ppermute x2 -> x0, starting transfers between devices: 5.02 us -> none  [the longest x1 4.37 us: body(): near = lax.ppermute(edges[0], 'space', near)]
    ppermute x9, starting transfers between devices: 14 us -> 10.9 us  [body(): parts = [lax.ppermute(total, ALL, pairs) for pairs in stage]]
    ppermute x9, waiting for transfers between devices: 5.97 us -> 8.64 us  [body(): parts = [lax.ppermute(total, ALL, pairs) for pairs in stage]]
    unnamed x15 -> x16, local copies, waits for them, and re-layouts: 6.62 us -> 5.09 us
    ppermute x1, starting transfers between devices: 0.59 us -> 1.94 us  [body(): total = mine + lax.ppermute(rest, ALL, cores)]
    pallas_call x7, Pallas kernels: 11.7 us -> 11 us  [call(): pl.pallas_call(kernel, name=name, out_shape=outs, in_specs=[pl.BlockSpec(...]
  transfers between devices with their start and end apart: 16 -> 14, of which waited for: 9 -> 8; matrix products, arithmetic and copies ran while one was open for 1% -> 1% of each run, Pallas kernels for 6% -> 5%
where the time goes in v2:
time: 60.5 us; the launch traced here: 60.2 us
  starting transfers between devices  27 us (45%)
  waiting for transfers between devices  16 us (26%)
  Pallas kernels  11 us (18%)
  local copies, waits for them, and re-layouts  5.48 us (9%)
  between operations  0.76 us (1%)
    pallas_call x7, Pallas kernels, call(): pl.pallas_call(kernel, name=name, out_shape=outs, in_specs=[pl.BlockSpec(...  11 us
    ppermute x9, starting transfers between devices, body(): parts = [lax.ppermute(total, ALL, pairs) for pairs in stage]  10.9 us
    ppermute x9, waiting for transfers between devices, body(): parts = [lax.ppermute(total, ALL, pairs) for pairs in stage]  8.64 us
    all_to_all x1, starting transfers between devices, body(): strips = lax.all_to_all(strips, 'space', 0, 0, tiled=True)  6.39 us
    ppermute x1, waiting for transfers between devices, body(): recv = lax.ppermute(send, 'space', swap)  6.34 us
    unnamed x16, local copies, waits for them, and re-layouts  5.09 us
    ppermute x1, starting transfers between devices, body(): other = lax.ppermute(total, ALL, cores)  4.73 us
    ppermute x1, starting transfers between devices, body(): total = mine + lax.ppermute(rest, ALL, cores)  1.94 us
  transfers between devices with their start and end apart: 14, of which 8 were waited for; matrix products, arithmetic and copies ran while one was open for 1% of the time, Pallas kernels for 5%

profile of v2, /device:TPU:1, one launch (start us, length us, event | category | flops | bytes accessed | tf_op | source)
XLA Modules:
  0.0 60.2 jit_solution(12888003047812678393)
XLA Ops:
  0.6 0.0 copy-start
  0.6 1.0 %copy-done = bf16[1,1,32,16,512]{4,3,2,1,0:T(8,128)(2,1)S(1)} copy-done((bf16[1,1,32,16,512]{4,3,2,1,0:T(8,128)(2,1)S(1)}, bf16[1,1,32,16,512]{4,3,2,1,0:T(8,128)(2,1)}, u32[]{:S(2)}) %copy-start) | copy-done | bytes 524312
  1.7 0.0 copy-start.1
  1.7 0.9 %copy-done.1 = bf16[1,1,16,8,8,128]{5,4,3,2,1,0:T(8,128)(2,1)S(1)} copy-done((bf16[1,1,16,8,8,128]{5,4,3,2,1,0:T(8,128)(2,1)S(1)}, bf16[1,1,16,8,8,128]{5,4,3,2,1,0:T(8,128)(2,1)}, u32[]{:S(2)}) %copy-start.1) | copy-done | bytes 262168
  2.6 0.0 copy-start.2
  2.6 0.0 copy-start.5
  2.6 0.0 copy-start.7
  2.6 0.0 copy-start.6
  2.6 2.2 %cut.1 = bf16[8,72,512]{2,1,0:T(8,128)(2,1)} custom-call(bf16[32,16,512]{2,1,0:T(8,128)(2,1)S(1)} %bitcast.10, bf16[16,8,8,128]{3,2,1,0:T(8,128)(2,1)S(1)} %bitcast.12), custom_call_target="tpu_custom_call" | custom-call | flops 300000000 | bytes 1200000 | tf_op jit(solution)/shard_map/cut/pallas_call | solution.py:37
  4.9 6.4 %all-to-all-start = ((bf16[8,72,512]{2,1,0:T(8,128)(2,1)}), bf16[8,72,512]{2,1,0:T(8,128)(2,1)S(1)}, u32[]{:S(2)}, u32[]{:S(2)}) async-start(bf16[8,72,512]{2,1,0:T(8,128)(2,1)} %cut.1), calls=%async_computation | async-start | bytes 1179648 | tf_op jit(solution)/shard_map/all_to_all | solution.py:344
  11.3 0.0 copy-done.2
  11.3 0.0 copy-done.5
  11.3 0.9 %turn.1 = (bf16[10,72,128]{2,1,0:T(8,128)(2,1)S(1)}, bf16[10,72,128]{2,1,0:T(8,128)(2,1)S(1)}) custom-call(bf16[16,8,8,128]{3,2,1,0:T(8,128)(2,1)S(1)} %bitcast.13, bf16[4,8,8,128]{3,2,1,0:T(8,128)(2,1)S(1)} %bitcast.14), custom_call_target="tpu_custom_call" | custom-call | flops 100000000 | bytes 1000000 | tf_op jit(solution)/shard_map/turn/pallas_call | solution.py:37
  12.2 1.5 %collective-permute-start = (bf16[10,72,128]{2,1,0:T(8,128)(2,1)S(1)}, bf16[10,72,128]{2,1,0:T(8,128)(2,1)S(1)}, u32[]{:S(2)}, u32[]{:S(2)}) collective-permute-start(bf16[10,72,128]{2,1,0:T(8,128)(2,1)S(1)} %get-tuple-element.17), channel_id=1, source_target_pairs={{0,1},{1,0},{2,3},{3,2},{4,5},{5,4},{6,7},{7,6},{8,9},{9,8},{10,11... | collective-permute-start | bytes 552968 | tf_op jit(solution)/shard_map/ppermute | solution.py:351
  13.7 0.0 copy-done.7
  13.7 0.2 copy.9
  13.9 0.0 copy-done.6
  13.9 0.2 copy.8
  14.1 1.1 %band.1 = (bf16[1536,768]{1,0:T(8,128)(2,1)S(1)}, bf16[768,384]{1,0:T(8,128)(2,1)S(1)}) custom-call(bf16[864,16]{1,0:T(8,128)(2,1)S(1)} %bitcast.9, bf16[432,4]{1,0:T(8,128)(2,1)S(1)} %bitcast.11), custom_call_target="tpu_custom_call" | custom-call | flops 10000000 | bytes 3000000 | tf_op jit(solution)/shard_map/band/pallas_call | solution.py:37
  15.2 0.0 copy-start.3
  15.2 1.4 %copy-done.3 = bf16[1536,768]{1,0:T(8,128)(2,1)} copy-done((bf16[1536,768]{1,0:T(8,128)(2,1)}, bf16[1536,768]{1,0:T(8,128)(2,1)S(1)}, u32[]{:S(2)}) %copy-start.3) | copy-done | bytes 2359320
  16.6 6.3 %collective-permute-done.recv_ref = bf16[10,72,128]{2,1,0:T(8,128)(2,1)S(1)} collective-permute-done((bf16[10,72,128]{2,1,0:T(8,128)(2,1)S(1)}, bf16[10,72,128]{2,1,0:T(8,128)(2,1)S(1)}, u32[]{:S(2)}, u32[]{:S(2)}) %collective-permute-start) | collective-permute-done | bytes 184352 | tf_op jit(solution)/shard_map/ppermute | solution.py:351
  23.0 0.6 %join.1 = (bf16[8,80,256]{2,1,0:T(8,128)(2,1)S(1)}, bf16[768,640]{1,0:T(8,128)(2,1)S(1)}, bf16[192,640]{1,0:T(8,128)(2,1)S(1)}) custom-call(bf16[10,72,128]{2,1,0:T(8,128)(2,1)S(1)} %get-tuple-element.16.keep_ref, bf16[10,72,128]{2,1,0:T(8,128)(2,1)S(1)} %collective-permute-done.recv_ref), custom_call_target="tpu_custom_call" | custom-call | flops 10000000 | bytes 2000000 | tf_op jit(solution)/shard_map/join/pallas_call | solution.py:37
  23.6 0.0 all-to-all-done.grad_ref
  23.6 0.0 copy-start.4
  23.6 1.7 %copy-done.4 = bf16[1536,768]{1,0:T(8,128)(2,1)S(1)} copy-done((bf16[1536,768]{1,0:T(8,128)(2,1)S(1)}, bf16[1536,768]{1,0:T(8,128)(2,1)}, u32[]{:S(2)}) %copy-start.4) | copy-done | bytes 2359320
  25.3 4.6 %grads.1 = (bf16[4,32,128]{2,1,0:T(8,128)(2,1)S(1)}, bf16[4,32,128]{2,1,0:T(8,128)(2,1)S(1)}, f32[64,128]{1,0:T(8,128)S(1)}, f32[64,128]{1,0:T(8,128)S(1)}) custom-call(bf16[8,72,512]{2,1,0:T(8,128)(2,1)S(1)} %all-to-all-done.grad_ref, bf16[8,80,256]{2,1,0:T(8,128)(2,1)S(1)} %get-tuple-element.18.pre_ref, bf16[768,640]{1,0:T(8,128)(2,1)S(1)} %get-tuple-element.19.hid_ref, ...), custom_call_target="tpu_custom_call" | custom-call | flops 3000000000 | bytes 4000000 | tf_op jit(solution)/shard_map/grads/pallas_call | solution.py:37
  29.9 1.9 %collective-permute-start.2 = (f32[64,128]{1,0:T(8,128)S(1)}, f32[64,128]{1,0:T(8,128)S(1)}, u32[]{:S(2)}, u32[]{:S(2)}) collective-permute-start(f32[64,128]{1,0:T(8,128)S(1)} %get-tuple-element.26), channel_id=1, source_target_pairs={{0,8},{1,9},{2,10},{3,11},{4,12},{5,13},{6,14},{7,15},{8,0},{9,1},... | collective-permute-start | bytes 98312 | tf_op jit(solution)/shard_map/ppermute | solution.py:370
  31.8 0.9 %collective-permute-done.2 = f32[64,128]{1,0:T(8,128)S(1)} collective-permute-done((f32[64,128]{1,0:T(8,128)S(1)}, f32[64,128]{1,0:T(8,128)S(1)}, u32[]{:S(2)}, u32[]{:S(2)}) %collective-permute-start.2) | collective-permute-done | bytes 32800 | tf_op jit(solution)/shard_map/ppermute | solution.py:370
  32.7 2.7 %collective-permute-start.5 = (f32[64,128]{1,0:T(8,128)S(1)}, f32[64,128]{1,0:T(8,128)S(1)}, u32[]{:S(2)}, u32[]{:S(2)}) collective-permute-start(f32[64,128]{1,0:T(8,128)S(1)} %add.30), channel_id=1, source_target_pairs={{0,32},{1,33},{2,34},{3,35},{4,36},{5,37},{6,38},{7,39},{8,40},{9,... | collective-permute-start | bytes 98312 | tf_op jit(solution)/shard_map/ppermute | solution.py:373
  35.4 0.9 %collective-permute-start.4 = (f32[64,128]{1,0:T(8,128)S(1)}, f32[64,128]{1,0:T(8,128)S(1)}, u32[]{:S(2)}, u32[]{:S(2)}) collective-permute-start(f32[64,128]{1,0:T(8,128)S(1)} %add.30), channel_id=1, source_target_pairs={{0,48},{1,49},{2,50},{3,51},{4,52},{5,53},{6,54},{7,55},{8,56},{9,... | collective-permute-start | bytes 98312 | tf_op jit(solution)/shard_map/ppermute | solution.py:373
  36.3 0.0 collective-permute-start.3
  36.3 0.7 %collective-permute-done.5 = f32[64,128]{1,0:T(8,128)S(1)} collective-permute-done((f32[64,128]{1,0:T(8,128)S(1)}, f32[64,128]{1,0:T(8,128)S(1)}, u32[]{:S(2)}, u32[]{:S(2)}) %collective-permute-start.5) | collective-permute-done | bytes 32800 | tf_op jit(solution)/shard_map/ppermute | solution.py:373
  37.0 2.5 %collective-permute-done.4 = f32[64,128]{1,0:T(8,128)S(1)} collective-permute-done((f32[64,128]{1,0:T(8,128)S(1)}, f32[64,128]{1,0:T(8,128)S(1)}, u32[]{:S(2)}, u32[]{:S(2)}) %collective-permute-start.4) | collective-permute-done | bytes 32800 | tf_op jit(solution)/shard_map/ppermute | solution.py:373
  39.4 0.0 collective-permute-done.3
  39.4 2.8 %collective-permute-start.8 = (f32[64,128]{1,0:T(8,128)S(1)}, f32[64,128]{1,0:T(8,128)S(1)}, u32[]{:S(2)}, u32[]{:S(2)}) collective-permute-start(f32[64,128]{1,0:T(8,128)S(1)} %add_add_fusion.2), channel_id=1, source_target_pairs={{0,4},{1,5},{2,6},{3,7},{4,0},{5,1},{6,2},{7,3},{8,12},{9,13},{10,... | collective-permute-start | bytes 98312 | tf_op jit(solution)/shard_map/ppermute | solution.py:373
  42.2 1.1 %collective-permute-start.7 = (f32[64,128]{1,0:T(8,128)S(1)}, f32[64,128]{1,0:T(8,128)S(1)}, u32[]{:S(2)}, u32[]{:S(2)}) collective-permute-start(f32[64,128]{1,0:T(8,128)S(1)} %add_add_fusion.2), channel_id=1, source_target_pairs={{0,6},{1,7},{2,4},{3,5},{4,2},{5,3},{6,0},{7,1},{8,14},{9,15},{10,... | collective-permute-start | bytes 98312 | tf_op jit(solution)/shard_map/ppermute | solution.py:373
  43.3 0.0 collective-permute-start.6
  43.4 0.4 collective-permute-done.8
  43.8 2.6 %collective-permute-done.7 = f32[64,128]{1,0:T(8,128)S(1)} collective-permute-done((f32[64,128]{1,0:T(8,128)S(1)}, f32[64,128]{1,0:T(8,128)S(1)}, u32[]{:S(2)}, u32[]{:S(2)}) %collective-permute-start.7) | collective-permute-done | bytes 32800 | tf_op jit(solution)/shard_map/ppermute | solution.py:373
  46.4 0.0 collective-permute-done.6
  46.4 3.4 %collective-permute-start.11 = (f32[64,128]{1,0:T(8,128)S(1)}, f32[64,128]{1,0:T(8,128)S(1)}, u32[]{:S(2)}, u32[]{:S(2)}) collective-permute-start(f32[64,128]{1,0:T(8,128)S(1)} %add_add_fusion.1), channel_id=1, source_target_pairs={{0,64},{1,65},{2,66},{3,67},{4,68},{5,69},{6,70},{7,71},{8,72},{9,... | collective-permute-start | bytes 98312 | tf_op jit(solution)/shard_map/ppermute | solution.py:373
  49.8 0.0 collective-permute-start.10
  49.8 0.0 collective-permute-start.9
  49.8 1.5 %collective-permute-start.1 = (bf16[4,32,128]{2,1,0:T(8,128)(2,1)S(1)}, bf16[4,32,128]{2,1,0:T(8,128)(2,1)S(1)}, u32[]{:S(2)}, u32[]{:S(2)}) collective-permute-start(bf16[4,32,128]{2,1,0:T(8,128)(2,1)S(1)} %get-tuple-element.24), channel_id=1, source_target_pairs={{0,1},{1,0},{2,3},{3,2},{4,5},{5,4},{6,7},{7,6},{8,9},{9,8},{10,11... | collective-permute-start | bytes 98312 | tf_op jit(solution)/shard_map/ppermute | solution.py:371
  51.2 0.0 collective-permute-done.11
  51.2 2.5 %collective-permute-done.10 = f32[64,128]{1,0:T(8,128)S(1)} collective-permute-done((f32[64,128]{1,0:T(8,128)S(1)}, f32[64,128]{1,0:T(8,128)S(1)}, u32[]{:S(2)}, u32[]{:S(2)}) %collective-permute-start.10) | collective-permute-done | bytes 32800 | tf_op jit(solution)/shard_map/ppermute | solution.py:373
  53.7 0.0 collective-permute-done.9
  53.8 4.7 %collective-permute-start.12 = (f32[64,128]{1,0:T(8,128)S(1)}, f32[64,128]{1,0:T(8,128)S(1)}, u32[]{:S(2)}, u32[]{:S(2)}) collective-permute-start(f32[64,128]{1,0:T(8,128)S(1)} %add_add_fusion.mine_ref), channel_id=1, source_target_pairs={{0,8},{1,9},{2,10},{3,11},{4,12},{5,13},{6,14},{7,15},{8,0},{9,1},... | collective-permute-start | bytes 98312 | tf_op jit(solution)/shard_map/ppermute | solution.py:375
  58.5 0.0 collective-permute-done.1.recv_ref
  58.5 0.7 %tile.1 = bf16[4,8,8,128]{3,2,1,0:T(8,128)(2,1)} custom-call(bf16[4,32,128]{2,1,0:T(8,128)(2,1)S(1)} %get-tuple-element.23.own_ref, bf16[4,32,128]{2,1,0:T(8,128)(2,1)S(1)} %collective-permute-done.1.recv_ref), custom_call_target="tpu_custom_call" | custom-call | flops 1000000 | bytes 200000 | tf_op jit(solution)/shard_map/tile/pallas_call | solution.py:37
  59.2 0.1 collective-permute-done.12.rest_ref
  59.4 0.9 %unpack.1 = (f32[4,16,27]{2,1,0:T(8,128)}, f32[27,16,32]{2,1,0:T(8,128)}) custom-call(f32[64,128]{1,0:T(8,128)S(1)} %add_add_fusion.mine_ref, f32[64,128]{1,0:T(8,128)S(1)} %collective-permute-done.12.rest_ref), custom_call_target="tpu_custom_call" | custom-call | flops 1000000 | bytes 200000 | tf_op jit(solution)/shard_map/unpack/pallas_call | solution.py:37
  (4 shorter events, 0.0 us)
Async XLA Ops:
  0.6 1.0 %copy-start = (bf16[1,1,32,16,512]{4,3,2,1,0:T(8,128)(2,1)S(1)}, bf16[1,1,32,16,512]{4,3,2,1,0:T(8,128)(2,1)}, u32[]{:S(2)}) copy-start(bf16[1,1,32,16,512]{4,3,2,1,0:T(8,128)(2,1)} %param.7) | copy-start | bytes 1572868
  1.7 0.9 %copy-start.1 = (bf16[1,1,16,8,8,128]{5,4,3,2,1,0:T(8,128)(2,1)S(1)}, bf16[1,1,16,8,8,128]{5,4,3,2,1,0:T(8,128)(2,1)}, u32[]{:S(2)}) copy-start(bf16[1,1,16,8,8,128]{5,4,3,2,1,0:T(8,128)(2,1)} %param.6) | copy-start | bytes 786436
  2.6 8.6 %copy-start.2 = (bf16[1,1,16,8,8,128]{5,4,3,2,1,0:T(8,128)(2,1)S(1)}, bf16[1,1,16,8,8,128]{5,4,3,2,1,0:T(8,128)(2,1)}, u32[]{:S(2)}) copy-start(bf16[1,1,16,8,8,128]{5,4,3,2,1,0:T(8,128)(2,1)} %param.6) | copy-start | bytes 786436
  2.6 8.6 %copy-start.5 = (bf16[1,1,4,8,8,128]{5,4,3,2,1,0:T(8,128)(2,1)S(1)}, bf16[1,1,4,8,8,128]{5,4,3,2,1,0:T(8,128)(2,1)}, u32[]{:S(2)}) copy-start(bf16[1,1,4,8,8,128]{5,4,3,2,1,0:T(8,128)(2,1)} %param.5) | copy-start | bytes 196612
  2.6 11.1 %copy-start.7 = (bf16[27,4,16]{0,2,1:T(8,128)(2,1)S(1)}, bf16[27,4,16]{0,2,1:T(8,128)(2,1)}, u32[]{:S(2)}) copy-start(bf16[27,4,16]{0,2,1:T(8,128)(2,1)} %param.8) | copy-start | bytes 10372
  2.6 11.3 %copy-start.6 = (bf16[27,16,32]{2,1,0:T(8,128)(2,1)S(1)}, bf16[27,16,32]{2,1,0:T(8,128)(2,1)}, u32[]{:S(2)}) copy-start(bf16[27,16,32]{2,1,0:T(8,128)(2,1)} %param.9) | copy-start | bytes 82948
  4.9 18.7 %all-to-all-start = ((bf16[8,72,512]{2,1,0:T(8,128)(2,1)}), bf16[8,72,512]{2,1,0:T(8,128)(2,1)S(1)}, u32[]{:S(2)}, u32[]{:S(2)}) async-start(bf16[8,72,512]{2,1,0:T(8,128)(2,1)} %cut.1), calls=%async_computation | async-start | bytes 1179648 | tf_op jit(solution)/shard_map/all_to_all | solution.py:344
  12.2 10.8 %collective-permute-start = (bf16[10,72,128]{2,1,0:T(8,128)(2,1)S(1)}, bf16[10,72,128]{2,1,0:T(8,128)(2,1)S(1)}, u32[]{:S(2)}, u32[]{:S(2)}) collective-permute-start(bf16[10,72,128]{2,1,0:T(8,128)(2,1)S(1)} %get-tuple-element.17), channel_id=1, source_target_pairs={{0,1},{1,0},{2,3},{3,2},{4,5},{5,4},{6,7},{7,6},{8,9},{9,8},{10,11... | collective-permute-start | bytes 552968 | tf_op jit(solution)/shard_map/ppermute | solution.py:351
  15.2 1.4 %copy-start.3 = (bf16[1536,768]{1,0:T(8,128)(2,1)}, bf16[1536,768]{1,0:T(8,128)(2,1)S(1)}, u32[]{:S(2)}) copy-start(bf16[1536,768]{1,0:T(8,128)(2,1)S(1)} %get-tuple-element.21.wide_ref) | copy-start | bytes 7077892
  23.6 1.7 %copy-start.4 = (bf16[1536,768]{1,0:T(8,128)(2,1)S(1)}, bf16[1536,768]{1,0:T(8,128)(2,1)}, u32[]{:S(2)}) copy-start(bf16[1536,768]{1,0:T(8,128)(2,1)} %copy-done.3) | copy-start | bytes 7077892
  29.9 2.8 %collective-permute-start.2 = (f32[64,128]{1,0:T(8,128)S(1)}, f32[64,128]{1,0:T(8,128)S(1)}, u32[]{:S(2)}, u32[]{:S(2)}) collective-permute-start(f32[64,128]{1,0:T(8,128)S(1)} %get-tuple-element.26), channel_id=1, source_target_pairs={{0,8},{1,9},{2,10},{3,11},{4,12},{5,13},{6,14},{7,15},{8,0},{9,1},... | collective-permute-start | bytes 98312 | tf_op jit(solution)/shard_map/ppermute | solution.py:370
  32.7 4.3 %collective-permute-start.5 = (f32[64,128]{1,0:T(8,128)S(1)}, f32[64,128]{1,0:T(8,128)S(1)}, u32[]{:S(2)}, u32[]{:S(2)}) collective-permute-start(f32[64,128]{1,0:T(8,128)S(1)} %add.30), channel_id=1, source_target_pairs={{0,32},{1,33},{2,34},{3,35},{4,36},{5,37},{6,38},{7,39},{8,40},{9,... | collective-permute-start | bytes 98312 | tf_op jit(solution)/shard_map/ppermute | solution.py:373
  35.4 4.0 %collective-permute-start.4 = (f32[64,128]{1,0:T(8,128)S(1)}, f32[64,128]{1,0:T(8,128)S(1)}, u32[]{:S(2)}, u32[]{:S(2)}) collective-permute-start(f32[64,128]{1,0:T(8,128)S(1)} %add.30), channel_id=1, source_target_pairs={{0,48},{1,49},{2,50},{3,51},{4,52},{5,53},{6,54},{7,55},{8,56},{9,... | collective-permute-start | bytes 98312 | tf_op jit(solution)/shard_map/ppermute | solution.py:373
  36.3 3.1 %collective-permute-start.3 = (f32[64,128]{1,0:T(8,128)S(1)}, f32[64,128]{1,0:T(8,128)S(1)}, u32[]{:S(2)}, u32[]{:S(2)}) collective-permute-start(f32[64,128]{1,0:T(8,128)S(1)} %add.30), channel_id=1, source_target_pairs={{0,16},{1,17},{2,18},{3,19},{4,20},{5,21},{6,22},{7,23},{8,24},{9,... | collective-permute-start | bytes 98312 | tf_op jit(solution)/shard_map/ppermute | solution.py:373
  39.4 4.3 %collective-permute-start.8 = (f32[64,128]{1,0:T(8,128)S(1)}, f32[64,128]{1,0:T(8,128)S(1)}, u32[]{:S(2)}, u32[]{:S(2)}) collective-permute-start(f32[64,128]{1,0:T(8,128)S(1)} %add_add_fusion.2), channel_id=1, source_target_pairs={{0,4},{1,5},{2,6},{3,7},{4,0},{5,1},{6,2},{7,3},{8,12},{9,13},{10,... | collective-permute-start | bytes 98312 | tf_op jit(solution)/shard_map/ppermute | solution.py:373
  42.2 4.2 %collective-permute-start.7 = (f32[64,128]{1,0:T(8,128)S(1)}, f32[64,128]{1,0:T(8,128)S(1)}, u32[]{:S(2)}, u32[]{:S(2)}) collective-permute-start(f32[64,128]{1,0:T(8,128)S(1)} %add_add_fusion.2), channel_id=1, source_target_pairs={{0,6},{1,7},{2,4},{3,5},{4,2},{5,3},{6,0},{7,1},{8,14},{9,15},{10,... | collective-permute-start | bytes 98312 | tf_op jit(solution)/shard_map/ppermute | solution.py:373
  43.3 3.0 %collective-permute-start.6 = (f32[64,128]{1,0:T(8,128)S(1)}, f32[64,128]{1,0:T(8,128)S(1)}, u32[]{:S(2)}, u32[]{:S(2)}) collective-permute-start(f32[64,128]{1,0:T(8,128)S(1)} %add_add_fusion.2), channel_id=1, source_target_pairs={{0,2},{1,3},{2,0},{3,1},{4,6},{5,7},{6,4},{7,5},{8,10},{9,11},{10,... | collective-permute-start | bytes 98312 | tf_op jit(solution)/shard_map/ppermute | solution.py:373
  46.4 4.9 %collective-permute-start.11 = (f32[64,128]{1,0:T(8,128)S(1)}, f32[64,128]{1,0:T(8,128)S(1)}, u32[]{:S(2)}, u32[]{:S(2)}) collective-permute-start(f32[64,128]{1,0:T(8,128)S(1)} %add_add_fusion.1), channel_id=1, source_target_pairs={{0,64},{1,65},{2,66},{3,67},{4,68},{5,69},{6,70},{7,71},{8,72},{9,... | collective-permute-start | bytes 98312 | tf_op jit(solution)/shard_map/ppermute | solution.py:373
  49.8 4.0 %collective-permute-start.10 = (f32[64,128]{1,0:T(8,128)S(1)}, f32[64,128]{1,0:T(8,128)S(1)}, u32[]{:S(2)}, u32[]{:S(2)}) collective-permute-start(f32[64,128]{1,0:T(8,128)S(1)} %add_add_fusion.1), channel_id=1, source_target_pairs={{0,65},{1,64},{2,67},{3,66},{4,69},{5,68},{6,71},{7,70},{8,73},{9,... | collective-permute-start | bytes 98312 | tf_op jit(solution)/shard_map/ppermute | solution.py:373
  49.8 4.0 %collective-permute-start.9 = (f32[64,128]{1,0:T(8,128)S(1)}, f32[64,128]{1,0:T(8,128)S(1)}, u32[]{:S(2)}, u32[]{:S(2)}) collective-permute-start(f32[64,128]{1,0:T(8,128)S(1)} %add_add_fusion.1), channel_id=1, source_target_pairs={{0,1},{1,0},{2,3},{3,2},{4,5},{5,4},{6,7},{7,6},{8,9},{9,8},{10,11... | collective-permute-start | bytes 98312 | tf_op jit(solution)/shard_map/ppermute | solution.py:373
  49.8 8.7 %collective-permute-start.1 = (bf16[4,32,128]{2,1,0:T(8,128)(2,1)S(1)}, bf16[4,32,128]{2,1,0:T(8,128)(2,1)S(1)}, u32[]{:S(2)}, u32[]{:S(2)}) collective-permute-start(bf16[4,32,128]{2,1,0:T(8,128)(2,1)S(1)} %get-tuple-element.24), channel_id=1, source_target_pairs={{0,1},{1,0},{2,3},{3,2},{4,5},{5,4},{6,7},{7,6},{8,9},{9,8},{10,11... | collective-permute-start | bytes 98312 | tf_op jit(solution)/shard_map/ppermute | solution.py:371
  53.8 5.6 %collective-permute-start.12 = (f32[64,128]{1,0:T(8,128)S(1)}, f32[64,128]{1,0:T(8,128)S(1)}, u32[]{:S(2)}, u32[]{:S(2)}) collective-permute-start(f32[64,128]{1,0:T(8,128)S(1)} %add_add_fusion.mine_ref), channel_id=1, source_target_pairs={{0,8},{1,9},{2,10},{3,11},{4,12},{5,13},{6,14},{7,15},{8,0},{9,1},... | collective-permute-start | bytes 98312 | tf_op jit(solution)/shard_map/ppermute | solution.py:375

commit v3 on v2

--- a/solution.py
+++ b/solution.py
@@ -12,6 +12,7 @@
 WIDE = 72
 PAD = 80
 ROWS = 8 * PAD
+FULL = 62
 ALL = ("dp", "space")
 F32 = jnp.float32
 BF16 = jnp.bfloat16
@@ -33,13 +34,16 @@
     return lax.dot_general(a, b, (((1,), (1,)), ((), ())), preferred_element_type=F32)
 
 
-def call(kernel, name, outs, scratch, args, flops=1e8, size=4e6, space=pltpu.VMEM, limit=10):
+def call(kernel, name, outs, scratch, args, flops, size, limit=10, far_args=()):
+    def spec(far):
+        return pl.BlockSpec(memory_space=pltpu.HBM if far else pltpu.VMEM)
+
     return pl.pallas_call(
         kernel,
         name=name,
         out_shape=outs,
-        in_specs=[pl.BlockSpec(memory_space=space)] * len(args),
-        out_specs=jax.tree.map(lambda _: pl.BlockSpec(memory_space=pltpu.VMEM), outs),
+        in_specs=[spec(i in far_args) for i in range(len(args))],
+        out_specs=[spec(False)] * len(outs),
         scratch_shapes=scratch,
         compiler_params=pltpu.CompilerParams(vmem_limit_bytes=limit << 20),
         cost_estimate=pl.CostEstimate(flops=int(flops), bytes_accessed=int(size), transcendentals=0),
@@ -55,16 +59,53 @@
     return one_hot((src // 8 == dst % 16) & (src % 8 == dst // 16))
 
 
-def cut_kernel(slab_hbm, pre_hbm, out_ref, slab_ref, pre_ref, wide_ref, turned_ref, sems):
+def turn_kernel(pre_hbm, in_hbm, keep_ref, send_ref, edge_ref, pre_ref, in_ref, sems):
+    copies = [
+        pltpu.make_async_copy(in_hbm, in_ref, sems.at[0]),
+        pltpu.make_async_copy(pre_hbm, pre_ref, sems.at[1]),
+    ]
+    for copy in copies:
+        copy.start()
+    r = lax.rem(lax.axis_index("space"), 2)
+    a, x = iota((WIDE, 128), 0), iota((WIDE, 128), 1)
+    src, dst = iota((256, 256), 0), iota((256, 256), 1)
+    same = (src // 64 == dst // 8 % 4) & (src // 8 % 8 == dst // 32) & (src % 8 == dst % 8)
+    same = one_hot(same)
+    order = row_major()
+    gap = jnp.where(a < STRIP, x - a, -9999)
+    pick = jnp.concatenate(
+        [jnp.where(gap == STRIP * r, 1.0, 0.0), jnp.where(gap == STRIP * (1 - r), 1.0, 0.0)], axis=0
+    ).astype(BF16)
+    copies[0].wait()
+    rows = in_ref[...].astype(F32).reshape(256, 128).astype(BF16)
+    got = dot(dot_t(pick, rows).astype(BF16), same)
+    for half in range(2):
+        keep_ref[8 + half] = got[:WIDE, 128 * half : 128 * half + 128].astype(BF16)
+        send_ref[8 + half] = got[WIDE:, 128 * half : 128 * half + 128].astype(BF16)
+    gap = jnp.where(a < STRIP + 2, x - a, -9999)
+    picks = [jnp.where(gap == STRIP * r - 1, 1.0, 0.0), jnp.where(gap == STRIP * (1 - r) - 1, 1.0, 0.0)]
+    end, x1 = iota((16, 128), 0), iota((16, 128), 1)
+    edges = jnp.zeros((16, 128), F32)
+    copies[1].wait()
+    for z in range(8):
+        ends = jnp.where((end % 8 == z) & (x1 == jnp.where(end < 8, 127, 0)), 1.0, 0.0)
+        pick = jnp.concatenate(picks + [ends], axis=0).astype(BF16)
+        got = dot(dot_t(pick, plane_rows(pre_ref, z)).astype(BF16), order)
+        keep_ref[z] = got[:WIDE].astype(BF16)
+        send_ref[z] = got[WIDE : 2 * WIDE].astype(BF16)
+        edges = edges + got[2 * WIDE :]
+    edge_ref[...] = edges
+
+
+def cut_kernel(slab_hbm, edge_ref, out_ref, slab_ref, wide_ref, turned_ref, sems):
     copies = [
         pltpu.make_async_copy(slab_hbm.at[:, :, pl.ds(128 * b, 128)], slab_ref.at[b], sems.at[b]) for b in range(4)
     ]
-    copies.append(pltpu.make_async_copy(pre_hbm, pre_ref, sems.at[4]))
     for copy in copies:
         copy.start()
     p, x = iota((WIDE, 512), 0), iota((WIDE, 512), 1)
     gap = jnp.where(p < STRIP + 4, x - p, -9999)
-    pick = jnp.concatenate([jnp.where(gap == STRIP * t - 2, 1.0, 0.0) for t in range(8)], axis=0).astype(BF16)
+    strips = jnp.concatenate([jnp.where(gap == STRIP * t - 2, 1.0, 0.0) for t in range(8)], axis=0).astype(BF16)
     for b in range(4):
         copies[b].wait()
         wide_ref[b] = slab_ref[b].astype(F32).reshape(512, 128)
@@ -72,17 +113,12 @@
             turned_ref[32 * y : 32 * y + 32, 128 * b : 128 * b + 128] = wide_ref[
                 b, pl.ds(y, 32, stride=16), :
             ].astype(BF16)
-    copies[4].wait()
-    row, lane = iota((16, 1024), 0), iota((16, 1024), 1)
-    ends = one_hot((lane // 128 == row % 8) & (lane % 128 == jnp.where(row < 8, 127, 0)))
-    edges = dot_t(ends, jnp.concatenate([plane_rows(pre_ref, z) for z in range(8)], axis=1))
-    edges = dot(edges.astype(BF16), row_major())
-    cut = dot_t(pick, turned_ref[...])
+    cut = dot_t(strips, turned_ref[...])
     late = iota((8, 128), 0) >= 4
     for t in range(8):
         out_ref[t, :STRIP] = cut[WIDE * t : WIDE * t + STRIP].astype(BF16)
         last = cut[WIDE * t + STRIP : WIDE * t + WIDE]
-        edge = edges[:8] if t % 2 == 0 else edges[8:]
+        edge = edge_ref[:8] if t % 2 == 0 else edge_ref[8:]
         last = jnp.concatenate(
             [
                 jnp.where(late, pltpu.roll(edge, 4, 0), last[:, :128]),
@@ -94,40 +130,7 @@
         out_ref[t, STRIP:] = last.astype(BF16)
 
 
-def turn_kernel(pre_hbm, in_hbm, keep_ref, send_ref, pre_ref, in_ref, sems):
-    copies = [
-        pltpu.make_async_copy(pre_hbm, pre_ref, sems.at[0]),
-        pltpu.make_async_copy(in_hbm, in_ref, sems.at[1]),
-    ]
-    for copy in copies:
-        copy.start()
-    r = lax.rem(lax.axis_index("space"), 2)
-    a, x = iota((WIDE, 128), 0), iota((WIDE, 128), 1)
-    gap = jnp.where(a < STRIP + 2, x - a, -9999)
-    pick = jnp.concatenate(
-        [jnp.where(gap == STRIP * r - 1, 1.0, 0.0), jnp.where(gap == STRIP * (1 - r) - 1, 1.0, 0.0)], axis=0
-    ).astype(BF16)
-    order = row_major()
-    for copy in copies:
-        copy.wait()
-    for z in range(8):
-        got = dot(dot_t(pick, plane_rows(pre_ref, z)).astype(BF16), order)
-        keep_ref[z] = got[:WIDE].astype(BF16)
-        send_ref[z] = got[WIDE:].astype(BF16)
-    gap = jnp.where(a < STRIP, x - a, -9999)
-    pick = jnp.concatenate(
-        [jnp.where(gap == STRIP * r, 1.0, 0.0), jnp.where(gap == STRIP * (1 - r), 1.0, 0.0)], axis=0
-    ).astype(BF16)
-    src, dst = iota((256, 256), 0), iota((256, 256), 1)
-    same = (src // 64 == dst // 8 % 4) & (src // 8 % 8 == dst // 32) & (src % 8 == dst % 8)
-    rows = in_ref[...].astype(F32).reshape(256, 128).astype(BF16)
-    got = dot(dot_t(pick, rows).astype(BF16), one_hot(same))
-    for half in range(2):
-        keep_ref[8 + half] = got[:WIDE, 128 * half : 128 * half + 128].astype(BF16)
-        send_ref[8 + half] = got[WIDE:, 128 * half : 128 * half + 128].astype(BF16)
-
-
-def join_kernel(keep_ref, recv_ref, pre_ref, hid_ref, ins_ref, wide_ref, thin_ref):
+def join(keep_ref, recv_ref, pre_ref, hid_ref, ins_ref, wide_ref, thin_ref):
     r = lax.rem(lax.axis_index("space"), 2)
     left = r == 0
     lane = iota((PAD, 128), 1)
@@ -161,7 +164,7 @@
         ins_ref[64 * kx : 64 * kx + 64, :] = shifted.astype(BF16)
 
 
-def band_kernel(two_ref, one_ref, wide_ref, thin_ref):
+def band(two_ref, one_ref, wide_refs, thin_ref):
     spread = one_hot(iota((16, 256), 1) % 16 == iota((16, 256), 0))
     two = dot(two_ref[...], spread)
     group = iota((32, 256), 1) // 16
@@ -172,7 +175,7 @@
                 block = jnp.zeros((32, 256), F32)
                 for ky in range(3):
                     block = jnp.where(group == y + ky - 1, terms[ky], block)
-                wide_ref[512 * kz + 32 * y : 512 * kz + 32 * y + 32, 256 * kx : 256 * kx + 256] = block.astype(BF16)
+                wide_refs[kz][32 * y : 32 * y + 32, 256 * kx : 256 * kx + 256] = block.astype(BF16)
     lane = iota((4, 128), 1)
     spread = one_hot((lane < 64) & (lane // 8 % 4 == iota((4, 128), 0)))
     one = dot(one_ref[...], spread)
@@ -188,23 +191,42 @@
                 thin_ref[256 * kz + 16 * y : 256 * kz + 16 * y + 16, 128 * kx : 128 * kx + 128] = block.astype(BF16)
 
 
+def ready_kernel(
+    keep_ref, recv_ref, two_ref, one_ref,
+    pre_ref, hid_ref, ins_ref, wide0_ref, wide1_ref, wide2_ref, thin_ref, hidden_ref, inputs_ref,
+):
+    band(two_ref, one_ref, (wide0_ref, wide1_ref, wide2_ref), thin_ref)
+    join(keep_ref, recv_ref, pre_ref, hid_ref, ins_ref, hidden_ref, inputs_ref)
+
+
 def planes(ref, kz):
     return ref[(2 - kz) * PAD : (2 - kz) * PAD + ROWS, :]
 
 
 def grads_kernel(
-    grad_ref, pre_ref, hid_ref, ins_ref, wide_ref, thin_ref,
+    grad_hbm, pre_hbm, hid_hbm, ins_hbm, wide0_hbm, wide1_hbm, wide2_hbm, thin_hbm,
     own_ref, give_ref, mine_ref, rest_ref, grad_s, act_s, out_s, terms_s,
+    grad_ref, pre_ref, hid_ref, ins_ref, wide0_ref, wide1_ref, wide2_ref, thin_ref, sems,
 ):
+    pairs = [(grad_hbm.at[z], grad_ref.at[z]) for z in range(8)]
+    pairs += [(hid_hbm.at[pl.ds(192 * i, 192)], hid_ref.at[pl.ds(192 * i, 192)]) for i in range(4)]
+    pairs += [(wide0_hbm, wide0_ref), (wide1_hbm, wide1_ref), (wide2_hbm, wide2_ref)]
+    pairs += [(pre_hbm, pre_ref), (thin_hbm, thin_ref), (ins_hbm, ins_ref)]
+    copies = [pltpu.make_async_copy(source, target, sems.at[i]) for i, (source, target) in enumerate(pairs)]
+    for copy in copies:
+        copy.start()
     space = lax.axis_index("space")
     left = lax.rem(space, 2) == 0
     for block in (0, 9):
         grad_s[PAD * block : PAD * block + PAD, :] = jnp.zeros((PAD, 512), BF16)
         act_s[PAD * block : PAD * block + PAD, :] = jnp.zeros((PAD, 256), BF16)
     for z in range(8):
+        copies[z].wait()
         plane = jnp.concatenate([grad_ref[z].astype(F32), jnp.zeros((PAD - WIDE, 512), F32)], axis=0)
         grad_s[PAD * (z + 1) : PAD * (z + 2), :] = plane.astype(BF16)
 
+    for copy in copies[8:12]:
+        copy.wait()
     lane = iota((16, 128), 1)
     taps = [None] * 28
     for kz in range(3):
@@ -227,8 +249,11 @@
                 total = total + pltpu.roll(total, 64, 1)
                 taps[9 * kz + 3 * ky + kx] = total + pltpu.roll(total, 32, 1)
 
-    left_side = jnp.concatenate([planes(grad_s, kz) for kz in range(3)], axis=1)
-    sums = dot(left_side, wide_ref[...])
+    for copy in copies[12:]:
+        copy.wait()
+    sums = dot(planes(grad_s, 0), wide0_ref[...])
+    sums = sums + dot(planes(grad_s, 1), wide1_ref[...])
+    sums = sums + dot(planes(grad_s, 2), wide2_ref[...])
     act = sums[:, 512:] + pltpu.roll(sums[:, 256:512], ROWS - 1, 0) + pltpu.roll(sums[:, :256], ROWS - 2, 0)
     row = iota((PAD, 256), 0)
     at = STRIP * space - 1 + row
@@ -333,30 +358,34 @@
 def body(inputs, pre_act, out_grad, conv1_weight, conv2_weight):
     shape = jax.ShapeDtypeStruct
     cores, stages = routes()
-    strips = call(
-        cut_kernel, "cut", shape((8, WIDE, 512), BF16),
-        [
-            pltpu.VMEM((4, 32, 16, 128), BF16), pltpu.VMEM((16, 8, 8, 128), BF16), pltpu.VMEM((4, 512, 128), F32),
-            pltpu.VMEM((512, 512), BF16), pltpu.SemaphoreType.DMA((5,)),
-        ],
-        [out_grad[0, 0], pre_act[0, 0]], 3e8, 1.2e6, pl.ANY,
-    )
-    strips = lax.all_to_all(strips, "space", 0, 0, tiled=True)
-    keep, send = call(
-        turn_kernel, "turn", [shape((10, WIDE, 128), BF16), shape((10, WIDE, 128), BF16)],
+    keep, send, edges = call(
+        turn_kernel, "turn", [shape((10, WIDE, 128), BF16), shape((10, WIDE, 128), BF16), shape((16, 128), F32)],
         [pltpu.VMEM((16, 8, 8, 128), BF16), pltpu.VMEM((4, 8, 8, 128), BF16), pltpu.SemaphoreType.DMA((2,))],
-        [pre_act[0, 0], inputs[0, 0]], 1e8, 1e6, pl.ANY,
+        [pre_act[0, 0], inputs[0, 0]], 1e8, 1e6, limit=FULL, far_args=(0, 1),
     )
     swap = [(i, i ^ 1) for i in range(8)]
     recv = lax.ppermute(send, "space", swap)
-    pre, hid, ins = call(
-        join_kernel, "join",
-        [shape((8, PAD, 256), BF16), shape((768, ROWS), BF16), shape((192, ROWS), BF16)],
-        [pltpu.VMEM((ROWS, 256), F32), pltpu.VMEM((ROWS, 128), F32)], [keep, recv], 1e7, 2e6,
-    )
-    wide, thin = call(
-        band_kernel, "band", [shape((1536, 768), BF16), shape((768, 384), BF16)], [],
-        [conv2_weight.transpose(0, 2, 1).reshape(864, 16), conv1_weight.transpose(0, 2, 1).reshape(432, 4)], 1e7, 3e6,
+    (strips,) = call(
+        cut_kernel, "cut", [shape((8, WIDE, 512), BF16)],
+        [
+            pltpu.VMEM((4, 32, 16, 128), BF16), pltpu.VMEM((4, 512, 128), F32),
+            pltpu.VMEM((512, 512), BF16), pltpu.SemaphoreType.DMA((4,)),
+        ],
+        [out_grad[0, 0], edges], 4e8, 2e6, limit=FULL, far_args=(0,),
+    )
+    strips = lax.all_to_all(strips, "space", 0, 0, tiled=True)
+    pre, hid, ins, wide0, wide1, wide2, thin = call(
+        ready_kernel, "ready",
+        [
+            shape((8, PAD, 256), BF16), shape((768, ROWS), BF16), shape((192, ROWS), BF16),
+            shape((512, 768), BF16), shape((512, 768), BF16), shape((512, 768), BF16), shape((768, 384), BF16),
+        ],
+        [pltpu.VMEM((ROWS, 256), F32), pltpu.VMEM((ROWS, 128), F32)],
+        [
+            keep, recv, conv2_weight.transpose(0, 2, 1).reshape(864, 16),
+            conv1_weight.transpose(0, 2, 1).reshape(432, 4),
+        ],
+        1e12, 5e6, limit=FULL,
     )
     own, give, mine, rest = call(
         grads_kernel, "grads",
@@ -364,8 +393,11 @@
         [
             pltpu.VMEM((10 * PAD, 512), BF16), pltpu.VMEM((10 * PAD, 256), BF16),
             pltpu.VMEM((ROWS, 128), F32), pltpu.VMEM((2, 432, 256), F32),
+            pltpu.VMEM((8, WIDE, 512), BF16), pltpu.VMEM((8, PAD, 256), BF16), pltpu.VMEM((768, ROWS), BF16),
+            pltpu.VMEM((192, ROWS), BF16), pltpu.VMEM((512, 768), BF16), pltpu.VMEM((512, 768), BF16),
+            pltpu.VMEM((512, 768), BF16), pltpu.VMEM((768, 384), BF16), pltpu.SemaphoreType.DMA((18,)),
         ],
-        [strips, pre, hid, ins, wide, thin], 3e9, 4e6, limit=20,
+        [strips, pre, hid, ins, wide0, wide1, wide2, thin], 3e9, 4e6, limit=FULL, far_args=range(8),
     )
     total = mine + lax.ppermute(rest, ALL, cores)
     got = lax.ppermute(give, "space", swap)
@@ -373,7 +405,7 @@
         parts = [lax.ppermute(total, ALL, pairs) for pairs in stage]
         total = (total + parts[0]) + (parts[1] + parts[2])
     other = lax.ppermute(total, ALL, cores)
-    input_grad = call(tile_kernel, "tile", shape((4, 8, 8, 128), BF16), [], [own, got], 1e6, 2e5)
+    (input_grad,) = call(tile_kernel, "tile", [shape((4, 8, 8, 128), BF16)], [], [own, got], 1e6, 2e5)
     first, second = call(
         unpack_kernel, "unpack", [shape((4, 16, 27), F32), shape((27, 16, 32), F32)], [pltpu.VMEM((128, 128), F32)],
         [total, other], 1e6, 2e5,

time: 60.5 us -> 61.9 us (1.023)
  Pallas kernels: 11 us -> 19.5 us
  waiting for transfers between devices: 16 us -> 12.3 us
  local copies, waits for them, and re-layouts: 5.48 us -> 2.39 us
  starting transfers between devices: 27 us -> 25.8 us
  other arithmetic: 0.03 us -> 0.79 us
    pallas_call x7 -> x6, Pallas kernels: 11 us -> 19.5 us  [call(): pl.pallas_call(kernel, name=name, out_shape=outs, in_specs=[spec(i in far...]
    ppermute x1, waiting for transfers between devices: 6.34 us -> 0.01 us  [body(): recv = lax.ppermute(send, 'space', swap)]
    unnamed x16 -> x10, local copies, waits for them, and re-layouts: 5.09 us -> 0.71 us
    all_to_all x1, waiting for transfers between devices: 0.01 us -> 2.79 us  [body(): strips = lax.all_to_all(strips, 'space', 0, 0, tiled=True)]
    all_to_all x1, starting transfers between devices: 6.39 us -> 4.34 us  [body(): strips = lax.all_to_all(strips, 'space', 0, 0, tiled=True)]
    ppermute x1, starting transfers between devices: 1.53 us -> 2.55 us  [body(): recv = lax.ppermute(send, 'space', swap)]
    add x1, other arithmetic: 0.01 us -> 0.77 us  [body(): total = mine + lax.ppermute(rest, ALL, cores)]
    transpose x1, local copies, waits for them, and re-layouts: 0.16 us -> 0.82 us  [body(): conv2_weight.transpose(0, 2, 1).reshape(864, 16)]
  transfers between devices with their start and end apart: 14 -> 14, of which waited for: 8 -> 8; matrix products, arithmetic and copies ran while one was open for 1% -> 3% of each run, Pallas kernels for 5% -> 13%
where the time goes in v3:
time: 61.9 us; the launch traced here: 61.5 us
  starting transfers between devices  25.8 us (42%)
  Pallas kernels  19.5 us (32%)
  waiting for transfers between devices  12.3 us (20%)
  local copies, waits for them, and re-layouts  2.39 us (4%)
  other arithmetic  0.79 us (1%)
  between operations  0.72 us (1%)
    pallas_call x6, Pallas kernels, call(): pl.pallas_call(kernel, name=name, out_shape=outs, in_specs=[spec(i in far...  19.5 us
    ppermute x9, starting transfers between devices, body(): parts = [lax.ppermute(total, ALL, pairs) for pairs in stage]  10.5 us
    ppermute x9, waiting for transfers between devices, body(): parts = [lax.ppermute(total, ALL, pairs) for pairs in stage]  8.34 us
    ppermute x1, starting transfers between devices, body(): other = lax.ppermute(total, ALL, cores)  5 us
    all_to_all x1, starting transfers between devices, body(): strips = lax.all_to_all(strips, 'space', 0, 0, tiled=True)  4.34 us
    all_to_all x1, waiting for transfers between devices, body(): strips = lax.all_to_all(strips, 'space', 0, 0, tiled=True)  2.79 us
    ppermute x1, starting transfers between devices, body(): recv = lax.ppermute(send, 'space', swap)  2.55 us
    ppermute x1, starting transfers between devices, body(): total = mine + lax.ppermute(rest, ALL, cores)  2.02 us
  transfers between devices with their start and end apart: 14, of which 8 were waited for; matrix products, arithmetic and copies ran while one was open for 3% of the time, Pallas kernels for 13%

profile of v3, /device:TPU:1, one launch (start us, length us, event | category | flops | bytes accessed | tf_op | source)
XLA Modules:
  0.0 61.5 jit_solution(2704702038640342432)
XLA Ops:
  0.6 3.1 %turn.1 = (bf16[10,72,128]{2,1,0:T(8,128)(2,1)}, bf16[10,72,128]{2,1,0:T(8,128)(2,1)}, f32[16,128]{1,0:T(8,128)}) custom-call(bf16[16,8,8,128]{3,2,1,0:T(8,128)(2,1)} %bitcast.15, bf16[4,8,8,128]{3,2,1,0:T(8,128)(2,1)} %bitcast.16), custom_call_target="tpu_custom_call" | custom-call | flops 100000000 | bytes 1000000 | tf_op jit(solution)/shard_map/turn/pallas_call | solution.py:41
  3.8 2.5 %collective-permute-start = (bf16[10,72,128]{2,1,0:T(8,128)(2,1)}, bf16[10,72,128]{2,1,0:T(8,128)(2,1)S(1)}, u32[]{:S(2)}, u32[]{:S(2)}) collective-permute-start(bf16[10,72,128]{2,1,0:T(8,128)(2,1)} %get-tuple-element.21), channel_id=1, source_target_pairs={{0,1},{1,0},{2,3},{3,2},{4,5},{5,4},{6,7},{7,6},{8,9},{9,8},{10,11... | collective-permute-start | bytes 552968 | tf_op jit(solution)/shard_map/ppermute | solution.py:367
  6.3 3.3 %cut.1 = bf16[8,72,512]{2,1,0:T(8,128)(2,1)} custom-call(bf16[32,16,512]{2,1,0:T(8,128)(2,1)} %bitcast.14, f32[16,128]{1,0:T(8,128)} %get-tuple-element.19.edge_ref), custom_call_target="tpu_custom_call" | custom-call | flops 400000000 | bytes 2000000 | tf_op jit(solution)/shard_map/cut/pallas_call | solution.py:41
  9.7 0.0 copy-start.1
  9.7 4.3 %all-to-all-start = ((bf16[8,72,512]{2,1,0:T(8,128)(2,1)}), bf16[8,72,512]{2,1,0:T(8,128)(2,1)}, u32[]{:S(2)}, u32[]{:S(2)}) async-start(bf16[8,72,512]{2,1,0:T(8,128)(2,1)} %cut.1), calls=%async_computation | async-start | bytes 1179648 | tf_op jit(solution)/shard_map/all_to_all | solution.py:376
  14.0 0.0 copy-done.1
  14.0 0.0 copy-start.2
  14.0 0.8 %copy.8 = bf16[27,32,16]{2,1,0:T(8,128)(2,1)} copy(bf16[27,32,16]{1,2,0:T(8,128)(2,1)S(1)} %bitcast.11) | data formatting | bytes 55296 | tf_op jit(solution)/shard_map/transpose | solution.py:385
  14.9 0.0 copy-done.2
  14.9 0.9 %copy.9 = bf16[27,16,4]{2,1,0:T(8,128)(2,1)} copy(bf16[27,16,4]{0,1,2:T(8,128)(2,1)S(1)} %bitcast.13) | data formatting | bytes 6912 | tf_op jit(solution)/shard_map/transpose | solution.py:386
  15.7 0.0 collective-permute-done.recv_ref
  15.7 0.0 copy-start.3
  15.7 0.7 %copy-done.3 = bf16[10,72,128]{2,1,0:T(8,128)(2,1)} copy-done((bf16[10,72,128]{2,1,0:T(8,128)(2,1)}, bf16[10,72,128]{2,1,0:T(8,128)(2,1)S(1)}, u32[]{:S(2)}) %copy-start.3) | copy-done | bytes 184344
  16.4 4.1 %ready.1 = (bf16[8,80,256]{2,1,0:T(8,128)(2,1)}, bf16[768,640]{1,0:T(8,128)(2,1)}, bf16[192,640]{1,0:T(8,128)(2,1)}, bf16[512,768]{1,0:T(8,128)(2,1)}, bf16[512,...) custom-call(bf16[10,72,128]{2,1,0:T(8,128)(2,1)} %get-tuple-element.20.keep_ref, ...), custom_call_target="tpu_custom_call" | custom-call | flops 999999995904 | bytes 5000000 | tf_op jit(solution)/shard_map/ready/pallas_call | solution.py:41
  20.5 2.8 %all-to-all-done.grad_hbm = bf16[8,72,512]{2,1,0:T(8,128)(2,1)} async-done(((bf16[8,72,512]{2,1,0:T(8,128)(2,1)}), bf16[8,72,512]{2,1,0:T(8,128)(2,1)}, u32[]{:S(2)}, u32[]{:S(2)}) %all-to-all-start) | async-done | bytes 589856 | tf_op jit(solution)/shard_map/all_to_all | solution.py:376
  23.3 7.3 %grads.1 = (bf16[4,32,128]{2,1,0:T(8,128)(2,1)}, bf16[4,32,128]{2,1,0:T(8,128)(2,1)}, f32[64,128]{1,0:T(8,128)}, f32[64,128]{1,0:T(8,128)}) custom-call(bf16[8,72,512]{2,1,0:T(8,128)(2,1)} %all-to-all-done.grad_hbm, bf16[8,80,256]{2,1,0:T(8,128)(2,1)} %get-tuple-element.22.pre_hbm, bf16[768,640]{1,0:T(8,128)(2,1)} %get-tuple-element.23.hid_hbm, ...), custom_call_target="tpu_custom_call" | custom-call | flops 3000000000 | bytes 4000000 | tf_op jit(solution)/shard_map/grads/pallas_call | solution.py:41
  30.6 2.0 %collective-permute-start.2 = (f32[64,128]{1,0:T(8,128)}, f32[64,128]{1,0:T(8,128)S(1)}, u32[]{:S(2)}, u32[]{:S(2)}) collective-permute-start(f32[64,128]{1,0:T(8,128)} %get-tuple-element.32), channel_id=1, source_target_pairs={{0,8},{1,9},{2,10},{3,11},{4,12},{5,13},{6,14},{7,15},{8,0},{9,1},... | collective-permute-start | bytes 98312 | tf_op jit(solution)/shard_map/ppermute | solution.py:402
  32.6 1.1 %collective-permute-done.2 = f32[64,128]{1,0:T(8,128)S(1)} collective-permute-done((f32[64,128]{1,0:T(8,128)}, f32[64,128]{1,0:T(8,128)S(1)}, u32[]{:S(2)}, u32[]{:S(2)}) %collective-permute-start.2) | collective-permute-done | bytes 32800 | tf_op jit(solution)/shard_map/ppermute | solution.py:402
  33.7 0.8 %add.30 = f32[64,128]{1,0:T(8,128)S(1)} add(f32[64,128]{1,0:T(8,128)} %get-tuple-element.31, f32[64,128]{1,0:T(8,128)S(1)} %collective-permute-done.2) | non-fusion elementwise | flops 8192 | bytes 98304 | tf_op jit(solution)/shard_map/add | solution.py:402
  34.5 1.2 %collective-permute-start.3 = (f32[64,128]{1,0:T(8,128)S(1)}, f32[64,128]{1,0:T(8,128)S(1)}, u32[]{:S(2)}, u32[]{:S(2)}) collective-permute-start(f32[64,128]{1,0:T(8,128)S(1)} %add.30), channel_id=1, source_target_pairs={{0,16},{1,17},{2,18},{3,19},{4,20},{5,21},{6,22},{7,23},{8,24},{9,... | collective-permute-start | bytes 98312 | tf_op jit(solution)/shard_map/ppermute | solution.py:405
  35.7 1.8 %collective-permute-start.4 = (f32[64,128]{1,0:T(8,128)S(1)}, f32[64,128]{1,0:T(8,128)S(1)}, u32[]{:S(2)}, u32[]{:S(2)}) collective-permute-start(f32[64,128]{1,0:T(8,128)S(1)} %add.30), channel_id=1, source_target_pairs={{0,48},{1,49},{2,50},{3,51},{4,52},{5,53},{6,54},{7,55},{8,56},{9,... | collective-permute-start | bytes 98312 | tf_op jit(solution)/shard_map/ppermute | solution.py:405
  37.5 0.6 %collective-permute-start.5 = (f32[64,128]{1,0:T(8,128)S(1)}, f32[64,128]{1,0:T(8,128)S(1)}, u32[]{:S(2)}, u32[]{:S(2)}) collective-permute-start(f32[64,128]{1,0:T(8,128)S(1)} %add.30), channel_id=1, source_target_pairs={{0,32},{1,33},{2,34},{3,35},{4,36},{5,37},{6,38},{7,39},{8,40},{9,... | collective-permute-start | bytes 98312 | tf_op jit(solution)/shard_map/ppermute | solution.py:405
  38.1 0.0 collective-permute-done.3
  38.1 1.5 %collective-permute-done.4 = f32[64,128]{1,0:T(8,128)S(1)} collective-permute-done((f32[64,128]{1,0:T(8,128)S(1)}, f32[64,128]{1,0:T(8,128)S(1)}, u32[]{:S(2)}, u32[]{:S(2)}) %collective-permute-start.4) | collective-permute-done | bytes 32800 | tf_op jit(solution)/shard_map/ppermute | solution.py:405
  39.7 2.1 %collective-permute-done.5 = f32[64,128]{1,0:T(8,128)S(1)} collective-permute-done((f32[64,128]{1,0:T(8,128)S(1)}, f32[64,128]{1,0:T(8,128)S(1)}, u32[]{:S(2)}, u32[]{:S(2)}) %collective-permute-start.5) | collective-permute-done | bytes 32800 | tf_op jit(solution)/shard_map/ppermute | solution.py:405
  41.8 0.0 copy-start.4
  41.8 0.5 collective-permute-start.6
  42.3 1.0 %collective-permute-start.7 = (f32[64,128]{1,0:T(8,128)S(1)}, f32[64,128]{1,0:T(8,128)S(1)}, u32[]{:S(2)}, u32[]{:S(2)}) collective-permute-start(f32[64,128]{1,0:T(8,128)S(1)} %add_add_fusion.2), channel_id=1, source_target_pairs={{0,6},{1,7},{2,4},{3,5},{4,2},{5,3},{6,0},{7,1},{8,14},{9,15},{10,... | collective-permute-start | bytes 98312 | tf_op jit(solution)/shard_map/ppermute | solution.py:405
  43.3 1.8 %collective-permute-start.8 = (f32[64,128]{1,0:T(8,128)S(1)}, f32[64,128]{1,0:T(8,128)S(1)}, u32[]{:S(2)}, u32[]{:S(2)}) collective-permute-start(f32[64,128]{1,0:T(8,128)S(1)} %add_add_fusion.2), channel_id=1, source_target_pairs={{0,4},{1,5},{2,6},{3,7},{4,0},{5,1},{6,2},{7,3},{8,12},{9,13},{10,... | collective-permute-start | bytes 98312 | tf_op jit(solution)/shard_map/ppermute | solution.py:405
  45.1 0.0 collective-permute-done.6
  45.1 1.2 %collective-permute-done.7 = f32[64,128]{1,0:T(8,128)S(1)} collective-permute-done((f32[64,128]{1,0:T(8,128)S(1)}, f32[64,128]{1,0:T(8,128)S(1)}, u32[]{:S(2)}, u32[]{:S(2)}) %collective-permute-start.7) | collective-permute-done | bytes 32800 | tf_op jit(solution)/shard_map/ppermute | solution.py:405
  46.3 1.5 %collective-permute-done.8 = f32[64,128]{1,0:T(8,128)S(1)} collective-permute-done((f32[64,128]{1,0:T(8,128)S(1)}, f32[64,128]{1,0:T(8,128)S(1)}, u32[]{:S(2)}, u32[]{:S(2)}) %collective-permute-start.8) | collective-permute-done | bytes 32800 | tf_op jit(solution)/shard_map/ppermute | solution.py:405
  47.8 2.7 %collective-permute-start.10 = (f32[64,128]{1,0:T(8,128)S(1)}, f32[64,128]{1,0:T(8,128)S(1)}, u32[]{:S(2)}, u32[]{:S(2)}) collective-permute-start(f32[64,128]{1,0:T(8,128)S(1)} %add_add_fusion.1), channel_id=1, source_target_pairs={{0,65},{1,64},{2,67},{3,66},{4,69},{5,68},{6,71},{7,70},{8,73},{9,... | collective-permute-start | bytes 98312 | tf_op jit(solution)/shard_map/ppermute | solution.py:405
  50.5 0.8 %collective-permute-start.11 = (f32[64,128]{1,0:T(8,128)S(1)}, f32[64,128]{1,0:T(8,128)S(1)}, u32[]{:S(2)}, u32[]{:S(2)}) collective-permute-start(f32[64,128]{1,0:T(8,128)S(1)} %add_add_fusion.1), channel_id=1, source_target_pairs={{0,64},{1,65},{2,66},{3,67},{4,68},{5,69},{6,70},{7,71},{8,72},{9,... | collective-permute-start | bytes 98312 | tf_op jit(solution)/shard_map/ppermute | solution.py:405
  51.3 0.0 collective-permute-start.9
  51.3 0.0 copy-done.4
  51.3 0.0 copy-start
  51.3 1.5 %collective-permute-start.1 = (bf16[4,32,128]{2,1,0:T(8,128)(2,1)S(1)}, bf16[4,32,128]{2,1,0:T(8,128)(2,1)S(1)}, u32[]{:S(2)}, u32[]{:S(2)}) collective-permute-start(bf16[4,32,128]{2,1,0:T(8,128)(2,1)S(1)} %copy-done.4), channel_id=1, source_target_pairs={{0,1},{1,0},{2,3},{3,2},{4,5},{5,4},{6,7},{7,6},{8,9},{9,8},{10,11... | collective-permute-start | bytes 98312 | tf_op jit(solution)/shard_map/ppermute | solution.py:403
  52.8 0.0 collective-permute-done.10
  52.8 2.0 %collective-permute-done.11 = f32[64,128]{1,0:T(8,128)S(1)} collective-permute-done((f32[64,128]{1,0:T(8,128)S(1)}, f32[64,128]{1,0:T(8,128)S(1)}, u32[]{:S(2)}, u32[]{:S(2)}) %collective-permute-start.11) | collective-permute-done | bytes 32800 | tf_op jit(solution)/shard_map/ppermute | solution.py:405
  54.8 0.0 collective-permute-done.9
  54.8 5.0 %collective-permute-start.12 = (f32[64,128]{1,0:T(8,128)S(1)}, f32[64,128]{1,0:T(8,128)S(1)}, u32[]{:S(2)}, u32[]{:S(2)}) collective-permute-start(f32[64,128]{1,0:T(8,128)S(1)} %add_add_fusion.mine_ref), channel_id=1, source_target_pairs={{0,8},{1,9},{2,10},{3,11},{4,12},{5,13},{6,14},{7,15},{8,0},{9,1},... | collective-permute-start | bytes 98312 | tf_op jit(solution)/shard_map/ppermute | solution.py:407
  59.8 0.0 collective-permute-done.1.recv_ref
  59.8 0.0 copy-done
  59.8 0.7 %tile.1 = bf16[4,8,8,128]{3,2,1,0:T(8,128)(2,1)} custom-call(bf16[4,32,128]{2,1,0:T(8,128)(2,1)S(1)} %copy-done, bf16[4,32,128]{2,1,0:T(8,128)(2,1)S(1)} %collective-permute-done.1.recv_ref), custom_call_target="tpu_custom_call" | custom-call | flops 1000000 | bytes 200000 | tf_op jit(solution)/shard_map/tile/pallas_call | solution.py:41
  60.5 0.1 collective-permute-done.12.rest_ref
  60.7 0.9 %unpack.1 = (f32[4,16,27]{2,1,0:T(8,128)}, f32[27,16,32]{2,1,0:T(8,128)}) custom-call(f32[64,128]{1,0:T(8,128)S(1)} %add_add_fusion.mine_ref, f32[64,128]{1,0:T(8,128)S(1)} %collective-permute-done.12.rest_ref), custom_call_target="tpu_custom_call" | custom-call | flops 1000000 | bytes 200000 | tf_op jit(solution)/shard_map/unpack/pallas_call | solution.py:41
  (3 shorter events, 0.0 us)
Async XLA Ops:
  3.8 11.9 %collective-permute-start = (bf16[10,72,128]{2,1,0:T(8,128)(2,1)}, bf16[10,72,128]{2,1,0:T(8,128)(2,1)S(1)}, u32[]{:S(2)}, u32[]{:S(2)}) collective-permute-start(bf16[10,72,128]{2,1,0:T(8,128)(2,1)} %get-tuple-element.21), channel_id=1, source_target_pairs={{0,1},{1,0},{2,3},{3,2},{4,5},{5,4},{6,7},{7,6},{8,9},{9,8},{10,11... | collective-permute-start | bytes 552968 | tf_op jit(solution)/shard_map/ppermute | solution.py:367
  9.7 4.4 %copy-start.1 = (bf16[27,16,32]{2,1,0:T(8,128)(2,1)S(1)}, bf16[27,16,32]{2,1,0:T(8,128)(2,1)}, u32[]{:S(2)}) copy-start(bf16[27,16,32]{2,1,0:T(8,128)(2,1)} %param.9) | copy-start | bytes 82948
  9.7 13.6 %all-to-all-start = ((bf16[8,72,512]{2,1,0:T(8,128)(2,1)}), bf16[8,72,512]{2,1,0:T(8,128)(2,1)}, u32[]{:S(2)}, u32[]{:S(2)}) async-start(bf16[8,72,512]{2,1,0:T(8,128)(2,1)} %cut.1), calls=%async_computation | async-start | bytes 1179648 | tf_op jit(solution)/shard_map/all_to_all | solution.py:376
  14.0 0.8 %copy-start.2 = (bf16[27,4,16]{0,2,1:T(8,128)(2,1)S(1)}, bf16[27,4,16]{0,2,1:T(8,128)(2,1)}, u32[]{:S(2)}) copy-start(bf16[27,4,16]{0,2,1:T(8,128)(2,1)} %param.8) | copy-start | bytes 10372
  15.7 0.7 %copy-start.3 = (bf16[10,72,128]{2,1,0:T(8,128)(2,1)}, bf16[10,72,128]{2,1,0:T(8,128)(2,1)S(1)}, u32[]{:S(2)}) copy-start(bf16[10,72,128]{2,1,0:T(8,128)(2,1)S(1)} %collective-permute-done.recv_ref) | copy-start | bytes 552964
  30.6 3.1 %collective-permute-start.2 = (f32[64,128]{1,0:T(8,128)}, f32[64,128]{1,0:T(8,128)S(1)}, u32[]{:S(2)}, u32[]{:S(2)}) collective-permute-start(f32[64,128]{1,0:T(8,128)} %get-tuple-element.32), channel_id=1, source_target_pairs={{0,8},{1,9},{2,10},{3,11},{4,12},{5,13},{6,14},{7,15},{8,0},{9,1},... | collective-permute-start | bytes 98312 | tf_op jit(solution)/shard_map/ppermute | solution.py:402
  34.5 3.7 %collective-permute-start.3 = (f32[64,128]{1,0:T(8,128)S(1)}, f32[64,128]{1,0:T(8,128)S(1)}, u32[]{:S(2)}, u32[]{:S(2)}) collective-permute-start(f32[64,128]{1,0:T(8,128)S(1)} %add.30), channel_id=1, source_target_pairs={{0,16},{1,17},{2,18},{3,19},{4,20},{5,21},{6,22},{7,23},{8,24},{9,... | collective-permute-start | bytes 98312 | tf_op jit(solution)/shard_map/ppermute | solution.py:405
  35.7 4.0 %collective-permute-start.4 = (f32[64,128]{1,0:T(8,128)S(1)}, f32[64,128]{1,0:T(8,128)S(1)}, u32[]{:S(2)}, u32[]{:S(2)}) collective-permute-start(f32[64,128]{1,0:T(8,128)S(1)} %add.30), channel_id=1, source_target_pairs={{0,48},{1,49},{2,50},{3,51},{4,52},{5,53},{6,54},{7,55},{8,56},{9,... | collective-permute-start | bytes 98312 | tf_op jit(solution)/shard_map/ppermute | solution.py:405
  37.5 4.3 %collective-permute-start.5 = (f32[64,128]{1,0:T(8,128)S(1)}, f32[64,128]{1,0:T(8,128)S(1)}, u32[]{:S(2)}, u32[]{:S(2)}) collective-permute-start(f32[64,128]{1,0:T(8,128)S(1)} %add.30), channel_id=1, source_target_pairs={{0,32},{1,33},{2,34},{3,35},{4,36},{5,37},{6,38},{7,39},{8,40},{9,... | collective-permute-start | bytes 98312 | tf_op jit(solution)/shard_map/ppermute | solution.py:405
  41.8 9.5 %copy-start.4 = (bf16[4,32,128]{2,1,0:T(8,128)(2,1)S(1)}, bf16[4,32,128]{2,1,0:T(8,128)(2,1)}, u32[]{:S(2)}) copy-start(bf16[4,32,128]{2,1,0:T(8,128)(2,1)} %get-tuple-element.30) | copy-start | bytes 98308
  41.8 3.3 %collective-permute-start.6 = (f32[64,128]{1,0:T(8,128)S(1)}, f32[64,128]{1,0:T(8,128)S(1)}, u32[]{:S(2)}, u32[]{:S(2)}) collective-permute-start(f32[64,128]{1,0:T(8,128)S(1)} %add_add_fusion.2), channel_id=1, source_target_pairs={{0,2},{1,3},{2,0},{3,1},{4,6},{5,7},{6,4},{7,5},{8,10},{9,11},{10,... | collective-permute-start | bytes 98312 | tf_op jit(solution)/shard_map/ppermute | solution.py:405
  42.3 4.0 %collective-permute-start.7 = (f32[64,128]{1,0:T(8,128)S(1)}, f32[64,128]{1,0:T(8,128)S(1)}, u32[]{:S(2)}, u32[]{:S(2)}) collective-permute-start(f32[64,128]{1,0:T(8,128)S(1)} %add_add_fusion.2), channel_id=1, source_target_pairs={{0,6},{1,7},{2,4},{3,5},{4,2},{5,3},{6,0},{7,1},{8,14},{9,15},{10,... | collective-permute-start | bytes 98312 | tf_op jit(solution)/shard_map/ppermute | solution.py:405
  43.3 4.5 %collective-permute-start.8 = (f32[64,128]{1,0:T(8,128)S(1)}, f32[64,128]{1,0:T(8,128)S(1)}, u32[]{:S(2)}, u32[]{:S(2)}) collective-permute-start(f32[64,128]{1,0:T(8,128)S(1)} %add_add_fusion.2), channel_id=1, source_target_pairs={{0,4},{1,5},{2,6},{3,7},{4,0},{5,1},{6,2},{7,3},{8,12},{9,13},{10,... | collective-permute-start | bytes 98312 | tf_op jit(solution)/shard_map/ppermute | solution.py:405
  47.8 5.0 %collective-permute-start.10 = (f32[64,128]{1,0:T(8,128)S(1)}, f32[64,128]{1,0:T(8,128)S(1)}, u32[]{:S(2)}, u32[]{:S(2)}) collective-permute-start(f32[64,128]{1,0:T(8,128)S(1)} %add_add_fusion.1), channel_id=1, source_target_pairs={{0,65},{1,64},{2,67},{3,66},{4,69},{5,68},{6,71},{7,70},{8,73},{9,... | collective-permute-start | bytes 98312 | tf_op jit(solution)/shard_map/ppermute | solution.py:405
  50.5 4.3 %collective-permute-start.11 = (f32[64,128]{1,0:T(8,128)S(1)}, f32[64,128]{1,0:T(8,128)S(1)}, u32[]{:S(2)}, u32[]{:S(2)}) collective-permute-start(f32[64,128]{1,0:T(8,128)S(1)} %add_add_fusion.1), channel_id=1, source_target_pairs={{0,64},{1,65},{2,66},{3,67},{4,68},{5,69},{6,70},{7,71},{8,72},{9,... | collective-permute-start | bytes 98312 | tf_op jit(solution)/shard_map/ppermute | solution.py:405
  51.3 3.5 %collective-permute-start.9 = (f32[64,128]{1,0:T(8,128)S(1)}, f32[64,128]{1,0:T(8,128)S(1)}, u32[]{:S(2)}, u32[]{:S(2)}) collective-permute-start(f32[64,128]{1,0:T(8,128)S(1)} %add_add_fusion.1), channel_id=1, source_target_pairs={{0,1},{1,0},{2,3},{3,2},{4,5},{5,4},{6,7},{7,6},{8,9},{9,8},{10,11... | collective-permute-start | bytes 98312 | tf_op jit(solution)/shard_map/ppermute | solution.py:405
  51.3 8.5 %copy-start = (bf16[4,32,128]{2,1,0:T(8,128)(2,1)S(1)}, bf16[4,32,128]{2,1,0:T(8,128)(2,1)}, u32[]{:S(2)}) copy-start(bf16[4,32,128]{2,1,0:T(8,128)(2,1)} %get-tuple-element.29.own_ref) | copy-start | bytes 98308
  51.3 8.5 %collective-permute-start.1 = (bf16[4,32,128]{2,1,0:T(8,128)(2,1)S(1)}, bf16[4,32,128]{2,1,0:T(8,128)(2,1)S(1)}, u32[]{:S(2)}, u32[]{:S(2)}) collective-permute-start(bf16[4,32,128]{2,1,0:T(8,128)(2,1)S(1)} %copy-done.4), channel_id=1, source_target_pairs={{0,1},{1,0},{2,3},{3,2},{4,5},{5,4},{6,7},{7,6},{8,9},{9,8},{10,11... | collective-permute-start | bytes 98312 | tf_op jit(solution)/shard_map/ppermute | solution.py:403
  54.8 5.9 %collective-permute-start.12 = (f32[64,128]{1,0:T(8,128)S(1)}, f32[64,128]{1,0:T(8,128)S(1)}, u32[]{:S(2)}, u32[]{:S(2)}) collective-permute-start(f32[64,128]{1,0:T(8,128)S(1)} %add_add_fusion.mine_ref), channel_id=1, source_target_pairs={{0,8},{1,9},{2,10},{3,11},{4,12},{5,13},{6,14},{7,15},{8,0},{9,1},... | collective-permute-start | bytes 98312 | tf_op jit(solution)/shard_map/ppermute | solution.py:407

commit v4 on v3

--- a/solution.py
+++ b/solution.py
@@ -34,7 +34,7 @@
     return lax.dot_general(a, b, (((1,), (1,)), ((), ())), preferred_element_type=F32)
 
 
-def call(kernel, name, outs, scratch, args, flops, size, limit=10, far_args=()):
+def call(kernel, name, outs, scratch, args, flops, size, limit=10, far_args=(), far_outs=()):
     def spec(far):
         return pl.BlockSpec(memory_space=pltpu.HBM if far else pltpu.VMEM)
 
@@ -43,34 +43,35 @@
         name=name,
         out_shape=outs,
         in_specs=[spec(i in far_args) for i in range(len(args))],
-        out_specs=[spec(False)] * len(outs),
+        out_specs=[spec(i in far_outs) for i in range(len(outs))],
         scratch_shapes=scratch,
         compiler_params=pltpu.CompilerParams(vmem_limit_bytes=limit << 20),
         cost_estimate=pl.CostEstimate(flops=int(flops), bytes_accessed=int(size), transcendentals=0),
     )(*args)
 
 
-def plane_rows(ref, z):
-    return ref[:, z].astype(F32).reshape(128, 128).astype(BF16)
-
-
 def row_major():
     src, dst = iota((128, 128), 0), iota((128, 128), 1)
     return one_hot((src // 8 == dst % 16) & (src % 8 == dst // 16))
 
 
-def turn_kernel(pre_hbm, in_hbm, keep_ref, send_ref, edge_ref, pre_ref, in_ref, sems):
-    copies = [
-        pltpu.make_async_copy(in_hbm, in_ref, sems.at[0]),
-        pltpu.make_async_copy(pre_hbm, pre_ref, sems.at[1]),
+def cut_kernel(
+    slab_hbm, pre_hbm, in_hbm, keep_hbm, send_hbm, out_hbm,
+    slab_ref, pre_ref, in_ref, keep_ref, send_ref, out_ref, wide_ref, turned_ref, sems, done,
+):
+    copies = [pltpu.make_async_copy(in_hbm, in_ref, sems.at[0])]
+    copies += [
+        pltpu.make_async_copy(pre_hbm.at[:, pl.ds(4 * i, 4)], pre_ref.at[i], sems.at[1 + i]) for i in range(2)
+    ]
+    copies += [
+        pltpu.make_async_copy(slab_hbm.at[:, :, pl.ds(128 * b, 128)], slab_ref.at[b], sems.at[3 + b]) for b in range(4)
     ]
     for copy in copies:
         copy.start()
     r = lax.rem(lax.axis_index("space"), 2)
     a, x = iota((WIDE, 128), 0), iota((WIDE, 128), 1)
     src, dst = iota((256, 256), 0), iota((256, 256), 1)
-    same = (src // 64 == dst // 8 % 4) & (src // 8 % 8 == dst // 32) & (src % 8 == dst % 8)
-    same = one_hot(same)
+    same = one_hot((src // 64 == dst // 8 % 4) & (src // 8 % 8 == dst // 32) & (src % 8 == dst % 8))
     order = row_major()
     gap = jnp.where(a < STRIP, x - a, -9999)
     pick = jnp.concatenate(
@@ -86,48 +87,53 @@
     picks = [jnp.where(gap == STRIP * r - 1, 1.0, 0.0), jnp.where(gap == STRIP * (1 - r) - 1, 1.0, 0.0)]
     end, x1 = iota((16, 128), 0), iota((16, 128), 1)
     edges = jnp.zeros((16, 128), F32)
-    copies[1].wait()
     for z in range(8):
+        if z % 4 == 0:
+            copies[1 + z // 4].wait()
         ends = jnp.where((end % 8 == z) & (x1 == jnp.where(end < 8, 127, 0)), 1.0, 0.0)
         pick = jnp.concatenate(picks + [ends], axis=0).astype(BF16)
-        got = dot(dot_t(pick, plane_rows(pre_ref, z)).astype(BF16), order)
+        rows = pre_ref[z // 4, :, z % 4].astype(F32).reshape(128, 128).astype(BF16)
+        got = dot(dot_t(pick, rows).astype(BF16), order)
         keep_ref[z] = got[:WIDE].astype(BF16)
         send_ref[z] = got[WIDE : 2 * WIDE].astype(BF16)
         edges = edges + got[2 * WIDE :]
-    edge_ref[...] = edges
-
-
-def cut_kernel(slab_hbm, edge_ref, out_ref, slab_ref, wide_ref, turned_ref, sems):
-    copies = [
-        pltpu.make_async_copy(slab_hbm.at[:, :, pl.ds(128 * b, 128)], slab_ref.at[b], sems.at[b]) for b in range(4)
+    results = [
+        pltpu.make_async_copy(send_ref, send_hbm, done.at[8]), pltpu.make_async_copy(keep_ref, keep_hbm, done.at[9])
     ]
-    for copy in copies:
+    for copy in results:
         copy.start()
-    p, x = iota((WIDE, 512), 0), iota((WIDE, 512), 1)
-    gap = jnp.where(p < STRIP + 4, x - p, -9999)
-    strips = jnp.concatenate([jnp.where(gap == STRIP * t - 2, 1.0, 0.0) for t in range(8)], axis=0).astype(BF16)
+
     for b in range(4):
-        copies[b].wait()
+        copies[3 + b].wait()
         wide_ref[b] = slab_ref[b].astype(F32).reshape(512, 128)
         for y in range(16):
             turned_ref[32 * y : 32 * y + 32, 128 * b : 128 * b + 128] = wide_ref[
                 b, pl.ds(y, 32, stride=16), :
             ].astype(BF16)
-    cut = dot_t(strips, turned_ref[...])
+    p, x = iota((WIDE, 512), 0), iota((WIDE, 512), 1)
+    gap = jnp.where(p < STRIP + 4, x - p, -9999)
     late = iota((8, 128), 0) >= 4
-    for t in range(8):
-        out_ref[t, :STRIP] = cut[WIDE * t : WIDE * t + STRIP].astype(BF16)
-        last = cut[WIDE * t + STRIP : WIDE * t + WIDE]
-        edge = edge_ref[:8] if t % 2 == 0 else edge_ref[8:]
-        last = jnp.concatenate(
-            [
-                jnp.where(late, pltpu.roll(edge, 4, 0), last[:, :128]),
-                jnp.where(late, edge, last[:, 128:256]),
-                last[:, 256:],
-            ],
-            axis=1,
-        )
-        out_ref[t, STRIP:] = last.astype(BF16)
+    for pair in range(2):
+        strips = [jnp.where(gap == STRIP * t - 2, 1.0, 0.0) for t in range(4 * pair, 4 * pair + 4)]
+        cut = dot_t(jnp.concatenate(strips, axis=0).astype(BF16), turned_ref[...])
+        for i in range(4):
+            t = 4 * pair + i
+            out_ref[t, :STRIP] = cut[WIDE * i : WIDE * i + STRIP].astype(BF16)
+            last = cut[WIDE * i + STRIP : WIDE * i + WIDE]
+            edge = edges[:8] if t % 2 == 0 else edges[8:]
+            last = jnp.concatenate(
+                [
+                    jnp.where(late, pltpu.roll(edge, 4, 0), last[:, :128]),
+                    jnp.where(late, edge, last[:, 128:256]),
+                    last[:, 256:],
+                ],
+                axis=1,
+            )
+            out_ref[t, STRIP:] = last.astype(BF16)
+            results.append(pltpu.make_async_copy(out_ref.at[t], out_hbm.at[t], done.at[t]))
+            results[-1].start()
+    for copy in results:
+        copy.wait()
 
 
 def join(keep_ref, recv_ref, pre_ref, hid_ref, ins_ref, wide_ref, thin_ref):
@@ -213,7 +219,7 @@
     pairs += [(wide0_hbm, wide0_ref), (wide1_hbm, wide1_ref), (wide2_hbm, wide2_ref)]
     pairs += [(pre_hbm, pre_ref), (thin_hbm, thin_ref), (ins_hbm, ins_ref)]
     copies = [pltpu.make_async_copy(source, target, sems.at[i]) for i, (source, target) in enumerate(pairs)]
-    for copy in copies:
+    for copy in copies[:12]:
         copy.start()
     space = lax.axis_index("space")
     left = lax.rem(space, 2) == 0
@@ -227,6 +233,8 @@
 
     for copy in copies[8:12]:
         copy.wait()
+    for copy in copies[12:]:
+        copy.start()
     lane = iota((16, 128), 1)
     taps = [None] * 28
     for kz in range(3):
@@ -358,21 +366,19 @@
 def body(inputs, pre_act, out_grad, conv1_weight, conv2_weight):
     shape = jax.ShapeDtypeStruct
     cores, stages = routes()
-    keep, send, edges = call(
-        turn_kernel, "turn", [shape((10, WIDE, 128), BF16), shape((10, WIDE, 128), BF16), shape((16, 128), F32)],
-        [pltpu.VMEM((16, 8, 8, 128), BF16), pltpu.VMEM((4, 8, 8, 128), BF16), pltpu.SemaphoreType.DMA((2,))],
-        [pre_act[0, 0], inputs[0, 0]], 1e8, 1e6, limit=FULL, far_args=(0, 1),
+    keep, send, strips = call(
+        cut_kernel, "cut",
+        [shape((10, WIDE, 128), BF16), shape((10, WIDE, 128), BF16), shape((8, WIDE, 512), BF16)],
+        [
+            pltpu.VMEM((4, 32, 16, 128), BF16), pltpu.VMEM((2, 16, 4, 8, 128), BF16), pltpu.VMEM((4, 8, 8, 128), BF16),
+            pltpu.VMEM((10, WIDE, 128), BF16), pltpu.VMEM((10, WIDE, 128), BF16), pltpu.VMEM((8, WIDE, 512), BF16),
+            pltpu.VMEM((4, 512, 128), F32), pltpu.VMEM((512, 512), BF16),
+            pltpu.SemaphoreType.DMA((7,)), pltpu.SemaphoreType.DMA((10,)),
+        ],
+        [out_grad[0, 0], pre_act[0, 0], inputs[0, 0]], 4e8, 2e6, limit=FULL, far_args=(0, 1, 2), far_outs=(0, 1, 2),
     )
     swap = [(i, i ^ 1) for i in range(8)]
     recv = lax.ppermute(send, "space", swap)
-    (strips,) = call(
-        cut_kernel, "cut", [shape((8, WIDE, 512), BF16)],
-        [
-            pltpu.VMEM((4, 32, 16, 128), BF16), pltpu.VMEM((4, 512, 128), F32),
-            pltpu.VMEM((512, 512), BF16), pltpu.SemaphoreType.DMA((4,)),
-        ],
-        [out_grad[0, 0], edges], 4e8, 2e6, limit=FULL, far_args=(0,),
-    )
     strips = lax.all_to_all(strips, "space", 0, 0, tiled=True)
     pre, hid, ins, wide0, wide1, wide2, thin = call(
         ready_kernel, "ready",

time: 61.9 us -> 59.6 us (0.963)
  Pallas kernels: 19.5 us -> 17.7 us
    pallas_call x6 -> x5, Pallas kernels: 19.5 us -> 17.7 us  [call(): pl.pallas_call(kernel, name=name, out_shape=outs, in_specs=[spec(i in far...]
  transfers between devices with their start and end apart: 14 -> 14, of which waited for: 8 -> 9; matrix products, arithmetic and copies ran while one was open for 3% -> 3% of each run, Pallas kernels for 13% -> 8%
where the time goes in v4:
time: 59.6 us; the launch traced here: 59.2 us
  starting transfers between devices  25.4 us (43%)
  Pallas kernels  17.7 us (30%)
  waiting for transfers between devices  12.2 us (20%)
  local copies, waits for them, and re-layouts  2.4 us (4%)
  other arithmetic  0.79 us (1%)
  between operations  0.71 us (1%)
    pallas_call x5, Pallas kernels, call(): pl.pallas_call(kernel, name=name, out_shape=outs, in_specs=[spec(i in far...  17.7 us
    ppermute x9, starting transfers between devices, body(): parts = [lax.ppermute(total, ALL, pairs) for pairs in stage]  10.3 us
    ppermute x9, waiting for transfers between devices, body(): parts = [lax.ppermute(total, ALL, pairs) for pairs in stage]  8.28 us
    ppermute x1, starting transfers between devices, body(): other = lax.ppermute(total, ALL, cores)  5 us
    all_to_all x1, starting transfers between devices, body(): strips = lax.all_to_all(strips, 'space', 0, 0, tiled=True)  4.33 us
    all_to_all x1, waiting for transfers between devices, body(): strips = lax.all_to_all(strips, 'space', 0, 0, tiled=True)  2.76 us
    ppermute x1, starting transfers between devices, body(): recv = lax.ppermute(send, 'space', swap)  2.55 us
    ppermute x1, starting transfers between devices, body(): total = mine + lax.ppermute(rest, ALL, cores)  2.02 us
  transfers between devices with their start and end apart: 14, of which 9 were waited for; matrix products, arithmetic and copies ran while one was open for 3% of the time, Pallas kernels for 8%

profile of v4, /device:TPU:1, one launch (start us, length us, event | category | flops | bytes accessed | tf_op | source)
XLA Modules:
  0.0 59.2 jit_solution(9014845751612283207)
XLA Ops:
  0.6 4.2 %cut.1 = (bf16[10,72,128]{2,1,0:T(8,128)(2,1)}, bf16[10,72,128]{2,1,0:T(8,128)(2,1)}, bf16[8,72,512]{2,1,0:T(8,128)(2,1)}) custom-call(bf16[32,16,512]{2,1,0:T(8,128)(2,1)} %bitcast.14, bf16[16,8,8,128]{3,2,1,0:T(8,128)(2,1)} %bitcast.15, bf16[4,8,8,128]{3,2,1,0:T(8,128)(2,1)} %bitcast.16), custom_call_target="tpu_custom_call" | custom-call | flops 400000000 | bytes 2000000 | tf_op jit(solution)/shard_map/cut/pallas_call | solution.py:41
  4.8 2.5 %collective-permute-start = (bf16[10,72,128]{2,1,0:T(8,128)(2,1)}, bf16[10,72,128]{2,1,0:T(8,128)(2,1)S(1)}, u32[]{:S(2)}, u32[]{:S(2)}) collective-permute-start(bf16[10,72,128]{2,1,0:T(8,128)(2,1)} %get-tuple-element.21), channel_id=1, source_target_pairs={{0,1},{1,0},{2,3},{3,2},{4,5},{5,4},{6,7},{7,6},{8,9},{9,8},{10,11... | collective-permute-start | bytes 552968 | tf_op jit(solution)/shard_map/ppermute | solution.py:381
  7.4 0.0 copy-start.2
  7.4 4.3 %all-to-all-start = ((bf16[8,72,512]{2,1,0:T(8,128)(2,1)}), bf16[8,72,512]{2,1,0:T(8,128)(2,1)}, u32[]{:S(2)}, u32[]{:S(2)}) async-start(bf16[8,72,512]{2,1,0:T(8,128)(2,1)} %get-tuple-element.19), calls=%async_computation | async-start | bytes 1179648 | tf_op jit(solution)/shard_map/all_to_all | solution.py:382
  11.7 0.0 copy-start.1
  11.7 0.0 copy-done.2
  11.7 0.9 %copy.9 = bf16[27,16,4]{2,1,0:T(8,128)(2,1)} copy(bf16[27,16,4]{0,1,2:T(8,128)(2,1)S(1)} %bitcast.13) | data formatting | bytes 6912 | tf_op jit(solution)/shard_map/transpose | solution.py:392
  12.6 0.0 copy-done.1
  12.6 0.8 %copy.8 = bf16[27,32,16]{2,1,0:T(8,128)(2,1)} copy(bf16[27,32,16]{1,2,0:T(8,128)(2,1)S(1)} %bitcast.11) | data formatting | bytes 55296 | tf_op jit(solution)/shard_map/transpose | solution.py:391
  13.4 0.0 collective-permute-done.recv_ref
  13.4 0.0 copy-start.3
  13.4 0.7 %copy-done.3 = bf16[10,72,128]{2,1,0:T(8,128)(2,1)} copy-done((bf16[10,72,128]{2,1,0:T(8,128)(2,1)}, bf16[10,72,128]{2,1,0:T(8,128)(2,1)S(1)}, u32[]{:S(2)}) %copy-start.3) | copy-done | bytes 184344
  14.1 4.1 %ready.1 = (bf16[8,80,256]{2,1,0:T(8,128)(2,1)}, bf16[768,640]{1,0:T(8,128)(2,1)}, bf16[192,640]{1,0:T(8,128)(2,1)}, bf16[512,768]{1,0:T(8,128)(2,1)}, bf16[512,...) custom-call(bf16[10,72,128]{2,1,0:T(8,128)(2,1)} %get-tuple-element.20.keep_ref, ...), custom_call_target="tpu_custom_call" | custom-call | flops 999999995904 | bytes 5000000 | tf_op jit(solution)/shard_map/ready/pallas_call | solution.py:41
  18.2 2.8 %all-to-all-done.grad_hbm = bf16[8,72,512]{2,1,0:T(8,128)(2,1)} async-done(((bf16[8,72,512]{2,1,0:T(8,128)(2,1)}), bf16[8,72,512]{2,1,0:T(8,128)(2,1)}, u32[]{:S(2)}, u32[]{:S(2)}) %all-to-all-start) | async-done | bytes 589856 | tf_op jit(solution)/shard_map/all_to_all | solution.py:382
  21.0 7.8 %grads.1 = (bf16[4,32,128]{2,1,0:T(8,128)(2,1)}, bf16[4,32,128]{2,1,0:T(8,128)(2,1)}, f32[64,128]{1,0:T(8,128)}, f32[64,128]{1,0:T(8,128)}) custom-call(bf16[8,72,512]{2,1,0:T(8,128)(2,1)} %all-to-all-done.grad_hbm, bf16[8,80,256]{2,1,0:T(8,128)(2,1)} %get-tuple-element.22.pre_hbm, bf16[768,640]{1,0:T(8,128)(2,1)} %get-tuple-element.23.hid_hbm, ...), custom_call_target="tpu_custom_call" | custom-call | flops 3000000000 | bytes 4000000 | tf_op jit(solution)/shard_map/grads/pallas_call | solution.py:41
  28.8 2.0 %collective-permute-start.2 = (f32[64,128]{1,0:T(8,128)}, f32[64,128]{1,0:T(8,128)S(1)}, u32[]{:S(2)}, u32[]{:S(2)}) collective-permute-start(f32[64,128]{1,0:T(8,128)} %get-tuple-element.32), channel_id=1, source_target_pairs={{0,8},{1,9},{2,10},{3,11},{4,12},{5,13},{6,14},{7,15},{8,0},{9,1},... | collective-permute-start | bytes 98312 | tf_op jit(solution)/shard_map/ppermute | solution.py:408
  30.8 1.1 %collective-permute-done.2 = f32[64,128]{1,0:T(8,128)S(1)} collective-permute-done((f32[64,128]{1,0:T(8,128)}, f32[64,128]{1,0:T(8,128)S(1)}, u32[]{:S(2)}, u32[]{:S(2)}) %collective-permute-start.2) | collective-permute-done | bytes 32800 | tf_op jit(solution)/shard_map/ppermute | solution.py:408
  31.9 0.8 %add.30 = f32[64,128]{1,0:T(8,128)S(1)} add(f32[64,128]{1,0:T(8,128)} %get-tuple-element.31, f32[64,128]{1,0:T(8,128)S(1)} %collective-permute-done.2) | non-fusion elementwise | flops 8192 | bytes 98304 | tf_op jit(solution)/shard_map/add | solution.py:408
  32.7 2.7 %collective-permute-start.5 = (f32[64,128]{1,0:T(8,128)S(1)}, f32[64,128]{1,0:T(8,128)S(1)}, u32[]{:S(2)}, u32[]{:S(2)}) collective-permute-start(f32[64,128]{1,0:T(8,128)S(1)} %add.30), channel_id=1, source_target_pairs={{0,32},{1,33},{2,34},{3,35},{4,36},{5,37},{6,38},{7,39},{8,40},{9,... | collective-permute-start | bytes 98312 | tf_op jit(solution)/shard_map/ppermute | solution.py:411
  35.4 0.9 %collective-permute-start.4 = (f32[64,128]{1,0:T(8,128)S(1)}, f32[64,128]{1,0:T(8,128)S(1)}, u32[]{:S(2)}, u32[]{:S(2)}) collective-permute-start(f32[64,128]{1,0:T(8,128)S(1)} %add.30), channel_id=1, source_target_pairs={{0,48},{1,49},{2,50},{3,51},{4,52},{5,53},{6,54},{7,55},{8,56},{9,... | collective-permute-start | bytes 98312 | tf_op jit(solution)/shard_map/ppermute | solution.py:411
  36.3 0.0 collective-permute-start.3
  36.3 0.7 %collective-permute-done.5 = f32[64,128]{1,0:T(8,128)S(1)} collective-permute-done((f32[64,128]{1,0:T(8,128)S(1)}, f32[64,128]{1,0:T(8,128)S(1)}, u32[]{:S(2)}, u32[]{:S(2)}) %collective-permute-start.5) | collective-permute-done | bytes 32800 | tf_op jit(solution)/shard_map/ppermute | solution.py:411
  36.9 2.5 %collective-permute-done.4 = f32[64,128]{1,0:T(8,128)S(1)} collective-permute-done((f32[64,128]{1,0:T(8,128)S(1)}, f32[64,128]{1,0:T(8,128)S(1)}, u32[]{:S(2)}, u32[]{:S(2)}) %collective-permute-start.4) | collective-permute-done | bytes 32800 | tf_op jit(solution)/shard_map/ppermute | solution.py:411
  39.4 0.0 collective-permute-done.3
  39.4 0.0 copy-start.4
  39.4 1.3 %collective-permute-start.8 = (f32[64,128]{1,0:T(8,128)S(1)}, f32[64,128]{1,0:T(8,128)S(1)}, u32[]{:S(2)}, u32[]{:S(2)}) collective-permute-start(f32[64,128]{1,0:T(8,128)S(1)} %add_add_fusion.2), channel_id=1, source_target_pairs={{0,4},{1,5},{2,6},{3,7},{4,0},{5,1},{6,2},{7,3},{8,12},{9,13},{10,... | collective-permute-start | bytes 98312 | tf_op jit(solution)/shard_map/ppermute | solution.py:411
  40.7 1.7 %collective-permute-start.7 = (f32[64,128]{1,0:T(8,128)S(1)}, f32[64,128]{1,0:T(8,128)S(1)}, u32[]{:S(2)}, u32[]{:S(2)}) collective-permute-start(f32[64,128]{1,0:T(8,128)S(1)} %add_add_fusion.2), channel_id=1, source_target_pairs={{0,6},{1,7},{2,4},{3,5},{4,2},{5,3},{6,0},{7,1},{8,14},{9,15},{10,... | collective-permute-start | bytes 98312 | tf_op jit(solution)/shard_map/ppermute | solution.py:411
  42.4 0.0 collective-permute-start.6
  42.4 1.4 %collective-permute-done.8 = f32[64,128]{1,0:T(8,128)S(1)} collective-permute-done((f32[64,128]{1,0:T(8,128)S(1)}, f32[64,128]{1,0:T(8,128)S(1)}, u32[]{:S(2)}, u32[]{:S(2)}) %collective-permute-start.8) | collective-permute-done | bytes 32800 | tf_op jit(solution)/shard_map/ppermute | solution.py:411
  43.8 0.9 %collective-permute-done.7 = f32[64,128]{1,0:T(8,128)S(1)} collective-permute-done((f32[64,128]{1,0:T(8,128)S(1)}, f32[64,128]{1,0:T(8,128)S(1)}, u32[]{:S(2)}, u32[]{:S(2)}) %collective-permute-start.7) | collective-permute-done | bytes 32800 | tf_op jit(solution)/shard_map/ppermute | solution.py:411
  44.7 0.5 collective-permute-done.6
  45.1 3.4 %collective-permute-start.11 = (f32[64,128]{1,0:T(8,128)S(1)}, f32[64,128]{1,0:T(8,128)S(1)}, u32[]{:S(2)}, u32[]{:S(2)}) collective-permute-start(f32[64,128]{1,0:T(8,128)S(1)} %add_add_fusion.1), channel_id=1, source_target_pairs={{0,64},{1,65},{2,66},{3,67},{4,68},{5,69},{6,70},{7,71},{8,72},{9,... | collective-permute-start | bytes 98312 | tf_op jit(solution)/shard_map/ppermute | solution.py:411
  48.5 0.1 collective-permute-start.10
  48.6 0.3 collective-permute-start.9
  48.9 0.0 copy-done.4
  48.9 0.0 copy-start
  48.9 1.2 %collective-permute-start.1 = (bf16[4,32,128]{2,1,0:T(8,128)(2,1)S(1)}, bf16[4,32,128]{2,1,0:T(8,128)(2,1)S(1)}, u32[]{:S(2)}, u32[]{:S(2)}) collective-permute-start(bf16[4,32,128]{2,1,0:T(8,128)(2,1)S(1)} %copy-done.4), channel_id=1, source_target_pairs={{0,1},{1,0},{2,3},{3,2},{4,5},{5,4},{6,7},{7,6},{8,9},{9,8},{10,11... | collective-permute-start | bytes 98312 | tf_op jit(solution)/shard_map/ppermute | solution.py:409
  50.1 0.0 collective-permute-done.11
  50.1 2.4 %collective-permute-done.10 = f32[64,128]{1,0:T(8,128)S(1)} collective-permute-done((f32[64,128]{1,0:T(8,128)S(1)}, f32[64,128]{1,0:T(8,128)S(1)}, u32[]{:S(2)}, u32[]{:S(2)}) %collective-permute-start.10) | collective-permute-done | bytes 32800 | tf_op jit(solution)/shard_map/ppermute | solution.py:411
  52.5 0.0 collective-permute-done.9
  52.5 5.0 %collective-permute-start.12 = (f32[64,128]{1,0:T(8,128)S(1)}, f32[64,128]{1,0:T(8,128)S(1)}, u32[]{:S(2)}, u32[]{:S(2)}) collective-permute-start(f32[64,128]{1,0:T(8,128)S(1)} %add_add_fusion.mine_ref), channel_id=1, source_target_pairs={{0,8},{1,9},{2,10},{3,11},{4,12},{5,13},{6,14},{7,15},{8,0},{9,1},... | collective-permute-start | bytes 98312 | tf_op jit(solution)/shard_map/ppermute | solution.py:413
  57.5 0.0 collective-permute-done.1.recv_ref
  57.5 0.0 copy-done
  57.5 0.7 %tile.1 = bf16[4,8,8,128]{3,2,1,0:T(8,128)(2,1)} custom-call(bf16[4,32,128]{2,1,0:T(8,128)(2,1)S(1)} %copy-done, bf16[4,32,128]{2,1,0:T(8,128)(2,1)S(1)} %collective-permute-done.1.recv_ref), custom_call_target="tpu_custom_call" | custom-call | flops 1000000 | bytes 200000 | tf_op jit(solution)/shard_map/tile/pallas_call | solution.py:41
  58.2 0.1 collective-permute-done.12.rest_ref
  58.4 0.9 %unpack.1 = (f32[4,16,27]{2,1,0:T(8,128)}, f32[27,16,32]{2,1,0:T(8,128)}) custom-call(f32[64,128]{1,0:T(8,128)S(1)} %add_add_fusion.mine_ref, f32[64,128]{1,0:T(8,128)S(1)} %collective-permute-done.12.rest_ref), custom_call_target="tpu_custom_call" | custom-call | flops 1000000 | bytes 200000 | tf_op jit(solution)/shard_map/unpack/pallas_call | solution.py:41
  (3 shorter events, 0.0 us)
Async XLA Ops:
  4.8 8.6 %collective-permute-start = (bf16[10,72,128]{2,1,0:T(8,128)(2,1)}, bf16[10,72,128]{2,1,0:T(8,128)(2,1)S(1)}, u32[]{:S(2)}, u32[]{:S(2)}) collective-permute-start(bf16[10,72,128]{2,1,0:T(8,128)(2,1)} %get-tuple-element.21), channel_id=1, source_target_pairs={{0,1},{1,0},{2,3},{3,2},{4,5},{5,4},{6,7},{7,6},{8,9},{9,8},{10,11... | collective-permute-start | bytes 552968 | tf_op jit(solution)/shard_map/ppermute | solution.py:381
  7.4 4.4 %copy-start.2 = (bf16[27,4,16]{0,2,1:T(8,128)(2,1)S(1)}, bf16[27,4,16]{0,2,1:T(8,128)(2,1)}, u32[]{:S(2)}) copy-start(bf16[27,4,16]{0,2,1:T(8,128)(2,1)} %param.8) | copy-start | bytes 10372
  7.4 13.6 %all-to-all-start = ((bf16[8,72,512]{2,1,0:T(8,128)(2,1)}), bf16[8,72,512]{2,1,0:T(8,128)(2,1)}, u32[]{:S(2)}, u32[]{:S(2)}) async-start(bf16[8,72,512]{2,1,0:T(8,128)(2,1)} %get-tuple-element.19), calls=%async_computation | async-start | bytes 1179648 | tf_op jit(solution)/shard_map/all_to_all | solution.py:382
  11.7 0.9 %copy-start.1 = (bf16[27,16,32]{2,1,0:T(8,128)(2,1)S(1)}, bf16[27,16,32]{2,1,0:T(8,128)(2,1)}, u32[]{:S(2)}) copy-start(bf16[27,16,32]{2,1,0:T(8,128)(2,1)} %param.9) | copy-start | bytes 82948
  13.4 0.7 %copy-start.3 = (bf16[10,72,128]{2,1,0:T(8,128)(2,1)}, bf16[10,72,128]{2,1,0:T(8,128)(2,1)S(1)}, u32[]{:S(2)}) copy-start(bf16[10,72,128]{2,1,0:T(8,128)(2,1)S(1)} %collective-permute-done.recv_ref) | copy-start | bytes 552964
  28.8 3.1 %collective-permute-start.2 = (f32[64,128]{1,0:T(8,128)}, f32[64,128]{1,0:T(8,128)S(1)}, u32[]{:S(2)}, u32[]{:S(2)}) collective-permute-start(f32[64,128]{1,0:T(8,128)} %get-tuple-element.32), channel_id=1, source_target_pairs={{0,8},{1,9},{2,10},{3,11},{4,12},{5,13},{6,14},{7,15},{8,0},{9,1},... | collective-permute-start | bytes 98312 | tf_op jit(solution)/shard_map/ppermute | solution.py:408
  32.7 4.3 %collective-permute-start.5 = (f32[64,128]{1,0:T(8,128)S(1)}, f32[64,128]{1,0:T(8,128)S(1)}, u32[]{:S(2)}, u32[]{:S(2)}) collective-permute-start(f32[64,128]{1,0:T(8,128)S(1)} %add.30), channel_id=1, source_target_pairs={{0,32},{1,33},{2,34},{3,35},{4,36},{5,37},{6,38},{7,39},{8,40},{9,... | collective-permute-start | bytes 98312 | tf_op jit(solution)/shard_map/ppermute | solution.py:411
  35.4 4.0 %collective-permute-start.4 = (f32[64,128]{1,0:T(8,128)S(1)}, f32[64,128]{1,0:T(8,128)S(1)}, u32[]{:S(2)}, u32[]{:S(2)}) collective-permute-start(f32[64,128]{1,0:T(8,128)S(1)} %add.30), channel_id=1, source_target_pairs={{0,48},{1,49},{2,50},{3,51},{4,52},{5,53},{6,54},{7,55},{8,56},{9,... | collective-permute-start | bytes 98312 | tf_op jit(solution)/shard_map/ppermute | solution.py:411
  36.3 3.1 %collective-permute-start.3 = (f32[64,128]{1,0:T(8,128)S(1)}, f32[64,128]{1,0:T(8,128)S(1)}, u32[]{:S(2)}, u32[]{:S(2)}) collective-permute-start(f32[64,128]{1,0:T(8,128)S(1)} %add.30), channel_id=1, source_target_pairs={{0,16},{1,17},{2,18},{3,19},{4,20},{5,21},{6,22},{7,23},{8,24},{9,... | collective-permute-start | bytes 98312 | tf_op jit(solution)/shard_map/ppermute | solution.py:411
  39.4 9.5 %copy-start.4 = (bf16[4,32,128]{2,1,0:T(8,128)(2,1)S(1)}, bf16[4,32,128]{2,1,0:T(8,128)(2,1)}, u32[]{:S(2)}) copy-start(bf16[4,32,128]{2,1,0:T(8,128)(2,1)} %get-tuple-element.30) | copy-start | bytes 98308
  39.4 4.3 %collective-permute-start.8 = (f32[64,128]{1,0:T(8,128)S(1)}, f32[64,128]{1,0:T(8,128)S(1)}, u32[]{:S(2)}, u32[]{:S(2)}) collective-permute-start(f32[64,128]{1,0:T(8,128)S(1)} %add_add_fusion.2), channel_id=1, source_target_pairs={{0,4},{1,5},{2,6},{3,7},{4,0},{5,1},{6,2},{7,3},{8,12},{9,13},{10,... | collective-permute-start | bytes 98312 | tf_op jit(solution)/shard_map/ppermute | solution.py:411
  40.7 4.0 %collective-permute-start.7 = (f32[64,128]{1,0:T(8,128)S(1)}, f32[64,128]{1,0:T(8,128)S(1)}, u32[]{:S(2)}, u32[]{:S(2)}) collective-permute-start(f32[64,128]{1,0:T(8,128)S(1)} %add_add_fusion.2), channel_id=1, source_target_pairs={{0,6},{1,7},{2,4},{3,5},{4,2},{5,3},{6,0},{7,1},{8,14},{9,15},{10,... | collective-permute-start | bytes 98312 | tf_op jit(solution)/shard_map/ppermute | solution.py:411
  42.4 2.8 %collective-permute-start.6 = (f32[64,128]{1,0:T(8,128)S(1)}, f32[64,128]{1,0:T(8,128)S(1)}, u32[]{:S(2)}, u32[]{:S(2)}) collective-permute-start(f32[64,128]{1,0:T(8,128)S(1)} %add_add_fusion.2), channel_id=1, source_target_pairs={{0,2},{1,3},{2,0},{3,1},{4,6},{5,7},{6,4},{7,5},{8,10},{9,11},{10,... | collective-permute-start | bytes 98312 | tf_op jit(solution)/shard_map/ppermute | solution.py:411
  45.1 5.0 %collective-permute-start.11 = (f32[64,128]{1,0:T(8,128)S(1)}, f32[64,128]{1,0:T(8,128)S(1)}, u32[]{:S(2)}, u32[]{:S(2)}) collective-permute-start(f32[64,128]{1,0:T(8,128)S(1)} %add_add_fusion.1), channel_id=1, source_target_pairs={{0,64},{1,65},{2,66},{3,67},{4,68},{5,69},{6,70},{7,71},{8,72},{9,... | collective-permute-start | bytes 98312 | tf_op jit(solution)/shard_map/ppermute | solution.py:411
  48.5 4.0 %collective-permute-start.10 = (f32[64,128]{1,0:T(8,128)S(1)}, f32[64,128]{1,0:T(8,128)S(1)}, u32[]{:S(2)}, u32[]{:S(2)}) collective-permute-start(f32[64,128]{1,0:T(8,128)S(1)} %add_add_fusion.1), channel_id=1, source_target_pairs={{0,65},{1,64},{2,67},{3,66},{4,69},{5,68},{6,71},{7,70},{8,73},{9,... | collective-permute-start | bytes 98312 | tf_op jit(solution)/shard_map/ppermute | solution.py:411
  48.6 3.9 %collective-permute-start.9 = (f32[64,128]{1,0:T(8,128)S(1)}, f32[64,128]{1,0:T(8,128)S(1)}, u32[]{:S(2)}, u32[]{:S(2)}) collective-permute-start(f32[64,128]{1,0:T(8,128)S(1)} %add_add_fusion.1), channel_id=1, source_target_pairs={{0,1},{1,0},{2,3},{3,2},{4,5},{5,4},{6,7},{7,6},{8,9},{9,8},{10,11... | collective-permute-start | bytes 98312 | tf_op jit(solution)/shard_map/ppermute | solution.py:411
  48.9 8.6 %copy-start = (bf16[4,32,128]{2,1,0:T(8,128)(2,1)S(1)}, bf16[4,32,128]{2,1,0:T(8,128)(2,1)}, u32[]{:S(2)}) copy-start(bf16[4,32,128]{2,1,0:T(8,128)(2,1)} %get-tuple-element.29.own_ref) | copy-start | bytes 98308
  48.9 8.6 %collective-permute-start.1 = (bf16[4,32,128]{2,1,0:T(8,128)(2,1)S(1)}, bf16[4,32,128]{2,1,0:T(8,128)(2,1)S(1)}, u32[]{:S(2)}, u32[]{:S(2)}) collective-permute-start(bf16[4,32,128]{2,1,0:T(8,128)(2,1)S(1)} %copy-done.4), channel_id=1, source_target_pairs={{0,1},{1,0},{2,3},{3,2},{4,5},{5,4},{6,7},{7,6},{8,9},{9,8},{10,11... | collective-permute-start | bytes 98312 | tf_op jit(solution)/shard_map/ppermute | solution.py:409
  52.5 5.9 %collective-permute-start.12 = (f32[64,128]{1,0:T(8,128)S(1)}, f32[64,128]{1,0:T(8,128)S(1)}, u32[]{:S(2)}, u32[]{:S(2)}) collective-permute-start(f32[64,128]{1,0:T(8,128)S(1)} %add_add_fusion.mine_ref), channel_id=1, source_target_pairs={{0,8},{1,9},{2,10},{3,11},{4,12},{5,13},{6,14},{7,15},{8,0},{9,1},... | collective-permute-start | bytes 98312 | tf_op jit(solution)/shard_map/ppermute | solution.py:413

commit v5 on v4

--- a/solution.py
+++ b/solution.py
@@ -13,6 +13,7 @@
 PAD = 80
 ROWS = 8 * PAD
 FULL = 62
+SOME = 20
 ALL = ("dp", "space")
 F32 = jnp.float32
 BF16 = jnp.bfloat16
@@ -107,7 +108,8 @@
         copies[3 + b].wait()
         wide_ref[b] = slab_ref[b].astype(F32).reshape(512, 128)
         for y in range(16):
-            turned_ref[32 * y : 32 * y + 32, 128 * b : 128 * b + 128] = wide_ref[
+            slot = (y + 1) % 16
+            turned_ref[32 * slot : 32 * slot + 32, 128 * b : 128 * b + 128] = wide_ref[
                 b, pl.ds(y, 32, stride=16), :
             ].astype(BF16)
     p, x = iota((WIDE, 512), 0), iota((WIDE, 512), 1)
@@ -161,108 +163,111 @@
         turned = wide_ref[:, 128 * part : 128 * part + 128].T
         for kx in range(3):
             shifted = pltpu.roll(turned, 2 - kx, 1) if kx < 2 else turned
-            for y in range(8):
-                at = 48 * (8 * part + y) + 16 * kx
-                hid_ref[at : at + 16, :] = shifted[16 * y : 16 * y + 16].astype(BF16)
+            for y in range(8 * part, 8 * part + 8):
+                rows = shifted[16 * (y % 8) : 16 * (y % 8) + 16].astype(BF16)
+                for slot in {(y + 2) % 16, y + 2}:
+                    hid_ref[48 * slot + 16 * kx : 48 * slot + 16 * kx + 16, :] = rows
     turned = thin_ref[...].T[:64]
     for kx in range(3):
         shifted = pltpu.roll(turned, 2 - kx, 1) if kx < 2 else turned
         ins_ref[64 * kx : 64 * kx + 64, :] = shifted.astype(BF16)
 
 
-def band(two_ref, one_ref, wide_refs, thin_ref):
-    spread = one_hot(iota((16, 256), 1) % 16 == iota((16, 256), 0))
-    two = dot(two_ref[...], spread)
-    group = iota((32, 256), 1) // 16
+def band(two_ref, one_ref, wide_ref, thin_ref):
+    def lay(terms, rows, kz, ky):
+        parts = [terms[rows * (9 * kz + 3 * ky + kx) :][:rows] for kx in range(3)]
+        return jnp.where(iota((rows, 128), 1) < 64, parts[0], parts[1]), parts[2]
+
+    two = dot(two_ref[...], one_hot(iota((16, 128), 1) % 16 == iota((16, 128), 0)))
+    group = iota((32, 128), 1) // 16 % 4
     for kz in range(3):
-        for kx in range(3):
-            terms = [two[32 * (9 * kz + 3 * ky + kx) :][:32] for ky in range(3)]
-            for y in range(16):
-                block = jnp.zeros((32, 256), F32)
+        terms = [lay(two, 32, kz, ky) for ky in range(3)]
+        for slot in range(8):
+            for half in range(2):
+                block = jnp.zeros((32, 128), F32)
                 for ky in range(3):
-                    block = jnp.where(group == y + ky - 1, terms[ky], block)
-                wide_refs[kz][32 * y : 32 * y + 32, 256 * kx : 256 * kx + 256] = block.astype(BF16)
-    lane = iota((4, 128), 1)
-    spread = one_hot((lane < 64) & (lane // 8 % 4 == iota((4, 128), 0)))
-    one = dot(one_ref[...], spread)
+                    block = jnp.where(group == ky + slot - 2, terms[ky][half], block)
+                at = 256 * kz + 32 * slot
+                wide_ref[at : at + 32, 128 * half : 128 * half + 128] = block.astype(BF16)
+    one = dot(one_ref[...], one_hot(iota((4, 128), 1) // 8 % 4 == iota((4, 128), 0)))
     lane = iota((16, 128), 1)
-    group = 8 * (lane // 32) + lane % 8
+    group = 8 * (lane // 32 % 2) + lane % 8
     for kz in range(3):
-        for kx in range(3):
-            terms = [one[16 * (9 * kz + 3 * ky + kx) :][:16] for ky in range(3)]
-            for y in range(16):
+        terms = [lay(one, 16, kz, ky) for ky in range(3)]
+        for y in range(16):
+            for half in range(2):
                 block = jnp.zeros((16, 128), F32)
                 for ky in range(3):
-                    block = jnp.where(group == y + ky - 1, terms[ky], block)
-                thin_ref[256 * kz + 16 * y : 256 * kz + 16 * y + 16, 128 * kx : 128 * kx + 128] = block.astype(BF16)
+                    block = jnp.where(group == y + ky - 1, terms[ky][half], block)
+                at = 256 * kz + 16 * y
+                thin_ref[at : at + 16, 128 * half : 128 * half + 128] = block.astype(BF16)
 
 
 def ready_kernel(
     keep_ref, recv_ref, two_ref, one_ref,
-    pre_ref, hid_ref, ins_ref, wide0_ref, wide1_ref, wide2_ref, thin_ref, hidden_ref, inputs_ref,
+    pre_ref, hid_ref, ins_ref, wide_ref, thin_ref, hidden_ref, inputs_ref,
 ):
-    band(two_ref, one_ref, (wide0_ref, wide1_ref, wide2_ref), thin_ref)
+    band(two_ref, one_ref, wide_ref, thin_ref)
     join(keep_ref, recv_ref, pre_ref, hid_ref, ins_ref, hidden_ref, inputs_ref)
 
 
-def planes(ref, kz):
-    return ref[(2 - kz) * PAD : (2 - kz) * PAD + ROWS, :]
+def planes(ref, kz, low, size):
+    return ref[(2 - kz) * PAD : (2 - kz) * PAD + ROWS, low : low + size]
+
+
+def across(sums):
+    pair = sums[:, :128]
+    pair = jnp.where(iota((ROWS, 128), 1) < 64, pltpu.roll(pair, ROWS - 2, 0), pltpu.roll(pair, ROWS - 1, 0))
+    return pair + pltpu.roll(pair, 64, 1) + sums[:, 128:]
 
 
 def grads_kernel(
-    grad_hbm, pre_hbm, hid_hbm, ins_hbm, wide0_hbm, wide1_hbm, wide2_hbm, thin_hbm,
+    grad_ref, pre_ref, hid_ref, ins_ref, wide_ref, thin_ref,
     own_ref, give_ref, mine_ref, rest_ref, grad_s, act_s, out_s, terms_s,
-    grad_ref, pre_ref, hid_ref, ins_ref, wide0_ref, wide1_ref, wide2_ref, thin_ref, sems,
 ):
-    pairs = [(grad_hbm.at[z], grad_ref.at[z]) for z in range(8)]
-    pairs += [(hid_hbm.at[pl.ds(192 * i, 192)], hid_ref.at[pl.ds(192 * i, 192)]) for i in range(4)]
-    pairs += [(wide0_hbm, wide0_ref), (wide1_hbm, wide1_ref), (wide2_hbm, wide2_ref)]
-    pairs += [(pre_hbm, pre_ref), (thin_hbm, thin_ref), (ins_hbm, ins_ref)]
-    copies = [pltpu.make_async_copy(source, target, sems.at[i]) for i, (source, target) in enumerate(pairs)]
-    for copy in copies[:12]:
-        copy.start()
     space = lax.axis_index("space")
     left = lax.rem(space, 2) == 0
     for block in (0, 9):
         grad_s[PAD * block : PAD * block + PAD, :] = jnp.zeros((PAD, 512), BF16)
         act_s[PAD * block : PAD * block + PAD, :] = jnp.zeros((PAD, 256), BF16)
     for z in range(8):
-        copies[z].wait()
         plane = jnp.concatenate([grad_ref[z].astype(F32), jnp.zeros((PAD - WIDE, 512), F32)], axis=0)
         grad_s[PAD * (z + 1) : PAD * (z + 2), :] = plane.astype(BF16)
 
-    for copy in copies[8:12]:
-        copy.wait()
-    for copy in copies[12:]:
-        copy.start()
     lane = iota((16, 128), 1)
     taps = [None] * 28
     for kz in range(3):
         for half in range(2):
-            low = 7 * half
-            terms_s[half] = dot(
-                hid_ref[48 * low : 48 * low + 432, :],
-                grad_s[(2 - kz) * PAD : (2 - kz) * PAD + ROWS, 256 * half : 256 * half + 256],
-            )
+            terms_s[half] = dot(hid_ref[384 * half : 384 * half + 480, :], planes(grad_s, kz, 256 * half, 256))
         for kx in range(3):
             for ky in range(3):
                 total = jnp.zeros((16, 128), F32)
                 for y in range(16):
                     at = y + ky - 1
                     if 0 <= at < 16:
-                        half = y // 8
-                        row, col = 48 * (at - 7 * half) + 16 * kx, 128 * (y % 8 // 4)
+                        slot = (y + 1) % 16
+                        half = slot // 8
+                        row = 48 * ((at + 2) % 16 if half == 0 else at - 6) + 16 * kx
+                        col = 128 * (slot % 8 // 4)
                         piece = terms_s[half, row : row + 16, col : col + 128]
-                        total = total + jnp.where(lane // 32 == y % 4, piece, 0.0)
+                        total = total + jnp.where(lane // 32 == slot % 4, piece, 0.0)
                 total = total + pltpu.roll(total, 64, 1)
                 taps[9 * kz + 3 * ky + kx] = total + pltpu.roll(total, 32, 1)
 
-    for copy in copies[12:]:
-        copy.wait()
-    sums = dot(planes(grad_s, 0), wide0_ref[...])
-    sums = sums + dot(planes(grad_s, 1), wide1_ref[...])
-    sums = sums + dot(planes(grad_s, 2), wide2_ref[...])
-    act = sums[:, 512:] + pltpu.roll(sums[:, 256:512], ROWS - 1, 0) + pltpu.roll(sums[:, :256], ROWS - 2, 0)
+    wide = [wide_ref[256 * kz : 256 * kz + 256, :] for kz in range(3)]
+    none = jnp.zeros((32, 256), BF16)
+    top = jnp.concatenate([part for w in wide for part in (none, w[32:])], axis=0)
+    bottom = jnp.concatenate([part for w in wide for part in (w[:160], none, w[192:])], axis=0)
+    parts = []
+    for group in range(4):
+        if group < 3:
+            sides = [planes(grad_s, kz, 128 * group, 256) for kz in range(3)]
+        else:
+            sides = [planes(grad_s, kz, low, 128) for kz in range(3) for low in (384, 0)]
+        weights = top if group == 0 else bottom if group == 3 else wide_ref[...]
+        parts.append(across(dot(jnp.concatenate(sides, axis=1), weights)))
+    low = iota((ROWS, 128), 1) < 64
+    act = jnp.concatenate([jnp.where(low, parts[0], parts[1]), jnp.where(low, parts[2], parts[3])], axis=1)
     row = iota((PAD, 256), 0)
     at = STRIP * space - 1 + row
     inside = (row < STRIP + 2) & (at >= 0) & (at < 512)
@@ -275,9 +280,8 @@
         value = act[PAD * z : PAD * z + PAD] * jnp.where(pre > 0, 1.0, LEAK)
         act_s[PAD * (z + 1) : PAD * (z + 2), :] = jnp.where(inside, value, 0.0).astype(BF16)
 
-    left_side = jnp.concatenate([planes(act_s, kz) for kz in range(3)], axis=1)
-    sums = dot(left_side, thin_ref[...])
-    out_s[...] = sums[:, 256:] + pltpu.roll(sums[:, 128:256], ROWS - 1, 0) + pltpu.roll(sums[:, :128], ROWS - 2, 0)
+    sides = jnp.concatenate([planes(act_s, kz, 0, 256) for kz in range(3)], axis=1)
+    out_s[...] = across(dot(sides, thin_ref[...]))
     for z in range(4):
         pair = jnp.concatenate([out_s[PAD * z : PAD * z + STRIP], out_s[PAD * (z + 4) : PAD * (z + 4) + STRIP]], axis=0).T
         own_ref[z] = jnp.where(left, pair[:32], pair[32:64]).astype(BF16)
@@ -287,7 +291,7 @@
     gap = 8 * (row // 32) + row % 8 - col // 16
     packed = jnp.zeros((12, 128), F32)
     for kz in range(3):
-        terms = dot(ins_ref[...], planes(act_s, kz)).reshape(3, 64, 256)
+        terms = dot(ins_ref[...], planes(act_s, kz, 0, 256)).reshape(3, 64, 256)
         for ky in range(3):
             part = jnp.where((gap == ky - 1)[None], terms, 0.0)
             part = (part[:, :, :128] + part[:, :, 128:]).reshape(3, 2, 4, 8, 128)
@@ -380,30 +384,27 @@
     swap = [(i, i ^ 1) for i in range(8)]
     recv = lax.ppermute(send, "space", swap)
     strips = lax.all_to_all(strips, "space", 0, 0, tiled=True)
-    pre, hid, ins, wide0, wide1, wide2, thin = call(
+    pre, hid, ins, wide, thin = call(
         ready_kernel, "ready",
         [
-            shape((8, PAD, 256), BF16), shape((768, ROWS), BF16), shape((192, ROWS), BF16),
-            shape((512, 768), BF16), shape((512, 768), BF16), shape((512, 768), BF16), shape((768, 384), BF16),
+            shape((8, PAD, 256), BF16), shape((864, ROWS), BF16), shape((192, ROWS), BF16),
+            shape((768, 256), BF16), shape((768, 256), BF16),
         ],
         [pltpu.VMEM((ROWS, 256), F32), pltpu.VMEM((ROWS, 128), F32)],
         [
             keep, recv, conv2_weight.transpose(0, 2, 1).reshape(864, 16),
             conv1_weight.transpose(0, 2, 1).reshape(432, 4),
         ],
-        1e12, 5e6, limit=FULL,
+        1e12, 5e6, limit=SOME,
     )
     own, give, mine, rest = call(
         grads_kernel, "grads",
         [shape((4, 32, 128), BF16), shape((4, 32, 128), BF16), shape((64, 128), F32), shape((64, 128), F32)],
         [
             pltpu.VMEM((10 * PAD, 512), BF16), pltpu.VMEM((10 * PAD, 256), BF16),
-            pltpu.VMEM((ROWS, 128), F32), pltpu.VMEM((2, 432, 256), F32),
-            pltpu.VMEM((8, WIDE, 512), BF16), pltpu.VMEM((8, PAD, 256), BF16), pltpu.VMEM((768, ROWS), BF16),
-            pltpu.VMEM((192, ROWS), BF16), pltpu.VMEM((512, 768), BF16), pltpu.VMEM((512, 768), BF16),
-            pltpu.VMEM((512, 768), BF16), pltpu.VMEM((768, 384), BF16), pltpu.SemaphoreType.DMA((18,)),
+            pltpu.VMEM((ROWS, 128), F32), pltpu.VMEM((2, 480, 256), F32),
         ],
-        [strips, pre, hid, ins, wide0, wide1, wide2, thin], 3e9, 4e6, limit=FULL, far_args=range(8),
+        [strips, pre, hid, ins, wide, thin], 3e9, 4e6, limit=SOME,
     )
     total = mine + lax.ppermute(rest, ALL, cores)
     got = lax.ppermute(give, "space", swap)

time: 59.6 us -> 56.3 us (0.945)
  Pallas kernels: 17.7 us -> 12.5 us
  waiting for transfers between devices: 12.2 us -> 17.2 us
  local copies, waits for them, and re-layouts: 2.4 us -> 0.41 us
  other arithmetic: 0.79 us -> 0.03 us
    pallas_call x5, Pallas kernels: 17.7 us -> 12.5 us  [call(): pl.pallas_call(kernel, name=name, out_shape=outs, in_specs=[spec(i in far...]
    all_to_all x1, waiting for transfers between devices: 2.76 us -> 7.9 us  [body(): strips = lax.all_to_all(strips, 'space', 0, 0, tiled=True)]
    add x1, other arithmetic: 0.77 us -> 0.01 us  [body(): total = mine + lax.ppermute(rest, ALL, cores)]
    unnamed x10 -> x6, local copies, waits for them, and re-layouts: 0.72 us -> 0.01 us
    transpose x1, local copies, waits for them, and re-layouts: 0.82 us -> 0.16 us  [body(): conv2_weight.transpose(0, 2, 1).reshape(864, 16)]
    transpose x1, local copies, waits for them, and re-layouts: 0.86 us -> 0.23 us  [body(): conv1_weight.transpose(0, 2, 1).reshape(432, 4)]
  transfers between devices with their start and end apart: 14 -> 14, of which waited for: 9 -> 9; matrix products, arithmetic and copies ran while one was open for 3% -> 1% of each run, Pallas kernels for 8% -> 3%
where the time goes in v5:
time: 56.3 us; the launch traced here: 56.1 us
  starting transfers between devices  25.2 us (45%)
  waiting for transfers between devices  17.2 us (31%)
  Pallas kernels  12.5 us (22%)
  between operations  0.75 us (1%)
    pallas_call x5, Pallas kernels, call(): pl.pallas_call(kernel, name=name, out_shape=outs, in_specs=[spec(i in far...  12.5 us
    ppermute x9, starting transfers between devices, body(): parts = [lax.ppermute(total, ALL, pairs) for pairs in stage]  10.3 us
    ppermute x9, waiting for transfers between devices, body(): parts = [lax.ppermute(total, ALL, pairs) for pairs in stage]  8.29 us
    all_to_all x1, waiting for transfers between devices, body(): strips = lax.all_to_all(strips, 'space', 0, 0, tiled=True)  7.9 us
    ppermute x1, starting transfers between devices, body(): other = lax.ppermute(total, ALL, cores)  5 us
    all_to_all x1, starting transfers between devices, body(): strips = lax.all_to_all(strips, 'space', 0, 0, tiled=True)  4.21 us
    ppermute x1, starting transfers between devices, body(): recv = lax.ppermute(send, 'space', swap)  2.55 us
    ppermute x1, starting transfers between devices, body(): total = mine + lax.ppermute(rest, ALL, cores)  2.01 us
  transfers between devices with their start and end apart: 14, of which 9 were waited for; matrix products, arithmetic and copies ran while one was open for 1% of the time, Pallas kernels for 3%

profile of v5, /device:TPU:1, one launch (start us, length us, event | category | flops | bytes accessed | tf_op | source)
XLA Modules:
  0.0 56.1 jit_solution(15814498794589490992)
XLA Ops:
  0.6 0.0 copy-start.2
  0.6 0.0 copy-start.1
  0.7 4.2 %cut.1 = (bf16[10,72,128]{2,1,0:T(8,128)(2,1)}, bf16[10,72,128]{2,1,0:T(8,128)(2,1)}, bf16[8,72,512]{2,1,0:T(8,128)(2,1)}) custom-call(bf16[32,16,512]{2,1,0:T(8,128)(2,1)} %bitcast.14, bf16[16,8,8,128]{3,2,1,0:T(8,128)(2,1)} %bitcast.15, bf16[4,8,8,128]{3,2,1,0:T(8,128)(2,1)} %bitcast.16), custom_call_target="tpu_custom_call" | custom-call | flops 400000000 | bytes 2000000 | tf_op jit(solution)/shard_map/cut/pallas_call | solution.py:42
  4.8 0.0 copy-start
  4.9 2.5 %collective-permute-start = (bf16[10,72,128]{2,1,0:T(8,128)(2,1)}, bf16[10,72,128]{2,1,0:T(8,128)(2,1)S(1)}, u32[]{:S(2)}, u32[]{:S(2)}) collective-permute-start(bf16[10,72,128]{2,1,0:T(8,128)(2,1)} %get-tuple-element.19), channel_id=1, source_target_pairs={{0,1},{1,0},{2,3},{3,2},{4,5},{5,4},{6,7},{7,6},{8,9},{9,8},{10,11... | collective-permute-start | bytes 552968 | tf_op jit(solution)/shard_map/ppermute | solution.py:385
  7.4 4.2 %all-to-all-start = ((bf16[8,72,512]{2,1,0:T(8,128)(2,1)}), bf16[8,72,512]{2,1,0:T(8,128)(2,1)}, u32[]{:S(2)}, u32[]{:S(2)}) async-start(bf16[8,72,512]{2,1,0:T(8,128)(2,1)} %get-tuple-element.17), calls=%async_computation | async-start | bytes 1179648 | tf_op jit(solution)/shard_map/all_to_all | solution.py:386
  11.6 0.0 copy-done.2
  11.6 0.2 copy.9
  11.9 0.0 copy-done.1
  11.9 0.2 copy.8
  12.0 0.0 collective-permute-done.recv_ref
  12.0 0.0 copy-done
  12.1 0.9 %ready.1 = (bf16[8,80,256]{2,1,0:T(8,128)(2,1)S(1)}, bf16[864,640]{1,0:T(8,128)(2,1)S(1)}, bf16[192,640]{1,0:T(8,128)(2,1)S(1)}, bf16[768,256]{1,0:T(8,128)(2,1)S(1)}, bf16[768,256]{1,0:T(8,128)(2,1)S(1)}) custom-call(bf16[10,72,128]{2,1,0:T(8,128)(2,1)S(1)} %copy-done, bf16[10,72,128]{2,1,0:T(8,128)(2,1)S(1)} %collective-permute-done.recv_ref, ...), custom_call_target="tpu_custom_call" | custom-call | flops 999999995904 | bytes 5000000 | tf_op jit(solution)/shard_map/ready/pallas_call | solution.py:42
  13.0 7.9 %all-to-all-done.grad_ref = bf16[8,72,512]{2,1,0:T(8,128)(2,1)} async-done(((bf16[8,72,512]{2,1,0:T(8,128)(2,1)}), bf16[8,72,512]{2,1,0:T(8,128)(2,1)}, u32[]{:S(2)}, u32[]{:S(2)}) %all-to-all-start) | async-done | bytes 589856 | tf_op jit(solution)/shard_map/all_to_all | solution.py:386
  20.9 5.7 %grads.1 = (bf16[4,32,128]{2,1,0:T(8,128)(2,1)S(1)}, bf16[4,32,128]{2,1,0:T(8,128)(2,1)S(1)}, f32[64,128]{1,0:T(8,128)S(1)}, f32[64,128]{1,0:T(8,128)S(1)}) custom-call(bf16[8,72,512]{2,1,0:T(8,128)(2,1)} %all-to-all-done.grad_ref, bf16[8,80,256]{2,1,0:T(8,128)(2,1)S(1)} %get-tuple-element.20.pre_ref, bf16[864,640]{1,0:T(8,128)(2,1)S(1)} %get-tuple-element.21.hid_ref, ...), custom_call_target="tpu_custom_call" | custom-call | flops 3000000000 | bytes 4000000 | tf_op jit(solution)/shard_map/grads/pallas_call | solution.py:42
  26.6 2.0 %collective-permute-start.2 = (f32[64,128]{1,0:T(8,128)S(1)}, f32[64,128]{1,0:T(8,128)S(1)}, u32[]{:S(2)}, u32[]{:S(2)}) collective-permute-start(f32[64,128]{1,0:T(8,128)S(1)} %get-tuple-element.28), channel_id=1, source_target_pairs={{0,8},{1,9},{2,10},{3,11},{4,12},{5,13},{6,14},{7,15},{8,0},{9,1},... | collective-permute-start | bytes 98312 | tf_op jit(solution)/shard_map/ppermute | solution.py:409
  28.7 0.9 %collective-permute-done.2 = f32[64,128]{1,0:T(8,128)S(1)} collective-permute-done((f32[64,128]{1,0:T(8,128)S(1)}, f32[64,128]{1,0:T(8,128)S(1)}, u32[]{:S(2)}, u32[]{:S(2)}) %collective-permute-start.2) | collective-permute-done | bytes 32800 | tf_op jit(solution)/shard_map/ppermute | solution.py:409
  29.5 2.7 %collective-permute-start.5 = (f32[64,128]{1,0:T(8,128)S(1)}, f32[64,128]{1,0:T(8,128)S(1)}, u32[]{:S(2)}, u32[]{:S(2)}) collective-permute-start(f32[64,128]{1,0:T(8,128)S(1)} %add.30), channel_id=1, source_target_pairs={{0,32},{1,33},{2,34},{3,35},{4,36},{5,37},{6,38},{7,39},{8,40},{9,... | collective-permute-start | bytes 98312 | tf_op jit(solution)/shard_map/ppermute | solution.py:412
  32.3 0.9 %collective-permute-start.4 = (f32[64,128]{1,0:T(8,128)S(1)}, f32[64,128]{1,0:T(8,128)S(1)}, u32[]{:S(2)}, u32[]{:S(2)}) collective-permute-start(f32[64,128]{1,0:T(8,128)S(1)} %add.30), channel_id=1, source_target_pairs={{0,48},{1,49},{2,50},{3,51},{4,52},{5,53},{6,54},{7,55},{8,56},{9,... | collective-permute-start | bytes 98312 | tf_op jit(solution)/shard_map/ppermute | solution.py:412
  33.1 0.0 collective-permute-start.3
  33.1 0.7 %collective-permute-done.5 = f32[64,128]{1,0:T(8,128)S(1)} collective-permute-done((f32[64,128]{1,0:T(8,128)S(1)}, f32[64,128]{1,0:T(8,128)S(1)}, u32[]{:S(2)}, u32[]{:S(2)}) %collective-permute-start.5) | collective-permute-done | bytes 32800 | tf_op jit(solution)/shard_map/ppermute | solution.py:412
  33.8 2.5 %collective-permute-done.4 = f32[64,128]{1,0:T(8,128)S(1)} collective-permute-done((f32[64,128]{1,0:T(8,128)S(1)}, f32[64,128]{1,0:T(8,128)S(1)}, u32[]{:S(2)}, u32[]{:S(2)}) %collective-permute-start.4) | collective-permute-done | bytes 32800 | tf_op jit(solution)/shard_map/ppermute | solution.py:412
  36.2 0.0 collective-permute-done.3
  36.3 1.3 %collective-permute-start.8 = (f32[64,128]{1,0:T(8,128)S(1)}, f32[64,128]{1,0:T(8,128)S(1)}, u32[]{:S(2)}, u32[]{:S(2)}) collective-permute-start(f32[64,128]{1,0:T(8,128)S(1)} %add_add_fusion.2), channel_id=1, source_target_pairs={{0,4},{1,5},{2,6},{3,7},{4,0},{5,1},{6,2},{7,3},{8,12},{9,13},{10,... | collective-permute-start | bytes 98312 | tf_op jit(solution)/shard_map/ppermute | solution.py:412
  37.5 1.7 %collective-permute-start.7 = (f32[64,128]{1,0:T(8,128)S(1)}, f32[64,128]{1,0:T(8,128)S(1)}, u32[]{:S(2)}, u32[]{:S(2)}) collective-permute-start(f32[64,128]{1,0:T(8,128)S(1)} %add_add_fusion.2), channel_id=1, source_target_pairs={{0,6},{1,7},{2,4},{3,5},{4,2},{5,3},{6,0},{7,1},{8,14},{9,15},{10,... | collective-permute-start | bytes 98312 | tf_op jit(solution)/shard_map/ppermute | solution.py:412
  39.2 0.0 collective-permute-start.6
  39.2 1.4 %collective-permute-done.8 = f32[64,128]{1,0:T(8,128)S(1)} collective-permute-done((f32[64,128]{1,0:T(8,128)S(1)}, f32[64,128]{1,0:T(8,128)S(1)}, u32[]{:S(2)}, u32[]{:S(2)}) %collective-permute-start.8) | collective-permute-done | bytes 32800 | tf_op jit(solution)/shard_map/ppermute | solution.py:412
  40.6 0.9 %collective-permute-done.7 = f32[64,128]{1,0:T(8,128)S(1)} collective-permute-done((f32[64,128]{1,0:T(8,128)S(1)}, f32[64,128]{1,0:T(8,128)S(1)}, u32[]{:S(2)}, u32[]{:S(2)}) %collective-permute-start.7) | collective-permute-done | bytes 32800 | tf_op jit(solution)/shard_map/ppermute | solution.py:412
  41.5 0.5 collective-permute-done.6
  42.0 3.4 %collective-permute-start.11 = (f32[64,128]{1,0:T(8,128)S(1)}, f32[64,128]{1,0:T(8,128)S(1)}, u32[]{:S(2)}, u32[]{:S(2)}) collective-permute-start(f32[64,128]{1,0:T(8,128)S(1)} %add_add_fusion.1), channel_id=1, source_target_pairs={{0,64},{1,65},{2,66},{3,67},{4,68},{5,69},{6,70},{7,71},{8,72},{9,... | collective-permute-start | bytes 98312 | tf_op jit(solution)/shard_map/ppermute | solution.py:412
  45.3 0.1 collective-permute-start.10
  45.5 0.3 collective-permute-start.9
  45.8 1.2 %collective-permute-start.1 = (bf16[4,32,128]{2,1,0:T(8,128)(2,1)S(1)}, bf16[4,32,128]{2,1,0:T(8,128)(2,1)S(1)}, u32[]{:S(2)}, u32[]{:S(2)}) collective-permute-start(bf16[4,32,128]{2,1,0:T(8,128)(2,1)S(1)} %get-tuple-element.26), channel_id=1, source_target_pairs={{0,1},{1,0},{2,3},{3,2},{4,5},{5,4},{6,7},{7,6},{8,9},{9,8},{10,11... | collective-permute-start | bytes 98312 | tf_op jit(solution)/shard_map/ppermute | solution.py:410
  46.9 0.0 collective-permute-done.11
  46.9 2.4 %collective-permute-done.10 = f32[64,128]{1,0:T(8,128)S(1)} collective-permute-done((f32[64,128]{1,0:T(8,128)S(1)}, f32[64,128]{1,0:T(8,128)S(1)}, u32[]{:S(2)}, u32[]{:S(2)}) %collective-permute-start.10) | collective-permute-done | bytes 32800 | tf_op jit(solution)/shard_map/ppermute | solution.py:412
  49.3 0.0 collective-permute-done.9
  49.3 5.0 %collective-permute-start.12 = (f32[64,128]{1,0:T(8,128)S(1)}, f32[64,128]{1,0:T(8,128)S(1)}, u32[]{:S(2)}, u32[]{:S(2)}) collective-permute-start(f32[64,128]{1,0:T(8,128)S(1)} %add_add_fusion.mine_ref), channel_id=1, source_target_pairs={{0,8},{1,9},{2,10},{3,11},{4,12},{5,13},{6,14},{7,15},{8,0},{9,1},... | collective-permute-start | bytes 98312 | tf_op jit(solution)/shard_map/ppermute | solution.py:414
  54.3 0.0 collective-permute-done.1.recv_ref
  54.3 0.7 %tile.1 = bf16[4,8,8,128]{3,2,1,0:T(8,128)(2,1)} custom-call(bf16[4,32,128]{2,1,0:T(8,128)(2,1)S(1)} %get-tuple-element.25.own_ref, bf16[4,32,128]{2,1,0:T(8,128)(2,1)S(1)} %collective-permute-done.1.recv_ref), custom_call_target="tpu_custom_call" | custom-call | flops 1000000 | bytes 200000 | tf_op jit(solution)/shard_map/tile/pallas_call | solution.py:42
  55.1 0.1 collective-permute-done.12.rest_ref
  55.2 0.9 %unpack.1 = (f32[4,16,27]{2,1,0:T(8,128)}, f32[27,16,32]{2,1,0:T(8,128)}) custom-call(f32[64,128]{1,0:T(8,128)S(1)} %add_add_fusion.mine_ref, f32[64,128]{1,0:T(8,128)S(1)} %collective-permute-done.12.rest_ref), custom_call_target="tpu_custom_call" | custom-call | flops 1000000 | bytes 200000 | tf_op jit(solution)/shard_map/unpack/pallas_call | solution.py:42
  (4 shorter events, 0.0 us)
Async XLA Ops:
  0.6 11.0 %copy-start.2 = (bf16[27,4,16]{0,2,1:T(8,128)(2,1)S(1)}, bf16[27,4,16]{0,2,1:T(8,128)(2,1)}, u32[]{:S(2)}) copy-start(bf16[27,4,16]{0,2,1:T(8,128)(2,1)} %param.8) | copy-start | bytes 10372
  0.6 11.2 %copy-start.1 = (bf16[27,16,32]{2,1,0:T(8,128)(2,1)S(1)}, bf16[27,16,32]{2,1,0:T(8,128)(2,1)}, u32[]{:S(2)}) copy-start(bf16[27,16,32]{2,1,0:T(8,128)(2,1)} %param.9) | copy-start | bytes 82948
  4.8 7.2 %copy-start = (bf16[10,72,128]{2,1,0:T(8,128)(2,1)S(1)}, bf16[10,72,128]{2,1,0:T(8,128)(2,1)}, u32[]{:S(2)}) copy-start(bf16[10,72,128]{2,1,0:T(8,128)(2,1)} %get-tuple-element.18.keep_ref) | copy-start | bytes 552964
  4.9 7.2 %collective-permute-start = (bf16[10,72,128]{2,1,0:T(8,128)(2,1)}, bf16[10,72,128]{2,1,0:T(8,128)(2,1)S(1)}, u32[]{:S(2)}, u32[]{:S(2)}) collective-permute-start(bf16[10,72,128]{2,1,0:T(8,128)(2,1)} %get-tuple-element.19), channel_id=1, source_target_pairs={{0,1},{1,0},{2,3},{3,2},{4,5},{5,4},{6,7},{7,6},{8,9},{9,8},{10,11... | collective-permute-start | bytes 552968 | tf_op jit(solution)/shard_map/ppermute | solution.py:385
  7.4 13.5 %all-to-all-start = ((bf16[8,72,512]{2,1,0:T(8,128)(2,1)}), bf16[8,72,512]{2,1,0:T(8,128)(2,1)}, u32[]{:S(2)}, u32[]{:S(2)}) async-start(bf16[8,72,512]{2,1,0:T(8,128)(2,1)} %get-tuple-element.17), calls=%async_computation | async-start | bytes 1179648 | tf_op jit(solution)/shard_map/all_to_all | solution.py:386
  26.6 2.9 %collective-permute-start.2 = (f32[64,128]{1,0:T(8,128)S(1)}, f32[64,128]{1,0:T(8,128)S(1)}, u32[]{:S(2)}, u32[]{:S(2)}) collective-permute-start(f32[64,128]{1,0:T(8,128)S(1)} %get-tuple-element.28), channel_id=1, source_target_pairs={{0,8},{1,9},{2,10},{3,11},{4,12},{5,13},{6,14},{7,15},{8,0},{9,1},... | collective-permute-start | bytes 98312 | tf_op jit(solution)/shard_map/ppermute | solution.py:409
  29.5 4.3 %collective-permute-start.5 = (f32[64,128]{1,0:T(8,128)S(1)}, f32[64,128]{1,0:T(8,128)S(1)}, u32[]{:S(2)}, u32[]{:S(2)}) collective-permute-start(f32[64,128]{1,0:T(8,128)S(1)} %add.30), channel_id=1, source_target_pairs={{0,32},{1,33},{2,34},{3,35},{4,36},{5,37},{6,38},{7,39},{8,40},{9,... | collective-permute-start | bytes 98312 | tf_op jit(solution)/shard_map/ppermute | solution.py:412
  32.3 4.0 %collective-permute-start.4 = (f32[64,128]{1,0:T(8,128)S(1)}, f32[64,128]{1,0:T(8,128)S(1)}, u32[]{:S(2)}, u32[]{:S(2)}) collective-permute-start(f32[64,128]{1,0:T(8,128)S(1)} %add.30), channel_id=1, source_target_pairs={{0,48},{1,49},{2,50},{3,51},{4,52},{5,53},{6,54},{7,55},{8,56},{9,... | collective-permute-start | bytes 98312 | tf_op jit(solution)/shard_map/ppermute | solution.py:412
  33.1 3.1 %collective-permute-start.3 = (f32[64,128]{1,0:T(8,128)S(1)}, f32[64,128]{1,0:T(8,128)S(1)}, u32[]{:S(2)}, u32[]{:S(2)}) collective-permute-start(f32[64,128]{1,0:T(8,128)S(1)} %add.30), channel_id=1, source_target_pairs={{0,16},{1,17},{2,18},{3,19},{4,20},{5,21},{6,22},{7,23},{8,24},{9,... | collective-permute-start | bytes 98312 | tf_op jit(solution)/shard_map/ppermute | solution.py:412
  36.3 4.3 %collective-permute-start.8 = (f32[64,128]{1,0:T(8,128)S(1)}, f32[64,128]{1,0:T(8,128)S(1)}, u32[]{:S(2)}, u32[]{:S(2)}) collective-permute-start(f32[64,128]{1,0:T(8,128)S(1)} %add_add_fusion.2), channel_id=1, source_target_pairs={{0,4},{1,5},{2,6},{3,7},{4,0},{5,1},{6,2},{7,3},{8,12},{9,13},{10,... | collective-permute-start | bytes 98312 | tf_op jit(solution)/shard_map/ppermute | solution.py:412
  37.5 4.0 %collective-permute-start.7 = (f32[64,128]{1,0:T(8,128)S(1)}, f32[64,128]{1,0:T(8,128)S(1)}, u32[]{:S(2)}, u32[]{:S(2)}) collective-permute-start(f32[64,128]{1,0:T(8,128)S(1)} %add_add_fusion.2), channel_id=1, source_target_pairs={{0,6},{1,7},{2,4},{3,5},{4,2},{5,3},{6,0},{7,1},{8,14},{9,15},{10,... | collective-permute-start | bytes 98312 | tf_op jit(solution)/shard_map/ppermute | solution.py:412
  39.2 2.8 %collective-permute-start.6 = (f32[64,128]{1,0:T(8,128)S(1)}, f32[64,128]{1,0:T(8,128)S(1)}, u32[]{:S(2)}, u32[]{:S(2)}) collective-permute-start(f32[64,128]{1,0:T(8,128)S(1)} %add_add_fusion.2), channel_id=1, source_target_pairs={{0,2},{1,3},{2,0},{3,1},{4,6},{5,7},{6,4},{7,5},{8,10},{9,11},{10,... | collective-permute-start | bytes 98312 | tf_op jit(solution)/shard_map/ppermute | solution.py:412
  42.0 5.0 %collective-permute-start.11 = (f32[64,128]{1,0:T(8,128)S(1)}, f32[64,128]{1,0:T(8,128)S(1)}, u32[]{:S(2)}, u32[]{:S(2)}) collective-permute-start(f32[64,128]{1,0:T(8,128)S(1)} %add_add_fusion.1), channel_id=1, source_target_pairs={{0,64},{1,65},{2,66},{3,67},{4,68},{5,69},{6,70},{7,71},{8,72},{9,... | collective-permute-start | bytes 98312 | tf_op jit(solution)/shard_map/ppermute | solution.py:412
  45.3 4.0 %collective-permute-start.10 = (f32[64,128]{1,0:T(8,128)S(1)}, f32[64,128]{1,0:T(8,128)S(1)}, u32[]{:S(2)}, u32[]{:S(2)}) collective-permute-start(f32[64,128]{1,0:T(8,128)S(1)} %add_add_fusion.1), channel_id=1, source_target_pairs={{0,65},{1,64},{2,67},{3,66},{4,69},{5,68},{6,71},{7,70},{8,73},{9,... | collective-permute-start | bytes 98312 | tf_op jit(solution)/shard_map/ppermute | solution.py:412
  45.5 3.9 %collective-permute-start.9 = (f32[64,128]{1,0:T(8,128)S(1)}, f32[64,128]{1,0:T(8,128)S(1)}, u32[]{:S(2)}, u32[]{:S(2)}) collective-permute-start(f32[64,128]{1,0:T(8,128)S(1)} %add_add_fusion.1), channel_id=1, source_target_pairs={{0,1},{1,0},{2,3},{3,2},{4,5},{5,4},{6,7},{7,6},{8,9},{9,8},{10,11... | collective-permute-start | bytes 98312 | tf_op jit(solution)/shard_map/ppermute | solution.py:412
  45.8 8.6 %collective-permute-start.1 = (bf16[4,32,128]{2,1,0:T(8,128)(2,1)S(1)}, bf16[4,32,128]{2,1,0:T(8,128)(2,1)S(1)}, u32[]{:S(2)}, u32[]{:S(2)}) collective-permute-start(bf16[4,32,128]{2,1,0:T(8,128)(2,1)S(1)} %get-tuple-element.26), channel_id=1, source_target_pairs={{0,1},{1,0},{2,3},{3,2},{4,5},{5,4},{6,7},{7,6},{8,9},{9,8},{10,11... | collective-permute-start | bytes 98312 | tf_op jit(solution)/shard_map/ppermute | solution.py:410
  49.3 5.9 %collective-permute-start.12 = (f32[64,128]{1,0:T(8,128)S(1)}, f32[64,128]{1,0:T(8,128)S(1)}, u32[]{:S(2)}, u32[]{:S(2)}) collective-permute-start(f32[64,128]{1,0:T(8,128)S(1)} %add_add_fusion.mine_ref), channel_id=1, source_target_pairs={{0,8},{1,9},{2,10},{3,11},{4,12},{5,13},{6,14},{7,15},{8,0},{9,1},... | collective-permute-start | bytes 98312 | tf_op jit(solution)/shard_map/ppermute | solution.py:414

commit v6 on v5

--- a/solution.py
+++ b/solution.py
@@ -62,17 +62,17 @@
 ):
     copies = [pltpu.make_async_copy(in_hbm, in_ref, sems.at[0])]
     copies += [
-        pltpu.make_async_copy(pre_hbm.at[:, pl.ds(4 * i, 4)], pre_ref.at[i], sems.at[1 + i]) for i in range(2)
+        pltpu.make_async_copy(pre_hbm.at[:, z], pre_ref.at[z], sems.at[5 + z]) for z in range(8)
     ]
     copies += [
-        pltpu.make_async_copy(slab_hbm.at[:, :, pl.ds(128 * b, 128)], slab_ref.at[b], sems.at[3 + b]) for b in range(4)
+        pltpu.make_async_copy(slab_hbm.at[:, :, pl.ds(128 * b, 128)], slab_ref.at[b], sems.at[1 + b]) for b in range(4)
     ]
     for copy in copies:
         copy.start()
     r = lax.rem(lax.axis_index("space"), 2)
     a, x = iota((WIDE, 128), 0), iota((WIDE, 128), 1)
     src, dst = iota((256, 256), 0), iota((256, 256), 1)
-    same = one_hot((src // 64 == dst // 8 % 4) & (src // 8 % 8 == dst // 32) & (src % 8 == dst % 8))
+    same = one_hot((src // 64 == dst % 4) & (src // 8 % 8 == dst // 32) & (src % 8 == dst // 4 % 8))
     order = row_major()
     gap = jnp.where(a < STRIP, x - a, -9999)
     pick = jnp.concatenate(
@@ -85,19 +85,26 @@
         keep_ref[8 + half] = got[:WIDE, 128 * half : 128 * half + 128].astype(BF16)
         send_ref[8 + half] = got[WIDE:, 128 * half : 128 * half + 128].astype(BF16)
     gap = jnp.where(a < STRIP + 2, x - a, -9999)
-    picks = [jnp.where(gap == STRIP * r - 1, 1.0, 0.0), jnp.where(gap == STRIP * (1 - r) - 1, 1.0, 0.0)]
-    end, x1 = iota((16, 128), 0), iota((16, 128), 1)
-    edges = jnp.zeros((16, 128), F32)
+    end = iota((16, 128), 0)
+    pick = jnp.concatenate(
+        [
+            jnp.where(gap == STRIP * r - 1, 1.0, 0.0),
+            jnp.where(gap == STRIP * (1 - r) - 1, 1.0, 0.0),
+            jnp.where(iota((16, 128), 1) == jnp.where(end == 0, 127, jnp.where(end == 8, 0, -1)), 1.0, 0.0),
+        ],
+        axis=0,
+    ).astype(BF16)
+    for copy in copies[1:9]:
+        copy.wait()
+    got = dot_t(pick, pre_ref[...].astype(F32).reshape(1024, 128).astype(BF16)).astype(BF16)
+    got = dot(jnp.concatenate([got[:, 128 * z : 128 * z + 128] for z in range(8)], axis=0), order)
+    edges = [jnp.zeros((8, 128), F32)] * 2
     for z in range(8):
-        if z % 4 == 0:
-            copies[1 + z // 4].wait()
-        ends = jnp.where((end % 8 == z) & (x1 == jnp.where(end < 8, 127, 0)), 1.0, 0.0)
-        pick = jnp.concatenate(picks + [ends], axis=0).astype(BF16)
-        rows = pre_ref[z // 4, :, z % 4].astype(F32).reshape(128, 128).astype(BF16)
-        got = dot(dot_t(pick, rows).astype(BF16), order)
-        keep_ref[z] = got[:WIDE].astype(BF16)
-        send_ref[z] = got[WIDE : 2 * WIDE].astype(BF16)
-        edges = edges + got[2 * WIDE :]
+        at = 160 * z
+        keep_ref[z] = got[at : at + WIDE].astype(BF16)
+        send_ref[z] = got[at + WIDE : at + 2 * WIDE].astype(BF16)
+        for i in range(2):
+            edges[i] = jnp.where(iota((8, 128), 0) == z, got[at + 144 + 8 * i : at + 145 + 8 * i], edges[i])
     results = [
         pltpu.make_async_copy(send_ref, send_hbm, done.at[8]), pltpu.make_async_copy(keep_ref, keep_hbm, done.at[9])
     ]
@@ -105,7 +112,7 @@
         copy.start()
 
     for b in range(4):
-        copies[3 + b].wait()
+        copies[9 + b].wait()
         wide_ref[b] = slab_ref[b].astype(F32).reshape(512, 128)
         for y in range(16):
             slot = (y + 1) % 16
@@ -122,7 +129,7 @@
             t = 4 * pair + i
             out_ref[t, :STRIP] = cut[WIDE * i : WIDE * i + STRIP].astype(BF16)
             last = cut[WIDE * i + STRIP : WIDE * i + WIDE]
-            edge = edges[:8] if t % 2 == 0 else edges[8:]
+            edge = edges[t % 2]
             last = jnp.concatenate(
                 [
                     jnp.where(late, pltpu.roll(edge, 4, 0), last[:, :128]),
@@ -138,7 +145,7 @@
         copy.wait()
 
 
-def join(keep_ref, recv_ref, pre_ref, hid_ref, ins_ref, wide_ref, thin_ref):
+def join(keep_ref, recv_ref, pre_ref, hid_ref, ins_ref, wide_ref, thin_ref, rows_ref):
     r = lax.rem(lax.axis_index("space"), 2)
     left = r == 0
     lane = iota((PAD, 128), 1)
@@ -168,9 +175,12 @@
                 for slot in {(y + 2) % 16, y + 2}:
                     hid_ref[48 * slot + 16 * kx : 48 * slot + 16 * kx + 16, :] = rows
     turned = thin_ref[...].T[:64]
+    rows_ref[...] = jnp.zeros((256, ROWS), F32)
     for kx in range(3):
         shifted = pltpu.roll(turned, 2 - kx, 1) if kx < 2 else turned
-        ins_ref[64 * kx : 64 * kx + 64, :] = shifted.astype(BF16)
+        for y in range(16):
+            rows_ref[16 * y + 4 * kx : 16 * y + 4 * kx + 4, :] = shifted[4 * y : 4 * y + 4]
+    ins_ref[...] = rows_ref[...].astype(BF16)
 
 
 def band(two_ref, one_ref, wide_ref, thin_ref):
@@ -205,10 +215,10 @@
 
 def ready_kernel(
     keep_ref, recv_ref, two_ref, one_ref,
-    pre_ref, hid_ref, ins_ref, wide_ref, thin_ref, hidden_ref, inputs_ref,
+    pre_ref, hid_ref, ins_ref, wide_ref, thin_ref, hidden_ref, inputs_ref, rows_ref,
 ):
     band(two_ref, one_ref, wide_ref, thin_ref)
-    join(keep_ref, recv_ref, pre_ref, hid_ref, ins_ref, hidden_ref, inputs_ref)
+    join(keep_ref, recv_ref, pre_ref, hid_ref, ins_ref, hidden_ref, inputs_ref, rows_ref)
 
 
 def planes(ref, kz, low, size):
@@ -222,37 +232,25 @@
 
 
 def grads_kernel(
-    grad_ref, pre_ref, hid_ref, ins_ref, wide_ref, thin_ref,
-    own_ref, give_ref, mine_ref, rest_ref, grad_s, act_s, out_s, terms_s,
+    grad_hbm, pre_ref, hid_ref, ins_ref, wide_ref, thin_ref,
+    own_ref, give_ref, mine_ref, rest_ref, grad_s, act_s, out_s, terms_s, first_s, sums_s, grad_ref, sems,
 ):
+    copies = [pltpu.make_async_copy(grad_hbm.at[z], grad_ref.at[z], sems.at[z]) for z in range(8)]
+    for copy in copies:
+        copy.start()
     space = lax.axis_index("space")
     left = lax.rem(space, 2) == 0
     for block in (0, 9):
         grad_s[PAD * block : PAD * block + PAD, :] = jnp.zeros((PAD, 512), BF16)
         act_s[PAD * block : PAD * block + PAD, :] = jnp.zeros((PAD, 256), BF16)
     for z in range(8):
+        copies[z].wait()
         plane = jnp.concatenate([grad_ref[z].astype(F32), jnp.zeros((PAD - WIDE, 512), F32)], axis=0)
         grad_s[PAD * (z + 1) : PAD * (z + 2), :] = plane.astype(BF16)
 
-    lane = iota((16, 128), 1)
-    taps = [None] * 28
     for kz in range(3):
         for half in range(2):
-            terms_s[half] = dot(hid_ref[384 * half : 384 * half + 480, :], planes(grad_s, kz, 256 * half, 256))
-        for kx in range(3):
-            for ky in range(3):
-                total = jnp.zeros((16, 128), F32)
-                for y in range(16):
-                    at = y + ky - 1
-                    if 0 <= at < 16:
-                        slot = (y + 1) % 16
-                        half = slot // 8
-                        row = 48 * ((at + 2) % 16 if half == 0 else at - 6) + 16 * kx
-                        col = 128 * (slot % 8 // 4)
-                        piece = terms_s[half, row : row + 16, col : col + 128]
-                        total = total + jnp.where(lane // 32 == slot % 4, piece, 0.0)
-                total = total + pltpu.roll(total, 64, 1)
-                taps[9 * kz + 3 * ky + kx] = total + pltpu.roll(total, 32, 1)
+            terms_s[kz, half] = dot(hid_ref[384 * half : 384 * half + 480, :], planes(grad_s, kz, 256 * half, 256))
 
     wide = [wide_ref[256 * kz : 256 * kz + 256, :] for kz in range(3)]
     none = jnp.zeros((32, 256), BF16)
@@ -282,42 +280,62 @@
 
     sides = jnp.concatenate([planes(act_s, kz, 0, 256) for kz in range(3)], axis=1)
     out_s[...] = across(dot(sides, thin_ref[...]))
-    for z in range(4):
-        pair = jnp.concatenate([out_s[PAD * z : PAD * z + STRIP], out_s[PAD * (z + 4) : PAD * (z + 4) + STRIP]], axis=0).T
-        own_ref[z] = jnp.where(left, pair[:32], pair[32:64]).astype(BF16)
-        give_ref[z] = jnp.where(left, pair[32:64], pair[:32]).astype(BF16)
-
-    row, col = iota((64, 256), 0), iota((64, 256), 1)
-    gap = 8 * (row // 32) + row % 8 - col // 16
-    packed = jnp.zeros((12, 128), F32)
-    for kz in range(3):
-        terms = dot(ins_ref[...], planes(act_s, kz, 0, 256)).reshape(3, 64, 256)
-        for ky in range(3):
-            part = jnp.where((gap == ky - 1)[None], terms, 0.0)
-            part = (part[:, :, :128] + part[:, :, 128:]).reshape(3, 2, 4, 8, 128)
-            part = jnp.sum(part[:, 0] + part[:, 1], axis=2).reshape(12, 128)
-            for by in (64, 32, 16):
-                part = part + pltpu.roll(part, by, 1)
-            if 3 * kz + ky < 8:
-                packed = jnp.where(iota((12, 128), 1) // 16 == 3 * kz + ky, part, packed)
-            else:
-                last = part
-    filler = jnp.zeros((4, 128), F32)
-    taps[27] = jnp.concatenate([last, filler], axis=0)
-    blocks = []
-    for q in range(7):
-        block = taps[4 * q]
-        for g in range(1, 4):
-            block = jnp.where(lane // 32 == g, taps[4 * q + g], block)
-        blocks.append(block)
-    blocks.append(jnp.concatenate([packed, filler], axis=0))
-    first = lax.rem(lax.axis_index("dp"), 2) == 0
+    for kz in range(3):
+        first_s[kz] = dot(ins_ref[...], planes(act_s, kz, 0, 256))
+
     cells = 16 * 8 * 16 * 512
     scale = cells**-0.5
-    for q in range(4):
-        low, high = blocks[q] * scale, blocks[q + 4] * scale
-        mine_ref[16 * q : 16 * q + 16, :] = jnp.where(first, low, high)
-        rest_ref[16 * q : 16 * q + 16, :] = jnp.where(first, high, low)
+    lane = iota((16, 128), 1)
+    for kz in range(3):
+        for ky in range(3):
+            for kx in range(3):
+                total = jnp.zeros((16, 128), F32)
+                for y in range(16):
+                    at = y + ky - 1
+                    if 0 <= at < 16:
+                        slot = (y + 1) % 16
+                        half = slot // 8
+                        row = 48 * ((at + 2) % 16 if half == 0 else at - 6) + 16 * kx
+                        col = 128 * (slot % 8 // 4)
+                        piece = terms_s[kz, half, row : row + 16, col : col + 128]
+                        total = total + jnp.where(lane // 32 == slot % 4, piece, 0.0)
+                total = total + pltpu.roll(total, 64, 1)
+                total = (total + pltpu.roll(total, 32, 1)) * scale
+                tap = 9 * kz + 3 * ky + kx
+                at = 16 * (tap // 4)
+                if tap % 4 == 0:
+                    sums_s[at : at + 16, :] = total
+                else:
+                    sums_s[at : at + 16, :] = jnp.where(lane // 32 == tap % 4, total, sums_s[at : at + 16, :])
+
+    row, col = iota((64, 128), 0), iota((64, 128), 1)
+    eye = one_hot(jnp.where(left, row, (row + 32) % 64) == col)
+    for z in range(4):
+        pair = jnp.concatenate([out_s[PAD * z : PAD * z + STRIP], out_s[PAD * (z + 4) : PAD * (z + 4) + STRIP]], axis=0)
+        pair = dot_t(eye, pair.astype(BF16))
+        own_ref[z] = pair[:32].astype(BF16)
+        give_ref[z] = pair[32:].astype(BF16)
+
+    packed = jnp.zeros((16, 128), F32)
+    for kz in range(3):
+        for ky in range(3):
+            total = jnp.zeros((16, 128), F32)
+            for y in range(16):
+                at = y + ky - 1
+                if 0 <= at < 16:
+                    piece = first_s[kz, 16 * at : 16 * at + 16, 128 * (y // 8) : 128 * (y // 8) + 128]
+                    total = total + jnp.where(lane // 16 == y % 8, piece, 0.0)
+            for by in (64, 32, 16):
+                total = total + pltpu.roll(total, by, 1)
+            total = total * scale
+            if 3 * kz + ky < 8:
+                packed = jnp.where(lane // 16 == 3 * kz + ky, total, packed)
+            else:
+                sums_s[96:112, :] = jnp.where(lane // 32 == 3, total, sums_s[96:112, :])
+    sums_s[112:128, :] = packed
+    first = lax.rem(lax.axis_index("dp"), 2) == 0
+    mine_ref[...] = jnp.where(first, sums_s[:64, :], sums_s[64:, :])
+    rest_ref[...] = jnp.where(first, sums_s[64:, :], sums_s[:64, :])
 
 
 def tile_kernel(own_ref, recv_ref, out_ref):
@@ -374,10 +392,10 @@
         cut_kernel, "cut",
         [shape((10, WIDE, 128), BF16), shape((10, WIDE, 128), BF16), shape((8, WIDE, 512), BF16)],
         [
-            pltpu.VMEM((4, 32, 16, 128), BF16), pltpu.VMEM((2, 16, 4, 8, 128), BF16), pltpu.VMEM((4, 8, 8, 128), BF16),
+            pltpu.VMEM((4, 32, 16, 128), BF16), pltpu.VMEM((8, 16, 8, 128), BF16), pltpu.VMEM((4, 8, 8, 128), BF16),
             pltpu.VMEM((10, WIDE, 128), BF16), pltpu.VMEM((10, WIDE, 128), BF16), pltpu.VMEM((8, WIDE, 512), BF16),
             pltpu.VMEM((4, 512, 128), F32), pltpu.VMEM((512, 512), BF16),
-            pltpu.SemaphoreType.DMA((7,)), pltpu.SemaphoreType.DMA((10,)),
+            pltpu.SemaphoreType.DMA((13,)), pltpu.SemaphoreType.DMA((10,)),
         ],
         [out_grad[0, 0], pre_act[0, 0], inputs[0, 0]], 4e8, 2e6, limit=FULL, far_args=(0, 1, 2), far_outs=(0, 1, 2),
     )
@@ -387,10 +405,10 @@
     pre, hid, ins, wide, thin = call(
         ready_kernel, "ready",
         [
-            shape((8, PAD, 256), BF16), shape((864, ROWS), BF16), shape((192, ROWS), BF16),
+            shape((8, PAD, 256), BF16), shape((864, ROWS), BF16), shape((256, ROWS), BF16),
             shape((768, 256), BF16), shape((768, 256), BF16),
         ],
-        [pltpu.VMEM((ROWS, 256), F32), pltpu.VMEM((ROWS, 128), F32)],
+        [pltpu.VMEM((ROWS, 256), F32), pltpu.VMEM((ROWS, 128), F32), pltpu.VMEM((256, ROWS), F32)],
         [
             keep, recv, conv2_weight.transpose(0, 2, 1).reshape(864, 16),
             conv1_weight.transpose(0, 2, 1).reshape(432, 4),
@@ -402,9 +420,10 @@
         [shape((4, 32, 128), BF16), shape((4, 32, 128), BF16), shape((64, 128), F32), shape((64, 128), F32)],
         [
             pltpu.VMEM((10 * PAD, 512), BF16), pltpu.VMEM((10 * PAD, 256), BF16),
-            pltpu.VMEM((ROWS, 128), F32), pltpu.VMEM((2, 480, 256), F32),
+            pltpu.VMEM((ROWS, 128), F32), pltpu.VMEM((3, 2, 480, 256), F32), pltpu.VMEM((3, 256, 256), F32), pltpu.VMEM((128, 128), F32),
+            pltpu.VMEM((8, WIDE, 512), BF16), pltpu.SemaphoreType.DMA((8,)),
         ],
-        [strips, pre, hid, ins, wide, thin], 3e9, 4e6, limit=SOME,
+        [strips, pre, hid, ins, wide, thin], 3e9, 4e6, limit=SOME, far_args=(0,),
     )
     total = mine + lax.ppermute(rest, ALL, cores)
     got = lax.ppermute(give, "space", swap)

time: 56.3 us -> 55.4 us (0.984)
  Pallas kernels: 12.5 us -> 11.6 us
    pallas_call x5, Pallas kernels: 12.5 us -> 11.6 us  [call(): pl.pallas_call(kernel, name=name, out_shape=outs, in_specs=[spec(i in far...]
where the time goes in v6:
time: 55.4 us; the launch traced here: 55.1 us
  starting transfers between devices  25.3 us (46%)
  waiting for transfers between devices  17.1 us (31%)
  Pallas kernels  11.6 us (21%)
  between operations  0.75 us (1%)
    pallas_call x5, Pallas kernels, call(): pl.pallas_call(kernel, name=name, out_shape=outs, in_specs=[spec(i in far...  11.6 us
    ppermute x9, starting transfers between devices, body(): parts = [lax.ppermute(total, ALL, pairs) for pairs in stage]  10.3 us
    ppermute x9, waiting for transfers between devices, body(): parts = [lax.ppermute(total, ALL, pairs) for pairs in stage]  8.28 us
    all_to_all x1, waiting for transfers between devices, body(): strips = lax.all_to_all(strips, 'space', 0, 0, tiled=True)  7.78 us
    ppermute x1, starting transfers between devices, body(): other = lax.ppermute(total, ALL, cores)  5 us
    all_to_all x1, starting transfers between devices, body(): strips = lax.all_to_all(strips, 'space', 0, 0, tiled=True)  4.21 us
    ppermute x1, starting transfers between devices, body(): recv = lax.ppermute(send, 'space', swap)  2.55 us
    ppermute x1, starting transfers between devices, body(): total = mine + lax.ppermute(rest, ALL, cores)  2.02 us
  transfers between devices with their start and end apart: 14, of which 9 were waited for; matrix products, arithmetic and copies ran while one was open for 1% of the time, Pallas kernels for 3%

profile of v6, /device:TPU:1, one launch (start us, length us, event | category | flops | bytes accessed | tf_op | source)
XLA Modules:
  0.0 55.1 jit_solution(4297182791815900064)
XLA Ops:
  0.6 0.0 copy-start.2
  0.6 0.0 copy-start.1
  0.7 3.3 %cut.1 = (bf16[10,72,128]{2,1,0:T(8,128)(2,1)}, bf16[10,72,128]{2,1,0:T(8,128)(2,1)}, bf16[8,72,512]{2,1,0:T(8,128)(2,1)}) custom-call(bf16[32,16,512]{2,1,0:T(8,128)(2,1)} %bitcast.14, bf16[16,8,8,128]{3,2,1,0:T(8,128)(2,1)} %bitcast.15, bf16[4,8,8,128]{3,2,1,0:T(8,128)(2,1)} %bitcast.16), custom_call_target="tpu_custom_call" | custom-call | flops 400000000 | bytes 2000000 | tf_op jit(solution)/shard_map/cut/pallas_call | solution.py:42
  4.0 0.0 copy-start
  4.0 2.5 %collective-permute-start = (bf16[10,72,128]{2,1,0:T(8,128)(2,1)}, bf16[10,72,128]{2,1,0:T(8,128)(2,1)S(1)}, u32[]{:S(2)}, u32[]{:S(2)}) collective-permute-start(bf16[10,72,128]{2,1,0:T(8,128)(2,1)} %get-tuple-element.19), channel_id=1, source_target_pairs={{0,1},{1,0},{2,3},{3,2},{4,5},{5,4},{6,7},{7,6},{8,9},{9,8},{10,11... | collective-permute-start | bytes 552968 | tf_op jit(solution)/shard_map/ppermute | solution.py:403
  6.5 4.2 %all-to-all-start = ((bf16[8,72,512]{2,1,0:T(8,128)(2,1)}), bf16[8,72,512]{2,1,0:T(8,128)(2,1)}, u32[]{:S(2)}, u32[]{:S(2)}) async-start(bf16[8,72,512]{2,1,0:T(8,128)(2,1)} %get-tuple-element.17), calls=%async_computation | async-start | bytes 1179648 | tf_op jit(solution)/shard_map/all_to_all | solution.py:404
  10.8 0.0 copy-done.2
  10.8 0.2 copy.9
  11.0 0.0 copy-done.1
  11.0 0.2 copy.8
  11.2 0.0 collective-permute-done.recv_ref
  11.2 0.0 copy-done
  11.2 1.0 %ready.1 = (bf16[8,80,256]{2,1,0:T(8,128)(2,1)S(1)}, bf16[864,640]{1,0:T(8,128)(2,1)S(1)}, bf16[256,640]{1,0:T(8,128)(2,1)S(1)}, bf16[768,256]{1,0:T(8,128)(2,1)S(1)}, bf16[768,256]{1,0:T(8,128)(2,1)S(1)}) custom-call(bf16[10,72,128]{2,1,0:T(8,128)(2,1)S(1)} %copy-done, bf16[10,72,128]{2,1,0:T(8,128)(2,1)S(1)} %collective-permute-done.recv_ref, ...), custom_call_target="tpu_custom_call" | custom-call | flops 999999995904 | bytes 5000000 | tf_op jit(solution)/shard_map/ready/pallas_call | solution.py:42
  12.2 7.8 %all-to-all-done.grad_hbm = bf16[8,72,512]{2,1,0:T(8,128)(2,1)} async-done(((bf16[8,72,512]{2,1,0:T(8,128)(2,1)}), bf16[8,72,512]{2,1,0:T(8,128)(2,1)}, u32[]{:S(2)}, u32[]{:S(2)}) %all-to-all-start) | async-done | bytes 589856 | tf_op jit(solution)/shard_map/all_to_all | solution.py:404
  20.0 5.7 %grads.1 = (bf16[4,32,128]{2,1,0:T(8,128)(2,1)S(1)}, bf16[4,32,128]{2,1,0:T(8,128)(2,1)S(1)}, f32[64,128]{1,0:T(8,128)S(1)}, f32[64,128]{1,0:T(8,128)S(1)}) custom-call(bf16[8,72,512]{2,1,0:T(8,128)(2,1)} %all-to-all-done.grad_hbm, bf16[8,80,256]{2,1,0:T(8,128)(2,1)S(1)} %get-tuple-element.20.pre_ref, bf16[864,640]{1,0:T(8,128)(2,1)S(1)} %get-tuple-element.21.hid_ref, ...), custom_call_target="tpu_custom_call" | custom-call | flops 3000000000 | bytes 4000000 | tf_op jit(solution)/shard_map/grads/pallas_call | solution.py:42
  25.7 2.0 %collective-permute-start.2 = (f32[64,128]{1,0:T(8,128)S(1)}, f32[64,128]{1,0:T(8,128)S(1)}, u32[]{:S(2)}, u32[]{:S(2)}) collective-permute-start(f32[64,128]{1,0:T(8,128)S(1)} %get-tuple-element.28), channel_id=1, source_target_pairs={{0,8},{1,9},{2,10},{3,11},{4,12},{5,13},{6,14},{7,15},{8,0},{9,1},... | collective-permute-start | bytes 98312 | tf_op jit(solution)/shard_map/ppermute | solution.py:428
  27.7 0.9 %collective-permute-done.2 = f32[64,128]{1,0:T(8,128)S(1)} collective-permute-done((f32[64,128]{1,0:T(8,128)S(1)}, f32[64,128]{1,0:T(8,128)S(1)}, u32[]{:S(2)}, u32[]{:S(2)}) %collective-permute-start.2) | collective-permute-done | bytes 32800 | tf_op jit(solution)/shard_map/ppermute | solution.py:428
  28.6 2.7 %collective-permute-start.5 = (f32[64,128]{1,0:T(8,128)S(1)}, f32[64,128]{1,0:T(8,128)S(1)}, u32[]{:S(2)}, u32[]{:S(2)}) collective-permute-start(f32[64,128]{1,0:T(8,128)S(1)} %add.30), channel_id=1, source_target_pairs={{0,32},{1,33},{2,34},{3,35},{4,36},{5,37},{6,38},{7,39},{8,40},{9,... | collective-permute-start | bytes 98312 | tf_op jit(solution)/shard_map/ppermute | solution.py:431
  31.3 0.9 %collective-permute-start.4 = (f32[64,128]{1,0:T(8,128)S(1)}, f32[64,128]{1,0:T(8,128)S(1)}, u32[]{:S(2)}, u32[]{:S(2)}) collective-permute-start(f32[64,128]{1,0:T(8,128)S(1)} %add.30), channel_id=1, source_target_pairs={{0,48},{1,49},{2,50},{3,51},{4,52},{5,53},{6,54},{7,55},{8,56},{9,... | collective-permute-start | bytes 98312 | tf_op jit(solution)/shard_map/ppermute | solution.py:431
  32.2 0.0 collective-permute-start.3
  32.2 0.7 %collective-permute-done.5 = f32[64,128]{1,0:T(8,128)S(1)} collective-permute-done((f32[64,128]{1,0:T(8,128)S(1)}, f32[64,128]{1,0:T(8,128)S(1)}, u32[]{:S(2)}, u32[]{:S(2)}) %collective-permute-start.5) | collective-permute-done | bytes 32800 | tf_op jit(solution)/shard_map/ppermute | solution.py:431
  32.9 2.4 %collective-permute-done.4 = f32[64,128]{1,0:T(8,128)S(1)} collective-permute-done((f32[64,128]{1,0:T(8,128)S(1)}, f32[64,128]{1,0:T(8,128)S(1)}, u32[]{:S(2)}, u32[]{:S(2)}) %collective-permute-start.4) | collective-permute-done | bytes 32800 | tf_op jit(solution)/shard_map/ppermute | solution.py:431
  35.3 0.0 collective-permute-done.3
  35.3 1.3 %collective-permute-start.8 = (f32[64,128]{1,0:T(8,128)S(1)}, f32[64,128]{1,0:T(8,128)S(1)}, u32[]{:S(2)}, u32[]{:S(2)}) collective-permute-start(f32[64,128]{1,0:T(8,128)S(1)} %add_add_fusion.2), channel_id=1, source_target_pairs={{0,4},{1,5},{2,6},{3,7},{4,0},{5,1},{6,2},{7,3},{8,12},{9,13},{10,... | collective-permute-start | bytes 98312 | tf_op jit(solution)/shard_map/ppermute | solution.py:431
  36.6 1.7 %collective-permute-start.7 = (f32[64,128]{1,0:T(8,128)S(1)}, f32[64,128]{1,0:T(8,128)S(1)}, u32[]{:S(2)}, u32[]{:S(2)}) collective-permute-start(f32[64,128]{1,0:T(8,128)S(1)} %add_add_fusion.2), channel_id=1, source_target_pairs={{0,6},{1,7},{2,4},{3,5},{4,2},{5,3},{6,0},{7,1},{8,14},{9,15},{10,... | collective-permute-start | bytes 98312 | tf_op jit(solution)/shard_map/ppermute | solution.py:431
  38.3 0.0 collective-permute-start.6
  38.3 1.4 %collective-permute-done.8 = f32[64,128]{1,0:T(8,128)S(1)} collective-permute-done((f32[64,128]{1,0:T(8,128)S(1)}, f32[64,128]{1,0:T(8,128)S(1)}, u32[]{:S(2)}, u32[]{:S(2)}) %collective-permute-start.8) | collective-permute-done | bytes 32800 | tf_op jit(solution)/shard_map/ppermute | solution.py:431
  39.7 0.9 %collective-permute-done.7 = f32[64,128]{1,0:T(8,128)S(1)} collective-permute-done((f32[64,128]{1,0:T(8,128)S(1)}, f32[64,128]{1,0:T(8,128)S(1)}, u32[]{:S(2)}, u32[]{:S(2)}) %collective-permute-start.7) | collective-permute-done | bytes 32800 | tf_op jit(solution)/shard_map/ppermute | solution.py:431
  40.6 0.5 collective-permute-done.6
  41.0 3.4 %collective-permute-start.11 = (f32[64,128]{1,0:T(8,128)S(1)}, f32[64,128]{1,0:T(8,128)S(1)}, u32[]{:S(2)}, u32[]{:S(2)}) collective-permute-start(f32[64,128]{1,0:T(8,128)S(1)} %add_add_fusion.1), channel_id=1, source_target_pairs={{0,64},{1,65},{2,66},{3,67},{4,68},{5,69},{6,70},{7,71},{8,72},{9,... | collective-permute-start | bytes 98312 | tf_op jit(solution)/shard_map/ppermute | solution.py:431
  44.4 0.1 collective-permute-start.10
  44.5 0.3 collective-permute-start.9
  44.8 1.2 %collective-permute-start.1 = (bf16[4,32,128]{2,1,0:T(8,128)(2,1)S(1)}, bf16[4,32,128]{2,1,0:T(8,128)(2,1)S(1)}, u32[]{:S(2)}, u32[]{:S(2)}) collective-permute-start(bf16[4,32,128]{2,1,0:T(8,128)(2,1)S(1)} %get-tuple-element.26), channel_id=1, source_target_pairs={{0,1},{1,0},{2,3},{3,2},{4,5},{5,4},{6,7},{7,6},{8,9},{9,8},{10,11... | collective-permute-start | bytes 98312 | tf_op jit(solution)/shard_map/ppermute | solution.py:429
  46.0 0.0 collective-permute-done.11
  46.0 2.4 %collective-permute-done.10 = f32[64,128]{1,0:T(8,128)S(1)} collective-permute-done((f32[64,128]{1,0:T(8,128)S(1)}, f32[64,128]{1,0:T(8,128)S(1)}, u32[]{:S(2)}, u32[]{:S(2)}) %collective-permute-start.10) | collective-permute-done | bytes 32800 | tf_op jit(solution)/shard_map/ppermute | solution.py:431
  48.4 0.0 collective-permute-done.9
  48.4 5.0 %collective-permute-start.12 = (f32[64,128]{1,0:T(8,128)S(1)}, f32[64,128]{1,0:T(8,128)S(1)}, u32[]{:S(2)}, u32[]{:S(2)}) collective-permute-start(f32[64,128]{1,0:T(8,128)S(1)} %add_add_fusion.mine_ref), channel_id=1, source_target_pairs={{0,8},{1,9},{2,10},{3,11},{4,12},{5,13},{6,14},{7,15},{8,0},{9,1},... | collective-permute-start | bytes 98312 | tf_op jit(solution)/shard_map/ppermute | solution.py:433
  53.4 0.0 collective-permute-done.1.recv_ref
  53.4 0.7 %tile.1 = bf16[4,8,8,128]{3,2,1,0:T(8,128)(2,1)} custom-call(bf16[4,32,128]{2,1,0:T(8,128)(2,1)S(1)} %get-tuple-element.25.own_ref, bf16[4,32,128]{2,1,0:T(8,128)(2,1)S(1)} %collective-permute-done.1.recv_ref), custom_call_target="tpu_custom_call" | custom-call | flops 1000000 | bytes 200000 | tf_op jit(solution)/shard_map/tile/pallas_call | solution.py:42
  54.1 0.1 collective-permute-done.12.rest_ref
  54.3 0.9 %unpack.1 = (f32[4,16,27]{2,1,0:T(8,128)}, f32[27,16,32]{2,1,0:T(8,128)}) custom-call(f32[64,128]{1,0:T(8,128)S(1)} %add_add_fusion.mine_ref, f32[64,128]{1,0:T(8,128)S(1)} %collective-permute-done.12.rest_ref), custom_call_target="tpu_custom_call" | custom-call | flops 1000000 | bytes 200000 | tf_op jit(solution)/shard_map/unpack/pallas_call | solution.py:42
  (4 shorter events, 0.0 us)
Async XLA Ops:
  0.6 10.1 %copy-start.2 = (bf16[27,4,16]{0,2,1:T(8,128)(2,1)S(1)}, bf16[27,4,16]{0,2,1:T(8,128)(2,1)}, u32[]{:S(2)}) copy-start(bf16[27,4,16]{0,2,1:T(8,128)(2,1)} %param.8) | copy-start | bytes 10372
  0.6 10.4 %copy-start.1 = (bf16[27,16,32]{2,1,0:T(8,128)(2,1)S(1)}, bf16[27,16,32]{2,1,0:T(8,128)(2,1)}, u32[]{:S(2)}) copy-start(bf16[27,16,32]{2,1,0:T(8,128)(2,1)} %param.9) | copy-start | bytes 82948
  4.0 7.2 %copy-start = (bf16[10,72,128]{2,1,0:T(8,128)(2,1)S(1)}, bf16[10,72,128]{2,1,0:T(8,128)(2,1)}, u32[]{:S(2)}) copy-start(bf16[10,72,128]{2,1,0:T(8,128)(2,1)} %get-tuple-element.18.keep_ref) | copy-start | bytes 552964
  4.0 7.2 %collective-permute-start = (bf16[10,72,128]{2,1,0:T(8,128)(2,1)}, bf16[10,72,128]{2,1,0:T(8,128)(2,1)S(1)}, u32[]{:S(2)}, u32[]{:S(2)}) collective-permute-start(bf16[10,72,128]{2,1,0:T(8,128)(2,1)} %get-tuple-element.19), channel_id=1, source_target_pairs={{0,1},{1,0},{2,3},{3,2},{4,5},{5,4},{6,7},{7,6},{8,9},{9,8},{10,11... | collective-permute-start | bytes 552968 | tf_op jit(solution)/shard_map/ppermute | solution.py:403
  6.5 13.5 %all-to-all-start = ((bf16[8,72,512]{2,1,0:T(8,128)(2,1)}), bf16[8,72,512]{2,1,0:T(8,128)(2,1)}, u32[]{:S(2)}, u32[]{:S(2)}) async-start(bf16[8,72,512]{2,1,0:T(8,128)(2,1)} %get-tuple-element.17), calls=%async_computation | async-start | bytes 1179648 | tf_op jit(solution)/shard_map/all_to_all | solution.py:404
  25.7 2.9 %collective-permute-start.2 = (f32[64,128]{1,0:T(8,128)S(1)}, f32[64,128]{1,0:T(8,128)S(1)}, u32[]{:S(2)}, u32[]{:S(2)}) collective-permute-start(f32[64,128]{1,0:T(8,128)S(1)} %get-tuple-element.28), channel_id=1, source_target_pairs={{0,8},{1,9},{2,10},{3,11},{4,12},{5,13},{6,14},{7,15},{8,0},{9,1},... | collective-permute-start | bytes 98312 | tf_op jit(solution)/shard_map/ppermute | solution.py:428
  28.6 4.3 %collective-permute-start.5 = (f32[64,128]{1,0:T(8,128)S(1)}, f32[64,128]{1,0:T(8,128)S(1)}, u32[]{:S(2)}, u32[]{:S(2)}) collective-permute-start(f32[64,128]{1,0:T(8,128)S(1)} %add.30), channel_id=1, source_target_pairs={{0,32},{1,33},{2,34},{3,35},{4,36},{5,37},{6,38},{7,39},{8,40},{9,... | collective-permute-start | bytes 98312 | tf_op jit(solution)/shard_map/ppermute | solution.py:431
  31.3 4.0 %collective-permute-start.4 = (f32[64,128]{1,0:T(8,128)S(1)}, f32[64,128]{1,0:T(8,128)S(1)}, u32[]{:S(2)}, u32[]{:S(2)}) collective-permute-start(f32[64,128]{1,0:T(8,128)S(1)} %add.30), channel_id=1, source_target_pairs={{0,48},{1,49},{2,50},{3,51},{4,52},{5,53},{6,54},{7,55},{8,56},{9,... | collective-permute-start | bytes 98312 | tf_op jit(solution)/shard_map/ppermute | solution.py:431
  32.2 3.1 %collective-permute-start.3 = (f32[64,128]{1,0:T(8,128)S(1)}, f32[64,128]{1,0:T(8,128)S(1)}, u32[]{:S(2)}, u32[]{:S(2)}) collective-permute-start(f32[64,128]{1,0:T(8,128)S(1)} %add.30), channel_id=1, source_target_pairs={{0,16},{1,17},{2,18},{3,19},{4,20},{5,21},{6,22},{7,23},{8,24},{9,... | collective-permute-start | bytes 98312 | tf_op jit(solution)/shard_map/ppermute | solution.py:431
  35.3 4.3 %collective-permute-start.8 = (f32[64,128]{1,0:T(8,128)S(1)}, f32[64,128]{1,0:T(8,128)S(1)}, u32[]{:S(2)}, u32[]{:S(2)}) collective-permute-start(f32[64,128]{1,0:T(8,128)S(1)} %add_add_fusion.2), channel_id=1, source_target_pairs={{0,4},{1,5},{2,6},{3,7},{4,0},{5,1},{6,2},{7,3},{8,12},{9,13},{10,... | collective-permute-start | bytes 98312 | tf_op jit(solution)/shard_map/ppermute | solution.py:431
  36.6 4.0 %collective-permute-start.7 = (f32[64,128]{1,0:T(8,128)S(1)}, f32[64,128]{1,0:T(8,128)S(1)}, u32[]{:S(2)}, u32[]{:S(2)}) collective-permute-start(f32[64,128]{1,0:T(8,128)S(1)} %add_add_fusion.2), channel_id=1, source_target_pairs={{0,6},{1,7},{2,4},{3,5},{4,2},{5,3},{6,0},{7,1},{8,14},{9,15},{10,... | collective-permute-start | bytes 98312 | tf_op jit(solution)/shard_map/ppermute | solution.py:431
  38.3 2.8 %collective-permute-start.6 = (f32[64,128]{1,0:T(8,128)S(1)}, f32[64,128]{1,0:T(8,128)S(1)}, u32[]{:S(2)}, u32[]{:S(2)}) collective-permute-start(f32[64,128]{1,0:T(8,128)S(1)} %add_add_fusion.2), channel_id=1, source_target_pairs={{0,2},{1,3},{2,0},{3,1},{4,6},{5,7},{6,4},{7,5},{8,10},{9,11},{10,... | collective-permute-start | bytes 98312 | tf_op jit(solution)/shard_map/ppermute | solution.py:431
  41.0 5.0 %collective-permute-start.11 = (f32[64,128]{1,0:T(8,128)S(1)}, f32[64,128]{1,0:T(8,128)S(1)}, u32[]{:S(2)}, u32[]{:S(2)}) collective-permute-start(f32[64,128]{1,0:T(8,128)S(1)} %add_add_fusion.1), channel_id=1, source_target_pairs={{0,64},{1,65},{2,66},{3,67},{4,68},{5,69},{6,70},{7,71},{8,72},{9,... | collective-permute-start | bytes 98312 | tf_op jit(solution)/shard_map/ppermute | solution.py:431
  44.4 4.0 %collective-permute-start.10 = (f32[64,128]{1,0:T(8,128)S(1)}, f32[64,128]{1,0:T(8,128)S(1)}, u32[]{:S(2)}, u32[]{:S(2)}) collective-permute-start(f32[64,128]{1,0:T(8,128)S(1)} %add_add_fusion.1), channel_id=1, source_target_pairs={{0,65},{1,64},{2,67},{3,66},{4,69},{5,68},{6,71},{7,70},{8,73},{9,... | collective-permute-start | bytes 98312 | tf_op jit(solution)/shard_map/ppermute | solution.py:431
  44.5 3.9 %collective-permute-start.9 = (f32[64,128]{1,0:T(8,128)S(1)}, f32[64,128]{1,0:T(8,128)S(1)}, u32[]{:S(2)}, u32[]{:S(2)}) collective-permute-start(f32[64,128]{1,0:T(8,128)S(1)} %add_add_fusion.1), channel_id=1, source_target_pairs={{0,1},{1,0},{2,3},{3,2},{4,5},{5,4},{6,7},{7,6},{8,9},{9,8},{10,11... | collective-permute-start | bytes 98312 | tf_op jit(solution)/shard_map/ppermute | solution.py:431
  44.8 8.6 %collective-permute-start.1 = (bf16[4,32,128]{2,1,0:T(8,128)(2,1)S(1)}, bf16[4,32,128]{2,1,0:T(8,128)(2,1)S(1)}, u32[]{:S(2)}, u32[]{:S(2)}) collective-permute-start(bf16[4,32,128]{2,1,0:T(8,128)(2,1)S(1)} %get-tuple-element.26), channel_id=1, source_target_pairs={{0,1},{1,0},{2,3},{3,2},{4,5},{5,4},{6,7},{7,6},{8,9},{9,8},{10,11... | collective-permute-start | bytes 98312 | tf_op jit(solution)/shard_map/ppermute | solution.py:429
  48.4 5.9 %collective-permute-start.12 = (f32[64,128]{1,0:T(8,128)S(1)}, f32[64,128]{1,0:T(8,128)S(1)}, u32[]{:S(2)}, u32[]{:S(2)}) collective-permute-start(f32[64,128]{1,0:T(8,128)S(1)} %add_add_fusion.mine_ref), channel_id=1, source_target_pairs={{0,8},{1,9},{2,10},{3,11},{4,12},{5,13},{6,14},{7,15},{8,0},{9,1},... | collective-permute-start | bytes 98312 | tf_op jit(solution)/shard_map/ppermute | solution.py:433

commit v7 on v6

--- a/solution.py
+++ b/solution.py
@@ -183,11 +183,12 @@
     ins_ref[...] = rows_ref[...].astype(BF16)
 
 
-def band(two_ref, one_ref, wide_ref, thin_ref):
-    def lay(terms, rows, kz, ky):
-        parts = [terms[rows * (9 * kz + 3 * ky + kx) :][:rows] for kx in range(3)]
-        return jnp.where(iota((rows, 128), 1) < 64, parts[0], parts[1]), parts[2]
-
+def lay(terms, rows, kz, ky):
+    parts = [terms[rows * (9 * kz + 3 * ky + kx) :][:rows] for kx in range(3)]
+    return jnp.where(iota((rows, 128), 1) < 64, parts[0], parts[1]), parts[2]
+
+
+def band_two(two_ref, wide_ref):
     two = dot(two_ref[...], one_hot(iota((16, 128), 1) % 16 == iota((16, 128), 0)))
     group = iota((32, 128), 1) // 16 % 4
     for kz in range(3):
@@ -199,6 +200,9 @@
                     block = jnp.where(group == ky + slot - 2, terms[ky][half], block)
                 at = 256 * kz + 32 * slot
                 wide_ref[at : at + 32, 128 * half : 128 * half + 128] = block.astype(BF16)
+
+
+def band_one(one_ref, thin_ref):
     one = dot(one_ref[...], one_hot(iota((4, 128), 1) // 8 % 4 == iota((4, 128), 0)))
     lane = iota((16, 128), 1)
     group = 8 * (lane // 32 % 2) + lane % 8
@@ -214,10 +218,9 @@
 
 
 def ready_kernel(
-    keep_ref, recv_ref, two_ref, one_ref,
-    pre_ref, hid_ref, ins_ref, wide_ref, thin_ref, hidden_ref, inputs_ref, rows_ref,
+    keep_ref, recv_ref, two_ref, pre_ref, hid_ref, ins_ref, wide_ref, hidden_ref, inputs_ref, rows_ref
 ):
-    band(two_ref, one_ref, wide_ref, thin_ref)
+    band_two(two_ref, wide_ref)
     join(keep_ref, recv_ref, pre_ref, hid_ref, ins_ref, hidden_ref, inputs_ref, rows_ref)
 
 
@@ -232,19 +235,15 @@
 
 
 def grads_kernel(
-    grad_hbm, pre_ref, hid_ref, ins_ref, wide_ref, thin_ref,
-    own_ref, give_ref, mine_ref, rest_ref, grad_s, act_s, out_s, terms_s, first_s, sums_s, grad_ref, sems,
+    grad_ref, pre_ref, hid_ref, ins_ref, wide_ref,
+    act_s, mine_ref, rest_ref, grad_s, terms_s, first_s, sums_s,
 ):
-    copies = [pltpu.make_async_copy(grad_hbm.at[z], grad_ref.at[z], sems.at[z]) for z in range(8)]
-    for copy in copies:
-        copy.start()
     space = lax.axis_index("space")
     left = lax.rem(space, 2) == 0
     for block in (0, 9):
         grad_s[PAD * block : PAD * block + PAD, :] = jnp.zeros((PAD, 512), BF16)
         act_s[PAD * block : PAD * block + PAD, :] = jnp.zeros((PAD, 256), BF16)
     for z in range(8):
-        copies[z].wait()
         plane = jnp.concatenate([grad_ref[z].astype(F32), jnp.zeros((PAD - WIDE, 512), F32)], axis=0)
         grad_s[PAD * (z + 1) : PAD * (z + 2), :] = plane.astype(BF16)
 
@@ -278,8 +277,6 @@
         value = act[PAD * z : PAD * z + PAD] * jnp.where(pre > 0, 1.0, LEAK)
         act_s[PAD * (z + 1) : PAD * (z + 2), :] = jnp.where(inside, value, 0.0).astype(BF16)
 
-    sides = jnp.concatenate([planes(act_s, kz, 0, 256) for kz in range(3)], axis=1)
-    out_s[...] = across(dot(sides, thin_ref[...]))
     for kz in range(3):
         first_s[kz] = dot(ins_ref[...], planes(act_s, kz, 0, 256))
 
@@ -308,14 +305,6 @@
                 else:
                     sums_s[at : at + 16, :] = jnp.where(lane // 32 == tap % 4, total, sums_s[at : at + 16, :])
 
-    row, col = iota((64, 128), 0), iota((64, 128), 1)
-    eye = one_hot(jnp.where(left, row, (row + 32) % 64) == col)
-    for z in range(4):
-        pair = jnp.concatenate([out_s[PAD * z : PAD * z + STRIP], out_s[PAD * (z + 4) : PAD * (z + 4) + STRIP]], axis=0)
-        pair = dot_t(eye, pair.astype(BF16))
-        own_ref[z] = pair[:32].astype(BF16)
-        give_ref[z] = pair[32:].astype(BF16)
-
     packed = jnp.zeros((16, 128), F32)
     for kz in range(3):
         for ky in range(3):
@@ -338,6 +327,20 @@
     rest_ref[...] = jnp.where(first, sums_s[64:, :], sums_s[:64, :])
 
 
+def back_kernel(act_s, one_ref, own_ref, give_ref, out_s, thin_ref):
+    band_one(one_ref, thin_ref)
+    left = lax.rem(lax.axis_index("space"), 2) == 0
+    sides = jnp.concatenate([planes(act_s, kz, 0, 256) for kz in range(3)], axis=1)
+    out_s[...] = across(dot(sides, thin_ref[...]))
+    row, col = iota((64, 128), 0), iota((64, 128), 1)
+    eye = one_hot(jnp.where(left, row, (row + 32) % 64) == col)
+    for z in range(4):
+        pair = jnp.concatenate([out_s[PAD * z : PAD * z + STRIP], out_s[PAD * (z + 4) : PAD * (z + 4) + STRIP]], axis=0)
+        pair = dot_t(eye, pair.astype(BF16))
+        own_ref[z] = pair[:32].astype(BF16)
+        give_ref[z] = pair[32:].astype(BF16)
+
+
 def tile_kernel(own_ref, recv_ref, out_ref):
     left = lax.rem(lax.axis_index("space"), 2) == 0
     low_lanes = iota((32, 128), 1) < STRIP
@@ -402,28 +405,28 @@
     swap = [(i, i ^ 1) for i in range(8)]
     recv = lax.ppermute(send, "space", swap)
     strips = lax.all_to_all(strips, "space", 0, 0, tiled=True)
-    pre, hid, ins, wide, thin = call(
+    pre, hid, ins, wide = call(
         ready_kernel, "ready",
         [
             shape((8, PAD, 256), BF16), shape((864, ROWS), BF16), shape((256, ROWS), BF16),
-            shape((768, 256), BF16), shape((768, 256), BF16),
+            shape((768, 256), BF16),
         ],
         [pltpu.VMEM((ROWS, 256), F32), pltpu.VMEM((ROWS, 128), F32), pltpu.VMEM((256, ROWS), F32)],
+        [keep, recv, conv2_weight.transpose(0, 2, 1).reshape(864, 16)],
+        2e10, 5e6, limit=SOME,
+    )
+    act, mine, rest = call(
+        grads_kernel, "grads",
+        [shape((10 * PAD, 256), BF16), shape((64, 128), F32), shape((64, 128), F32)],
         [
-            keep, recv, conv2_weight.transpose(0, 2, 1).reshape(864, 16),
-            conv1_weight.transpose(0, 2, 1).reshape(432, 4),
+            pltpu.VMEM((10 * PAD, 512), BF16), pltpu.VMEM((3, 2, 480, 256), F32), pltpu.VMEM((3, 256, 256), F32),
+            pltpu.VMEM((128, 128), F32),
         ],
-        1e12, 5e6, limit=SOME,
-    )
-    own, give, mine, rest = call(
-        grads_kernel, "grads",
-        [shape((4, 32, 128), BF16), shape((4, 32, 128), BF16), shape((64, 128), F32), shape((64, 128), F32)],
-        [
-            pltpu.VMEM((10 * PAD, 512), BF16), pltpu.VMEM((10 * PAD, 256), BF16),
-            pltpu.VMEM((ROWS, 128), F32), pltpu.VMEM((3, 2, 480, 256), F32), pltpu.VMEM((3, 256, 256), F32), pltpu.VMEM((128, 128), F32),
-            pltpu.VMEM((8, WIDE, 512), BF16), pltpu.SemaphoreType.DMA((8,)),
-        ],
-        [strips, pre, hid, ins, wide, thin], 3e9, 4e6, limit=SOME, far_args=(0,),
+        [strips, pre, hid, ins, wide], 3e9, 4e6, limit=SOME,
+    )
+    own, give = call(
+        back_kernel, "back", [shape((4, 32, 128), BF16), shape((4, 32, 128), BF16)], [pltpu.VMEM((ROWS, 128), F32), pltpu.VMEM((768, 256), BF16)],
+        [act, conv1_weight.transpose(0, 2, 1).reshape(432, 4)], 5e8, 1e6,
     )
     total = mine + lax.ppermute(rest, ALL, cores)
     got = lax.ppermute(give, "space", swap)

time: 55.4 us -> 53.3 us (0.962)
  waiting for transfers between devices: 17.1 us -> 16.1 us
  Pallas kernels: 11.6 us -> 10.8 us
    ppermute x9, waiting for transfers between devices: 8.28 us -> 6.9 us  [body(): parts = [lax.ppermute(total, ALL, pairs) for pairs in stage]]
    pallas_call x5 -> x6, Pallas kernels: 11.6 us -> 10.8 us  [call(): pl.pallas_call(kernel, name=name, out_shape=outs, in_specs=[spec(i in far...]
  transfers between devices with their start and end apart: 14 -> 14, of which waited for: 9 -> 9; matrix products, arithmetic and copies ran while one was open for 1% -> 1% of each run, Pallas kernels for 3% -> 5%
where the time goes in v7:
time: 53.3 us; the launch traced here: 53.1 us
  starting transfers between devices  25.1 us (47%)
  waiting for transfers between devices  16.1 us (30%)
  Pallas kernels  10.8 us (20%)
  between operations  0.71 us (1%)
    pallas_call x6, Pallas kernels, call(): pl.pallas_call(kernel, name=name, out_shape=outs, in_specs=[spec(i in far...  10.8 us
    ppermute x9, starting transfers between devices, body(): parts = [lax.ppermute(total, ALL, pairs) for pairs in stage]  10.6 us
    all_to_all x1, waiting for transfers between devices, body(): strips = lax.all_to_all(strips, 'space', 0, 0, tiled=True)  8.02 us
    ppermute x9, waiting for transfers between devices, body(): parts = [lax.ppermute(total, ALL, pairs) for pairs in stage]  6.9 us
    ppermute x1, starting transfers between devices, body(): other = lax.ppermute(total, ALL, cores)  4.72 us
    all_to_all x1, starting transfers between devices, body(): strips = lax.all_to_all(strips, 'space', 0, 0, tiled=True)  4.19 us
    ppermute x1, starting transfers between devices, body(): recv = lax.ppermute(send, 'space', swap)  2.55 us
    ppermute x1, starting transfers between devices, body(): total = mine + lax.ppermute(rest, ALL, cores)  2.01 us
  transfers between devices with their start and end apart: 14, of which 9 were waited for; matrix products, arithmetic and copies ran while one was open for 1% of the time, Pallas kernels for 5%

profile of v7, /device:TPU:1, one launch (start us, length us, event | category | flops | bytes accessed | tf_op | source)
XLA Modules:
  0.0 53.1 jit_solution(16456796154868269608)
XLA Ops:
  0.6 0.0 copy-start.1
  0.6 3.3 %cut.1 = (bf16[10,72,128]{2,1,0:T(8,128)(2,1)}, bf16[10,72,128]{2,1,0:T(8,128)(2,1)}, bf16[8,72,512]{2,1,0:T(8,128)(2,1)}) custom-call(bf16[32,16,512]{2,1,0:T(8,128)(2,1)} %bitcast.14, bf16[16,8,8,128]{3,2,1,0:T(8,128)(2,1)} %bitcast.15, bf16[4,8,8,128]{3,2,1,0:T(8,128)(2,1)} %bitcast.16), custom_call_target="tpu_custom_call" | custom-call | flops 400000000 | bytes 2000000 | tf_op jit(solution)/shard_map/cut/pallas_call | solution.py:42
  4.0 0.0 copy-start
  4.0 2.5 %collective-permute-start = (bf16[10,72,128]{2,1,0:T(8,128)(2,1)}, bf16[10,72,128]{2,1,0:T(8,128)(2,1)S(1)}, u32[]{:S(2)}, u32[]{:S(2)}) collective-permute-start(bf16[10,72,128]{2,1,0:T(8,128)(2,1)} %get-tuple-element.19), channel_id=1, source_target_pairs={{0,1},{1,0},{2,3},{3,2},{4,5},{5,4},{6,7},{7,6},{8,9},{9,8},{10,11... | collective-permute-start | bytes 552968 | tf_op jit(solution)/shard_map/ppermute | solution.py:406
  6.5 4.2 %all-to-all-start = ((bf16[8,72,512]{2,1,0:T(8,128)(2,1)}), bf16[8,72,512]{2,1,0:T(8,128)(2,1)S(1)}, u32[]{:S(2)}, u32[]{:S(2)}) async-start(bf16[8,72,512]{2,1,0:T(8,128)(2,1)} %get-tuple-element.17), calls=%async_computation | async-start | bytes 1179648 | tf_op jit(solution)/shard_map/all_to_all | solution.py:407
  10.7 0.0 copy-done.1
  10.7 0.2 copy.8
  10.9 0.2 collective-permute-done.recv_ref
  11.1 0.0 copy-done
  11.1 0.8 %ready.1 = (bf16[8,80,256]{2,1,0:T(8,128)(2,1)S(1)}, bf16[864,640]{1,0:T(8,128)(2,1)S(1)}, bf16[256,640]{1,0:T(8,128)(2,1)S(1)}, bf16[768,256]{1,0:T(8,128)(2,1)S(1)}) custom-call(bf16[10,72,128]{2,1,0:T(8,128)(2,1)S(1)} %copy-done, bf16[10,72,128]{2,1,0:T(8,128)(2,1)S(1)} %collective-permute-done.recv_ref, bf16[864,16]{1,0:T(8,128)(2,1)S(1)} %bitcast.9), custom_call_target="tpu_custom_call" | custom-call | flops 20000000000 | bytes 5000000 | tf_op jit(solution)/shard_map/ready/pallas_call | solution.py:42
  11.9 8.0 %all-to-all-done.grad_ref = bf16[8,72,512]{2,1,0:T(8,128)(2,1)S(1)} async-done(((bf16[8,72,512]{2,1,0:T(8,128)(2,1)}), bf16[8,72,512]{2,1,0:T(8,128)(2,1)S(1)}, u32[]{:S(2)}, u32[]{:S(2)}) %all-to-all-start) | async-done | bytes 589856 | tf_op jit(solution)/shard_map/all_to_all | solution.py:407
  19.9 0.0 copy-start.2
  19.9 4.2 %grads.1 = (bf16[800,256]{1,0:T(8,128)(2,1)S(1)}, f32[64,128]{1,0:T(8,128)S(1)}, f32[64,128]{1,0:T(8,128)S(1)}) custom-call(bf16[8,72,512]{2,1,0:T(8,128)(2,1)S(1)} %all-to-all-done.grad_ref, bf16[8,80,256]{2,1,0:T(8,128)(2,1)S(1)} %get-tuple-element.20.pre_ref, bf16[864,640]{1,0:T(8,128)(2,1)S(1)} %get-tuple-element.21.hid_ref, ...), custom_call_target="tpu_custom_call" | custom-call | flops 3000000000 | bytes 4000000 | tf_op jit(solution)/shard_map/grads/pallas_call | solution.py:42
  24.1 2.0 %collective-permute-start.2 = (f32[64,128]{1,0:T(8,128)S(1)}, f32[64,128]{1,0:T(8,128)S(1)}, u32[]{:S(2)}, u32[]{:S(2)}) collective-permute-start(f32[64,128]{1,0:T(8,128)S(1)} %get-tuple-element.28), channel_id=1, source_target_pairs={{0,8},{1,9},{2,10},{3,11},{4,12},{5,13},{6,14},{7,15},{8,0},{9,1},... | collective-permute-start | bytes 98312 | tf_op jit(solution)/shard_map/ppermute | solution.py:431
  26.1 0.9 %collective-permute-done.2 = f32[64,128]{1,0:T(8,128)S(1)} collective-permute-done((f32[64,128]{1,0:T(8,128)S(1)}, f32[64,128]{1,0:T(8,128)S(1)}, u32[]{:S(2)}, u32[]{:S(2)}) %collective-permute-start.2) | collective-permute-done | bytes 32800 | tf_op jit(solution)/shard_map/ppermute | solution.py:431
  27.0 2.5 %collective-permute-start.4 = (f32[64,128]{1,0:T(8,128)S(1)}, f32[64,128]{1,0:T(8,128)S(1)}, u32[]{:S(2)}, u32[]{:S(2)}) collective-permute-start(f32[64,128]{1,0:T(8,128)S(1)} %add.30), channel_id=1, source_target_pairs={{0,48},{1,49},{2,50},{3,51},{4,52},{5,53},{6,54},{7,55},{8,56},{9,... | collective-permute-start | bytes 98312 | tf_op jit(solution)/shard_map/ppermute | solution.py:434
  29.4 0.5 collective-permute-start.5
  30.0 0.3 collective-permute-start.3
  30.2 0.7 %collective-permute-done.4 = f32[64,128]{1,0:T(8,128)S(1)} collective-permute-done((f32[64,128]{1,0:T(8,128)S(1)}, f32[64,128]{1,0:T(8,128)S(1)}, u32[]{:S(2)}, u32[]{:S(2)}) %collective-permute-start.4) | collective-permute-done | bytes 32800 | tf_op jit(solution)/shard_map/ppermute | solution.py:434
  30.9 2.8 %collective-permute-done.5 = f32[64,128]{1,0:T(8,128)S(1)} collective-permute-done((f32[64,128]{1,0:T(8,128)S(1)}, f32[64,128]{1,0:T(8,128)S(1)}, u32[]{:S(2)}, u32[]{:S(2)}) %collective-permute-start.5) | collective-permute-done | bytes 32800 | tf_op jit(solution)/shard_map/ppermute | solution.py:434
  33.7 0.0 collective-permute-done.3
  33.7 1.0 %collective-permute-start.7 = (f32[64,128]{1,0:T(8,128)S(1)}, f32[64,128]{1,0:T(8,128)S(1)}, u32[]{:S(2)}, u32[]{:S(2)}) collective-permute-start(f32[64,128]{1,0:T(8,128)S(1)} %add_add_fusion.2), channel_id=1, source_target_pairs={{0,6},{1,7},{2,4},{3,5},{4,2},{5,3},{6,0},{7,1},{8,14},{9,15},{10,... | collective-permute-start | bytes 98312 | tf_op jit(solution)/shard_map/ppermute | solution.py:434
  34.7 1.4 %collective-permute-start.8 = (f32[64,128]{1,0:T(8,128)S(1)}, f32[64,128]{1,0:T(8,128)S(1)}, u32[]{:S(2)}, u32[]{:S(2)}) collective-permute-start(f32[64,128]{1,0:T(8,128)S(1)} %add_add_fusion.2), channel_id=1, source_target_pairs={{0,4},{1,5},{2,6},{3,7},{4,0},{5,1},{6,2},{7,3},{8,12},{9,13},{10,... | collective-permute-start | bytes 98312 | tf_op jit(solution)/shard_map/ppermute | solution.py:434
  36.0 1.0 %collective-permute-start.6 = (f32[64,128]{1,0:T(8,128)S(1)}, f32[64,128]{1,0:T(8,128)S(1)}, u32[]{:S(2)}, u32[]{:S(2)}) collective-permute-start(f32[64,128]{1,0:T(8,128)S(1)} %add_add_fusion.2), channel_id=1, source_target_pairs={{0,2},{1,3},{2,0},{3,1},{4,6},{5,7},{6,4},{7,5},{8,10},{9,11},{10,... | collective-permute-start | bytes 98312 | tf_op jit(solution)/shard_map/ppermute | solution.py:434
  37.1 0.0 copy-done.2
  37.1 0.2 copy.9
  37.3 0.5 collective-permute-done.7
  37.8 1.2 %collective-permute-done.8 = f32[64,128]{1,0:T(8,128)S(1)} collective-permute-done((f32[64,128]{1,0:T(8,128)S(1)}, f32[64,128]{1,0:T(8,128)S(1)}, u32[]{:S(2)}, u32[]{:S(2)}) %collective-permute-start.8) | collective-permute-done | bytes 32800 | tf_op jit(solution)/shard_map/ppermute | solution.py:434
  39.0 0.0 collective-permute-done.6
  39.0 3.4 %collective-permute-start.10 = (f32[64,128]{1,0:T(8,128)S(1)}, f32[64,128]{1,0:T(8,128)S(1)}, u32[]{:S(2)}, u32[]{:S(2)}) collective-permute-start(f32[64,128]{1,0:T(8,128)S(1)} %add_add_fusion.1), channel_id=1, source_target_pairs={{0,65},{1,64},{2,67},{3,66},{4,69},{5,68},{6,71},{7,70},{8,73},{9,... | collective-permute-start | bytes 98312 | tf_op jit(solution)/shard_map/ppermute | solution.py:434
  42.4 0.1 collective-permute-start.11
  42.5 0.6 %collective-permute-start.9 = (f32[64,128]{1,0:T(8,128)S(1)}, f32[64,128]{1,0:T(8,128)S(1)}, u32[]{:S(2)}, u32[]{:S(2)}) collective-permute-start(f32[64,128]{1,0:T(8,128)S(1)} %add_add_fusion.1), channel_id=1, source_target_pairs={{0,1},{1,0},{2,3},{3,2},{4,5},{5,4},{6,7},{7,6},{8,9},{9,8},{10,11... | collective-permute-start | bytes 98312 | tf_op jit(solution)/shard_map/ppermute | solution.py:434
  43.0 0.9 %back.1 = (bf16[4,32,128]{2,1,0:T(8,128)(2,1)S(1)}, bf16[4,32,128]{2,1,0:T(8,128)(2,1)S(1)}) custom-call(bf16[800,256]{1,0:T(8,128)(2,1)S(1)} %get-tuple-element.24.act_s, bf16[432,4]{1,0:T(8,128)(2,1)S(1)} %bitcast.10), custom_call_target="tpu_custom_call" | custom-call | flops 500000000 | bytes 1000000 | tf_op jit(solution)/shard_map/back/pallas_call | solution.py:42
  43.9 1.0 %collective-permute-start.1 = (bf16[4,32,128]{2,1,0:T(8,128)(2,1)S(1)}, bf16[4,32,128]{2,1,0:T(8,128)(2,1)S(1)}, u32[]{:S(2)}, u32[]{:S(2)}) collective-permute-start(bf16[4,32,128]{2,1,0:T(8,128)(2,1)S(1)} %get-tuple-element.26), channel_id=1, source_target_pairs={{0,1},{1,0},{2,3},{3,2},{4,5},{5,4},{6,7},{7,6},{8,9},{9,8},{10,11... | collective-permute-start | bytes 98312 | tf_op jit(solution)/shard_map/ppermute | solution.py:432
  44.9 0.0 collective-permute-done.10
  44.9 1.7 %collective-permute-done.11 = f32[64,128]{1,0:T(8,128)S(1)} collective-permute-done((f32[64,128]{1,0:T(8,128)S(1)}, f32[64,128]{1,0:T(8,128)S(1)}, u32[]{:S(2)}, u32[]{:S(2)}) %collective-permute-start.11) | collective-permute-done | bytes 32800 | tf_op jit(solution)/shard_map/ppermute | solution.py:434
  46.6 0.0 collective-permute-done.9
  46.6 4.7 %collective-permute-start.12 = (f32[64,128]{1,0:T(8,128)S(1)}, f32[64,128]{1,0:T(8,128)S(1)}, u32[]{:S(2)}, u32[]{:S(2)}) collective-permute-start(f32[64,128]{1,0:T(8,128)S(1)} %add_add_fusion.mine_ref), channel_id=1, source_target_pairs={{0,8},{1,9},{2,10},{3,11},{4,12},{5,13},{6,14},{7,15},{8,0},{9,1},... | collective-permute-start | bytes 98312 | tf_op jit(solution)/shard_map/ppermute | solution.py:436
  51.4 0.0 collective-permute-done.1.recv_ref
  51.4 0.7 %tile.1 = bf16[4,8,8,128]{3,2,1,0:T(8,128)(2,1)} custom-call(bf16[4,32,128]{2,1,0:T(8,128)(2,1)S(1)} %get-tuple-element.25.own_ref, bf16[4,32,128]{2,1,0:T(8,128)(2,1)S(1)} %collective-permute-done.1.recv_ref), custom_call_target="tpu_custom_call" | custom-call | flops 1000000 | bytes 200000 | tf_op jit(solution)/shard_map/tile/pallas_call | solution.py:42
  52.1 0.1 collective-permute-done.12.rest_ref
  52.2 0.9 %unpack.1 = (f32[4,16,27]{2,1,0:T(8,128)}, f32[27,16,32]{2,1,0:T(8,128)}) custom-call(f32[64,128]{1,0:T(8,128)S(1)} %add_add_fusion.mine_ref, f32[64,128]{1,0:T(8,128)S(1)} %collective-permute-done.12.rest_ref), custom_call_target="tpu_custom_call" | custom-call | flops 1000000 | bytes 200000 | tf_op jit(solution)/shard_map/unpack/pallas_call | solution.py:42
  (4 shorter events, 0.0 us)
Async XLA Ops:
  0.6 10.1 %copy-start.1 = (bf16[27,16,32]{2,1,0:T(8,128)(2,1)S(1)}, bf16[27,16,32]{2,1,0:T(8,128)(2,1)}, u32[]{:S(2)}) copy-start(bf16[27,16,32]{2,1,0:T(8,128)(2,1)} %param.9) | copy-start | bytes 82948
  4.0 7.1 %copy-start = (bf16[10,72,128]{2,1,0:T(8,128)(2,1)S(1)}, bf16[10,72,128]{2,1,0:T(8,128)(2,1)}, u32[]{:S(2)}) copy-start(bf16[10,72,128]{2,1,0:T(8,128)(2,1)} %get-tuple-element.18.keep_ref) | copy-start | bytes 552964
  4.0 7.1 %collective-permute-start = (bf16[10,72,128]{2,1,0:T(8,128)(2,1)}, bf16[10,72,128]{2,1,0:T(8,128)(2,1)S(1)}, u32[]{:S(2)}, u32[]{:S(2)}) collective-permute-start(bf16[10,72,128]{2,1,0:T(8,128)(2,1)} %get-tuple-element.19), channel_id=1, source_target_pairs={{0,1},{1,0},{2,3},{3,2},{4,5},{5,4},{6,7},{7,6},{8,9},{9,8},{10,11... | collective-permute-start | bytes 552968 | tf_op jit(solution)/shard_map/ppermute | solution.py:406
  6.5 13.4 %all-to-all-start = ((bf16[8,72,512]{2,1,0:T(8,128)(2,1)}), bf16[8,72,512]{2,1,0:T(8,128)(2,1)S(1)}, u32[]{:S(2)}, u32[]{:S(2)}) async-start(bf16[8,72,512]{2,1,0:T(8,128)(2,1)} %get-tuple-element.17), calls=%async_computation | async-start | bytes 1179648 | tf_op jit(solution)/shard_map/all_to_all | solution.py:407
  19.9 17.1 %copy-start.2 = (bf16[27,4,16]{0,2,1:T(8,128)(2,1)S(1)}, bf16[27,4,16]{0,2,1:T(8,128)(2,1)}, u32[]{:S(2)}) copy-start(bf16[27,4,16]{0,2,1:T(8,128)(2,1)} %param.8) | copy-start | bytes 10372
  24.1 2.9 %collective-permute-start.2 = (f32[64,128]{1,0:T(8,128)S(1)}, f32[64,128]{1,0:T(8,128)S(1)}, u32[]{:S(2)}, u32[]{:S(2)}) collective-permute-start(f32[64,128]{1,0:T(8,128)S(1)} %get-tuple-element.28), channel_id=1, source_target_pairs={{0,8},{1,9},{2,10},{3,11},{4,12},{5,13},{6,14},{7,15},{8,0},{9,1},... | collective-permute-start | bytes 98312 | tf_op jit(solution)/shard_map/ppermute | solution.py:431
  27.0 4.0 %collective-permute-start.4 = (f32[64,128]{1,0:T(8,128)S(1)}, f32[64,128]{1,0:T(8,128)S(1)}, u32[]{:S(2)}, u32[]{:S(2)}) collective-permute-start(f32[64,128]{1,0:T(8,128)S(1)} %add.30), channel_id=1, source_target_pairs={{0,48},{1,49},{2,50},{3,51},{4,52},{5,53},{6,54},{7,55},{8,56},{9,... | collective-permute-start | bytes 98312 | tf_op jit(solution)/shard_map/ppermute | solution.py:434
  29.4 4.3 %collective-permute-start.5 = (f32[64,128]{1,0:T(8,128)S(1)}, f32[64,128]{1,0:T(8,128)S(1)}, u32[]{:S(2)}, u32[]{:S(2)}) collective-permute-start(f32[64,128]{1,0:T(8,128)S(1)} %add.30), channel_id=1, source_target_pairs={{0,32},{1,33},{2,34},{3,35},{4,36},{5,37},{6,38},{7,39},{8,40},{9,... | collective-permute-start | bytes 98312 | tf_op jit(solution)/shard_map/ppermute | solution.py:434
  30.0 3.8 %collective-permute-start.3 = (f32[64,128]{1,0:T(8,128)S(1)}, f32[64,128]{1,0:T(8,128)S(1)}, u32[]{:S(2)}, u32[]{:S(2)}) collective-permute-start(f32[64,128]{1,0:T(8,128)S(1)} %add.30), channel_id=1, source_target_pairs={{0,16},{1,17},{2,18},{3,19},{4,20},{5,21},{6,22},{7,23},{8,24},{9,... | collective-permute-start | bytes 98312 | tf_op jit(solution)/shard_map/ppermute | solution.py:434
  33.7 4.1 %collective-permute-start.7 = (f32[64,128]{1,0:T(8,128)S(1)}, f32[64,128]{1,0:T(8,128)S(1)}, u32[]{:S(2)}, u32[]{:S(2)}) collective-permute-start(f32[64,128]{1,0:T(8,128)S(1)} %add_add_fusion.2), channel_id=1, source_target_pairs={{0,6},{1,7},{2,4},{3,5},{4,2},{5,3},{6,0},{7,1},{8,14},{9,15},{10,... | collective-permute-start | bytes 98312 | tf_op jit(solution)/shard_map/ppermute | solution.py:434
  34.7 4.3 %collective-permute-start.8 = (f32[64,128]{1,0:T(8,128)S(1)}, f32[64,128]{1,0:T(8,128)S(1)}, u32[]{:S(2)}, u32[]{:S(2)}) collective-permute-start(f32[64,128]{1,0:T(8,128)S(1)} %add_add_fusion.2), channel_id=1, source_target_pairs={{0,4},{1,5},{2,6},{3,7},{4,0},{5,1},{6,2},{7,3},{8,12},{9,13},{10,... | collective-permute-start | bytes 98312 | tf_op jit(solution)/shard_map/ppermute | solution.py:434
  36.0 2.9 %collective-permute-start.6 = (f32[64,128]{1,0:T(8,128)S(1)}, f32[64,128]{1,0:T(8,128)S(1)}, u32[]{:S(2)}, u32[]{:S(2)}) collective-permute-start(f32[64,128]{1,0:T(8,128)S(1)} %add_add_fusion.2), channel_id=1, source_target_pairs={{0,2},{1,3},{2,0},{3,1},{4,6},{5,7},{6,4},{7,5},{8,10},{9,11},{10,... | collective-permute-start | bytes 98312 | tf_op jit(solution)/shard_map/ppermute | solution.py:434
  39.0 5.9 %collective-permute-start.10 = (f32[64,128]{1,0:T(8,128)S(1)}, f32[64,128]{1,0:T(8,128)S(1)}, u32[]{:S(2)}, u32[]{:S(2)}) collective-permute-start(f32[64,128]{1,0:T(8,128)S(1)} %add_add_fusion.1), channel_id=1, source_target_pairs={{0,65},{1,64},{2,67},{3,66},{4,69},{5,68},{6,71},{7,70},{8,73},{9,... | collective-permute-start | bytes 98312 | tf_op jit(solution)/shard_map/ppermute | solution.py:434
  42.4 4.3 %collective-permute-start.11 = (f32[64,128]{1,0:T(8,128)S(1)}, f32[64,128]{1,0:T(8,128)S(1)}, u32[]{:S(2)}, u32[]{:S(2)}) collective-permute-start(f32[64,128]{1,0:T(8,128)S(1)} %add_add_fusion.1), channel_id=1, source_target_pairs={{0,64},{1,65},{2,66},{3,67},{4,68},{5,69},{6,70},{7,71},{8,72},{9,... | collective-permute-start | bytes 98312 | tf_op jit(solution)/shard_map/ppermute | solution.py:434
  42.5 4.2 %collective-permute-start.9 = (f32[64,128]{1,0:T(8,128)S(1)}, f32[64,128]{1,0:T(8,128)S(1)}, u32[]{:S(2)}, u32[]{:S(2)}) collective-permute-start(f32[64,128]{1,0:T(8,128)S(1)} %add_add_fusion.1), channel_id=1, source_target_pairs={{0,1},{1,0},{2,3},{3,2},{4,5},{5,4},{6,7},{7,6},{8,9},{9,8},{10,11... | collective-permute-start | bytes 98312 | tf_op jit(solution)/shard_map/ppermute | solution.py:434
  43.9 7.4 %collective-permute-start.1 = (bf16[4,32,128]{2,1,0:T(8,128)(2,1)S(1)}, bf16[4,32,128]{2,1,0:T(8,128)(2,1)S(1)}, u32[]{:S(2)}, u32[]{:S(2)}) collective-permute-start(bf16[4,32,128]{2,1,0:T(8,128)(2,1)S(1)} %get-tuple-element.26), channel_id=1, source_target_pairs={{0,1},{1,0},{2,3},{3,2},{4,5},{5,4},{6,7},{7,6},{8,9},{9,8},{10,11... | collective-permute-start | bytes 98312 | tf_op jit(solution)/shard_map/ppermute | solution.py:432
  46.6 5.6 %collective-permute-start.12 = (f32[64,128]{1,0:T(8,128)S(1)}, f32[64,128]{1,0:T(8,128)S(1)}, u32[]{:S(2)}, u32[]{:S(2)}) collective-permute-start(f32[64,128]{1,0:T(8,128)S(1)} %add_add_fusion.mine_ref), channel_id=1, source_target_pairs={{0,8},{1,9},{2,10},{3,11},{4,12},{5,13},{6,14},{7,15},{8,0},{9,1},... | collective-permute-start | bytes 98312 | tf_op jit(solution)/shard_map/ppermute | solution.py:436

commit v8 on v7

--- a/solution.py
+++ b/solution.py
@@ -236,7 +236,7 @@
 
 def grads_kernel(
     grad_ref, pre_ref, hid_ref, ins_ref, wide_ref,
-    act_s, mine_ref, rest_ref, grad_s, terms_s, first_s, sums_s,
+    act_s, sums_s, grad_s, terms_s, first_s,
 ):
     space = lax.axis_index("space")
     left = lax.rem(space, 2) == 0
@@ -244,8 +244,10 @@
         grad_s[PAD * block : PAD * block + PAD, :] = jnp.zeros((PAD, 512), BF16)
         act_s[PAD * block : PAD * block + PAD, :] = jnp.zeros((PAD, 256), BF16)
     for z in range(8):
-        plane = jnp.concatenate([grad_ref[z].astype(F32), jnp.zeros((PAD - WIDE, 512), F32)], axis=0)
-        grad_s[PAD * (z + 1) : PAD * (z + 2), :] = plane.astype(BF16)
+        at = PAD * (z + 1)
+        grad_s[at : at + STRIP, :] = grad_ref[z, :STRIP]
+        last = jnp.concatenate([grad_ref[z, STRIP:].astype(F32), jnp.zeros((PAD - WIDE, 512), F32)], axis=0)
+        grad_s[at + STRIP : at + PAD, :] = last.astype(BF16)
 
     for kz in range(3):
         for half in range(2):
@@ -322,9 +324,6 @@
             else:
                 sums_s[96:112, :] = jnp.where(lane // 32 == 3, total, sums_s[96:112, :])
     sums_s[112:128, :] = packed
-    first = lax.rem(lax.axis_index("dp"), 2) == 0
-    mine_ref[...] = jnp.where(first, sums_s[:64, :], sums_s[64:, :])
-    rest_ref[...] = jnp.where(first, sums_s[64:, :], sums_s[:64, :])
 
 
 def back_kernel(act_s, one_ref, own_ref, give_ref, out_s, thin_ref):
@@ -353,11 +352,8 @@
         out_ref[:, z + 4] = far.reshape(4, 8, 128).astype(BF16)
 
 
-def unpack_kernel(mine_ref, rest_ref, one_ref, two_ref, flat_ref):
-    first = lax.rem(lax.axis_index("dp"), 2) == 0
-    mine, rest = mine_ref[...], rest_ref[...]
-    low, high = jnp.where(first, mine, rest), jnp.where(first, rest, mine)
-    blocks = [low[16 * q : 16 * q + 16] for q in range(4)] + [high[16 * q : 16 * q + 16] for q in range(4)]
+def unpack_kernel(total_ref, one_ref, two_ref, flat_ref):
+    blocks = [total_ref[16 * q : 16 * q + 16] for q in range(8)]
     for pair in range(9):
         source, lane = (blocks[7], 16 * pair) if pair < 8 else (blocks[6], 96)
         source = pltpu.roll(source, 128 - lane, 1) if lane else source
@@ -415,12 +411,11 @@
         [keep, recv, conv2_weight.transpose(0, 2, 1).reshape(864, 16)],
         2e10, 5e6, limit=SOME,
     )
-    act, mine, rest = call(
+    act, sums = call(
         grads_kernel, "grads",
-        [shape((10 * PAD, 256), BF16), shape((64, 128), F32), shape((64, 128), F32)],
+        [shape((10 * PAD, 256), BF16), shape((128, 128), F32)],
         [
             pltpu.VMEM((10 * PAD, 512), BF16), pltpu.VMEM((3, 2, 480, 256), F32), pltpu.VMEM((3, 256, 256), F32),
-            pltpu.VMEM((128, 128), F32),
         ],
         [strips, pre, hid, ins, wide], 3e9, 4e6, limit=SOME,
     )
@@ -428,16 +423,20 @@
         back_kernel, "back", [shape((4, 32, 128), BF16), shape((4, 32, 128), BF16)], [pltpu.VMEM((ROWS, 128), F32), pltpu.VMEM((768, 256), BF16)],
         [act, conv1_weight.transpose(0, 2, 1).reshape(432, 4)], 5e8, 1e6,
     )
-    total = mine + lax.ppermute(rest, ALL, cores)
-    got = lax.ppermute(give, "space", swap)
+    total = sums + lax.ppermute(sums, ALL, cores)
+    got = None
     for stage in stages:
         parts = [lax.ppermute(total, ALL, pairs) for pairs in stage]
         total = (total + parts[0]) + (parts[1] + parts[2])
-    other = lax.ppermute(total, ALL, cores)
+        if got is None:
+            total, give = lax.optimization_barrier((total, give))
+            got = lax.ppermute(give, "space", swap)
+        elif stage is stages[1]:
+            total, got = lax.optimization_barrier((total, got))
     (input_grad,) = call(tile_kernel, "tile", [shape((4, 8, 8, 128), BF16)], [], [own, got], 1e6, 2e5)
     first, second = call(
         unpack_kernel, "unpack", [shape((4, 16, 27), F32), shape((27, 16, 32), F32)], [pltpu.VMEM((128, 128), F32)],
-        [total, other], 1e6, 2e5,
+        [total], 1e6, 2e5,
     )
     return input_grad[None, None], first.transpose(2, 0, 1), second
 

time: 53.3 us -> 53.2 us (level)
  the two profiles are of different devices: /device:TPU:1 before, /device:TPU:0 now
where the time goes in v8:
time: 53.2 us; the launch traced here: 53 us
  starting transfers between devices  20.9 us (39%)
  waiting for transfers between devices  20.4 us (38%)
  Pallas kernels  10.6 us (20%)
  between operations  0.72 us (1%)
    ppermute x9, starting transfers between devices, body(): parts = [lax.ppermute(total, ALL, pairs) for pairs in stage]  12.8 us
    pallas_call x6, Pallas kernels, call(): pl.pallas_call(kernel, name=name, out_shape=outs, in_specs=[spec(i in far...  10.6 us
    ppermute x9, waiting for transfers between devices, body(): parts = [lax.ppermute(total, ALL, pairs) for pairs in stage]  9.3 us
    all_to_all x1, waiting for transfers between devices, body(): strips = lax.all_to_all(strips, 'space', 0, 0, tiled=True)  8.7 us
    all_to_all x1, starting transfers between devices, body(): strips = lax.all_to_all(strips, 'space', 0, 0, tiled=True)  4.47 us
    ppermute x1, starting transfers between devices, body(): recv = lax.ppermute(send, 'space', swap)  2.08 us
    ppermute x1, starting transfers between devices, body(): got = lax.ppermute(give, 'space', swap)  1.47 us
    ppermute x1, waiting for transfers between devices, body(): total = sums + lax.ppermute(sums, ALL, cores)  1.24 us
  transfers between devices with their start and end apart: 13, of which 10 were waited for; matrix products, arithmetic and copies ran while one was open for 1% of the time, Pallas kernels for 5%

profile of v8, /device:TPU:0, one launch (start us, length us, event | category | flops | bytes accessed | tf_op | source)
XLA Modules:
  0.0 53.0 jit_solution(10009196371387343259)
XLA Ops:
  0.6 0.0 copy-start.1
  0.6 3.3 %cut.1 = (bf16[10,72,128]{2,1,0:T(8,128)(2,1)}, bf16[10,72,128]{2,1,0:T(8,128)(2,1)}, bf16[8,72,512]{2,1,0:T(8,128)(2,1)}) custom-call(bf16[32,16,512]{2,1,0:T(8,128)(2,1)} %bitcast.14, bf16[16,8,8,128]{3,2,1,0:T(8,128)(2,1)} %bitcast.15, bf16[4,8,8,128]{3,2,1,0:T(8,128)(2,1)} %bitcast.16), custom_call_target="tpu_custom_call" | custom-call | flops 400000000 | bytes 2000000 | tf_op jit(solution)/shard_map/cut/pallas_call | solution.py:42
  4.0 0.0 copy-start
  4.0 2.1 %collective-permute-start = (bf16[10,72,128]{2,1,0:T(8,128)(2,1)}, bf16[10,72,128]{2,1,0:T(8,128)(2,1)S(1)}, u32[]{:S(2)}, u32[]{:S(2)}) collective-permute-start(bf16[10,72,128]{2,1,0:T(8,128)(2,1)} %get-tuple-element.22), channel_id=1, source_target_pairs={{0,1},{1,0},{2,3},{3,2},{4,5},{5,4},{6,7},{7,6},{8,9},{9,8},{10,11... | collective-permute-start | bytes 552968 | tf_op jit(solution)/shard_map/ppermute | solution.py:402
  6.1 4.5 %all-to-all-start = ((bf16[8,72,512]{2,1,0:T(8,128)(2,1)}), bf16[8,72,512]{2,1,0:T(8,128)(2,1)S(1)}, u32[]{:S(2)}, u32[]{:S(2)}) async-start(bf16[8,72,512]{2,1,0:T(8,128)(2,1)} %get-tuple-element.20), calls=%async_computation | async-start | bytes 1179648 | tf_op jit(solution)/shard_map/all_to_all | solution.py:403
  10.5 0.0 copy-done.1
  10.5 0.2 copy.8
  10.7 0.2 collective-permute-done.recv_ref
  10.9 0.0 copy-done
  10.9 0.8 %ready.1 = (bf16[8,80,256]{2,1,0:T(8,128)(2,1)S(1)}, bf16[864,640]{1,0:T(8,128)(2,1)S(1)}, bf16[256,640]{1,0:T(8,128)(2,1)S(1)}, bf16[768,256]{1,0:T(8,128)(2,1)S(1)}) custom-call(bf16[10,72,128]{2,1,0:T(8,128)(2,1)S(1)} %copy-done, bf16[10,72,128]{2,1,0:T(8,128)(2,1)S(1)} %collective-permute-done.recv_ref, bf16[864,16]{1,0:T(8,128)(2,1)S(1)} %bitcast.9), custom_call_target="tpu_custom_call" | custom-call | flops 20000000000 | bytes 5000000 | tf_op jit(solution)/shard_map/ready/pallas_call | solution.py:42
  11.7 8.7 %all-to-all-done.grad_ref = bf16[8,72,512]{2,1,0:T(8,128)(2,1)S(1)} async-done(((bf16[8,72,512]{2,1,0:T(8,128)(2,1)}), bf16[8,72,512]{2,1,0:T(8,128)(2,1)S(1)}, u32[]{:S(2)}, u32[]{:S(2)}) %all-to-all-start) | async-done | bytes 589856 | tf_op jit(solution)/shard_map/all_to_all | solution.py:403
  20.4 0.0 copy-start.2
  20.4 4.0 %grads.1 = (bf16[800,256]{1,0:T(8,128)(2,1)S(1)}, f32[128,128]{1,0:T(8,128)S(1)}) custom-call(bf16[8,72,512]{2,1,0:T(8,128)(2,1)S(1)} %all-to-all-done.grad_ref, bf16[8,80,256]{2,1,0:T(8,128)(2,1)S(1)} %get-tuple-element.23.pre_ref, bf16[864,640]{1,0:T(8,128)(2,1)S(1)} %get-tuple-element.24.hid_ref, bf16[256,640]{1,0:T(8,128)(2,1)S(1)} %get-tuple-element.25.ins_ref, ...), custom_call_target="tpu_custom_call" | custom-call | flops 3000000000 | bytes 4000000 | tf_op jit(solution)/shard_map/grads/pallas_call | solution.py:42
  24.4 0.1 collective-permute-start.1
  24.5 1.2 %collective-permute-done.1 = f32[128,128]{1,0:T(8,128)S(1)} collective-permute-done((f32[128,128]{1,0:T(8,128)S(1)}, f32[128,128]{1,0:T(8,128)S(1)}, u32[]{:S(2)}, u32[]{:S(2)}) %collective-permute-start.1) | collective-permute-done | bytes 65568 | tf_op jit(solution)/shard_map/ppermute | solution.py:426
  25.7 2.8 %collective-permute-start.3 = (f32[128,128]{1,0:T(8,128)S(1)}, f32[128,128]{1,0:T(8,128)S(1)}, u32[]{:S(2)}, u32[]{:S(2)}) collective-permute-start(f32[128,128]{1,0:T(8,128)S(1)} %add.30), channel_id=1, source_target_pairs={{0,48},{1,49},{2,50},{3,51},{4,52},{5,53},{6,54},{7,55},{8,56},{9,... | collective-permute-start | bytes 196616 | tf_op jit(solution)/shard_map/ppermute | solution.py:429
  28.6 0.8 %collective-permute-start.4 = (f32[128,128]{1,0:T(8,128)S(1)}, f32[128,128]{1,0:T(8,128)S(1)}, u32[]{:S(2)}, u32[]{:S(2)}) collective-permute-start(f32[128,128]{1,0:T(8,128)S(1)} %add.30), channel_id=1, source_target_pairs={{0,32},{1,33},{2,34},{3,35},{4,36},{5,37},{6,38},{7,39},{8,40},{9,... | collective-permute-start | bytes 196616 | tf_op jit(solution)/shard_map/ppermute | solution.py:429
  29.4 0.5 %collective-permute-start.2 = (f32[128,128]{1,0:T(8,128)S(1)}, f32[128,128]{1,0:T(8,128)S(1)}, u32[]{:S(2)}, u32[]{:S(2)}) collective-permute-start(f32[128,128]{1,0:T(8,128)S(1)} %add.30), channel_id=1, source_target_pairs={{0,16},{1,17},{2,18},{3,19},{4,20},{5,21},{6,22},{7,23},{8,24},{9,... | collective-permute-start | bytes 196616 | tf_op jit(solution)/shard_map/ppermute | solution.py:429
  29.9 0.0 copy-done.2
  29.9 0.2 copy.9
  30.2 0.9 %back.1 = (bf16[4,32,128]{2,1,0:T(8,128)(2,1)S(1)}, bf16[4,32,128]{2,1,0:T(8,128)(2,1)S(1)}) custom-call(bf16[800,256]{1,0:T(8,128)(2,1)S(1)} %get-tuple-element.27.act_s, bf16[432,4]{1,0:T(8,128)(2,1)S(1)} %bitcast.10), custom_call_target="tpu_custom_call" | custom-call | flops 500000000 | bytes 1000000 | tf_op jit(solution)/shard_map/back/pallas_call | solution.py:42
  31.1 0.4 collective-permute-done.3
  31.4 3.2 %collective-permute-done.4 = f32[128,128]{1,0:T(8,128)S(1)} collective-permute-done((f32[128,128]{1,0:T(8,128)S(1)}, f32[128,128]{1,0:T(8,128)S(1)}, u32[]{:S(2)}, u32[]{:S(2)}) %collective-permute-start.4) | collective-permute-done | bytes 65568 | tf_op jit(solution)/shard_map/ppermute | solution.py:429
  34.7 0.0 collective-permute-done.2
  34.7 1.2 %collective-permute-start.6 = (f32[128,128]{1,0:T(8,128)S(1)}, f32[128,128]{1,0:T(8,128)S(1)}, u32[]{:S(2)}, u32[]{:S(2)}) collective-permute-start(f32[128,128]{1,0:T(8,128)S(1)} %add_add_fusion.2), channel_id=1, source_target_pairs={{0,6},{1,7},{2,4},{3,5},{4,2},{5,3},{6,0},{7,1},{8,14},{9,15},{10,... | collective-permute-start | bytes 196616 | tf_op jit(solution)/shard_map/ppermute | solution.py:429
  35.9 1.6 %collective-permute-start.7 = (f32[128,128]{1,0:T(8,128)S(1)}, f32[128,128]{1,0:T(8,128)S(1)}, u32[]{:S(2)}, u32[]{:S(2)}) collective-permute-start(f32[128,128]{1,0:T(8,128)S(1)} %add_add_fusion.2), channel_id=1, source_target_pairs={{0,4},{1,5},{2,6},{3,7},{4,0},{5,1},{6,2},{7,3},{8,12},{9,13},{10,... | collective-permute-start | bytes 196616 | tf_op jit(solution)/shard_map/ppermute | solution.py:429
  37.6 1.3 %collective-permute-start.5 = (f32[128,128]{1,0:T(8,128)S(1)}, f32[128,128]{1,0:T(8,128)S(1)}, u32[]{:S(2)}, u32[]{:S(2)}) collective-permute-start(f32[128,128]{1,0:T(8,128)S(1)} %add_add_fusion.2), channel_id=1, source_target_pairs={{0,2},{1,3},{2,0},{3,1},{4,6},{5,7},{6,4},{7,5},{8,10},{9,11},{10,... | collective-permute-start | bytes 196616 | tf_op jit(solution)/shard_map/ppermute | solution.py:429
  38.9 1.5 %collective-permute-start.8 = (bf16[4,32,128]{2,1,0:T(8,128)(2,1)S(1)}, bf16[4,32,128]{2,1,0:T(8,128)(2,1)S(1)}, u32[]{:S(2)}, u32[]{:S(2)}) collective-permute-start(bf16[4,32,128]{2,1,0:T(8,128)(2,1)S(1)} %get-tuple-element.32), channel_id=1, source_target_pairs={{0,1},{1,0},{2,3},{3,2},{4,5},{5,4},{6,7},{7,6},{8,9},{9,8},{10,11... | collective-permute-start | bytes 98312 | tf_op jit(solution)/shard_map/ppermute | solution.py:433
  40.3 0.0 collective-permute-done.6
  40.3 1.4 %collective-permute-done.7 = f32[128,128]{1,0:T(8,128)S(1)} collective-permute-done((f32[128,128]{1,0:T(8,128)S(1)}, f32[128,128]{1,0:T(8,128)S(1)}, u32[]{:S(2)}, u32[]{:S(2)}) %collective-permute-start.7) | collective-permute-done | bytes 65568 | tf_op jit(solution)/shard_map/ppermute | solution.py:429
  41.7 0.1 collective-permute-done.5
  41.9 0.9 %collective-permute-done.8.recv_ref = bf16[4,32,128]{2,1,0:T(8,128)(2,1)S(1)} collective-permute-done((bf16[4,32,128]{2,1,0:T(8,128)(2,1)S(1)}, bf16[4,32,128]{2,1,0:T(8,128)(2,1)S(1)}, u32[]{:S(2)}, u32[]{:S(2)}) %collective-permute-start.8) | collective-permute-done | bytes 32800 | tf_op jit(solution)/shard_map/ppermute | solution.py:433
  42.8 3.6 %collective-permute-start.10 = (f32[128,128]{1,0:T(8,128)S(1)}, f32[128,128]{1,0:T(8,128)S(1)}, u32[]{:S(2)}, u32[]{:S(2)}) collective-permute-start(f32[128,128]{1,0:T(8,128)S(1)} %add_add_fusion.1), channel_id=1, source_target_pairs={{0,65},{1,64},{2,67},{3,66},{4,69},{5,68},{6,71},{7,70},{8,73},{9,... | collective-permute-start | bytes 196616 | tf_op jit(solution)/shard_map/ppermute | solution.py:429
  46.4 0.0 collective-permute-start.11
  46.4 0.9 %collective-permute-start.9 = (f32[128,128]{1,0:T(8,128)S(1)}, f32[128,128]{1,0:T(8,128)S(1)}, u32[]{:S(2)}, u32[]{:S(2)}) collective-permute-start(f32[128,128]{1,0:T(8,128)S(1)} %add_add_fusion.1), channel_id=1, source_target_pairs={{0,1},{1,0},{2,3},{3,2},{4,5},{5,4},{6,7},{7,6},{8,9},{9,8},{10,11... | collective-permute-start | bytes 196616 | tf_op jit(solution)/shard_map/ppermute | solution.py:429
  47.2 0.7 %tile.1 = bf16[4,8,8,128]{3,2,1,0:T(8,128)(2,1)} custom-call(bf16[4,32,128]{2,1,0:T(8,128)(2,1)S(1)} %get-tuple-element.28.own_ref, bf16[4,32,128]{2,1,0:T(8,128)(2,1)S(1)} %collective-permute-done.8.recv_ref), custom_call_target="tpu_custom_call" | custom-call | flops 1000000 | bytes 200000 | tf_op jit(solution)/shard_map/tile/pallas_call | solution.py:42
  47.9 0.9 %collective-permute-done.10 = f32[128,128]{1,0:T(8,128)S(1)} collective-permute-done((f32[128,128]{1,0:T(8,128)S(1)}, f32[128,128]{1,0:T(8,128)S(1)}, u32[]{:S(2)}, u32[]{:S(2)}) %collective-permute-start.10) | collective-permute-done | bytes 65568 | tf_op jit(solution)/shard_map/ppermute | solution.py:429
  48.9 3.3 %collective-permute-done.11 = f32[128,128]{1,0:T(8,128)S(1)} collective-permute-done((f32[128,128]{1,0:T(8,128)S(1)}, f32[128,128]{1,0:T(8,128)S(1)}, u32[]{:S(2)}, u32[]{:S(2)}) %collective-permute-start.11) | collective-permute-done | bytes 65568 | tf_op jit(solution)/shard_map/ppermute | solution.py:429
  52.1 0.0 collective-permute-done.9
  52.2 0.9 %unpack.1 = (f32[4,16,27]{2,1,0:T(8,128)}, f32[27,16,32]{2,1,0:T(8,128)}) custom-call(f32[128,128]{1,0:T(8,128)S(1)} %add_add_fusion.total_ref), custom_call_target="tpu_custom_call" | custom-call | flops 1000000 | bytes 200000 | tf_op jit(solution)/shard_map/unpack/pallas_call | solution.py:42
  (4 shorter events, 0.1 us)
Async XLA Ops:
  0.6 9.9 %copy-start.1 = (bf16[27,16,32]{2,1,0:T(8,128)(2,1)S(1)}, bf16[27,16,32]{2,1,0:T(8,128)(2,1)}, u32[]{:S(2)}) copy-start(bf16[27,16,32]{2,1,0:T(8,128)(2,1)} %param.9) | copy-start | bytes 82948
  4.0 6.9 %copy-start = (bf16[10,72,128]{2,1,0:T(8,128)(2,1)S(1)}, bf16[10,72,128]{2,1,0:T(8,128)(2,1)}, u32[]{:S(2)}) copy-start(bf16[10,72,128]{2,1,0:T(8,128)(2,1)} %get-tuple-element.21.keep_ref) | copy-start | bytes 552964
  4.0 6.9 %collective-permute-start = (bf16[10,72,128]{2,1,0:T(8,128)(2,1)}, bf16[10,72,128]{2,1,0:T(8,128)(2,1)S(1)}, u32[]{:S(2)}, u32[]{:S(2)}) collective-permute-start(bf16[10,72,128]{2,1,0:T(8,128)(2,1)} %get-tuple-element.22), channel_id=1, source_target_pairs={{0,1},{1,0},{2,3},{3,2},{4,5},{5,4},{6,7},{7,6},{8,9},{9,8},{10,11... | collective-permute-start | bytes 552968 | tf_op jit(solution)/shard_map/ppermute | solution.py:402
  6.1 14.4 %all-to-all-start = ((bf16[8,72,512]{2,1,0:T(8,128)(2,1)}), bf16[8,72,512]{2,1,0:T(8,128)(2,1)S(1)}, u32[]{:S(2)}, u32[]{:S(2)}) async-start(bf16[8,72,512]{2,1,0:T(8,128)(2,1)} %get-tuple-element.20), calls=%async_computation | async-start | bytes 1179648 | tf_op jit(solution)/shard_map/all_to_all | solution.py:403
  20.4 9.5 %copy-start.2 = (bf16[27,4,16]{0,2,1:T(8,128)(2,1)S(1)}, bf16[27,4,16]{0,2,1:T(8,128)(2,1)}, u32[]{:S(2)}) copy-start(bf16[27,4,16]{0,2,1:T(8,128)(2,1)} %param.8) | copy-start | bytes 10372
  24.4 1.3 %collective-permute-start.1 = (f32[128,128]{1,0:T(8,128)S(1)}, f32[128,128]{1,0:T(8,128)S(1)}, u32[]{:S(2)}, u32[]{:S(2)}) collective-permute-start(f32[128,128]{1,0:T(8,128)S(1)} %get-tuple-element.29), channel_id=1, source_target_pairs={{0,8},{1,9},{2,10},{3,11},{4,12},{5,13},{6,14},{7,15},{8,0},{9,1},... | collective-permute-start | bytes 196616 | tf_op jit(solution)/shard_map/ppermute | solution.py:426
  25.7 5.7 %collective-permute-start.3 = (f32[128,128]{1,0:T(8,128)S(1)}, f32[128,128]{1,0:T(8,128)S(1)}, u32[]{:S(2)}, u32[]{:S(2)}) collective-permute-start(f32[128,128]{1,0:T(8,128)S(1)} %add.30), channel_id=1, source_target_pairs={{0,48},{1,49},{2,50},{3,51},{4,52},{5,53},{6,54},{7,55},{8,56},{9,... | collective-permute-start | bytes 196616 | tf_op jit(solution)/shard_map/ppermute | solution.py:429
  28.6 6.1 %collective-permute-start.4 = (f32[128,128]{1,0:T(8,128)S(1)}, f32[128,128]{1,0:T(8,128)S(1)}, u32[]{:S(2)}, u32[]{:S(2)}) collective-permute-start(f32[128,128]{1,0:T(8,128)S(1)} %add.30), channel_id=1, source_target_pairs={{0,32},{1,33},{2,34},{3,35},{4,36},{5,37},{6,38},{7,39},{8,40},{9,... | collective-permute-start | bytes 196616 | tf_op jit(solution)/shard_map/ppermute | solution.py:429
  29.4 5.3 %collective-permute-start.2 = (f32[128,128]{1,0:T(8,128)S(1)}, f32[128,128]{1,0:T(8,128)S(1)}, u32[]{:S(2)}, u32[]{:S(2)}) collective-permute-start(f32[128,128]{1,0:T(8,128)S(1)} %add.30), channel_id=1, source_target_pairs={{0,16},{1,17},{2,18},{3,19},{4,20},{5,21},{6,22},{7,23},{8,24},{9,... | collective-permute-start | bytes 196616 | tf_op jit(solution)/shard_map/ppermute | solution.py:429
  34.7 5.6 %collective-permute-start.6 = (f32[128,128]{1,0:T(8,128)S(1)}, f32[128,128]{1,0:T(8,128)S(1)}, u32[]{:S(2)}, u32[]{:S(2)}) collective-permute-start(f32[128,128]{1,0:T(8,128)S(1)} %add_add_fusion.2), channel_id=1, source_target_pairs={{0,6},{1,7},{2,4},{3,5},{4,2},{5,3},{6,0},{7,1},{8,14},{9,15},{10,... | collective-permute-start | bytes 196616 | tf_op jit(solution)/shard_map/ppermute | solution.py:429
  35.9 5.8 %collective-permute-start.7 = (f32[128,128]{1,0:T(8,128)S(1)}, f32[128,128]{1,0:T(8,128)S(1)}, u32[]{:S(2)}, u32[]{:S(2)}) collective-permute-start(f32[128,128]{1,0:T(8,128)S(1)} %add_add_fusion.2), channel_id=1, source_target_pairs={{0,4},{1,5},{2,6},{3,7},{4,0},{5,1},{6,2},{7,3},{8,12},{9,13},{10,... | collective-permute-start | bytes 196616 | tf_op jit(solution)/shard_map/ppermute | solution.py:429
  37.6 4.3 %collective-permute-start.5 = (f32[128,128]{1,0:T(8,128)S(1)}, f32[128,128]{1,0:T(8,128)S(1)}, u32[]{:S(2)}, u32[]{:S(2)}) collective-permute-start(f32[128,128]{1,0:T(8,128)S(1)} %add_add_fusion.2), channel_id=1, source_target_pairs={{0,2},{1,3},{2,0},{3,1},{4,6},{5,7},{6,4},{7,5},{8,10},{9,11},{10,... | collective-permute-start | bytes 196616 | tf_op jit(solution)/shard_map/ppermute | solution.py:429
  38.9 3.9 %collective-permute-start.8 = (bf16[4,32,128]{2,1,0:T(8,128)(2,1)S(1)}, bf16[4,32,128]{2,1,0:T(8,128)(2,1)S(1)}, u32[]{:S(2)}, u32[]{:S(2)}) collective-permute-start(bf16[4,32,128]{2,1,0:T(8,128)(2,1)S(1)} %get-tuple-element.32), channel_id=1, source_target_pairs={{0,1},{1,0},{2,3},{3,2},{4,5},{5,4},{6,7},{7,6},{8,9},{9,8},{10,11... | collective-permute-start | bytes 98312 | tf_op jit(solution)/shard_map/ppermute | solution.py:433
  42.8 6.1 %collective-permute-start.10 = (f32[128,128]{1,0:T(8,128)S(1)}, f32[128,128]{1,0:T(8,128)S(1)}, u32[]{:S(2)}, u32[]{:S(2)}) collective-permute-start(f32[128,128]{1,0:T(8,128)S(1)} %add_add_fusion.1), channel_id=1, source_target_pairs={{0,65},{1,64},{2,67},{3,66},{4,69},{5,68},{6,71},{7,70},{8,73},{9,... | collective-permute-start | bytes 196616 | tf_op jit(solution)/shard_map/ppermute | solution.py:429
  46.4 5.8 %collective-permute-start.11 = (f32[128,128]{1,0:T(8,128)S(1)}, f32[128,128]{1,0:T(8,128)S(1)}, u32[]{:S(2)}, u32[]{:S(2)}) collective-permute-start(f32[128,128]{1,0:T(8,128)S(1)} %add_add_fusion.1), channel_id=1, source_target_pairs={{0,64},{1,65},{2,66},{3,67},{4,68},{5,69},{6,70},{7,71},{8,72},{9,... | collective-permute-start | bytes 196616 | tf_op jit(solution)/shard_map/ppermute | solution.py:429
  46.4 5.8 %collective-permute-start.9 = (f32[128,128]{1,0:T(8,128)S(1)}, f32[128,128]{1,0:T(8,128)S(1)}, u32[]{:S(2)}, u32[]{:S(2)}) collective-permute-start(f32[128,128]{1,0:T(8,128)S(1)} %add_add_fusion.1), channel_id=1, source_target_pairs={{0,1},{1,0},{2,3},{3,2},{4,5},{5,4},{6,7},{7,6},{8,9},{9,8},{10,11... | collective-permute-start | bytes 196616 | tf_op jit(solution)/shard_map/ppermute | solution.py:429

commit v9 on v7

--- a/solution.py
+++ b/solution.py
@@ -236,7 +236,7 @@
 
 def grads_kernel(
     grad_ref, pre_ref, hid_ref, ins_ref, wide_ref,
-    act_s, mine_ref, rest_ref, grad_s, terms_s, first_s, sums_s,
+    act_s, mine_ref, rest_ref, grad_s, terms_s, first_s, sums_s, raw_s,
 ):
     space = lax.axis_index("space")
     left = lax.rem(space, 2) == 0
@@ -244,25 +244,26 @@
         grad_s[PAD * block : PAD * block + PAD, :] = jnp.zeros((PAD, 512), BF16)
         act_s[PAD * block : PAD * block + PAD, :] = jnp.zeros((PAD, 256), BF16)
     for z in range(8):
-        plane = jnp.concatenate([grad_ref[z].astype(F32), jnp.zeros((PAD - WIDE, 512), F32)], axis=0)
-        grad_s[PAD * (z + 1) : PAD * (z + 2), :] = plane.astype(BF16)
-
-    for kz in range(3):
-        for half in range(2):
-            terms_s[kz, half] = dot(hid_ref[384 * half : 384 * half + 480, :], planes(grad_s, kz, 256 * half, 256))
+        at = PAD * (z + 1)
+        grad_s[at : at + STRIP, :] = grad_ref[z, :STRIP]
+        last = jnp.concatenate([grad_ref[z, STRIP:].astype(F32), jnp.zeros((PAD - WIDE, 512), F32)], axis=0)
+        grad_s[at + STRIP : at + PAD, :] = last.astype(BF16)
 
     wide = [wide_ref[256 * kz : 256 * kz + 256, :] for kz in range(3)]
     none = jnp.zeros((32, 256), BF16)
     top = jnp.concatenate([part for w in wide for part in (none, w[32:])], axis=0)
     bottom = jnp.concatenate([part for w in wide for part in (w[:160], none, w[192:])], axis=0)
-    parts = []
     for group in range(4):
         if group < 3:
             sides = [planes(grad_s, kz, 128 * group, 256) for kz in range(3)]
         else:
             sides = [planes(grad_s, kz, low, 128) for kz in range(3) for low in (384, 0)]
         weights = top if group == 0 else bottom if group == 3 else wide_ref[...]
-        parts.append(across(dot(jnp.concatenate(sides, axis=1), weights)))
+        raw_s[group] = dot(jnp.concatenate(sides, axis=1), weights)
+    for kz in range(3):
+        for half in range(2):
+            terms_s[kz, half] = dot(hid_ref[384 * half : 384 * half + 480, :], planes(grad_s, kz, 256 * half, 256))
+    parts = [across(raw_s[group]) for group in range(4)]
     low = iota((ROWS, 128), 1) < 64
     act = jnp.concatenate([jnp.where(low, parts[0], parts[1]), jnp.where(low, parts[2], parts[3])], axis=1)
     row = iota((PAD, 256), 0)
@@ -420,7 +421,7 @@
         [shape((10 * PAD, 256), BF16), shape((64, 128), F32), shape((64, 128), F32)],
         [
             pltpu.VMEM((10 * PAD, 512), BF16), pltpu.VMEM((3, 2, 480, 256), F32), pltpu.VMEM((3, 256, 256), F32),
-            pltpu.VMEM((128, 128), F32),
+            pltpu.VMEM((128, 128), F32), pltpu.VMEM((4, ROWS, 256), F32),
         ],
         [strips, pre, hid, ins, wide], 3e9, 4e6, limit=SOME,
     )

time: 53.3 us -> 52.1 us (0.977)
  Pallas kernels: 10.8 us -> 9.56 us
    pallas_call x6, Pallas kernels: 10.8 us -> 9.56 us  [call(): pl.pallas_call(kernel, name=name, out_shape=outs, in_specs=[spec(i in far...]
where the time goes in v9:
time: 52.1 us; the launch traced here: 51.9 us
  starting transfers between devices  25.1 us (48%)
  waiting for transfers between devices  16.1 us (31%)
  Pallas kernels  9.56 us (18%)
  between operations  0.71 us (1%)
    ppermute x9, starting transfers between devices, body(): parts = [lax.ppermute(total, ALL, pairs) for pairs in stage]  10.6 us
    pallas_call x6, Pallas kernels, call(): pl.pallas_call(kernel, name=name, out_shape=outs, in_specs=[spec(i in far...  9.56 us
    all_to_all x1, waiting for transfers between devices, body(): strips = lax.all_to_all(strips, 'space', 0, 0, tiled=True)  8.02 us
    ppermute x9, waiting for transfers between devices, body(): parts = [lax.ppermute(total, ALL, pairs) for pairs in stage]  6.9 us
    ppermute x1, starting transfers between devices, body(): other = lax.ppermute(total, ALL, cores)  4.72 us
    all_to_all x1, starting transfers between devices, body(): strips = lax.all_to_all(strips, 'space', 0, 0, tiled=True)  4.19 us
    ppermute x1, starting transfers between devices, body(): recv = lax.ppermute(send, 'space', swap)  2.55 us
    ppermute x1, starting transfers between devices, body(): total = mine + lax.ppermute(rest, ALL, cores)  2.01 us
  transfers between devices with their start and end apart: 14, of which 9 were waited for; matrix products, arithmetic and copies ran while one was open for 1% of the time, Pallas kernels for 5%

profile of v9, /device:TPU:1, one launch (start us, length us, event | category | flops | bytes accessed | tf_op | source)
XLA Modules:
  0.0 51.9 jit_solution(10617911630505533821)
XLA Ops:
  0.6 0.0 copy-start.1
  0.6 3.3 %cut.1 = (bf16[10,72,128]{2,1,0:T(8,128)(2,1)}, bf16[10,72,128]{2,1,0:T(8,128)(2,1)}, bf16[8,72,512]{2,1,0:T(8,128)(2,1)}) custom-call(bf16[32,16,512]{2,1,0:T(8,128)(2,1)} %bitcast.14, bf16[16,8,8,128]{3,2,1,0:T(8,128)(2,1)} %bitcast.15, bf16[4,8,8,128]{3,2,1,0:T(8,128)(2,1)} %bitcast.16), custom_call_target="tpu_custom_call" | custom-call | flops 400000000 | bytes 2000000 | tf_op jit(solution)/shard_map/cut/pallas_call | solution.py:42
  4.0 0.0 copy-start
  4.0 2.5 %collective-permute-start = (bf16[10,72,128]{2,1,0:T(8,128)(2,1)}, bf16[10,72,128]{2,1,0:T(8,128)(2,1)S(1)}, u32[]{:S(2)}, u32[]{:S(2)}) collective-permute-start(bf16[10,72,128]{2,1,0:T(8,128)(2,1)} %get-tuple-element.19), channel_id=1, source_target_pairs={{0,1},{1,0},{2,3},{3,2},{4,5},{5,4},{6,7},{7,6},{8,9},{9,8},{10,11... | collective-permute-start | bytes 552968 | tf_op jit(solution)/shard_map/ppermute | solution.py:407
  6.5 4.2 %all-to-all-start = ((bf16[8,72,512]{2,1,0:T(8,128)(2,1)}), bf16[8,72,512]{2,1,0:T(8,128)(2,1)S(1)}, u32[]{:S(2)}, u32[]{:S(2)}) async-start(bf16[8,72,512]{2,1,0:T(8,128)(2,1)} %get-tuple-element.17), calls=%async_computation | async-start | bytes 1179648 | tf_op jit(solution)/shard_map/all_to_all | solution.py:408
  10.7 0.0 copy-done.1
  10.7 0.2 copy.8
  10.9 0.2 collective-permute-done.recv_ref
  11.1 0.0 copy-done
  11.1 0.8 %ready.1 = (bf16[8,80,256]{2,1,0:T(8,128)(2,1)S(1)}, bf16[864,640]{1,0:T(8,128)(2,1)S(1)}, bf16[256,640]{1,0:T(8,128)(2,1)S(1)}, bf16[768,256]{1,0:T(8,128)(2,1)S(1)}) custom-call(bf16[10,72,128]{2,1,0:T(8,128)(2,1)S(1)} %copy-done, bf16[10,72,128]{2,1,0:T(8,128)(2,1)S(1)} %collective-permute-done.recv_ref, bf16[864,16]{1,0:T(8,128)(2,1)S(1)} %bitcast.9), custom_call_target="tpu_custom_call" | custom-call | flops 20000000000 | bytes 5000000 | tf_op jit(solution)/shard_map/ready/pallas_call | solution.py:42
  11.9 8.0 %all-to-all-done.grad_ref = bf16[8,72,512]{2,1,0:T(8,128)(2,1)S(1)} async-done(((bf16[8,72,512]{2,1,0:T(8,128)(2,1)}), bf16[8,72,512]{2,1,0:T(8,128)(2,1)S(1)}, u32[]{:S(2)}, u32[]{:S(2)}) %all-to-all-start) | async-done | bytes 589856 | tf_op jit(solution)/shard_map/all_to_all | solution.py:408
  19.9 0.0 copy-start.2
  19.9 3.0 %grads.1 = (bf16[800,256]{1,0:T(8,128)(2,1)S(1)}, f32[64,128]{1,0:T(8,128)S(1)}, f32[64,128]{1,0:T(8,128)S(1)}) custom-call(bf16[8,72,512]{2,1,0:T(8,128)(2,1)S(1)} %all-to-all-done.grad_ref, bf16[8,80,256]{2,1,0:T(8,128)(2,1)S(1)} %get-tuple-element.20.pre_ref, bf16[864,640]{1,0:T(8,128)(2,1)S(1)} %get-tuple-element.21.hid_ref, ...), custom_call_target="tpu_custom_call" | custom-call | flops 3000000000 | bytes 4000000 | tf_op jit(solution)/shard_map/grads/pallas_call | solution.py:42
  22.9 2.0 %collective-permute-start.2 = (f32[64,128]{1,0:T(8,128)S(1)}, f32[64,128]{1,0:T(8,128)S(1)}, u32[]{:S(2)}, u32[]{:S(2)}) collective-permute-start(f32[64,128]{1,0:T(8,128)S(1)} %get-tuple-element.28), channel_id=1, source_target_pairs={{0,8},{1,9},{2,10},{3,11},{4,12},{5,13},{6,14},{7,15},{8,0},{9,1},... | collective-permute-start | bytes 98312 | tf_op jit(solution)/shard_map/ppermute | solution.py:432
  24.9 0.9 %collective-permute-done.2 = f32[64,128]{1,0:T(8,128)S(1)} collective-permute-done((f32[64,128]{1,0:T(8,128)S(1)}, f32[64,128]{1,0:T(8,128)S(1)}, u32[]{:S(2)}, u32[]{:S(2)}) %collective-permute-start.2) | collective-permute-done | bytes 32800 | tf_op jit(solution)/shard_map/ppermute | solution.py:432
  25.8 2.5 %collective-permute-start.4 = (f32[64,128]{1,0:T(8,128)S(1)}, f32[64,128]{1,0:T(8,128)S(1)}, u32[]{:S(2)}, u32[]{:S(2)}) collective-permute-start(f32[64,128]{1,0:T(8,128)S(1)} %add.30), channel_id=1, source_target_pairs={{0,48},{1,49},{2,50},{3,51},{4,52},{5,53},{6,54},{7,55},{8,56},{9,... | collective-permute-start | bytes 98312 | tf_op jit(solution)/shard_map/ppermute | solution.py:435
  28.2 0.5 collective-permute-start.5
  28.8 0.3 collective-permute-start.3
  29.0 0.7 %collective-permute-done.4 = f32[64,128]{1,0:T(8,128)S(1)} collective-permute-done((f32[64,128]{1,0:T(8,128)S(1)}, f32[64,128]{1,0:T(8,128)S(1)}, u32[]{:S(2)}, u32[]{:S(2)}) %collective-permute-start.4) | collective-permute-done | bytes 32800 | tf_op jit(solution)/shard_map/ppermute | solution.py:435
  29.7 2.8 %collective-permute-done.5 = f32[64,128]{1,0:T(8,128)S(1)} collective-permute-done((f32[64,128]{1,0:T(8,128)S(1)}, f32[64,128]{1,0:T(8,128)S(1)}, u32[]{:S(2)}, u32[]{:S(2)}) %collective-permute-start.5) | collective-permute-done | bytes 32800 | tf_op jit(solution)/shard_map/ppermute | solution.py:435
  32.5 0.0 collective-permute-done.3
  32.5 1.0 %collective-permute-start.7 = (f32[64,128]{1,0:T(8,128)S(1)}, f32[64,128]{1,0:T(8,128)S(1)}, u32[]{:S(2)}, u32[]{:S(2)}) collective-permute-start(f32[64,128]{1,0:T(8,128)S(1)} %add_add_fusion.2), channel_id=1, source_target_pairs={{0,6},{1,7},{2,4},{3,5},{4,2},{5,3},{6,0},{7,1},{8,14},{9,15},{10,... | collective-permute-start | bytes 98312 | tf_op jit(solution)/shard_map/ppermute | solution.py:435
  33.5 1.4 %collective-permute-start.8 = (f32[64,128]{1,0:T(8,128)S(1)}, f32[64,128]{1,0:T(8,128)S(1)}, u32[]{:S(2)}, u32[]{:S(2)}) collective-permute-start(f32[64,128]{1,0:T(8,128)S(1)} %add_add_fusion.2), channel_id=1, source_target_pairs={{0,4},{1,5},{2,6},{3,7},{4,0},{5,1},{6,2},{7,3},{8,12},{9,13},{10,... | collective-permute-start | bytes 98312 | tf_op jit(solution)/shard_map/ppermute | solution.py:435
  34.8 1.0 %collective-permute-start.6 = (f32[64,128]{1,0:T(8,128)S(1)}, f32[64,128]{1,0:T(8,128)S(1)}, u32[]{:S(2)}, u32[]{:S(2)}) collective-permute-start(f32[64,128]{1,0:T(8,128)S(1)} %add_add_fusion.2), channel_id=1, source_target_pairs={{0,2},{1,3},{2,0},{3,1},{4,6},{5,7},{6,4},{7,5},{8,10},{9,11},{10,... | collective-permute-start | bytes 98312 | tf_op jit(solution)/shard_map/ppermute | solution.py:435
  35.9 0.0 copy-done.2
  35.9 0.2 copy.9
  36.1 0.5 collective-permute-done.7
  36.6 1.2 %collective-permute-done.8 = f32[64,128]{1,0:T(8,128)S(1)} collective-permute-done((f32[64,128]{1,0:T(8,128)S(1)}, f32[64,128]{1,0:T(8,128)S(1)}, u32[]{:S(2)}, u32[]{:S(2)}) %collective-permute-start.8) | collective-permute-done | bytes 32800 | tf_op jit(solution)/shard_map/ppermute | solution.py:435
  37.8 0.0 collective-permute-done.6
  37.8 3.4 %collective-permute-start.10 = (f32[64,128]{1,0:T(8,128)S(1)}, f32[64,128]{1,0:T(8,128)S(1)}, u32[]{:S(2)}, u32[]{:S(2)}) collective-permute-start(f32[64,128]{1,0:T(8,128)S(1)} %add_add_fusion.1), channel_id=1, source_target_pairs={{0,65},{1,64},{2,67},{3,66},{4,69},{5,68},{6,71},{7,70},{8,73},{9,... | collective-permute-start | bytes 98312 | tf_op jit(solution)/shard_map/ppermute | solution.py:435
  41.2 0.1 collective-permute-start.11
  41.3 0.6 %collective-permute-start.9 = (f32[64,128]{1,0:T(8,128)S(1)}, f32[64,128]{1,0:T(8,128)S(1)}, u32[]{:S(2)}, u32[]{:S(2)}) collective-permute-start(f32[64,128]{1,0:T(8,128)S(1)} %add_add_fusion.1), channel_id=1, source_target_pairs={{0,1},{1,0},{2,3},{3,2},{4,5},{5,4},{6,7},{7,6},{8,9},{9,8},{10,11... | collective-permute-start | bytes 98312 | tf_op jit(solution)/shard_map/ppermute | solution.py:435
  41.8 0.9 %back.1 = (bf16[4,32,128]{2,1,0:T(8,128)(2,1)S(1)}, bf16[4,32,128]{2,1,0:T(8,128)(2,1)S(1)}) custom-call(bf16[800,256]{1,0:T(8,128)(2,1)S(1)} %get-tuple-element.24.act_s, bf16[432,4]{1,0:T(8,128)(2,1)S(1)} %bitcast.10), custom_call_target="tpu_custom_call" | custom-call | flops 500000000 | bytes 1000000 | tf_op jit(solution)/shard_map/back/pallas_call | solution.py:42
  42.7 1.0 %collective-permute-start.1 = (bf16[4,32,128]{2,1,0:T(8,128)(2,1)S(1)}, bf16[4,32,128]{2,1,0:T(8,128)(2,1)S(1)}, u32[]{:S(2)}, u32[]{:S(2)}) collective-permute-start(bf16[4,32,128]{2,1,0:T(8,128)(2,1)S(1)} %get-tuple-element.26), channel_id=1, source_target_pairs={{0,1},{1,0},{2,3},{3,2},{4,5},{5,4},{6,7},{7,6},{8,9},{9,8},{10,11... | collective-permute-start | bytes 98312 | tf_op jit(solution)/shard_map/ppermute | solution.py:433
  43.7 0.0 collective-permute-done.10
  43.7 1.7 %collective-permute-done.11 = f32[64,128]{1,0:T(8,128)S(1)} collective-permute-done((f32[64,128]{1,0:T(8,128)S(1)}, f32[64,128]{1,0:T(8,128)S(1)}, u32[]{:S(2)}, u32[]{:S(2)}) %collective-permute-start.11) | collective-permute-done | bytes 32800 | tf_op jit(solution)/shard_map/ppermute | solution.py:435
  45.4 0.0 collective-permute-done.9
  45.4 4.7 %collective-permute-start.12 = (f32[64,128]{1,0:T(8,128)S(1)}, f32[64,128]{1,0:T(8,128)S(1)}, u32[]{:S(2)}, u32[]{:S(2)}) collective-permute-start(f32[64,128]{1,0:T(8,128)S(1)} %add_add_fusion.mine_ref), channel_id=1, source_target_pairs={{0,8},{1,9},{2,10},{3,11},{4,12},{5,13},{6,14},{7,15},{8,0},{9,1},... | collective-permute-start | bytes 98312 | tf_op jit(solution)/shard_map/ppermute | solution.py:437
  50.2 0.0 collective-permute-done.1.recv_ref
  50.2 0.7 %tile.1 = bf16[4,8,8,128]{3,2,1,0:T(8,128)(2,1)} custom-call(bf16[4,32,128]{2,1,0:T(8,128)(2,1)S(1)} %get-tuple-element.25.own_ref, bf16[4,32,128]{2,1,0:T(8,128)(2,1)S(1)} %collective-permute-done.1.recv_ref), custom_call_target="tpu_custom_call" | custom-call | flops 1000000 | bytes 200000 | tf_op jit(solution)/shard_map/tile/pallas_call | solution.py:42
  50.9 0.1 collective-permute-done.12.rest_ref
  51.0 0.9 %unpack.1 = (f32[4,16,27]{2,1,0:T(8,128)}, f32[27,16,32]{2,1,0:T(8,128)}) custom-call(f32[64,128]{1,0:T(8,128)S(1)} %add_add_fusion.mine_ref, f32[64,128]{1,0:T(8,128)S(1)} %collective-permute-done.12.rest_ref), custom_call_target="tpu_custom_call" | custom-call | flops 1000000 | bytes 200000 | tf_op jit(solution)/shard_map/unpack/pallas_call | solution.py:42
  (4 shorter events, 0.0 us)
Async XLA Ops:
  0.6 10.1 %copy-start.1 = (bf16[27,16,32]{2,1,0:T(8,128)(2,1)S(1)}, bf16[27,16,32]{2,1,0:T(8,128)(2,1)}, u32[]{:S(2)}) copy-start(bf16[27,16,32]{2,1,0:T(8,128)(2,1)} %param.9) | copy-start | bytes 82948
  4.0 7.1 %copy-start = (bf16[10,72,128]{2,1,0:T(8,128)(2,1)S(1)}, bf16[10,72,128]{2,1,0:T(8,128)(2,1)}, u32[]{:S(2)}) copy-start(bf16[10,72,128]{2,1,0:T(8,128)(2,1)} %get-tuple-element.18.keep_ref) | copy-start | bytes 552964
  4.0 7.1 %collective-permute-start = (bf16[10,72,128]{2,1,0:T(8,128)(2,1)}, bf16[10,72,128]{2,1,0:T(8,128)(2,1)S(1)}, u32[]{:S(2)}, u32[]{:S(2)}) collective-permute-start(bf16[10,72,128]{2,1,0:T(8,128)(2,1)} %get-tuple-element.19), channel_id=1, source_target_pairs={{0,1},{1,0},{2,3},{3,2},{4,5},{5,4},{6,7},{7,6},{8,9},{9,8},{10,11... | collective-permute-start | bytes 552968 | tf_op jit(solution)/shard_map/ppermute | solution.py:407
  6.5 13.4 %all-to-all-start = ((bf16[8,72,512]{2,1,0:T(8,128)(2,1)}), bf16[8,72,512]{2,1,0:T(8,128)(2,1)S(1)}, u32[]{:S(2)}, u32[]{:S(2)}) async-start(bf16[8,72,512]{2,1,0:T(8,128)(2,1)} %get-tuple-element.17), calls=%async_computation | async-start | bytes 1179648 | tf_op jit(solution)/shard_map/all_to_all | solution.py:408
  19.9 15.9 %copy-start.2 = (bf16[27,4,16]{0,2,1:T(8,128)(2,1)S(1)}, bf16[27,4,16]{0,2,1:T(8,128)(2,1)}, u32[]{:S(2)}) copy-start(bf16[27,4,16]{0,2,1:T(8,128)(2,1)} %param.8) | copy-start | bytes 10372
  22.9 2.9 %collective-permute-start.2 = (f32[64,128]{1,0:T(8,128)S(1)}, f32[64,128]{1,0:T(8,128)S(1)}, u32[]{:S(2)}, u32[]{:S(2)}) collective-permute-start(f32[64,128]{1,0:T(8,128)S(1)} %get-tuple-element.28), channel_id=1, source_target_pairs={{0,8},{1,9},{2,10},{3,11},{4,12},{5,13},{6,14},{7,15},{8,0},{9,1},... | collective-permute-start | bytes 98312 | tf_op jit(solution)/shard_map/ppermute | solution.py:432
  25.8 4.0 %collective-permute-start.4 = (f32[64,128]{1,0:T(8,128)S(1)}, f32[64,128]{1,0:T(8,128)S(1)}, u32[]{:S(2)}, u32[]{:S(2)}) collective-permute-start(f32[64,128]{1,0:T(8,128)S(1)} %add.30), channel_id=1, source_target_pairs={{0,48},{1,49},{2,50},{3,51},{4,52},{5,53},{6,54},{7,55},{8,56},{9,... | collective-permute-start | bytes 98312 | tf_op jit(solution)/shard_map/ppermute | solution.py:435
  28.2 4.3 %collective-permute-start.5 = (f32[64,128]{1,0:T(8,128)S(1)}, f32[64,128]{1,0:T(8,128)S(1)}, u32[]{:S(2)}, u32[]{:S(2)}) collective-permute-start(f32[64,128]{1,0:T(8,128)S(1)} %add.30), channel_id=1, source_target_pairs={{0,32},{1,33},{2,34},{3,35},{4,36},{5,37},{6,38},{7,39},{8,40},{9,... | collective-permute-start | bytes 98312 | tf_op jit(solution)/shard_map/ppermute | solution.py:435
  28.8 3.8 %collective-permute-start.3 = (f32[64,128]{1,0:T(8,128)S(1)}, f32[64,128]{1,0:T(8,128)S(1)}, u32[]{:S(2)}, u32[]{:S(2)}) collective-permute-start(f32[64,128]{1,0:T(8,128)S(1)} %add.30), channel_id=1, source_target_pairs={{0,16},{1,17},{2,18},{3,19},{4,20},{5,21},{6,22},{7,23},{8,24},{9,... | collective-permute-start | bytes 98312 | tf_op jit(solution)/shard_map/ppermute | solution.py:435
  32.5 4.1 %collective-permute-start.7 = (f32[64,128]{1,0:T(8,128)S(1)}, f32[64,128]{1,0:T(8,128)S(1)}, u32[]{:S(2)}, u32[]{:S(2)}) collective-permute-start(f32[64,128]{1,0:T(8,128)S(1)} %add_add_fusion.2), channel_id=1, source_target_pairs={{0,6},{1,7},{2,4},{3,5},{4,2},{5,3},{6,0},{7,1},{8,14},{9,15},{10,... | collective-permute-start | bytes 98312 | tf_op jit(solution)/shard_map/ppermute | solution.py:435
  33.5 4.3 %collective-permute-start.8 = (f32[64,128]{1,0:T(8,128)S(1)}, f32[64,128]{1,0:T(8,128)S(1)}, u32[]{:S(2)}, u32[]{:S(2)}) collective-permute-start(f32[64,128]{1,0:T(8,128)S(1)} %add_add_fusion.2), channel_id=1, source_target_pairs={{0,4},{1,5},{2,6},{3,7},{4,0},{5,1},{6,2},{7,3},{8,12},{9,13},{10,... | collective-permute-start | bytes 98312 | tf_op jit(solution)/shard_map/ppermute | solution.py:435
  34.8 2.9 %collective-permute-start.6 = (f32[64,128]{1,0:T(8,128)S(1)}, f32[64,128]{1,0:T(8,128)S(1)}, u32[]{:S(2)}, u32[]{:S(2)}) collective-permute-start(f32[64,128]{1,0:T(8,128)S(1)} %add_add_fusion.2), channel_id=1, source_target_pairs={{0,2},{1,3},{2,0},{3,1},{4,6},{5,7},{6,4},{7,5},{8,10},{9,11},{10,... | collective-permute-start | bytes 98312 | tf_op jit(solution)/shard_map/ppermute | solution.py:435
  37.8 5.9 %collective-permute-start.10 = (f32[64,128]{1,0:T(8,128)S(1)}, f32[64,128]{1,0:T(8,128)S(1)}, u32[]{:S(2)}, u32[]{:S(2)}) collective-permute-start(f32[64,128]{1,0:T(8,128)S(1)} %add_add_fusion.1), channel_id=1, source_target_pairs={{0,65},{1,64},{2,67},{3,66},{4,69},{5,68},{6,71},{7,70},{8,73},{9,... | collective-permute-start | bytes 98312 | tf_op jit(solution)/shard_map/ppermute | solution.py:435
  41.2 4.3 %collective-permute-start.11 = (f32[64,128]{1,0:T(8,128)S(1)}, f32[64,128]{1,0:T(8,128)S(1)}, u32[]{:S(2)}, u32[]{:S(2)}) collective-permute-start(f32[64,128]{1,0:T(8,128)S(1)} %add_add_fusion.1), channel_id=1, source_target_pairs={{0,64},{1,65},{2,66},{3,67},{4,68},{5,69},{6,70},{7,71},{8,72},{9,... | collective-permute-start | bytes 98312 | tf_op jit(solution)/shard_map/ppermute | solution.py:435
  41.3 4.2 %collective-permute-start.9 = (f32[64,128]{1,0:T(8,128)S(1)}, f32[64,128]{1,0:T(8,128)S(1)}, u32[]{:S(2)}, u32[]{:S(2)}) collective-permute-start(f32[64,128]{1,0:T(8,128)S(1)} %add_add_fusion.1), channel_id=1, source_target_pairs={{0,1},{1,0},{2,3},{3,2},{4,5},{5,4},{6,7},{7,6},{8,9},{9,8},{10,11... | collective-permute-start | bytes 98312 | tf_op jit(solution)/shard_map/ppermute | solution.py:435
  42.7 7.4 %collective-permute-start.1 = (bf16[4,32,128]{2,1,0:T(8,128)(2,1)S(1)}, bf16[4,32,128]{2,1,0:T(8,128)(2,1)S(1)}, u32[]{:S(2)}, u32[]{:S(2)}) collective-permute-start(bf16[4,32,128]{2,1,0:T(8,128)(2,1)S(1)} %get-tuple-element.26), channel_id=1, source_target_pairs={{0,1},{1,0},{2,3},{3,2},{4,5},{5,4},{6,7},{7,6},{8,9},{9,8},{10,11... | collective-permute-start | bytes 98312 | tf_op jit(solution)/shard_map/ppermute | solution.py:433
  45.4 5.6 %collective-permute-start.12 = (f32[64,128]{1,0:T(8,128)S(1)}, f32[64,128]{1,0:T(8,128)S(1)}, u32[]{:S(2)}, u32[]{:S(2)}) collective-permute-start(f32[64,128]{1,0:T(8,128)S(1)} %add_add_fusion.mine_ref), channel_id=1, source_target_pairs={{0,8},{1,9},{2,10},{3,11},{4,12},{5,13},{6,14},{7,15},{8,0},{9,1},... | collective-permute-start | bytes 98312 | tf_op jit(solution)/shard_map/ppermute | solution.py:437

commit v10 on v9

--- a/solution.py
+++ b/solution.py
@@ -62,10 +62,10 @@
 ):
     copies = [pltpu.make_async_copy(in_hbm, in_ref, sems.at[0])]
     copies += [
-        pltpu.make_async_copy(pre_hbm.at[:, z], pre_ref.at[z], sems.at[5 + z]) for z in range(8)
+        pltpu.make_async_copy(pre_hbm.at[pl.ds(4 * i, 4)], pre_ref.at[pl.ds(4 * i, 4)], sems.at[5 + i]) for i in range(4)
     ]
     copies += [
-        pltpu.make_async_copy(slab_hbm.at[:, :, pl.ds(128 * b, 128)], slab_ref.at[b], sems.at[1 + b]) for b in range(4)
+        pltpu.make_async_copy(slab_hbm.at[pl.ds(8 * b, 8)], slab_ref.at[pl.ds(8 * b, 8)], sems.at[1 + b]) for b in range(4)
     ]
     for copy in copies:
         copy.start()
@@ -94,9 +94,10 @@
         ],
         axis=0,
     ).astype(BF16)
-    for copy in copies[1:9]:
+    for copy in copies[1:5]:
         copy.wait()
-    got = dot_t(pick, pre_ref[...].astype(F32).reshape(1024, 128).astype(BF16)).astype(BF16)
+    planes = [pre_ref[:, z].astype(F32).reshape(128, 128) for z in range(8)]
+    got = dot_t(pick, jnp.concatenate(planes, axis=0).astype(BF16)).astype(BF16)
     got = dot(jnp.concatenate([got[:, 128 * z : 128 * z + 128] for z in range(8)], axis=0), order)
     edges = [jnp.zeros((8, 128), F32)] * 2
     for z in range(8):
@@ -111,9 +112,10 @@
     for copy in results:
         copy.start()
 
+    for copy in copies[5:]:
+        copy.wait()
     for b in range(4):
-        copies[9 + b].wait()
-        wide_ref[b] = slab_ref[b].astype(F32).reshape(512, 128)
+        wide_ref[b] = slab_ref[:, :, 128 * b : 128 * b + 128].astype(F32).reshape(512, 128)
         for y in range(16):
             slot = (y + 1) % 16
             turned_ref[32 * slot : 32 * slot + 32, 128 * b : 128 * b + 128] = wide_ref[
@@ -354,21 +356,29 @@
         out_ref[:, z + 4] = far.reshape(4, 8, 128).astype(BF16)
 
 
-def unpack_kernel(mine_ref, rest_ref, one_ref, two_ref, flat_ref):
+def unpack_kernel(mine_ref, rest_ref, one_hbm, two_hbm, one_ref, two_ref, flat_ref, sems):
     first = lax.rem(lax.axis_index("dp"), 2) == 0
     mine, rest = mine_ref[...], rest_ref[...]
     low, high = jnp.where(first, mine, rest), jnp.where(first, rest, mine)
     blocks = [low[16 * q : 16 * q + 16] for q in range(4)] + [high[16 * q : 16 * q + 16] for q in range(4)]
+    copies = []
+    for q in range(3):
+        for k in range(9 * q, 9 * q + 9):
+            two_ref[k] = blocks[k // 4][:, 32 * (k % 4) : 32 * (k % 4) + 32]
+        copies.append(pltpu.make_async_copy(two_ref.at[pl.ds(9 * q, 9)], two_hbm.at[pl.ds(9 * q, 9)], sems.at[q]))
+        copies[-1].start()
     for pair in range(9):
         source, lane = (blocks[7], 16 * pair) if pair < 8 else (blocks[6], 96)
         source = pltpu.roll(source, 128 - lane, 1) if lane else source
         for kx in range(3):
             flat_ref[pl.ds(3 * pair + kx, 4, stride=32), :] = source[4 * kx : 4 * kx + 4]
-    for k in range(27):
-        two_ref[k] = blocks[k // 4][:, 32 * (k % 4) : 32 * (k % 4) + 32]
     turned = flat_ref[...].T
     for c in range(4):
         one_ref[c] = turned[:16, 32 * c : 32 * c + 27]
+    copies.append(pltpu.make_async_copy(one_ref, one_hbm, sems.at[3]))
+    copies[-1].start()
+    for copy in copies:
+        copy.wait()
 
 
 def routes():
@@ -396,10 +406,10 @@
         cut_kernel, "cut",
         [shape((10, WIDE, 128), BF16), shape((10, WIDE, 128), BF16), shape((8, WIDE, 512), BF16)],
         [
-            pltpu.VMEM((4, 32, 16, 128), BF16), pltpu.VMEM((8, 16, 8, 128), BF16), pltpu.VMEM((4, 8, 8, 128), BF16),
+            pltpu.VMEM((32, 16, 512), BF16), pltpu.VMEM((16, 8, 8, 128), BF16), pltpu.VMEM((4, 8, 8, 128), BF16),
             pltpu.VMEM((10, WIDE, 128), BF16), pltpu.VMEM((10, WIDE, 128), BF16), pltpu.VMEM((8, WIDE, 512), BF16),
             pltpu.VMEM((4, 512, 128), F32), pltpu.VMEM((512, 512), BF16),
-            pltpu.SemaphoreType.DMA((13,)), pltpu.SemaphoreType.DMA((10,)),
+            pltpu.SemaphoreType.DMA((9,)), pltpu.SemaphoreType.DMA((10,)),
         ],
         [out_grad[0, 0], pre_act[0, 0], inputs[0, 0]], 4e8, 2e6, limit=FULL, far_args=(0, 1, 2), far_outs=(0, 1, 2),
     )
@@ -437,8 +447,12 @@
     other = lax.ppermute(total, ALL, cores)
     (input_grad,) = call(tile_kernel, "tile", [shape((4, 8, 8, 128), BF16)], [], [own, got], 1e6, 2e5)
     first, second = call(
-        unpack_kernel, "unpack", [shape((4, 16, 27), F32), shape((27, 16, 32), F32)], [pltpu.VMEM((128, 128), F32)],
-        [total, other], 1e6, 2e5,
+        unpack_kernel, "unpack", [shape((4, 16, 27), F32), shape((27, 16, 32), F32)],
+        [
+            pltpu.VMEM((4, 16, 27), F32), pltpu.VMEM((27, 16, 32), F32), pltpu.VMEM((128, 128), F32),
+            pltpu.SemaphoreType.DMA((4,)),
+        ],
+        [total, other], 1e6, 2e5, far_outs=(0, 1),
     )
     return input_grad[None, None], first.transpose(2, 0, 1), second
 

time: 52.1 us -> 52.2 us (level)
  no operation moved by 1% of the time
where the time goes in v10:
time: 52.2 us; the launch traced here: 51.9 us
  starting transfers between devices  25.1 us (48%)
  waiting for transfers between devices  16.1 us (31%)
  Pallas kernels  9.61 us (18%)
  between operations  0.71 us (1%)
    ppermute x9, starting transfers between devices, body(): parts = [lax.ppermute(total, ALL, pairs) for pairs in stage]  10.6 us
    pallas_call x6, Pallas kernels, call(): pl.pallas_call(kernel, name=name, out_shape=outs, in_specs=[spec(i in far...  9.61 us
    all_to_all x1, waiting for transfers between devices, body(): strips = lax.all_to_all(strips, 'space', 0, 0, tiled=True)  8.02 us
    ppermute x9, waiting for transfers between devices, body(): parts = [lax.ppermute(total, ALL, pairs) for pairs in stage]  6.9 us
    ppermute x1, starting transfers between devices, body(): other = lax.ppermute(total, ALL, cores)  4.72 us
    all_to_all x1, starting transfers between devices, body(): strips = lax.all_to_all(strips, 'space', 0, 0, tiled=True)  4.19 us
    ppermute x1, starting transfers between devices, body(): recv = lax.ppermute(send, 'space', swap)  2.54 us
    ppermute x1, starting transfers between devices, body(): total = mine + lax.ppermute(rest, ALL, cores)  2.01 us
  transfers between devices with their start and end apart: 14, of which 9 were waited for; matrix products, arithmetic and copies ran while one was open for 1% of the time, Pallas kernels for 5%

profile of v10, /device:TPU:1, one launch (start us, length us, event | category | flops | bytes accessed | tf_op | source)
XLA Modules:
  0.0 51.9 jit_solution(6116624557123547894)
XLA Ops:
  0.6 0.0 copy-start.1
  0.6 3.3 %cut.1 = (bf16[10,72,128]{2,1,0:T(8,128)(2,1)}, bf16[10,72,128]{2,1,0:T(8,128)(2,1)}, bf16[8,72,512]{2,1,0:T(8,128)(2,1)}) custom-call(bf16[32,16,512]{2,1,0:T(8,128)(2,1)} %bitcast.14, bf16[16,8,8,128]{3,2,1,0:T(8,128)(2,1)} %bitcast.15, bf16[4,8,8,128]{3,2,1,0:T(8,128)(2,1)} %bitcast.16), custom_call_target="tpu_custom_call" | custom-call | flops 400000000 | bytes 2000000 | tf_op jit(solution)/shard_map/cut/pallas_call | solution.py:42
  4.0 0.0 copy-start
  4.0 2.5 %collective-permute-start = (bf16[10,72,128]{2,1,0:T(8,128)(2,1)}, bf16[10,72,128]{2,1,0:T(8,128)(2,1)S(1)}, u32[]{:S(2)}, u32[]{:S(2)}) collective-permute-start(bf16[10,72,128]{2,1,0:T(8,128)(2,1)} %get-tuple-element.19), channel_id=1, source_target_pairs={{0,1},{1,0},{2,3},{3,2},{4,5},{5,4},{6,7},{7,6},{8,9},{9,8},{10,11... | collective-permute-start | bytes 552968 | tf_op jit(solution)/shard_map/ppermute | solution.py:417
  6.5 4.2 %all-to-all-start = ((bf16[8,72,512]{2,1,0:T(8,128)(2,1)}), bf16[8,72,512]{2,1,0:T(8,128)(2,1)S(1)}, u32[]{:S(2)}, u32[]{:S(2)}) async-start(bf16[8,72,512]{2,1,0:T(8,128)(2,1)} %get-tuple-element.17), calls=%async_computation | async-start | bytes 1179648 | tf_op jit(solution)/shard_map/all_to_all | solution.py:418
  10.7 0.0 copy-done.1
  10.7 0.2 copy.8
  10.9 0.2 collective-permute-done.recv_ref
  11.1 0.0 copy-done
  11.1 0.8 %ready.1 = (bf16[8,80,256]{2,1,0:T(8,128)(2,1)S(1)}, bf16[864,640]{1,0:T(8,128)(2,1)S(1)}, bf16[256,640]{1,0:T(8,128)(2,1)S(1)}, bf16[768,256]{1,0:T(8,128)(2,1)S(1)}) custom-call(bf16[10,72,128]{2,1,0:T(8,128)(2,1)S(1)} %copy-done, bf16[10,72,128]{2,1,0:T(8,128)(2,1)S(1)} %collective-permute-done.recv_ref, bf16[864,16]{1,0:T(8,128)(2,1)S(1)} %bitcast.9), custom_call_target="tpu_custom_call" | custom-call | flops 20000000000 | bytes 5000000 | tf_op jit(solution)/shard_map/ready/pallas_call | solution.py:42
  11.9 8.0 %all-to-all-done.grad_ref = bf16[8,72,512]{2,1,0:T(8,128)(2,1)S(1)} async-done(((bf16[8,72,512]{2,1,0:T(8,128)(2,1)}), bf16[8,72,512]{2,1,0:T(8,128)(2,1)S(1)}, u32[]{:S(2)}, u32[]{:S(2)}) %all-to-all-start) | async-done | bytes 589856 | tf_op jit(solution)/shard_map/all_to_all | solution.py:418
  19.9 0.0 copy-start.2
  19.9 3.0 %grads.1 = (bf16[800,256]{1,0:T(8,128)(2,1)S(1)}, f32[64,128]{1,0:T(8,128)S(1)}, f32[64,128]{1,0:T(8,128)S(1)}) custom-call(bf16[8,72,512]{2,1,0:T(8,128)(2,1)S(1)} %all-to-all-done.grad_ref, bf16[8,80,256]{2,1,0:T(8,128)(2,1)S(1)} %get-tuple-element.20.pre_ref, bf16[864,640]{1,0:T(8,128)(2,1)S(1)} %get-tuple-element.21.hid_ref, ...), custom_call_target="tpu_custom_call" | custom-call | flops 3000000000 | bytes 4000000 | tf_op jit(solution)/shard_map/grads/pallas_call | solution.py:42
  22.9 2.0 %collective-permute-start.2 = (f32[64,128]{1,0:T(8,128)S(1)}, f32[64,128]{1,0:T(8,128)S(1)}, u32[]{:S(2)}, u32[]{:S(2)}) collective-permute-start(f32[64,128]{1,0:T(8,128)S(1)} %get-tuple-element.28), channel_id=1, source_target_pairs={{0,8},{1,9},{2,10},{3,11},{4,12},{5,13},{6,14},{7,15},{8,0},{9,1},... | collective-permute-start | bytes 98312 | tf_op jit(solution)/shard_map/ppermute | solution.py:442
  24.9 0.9 %collective-permute-done.2 = f32[64,128]{1,0:T(8,128)S(1)} collective-permute-done((f32[64,128]{1,0:T(8,128)S(1)}, f32[64,128]{1,0:T(8,128)S(1)}, u32[]{:S(2)}, u32[]{:S(2)}) %collective-permute-start.2) | collective-permute-done | bytes 32800 | tf_op jit(solution)/shard_map/ppermute | solution.py:442
  25.8 2.5 %collective-permute-start.4 = (f32[64,128]{1,0:T(8,128)S(1)}, f32[64,128]{1,0:T(8,128)S(1)}, u32[]{:S(2)}, u32[]{:S(2)}) collective-permute-start(f32[64,128]{1,0:T(8,128)S(1)} %add.30), channel_id=1, source_target_pairs={{0,48},{1,49},{2,50},{3,51},{4,52},{5,53},{6,54},{7,55},{8,56},{9,... | collective-permute-start | bytes 98312 | tf_op jit(solution)/shard_map/ppermute | solution.py:445
  28.3 0.5 collective-permute-start.5
  28.8 0.3 collective-permute-start.3
  29.0 0.7 %collective-permute-done.4 = f32[64,128]{1,0:T(8,128)S(1)} collective-permute-done((f32[64,128]{1,0:T(8,128)S(1)}, f32[64,128]{1,0:T(8,128)S(1)}, u32[]{:S(2)}, u32[]{:S(2)}) %collective-permute-start.4) | collective-permute-done | bytes 32800 | tf_op jit(solution)/shard_map/ppermute | solution.py:445
  29.8 2.8 %collective-permute-done.5 = f32[64,128]{1,0:T(8,128)S(1)} collective-permute-done((f32[64,128]{1,0:T(8,128)S(1)}, f32[64,128]{1,0:T(8,128)S(1)}, u32[]{:S(2)}, u32[]{:S(2)}) %collective-permute-start.5) | collective-permute-done | bytes 32800 | tf_op jit(solution)/shard_map/ppermute | solution.py:445
  32.5 0.0 collective-permute-done.3
  32.6 1.0 %collective-permute-start.7 = (f32[64,128]{1,0:T(8,128)S(1)}, f32[64,128]{1,0:T(8,128)S(1)}, u32[]{:S(2)}, u32[]{:S(2)}) collective-permute-start(f32[64,128]{1,0:T(8,128)S(1)} %add_add_fusion.2), channel_id=1, source_target_pairs={{0,6},{1,7},{2,4},{3,5},{4,2},{5,3},{6,0},{7,1},{8,14},{9,15},{10,... | collective-permute-start | bytes 98312 | tf_op jit(solution)/shard_map/ppermute | solution.py:445
  33.5 1.4 %collective-permute-start.8 = (f32[64,128]{1,0:T(8,128)S(1)}, f32[64,128]{1,0:T(8,128)S(1)}, u32[]{:S(2)}, u32[]{:S(2)}) collective-permute-start(f32[64,128]{1,0:T(8,128)S(1)} %add_add_fusion.2), channel_id=1, source_target_pairs={{0,4},{1,5},{2,6},{3,7},{4,0},{5,1},{6,2},{7,3},{8,12},{9,13},{10,... | collective-permute-start | bytes 98312 | tf_op jit(solution)/shard_map/ppermute | solution.py:445
  34.9 1.0 %collective-permute-start.6 = (f32[64,128]{1,0:T(8,128)S(1)}, f32[64,128]{1,0:T(8,128)S(1)}, u32[]{:S(2)}, u32[]{:S(2)}) collective-permute-start(f32[64,128]{1,0:T(8,128)S(1)} %add_add_fusion.2), channel_id=1, source_target_pairs={{0,2},{1,3},{2,0},{3,1},{4,6},{5,7},{6,4},{7,5},{8,10},{9,11},{10,... | collective-permute-start | bytes 98312 | tf_op jit(solution)/shard_map/ppermute | solution.py:445
  35.9 0.0 copy-done.2
  35.9 0.2 copy.9
  36.1 0.5 collective-permute-done.7
  36.6 1.2 %collective-permute-done.8 = f32[64,128]{1,0:T(8,128)S(1)} collective-permute-done((f32[64,128]{1,0:T(8,128)S(1)}, f32[64,128]{1,0:T(8,128)S(1)}, u32[]{:S(2)}, u32[]{:S(2)}) %collective-permute-start.8) | collective-permute-done | bytes 32800 | tf_op jit(solution)/shard_map/ppermute | solution.py:445
  37.8 0.0 collective-permute-done.6
  37.8 3.4 %collective-permute-start.10 = (f32[64,128]{1,0:T(8,128)S(1)}, f32[64,128]{1,0:T(8,128)S(1)}, u32[]{:S(2)}, u32[]{:S(2)}) collective-permute-start(f32[64,128]{1,0:T(8,128)S(1)} %add_add_fusion.1), channel_id=1, source_target_pairs={{0,65},{1,64},{2,67},{3,66},{4,69},{5,68},{6,71},{7,70},{8,73},{9,... | collective-permute-start | bytes 98312 | tf_op jit(solution)/shard_map/ppermute | solution.py:445
  41.2 0.1 collective-permute-start.11
  41.3 0.6 %collective-permute-start.9 = (f32[64,128]{1,0:T(8,128)S(1)}, f32[64,128]{1,0:T(8,128)S(1)}, u32[]{:S(2)}, u32[]{:S(2)}) collective-permute-start(f32[64,128]{1,0:T(8,128)S(1)} %add_add_fusion.1), channel_id=1, source_target_pairs={{0,1},{1,0},{2,3},{3,2},{4,5},{5,4},{6,7},{7,6},{8,9},{9,8},{10,11... | collective-permute-start | bytes 98312 | tf_op jit(solution)/shard_map/ppermute | solution.py:445
  41.9 0.9 %back.1 = (bf16[4,32,128]{2,1,0:T(8,128)(2,1)S(1)}, bf16[4,32,128]{2,1,0:T(8,128)(2,1)S(1)}) custom-call(bf16[800,256]{1,0:T(8,128)(2,1)S(1)} %get-tuple-element.24.act_s, bf16[432,4]{1,0:T(8,128)(2,1)S(1)} %bitcast.10), custom_call_target="tpu_custom_call" | custom-call | flops 500000000 | bytes 1000000 | tf_op jit(solution)/shard_map/back/pallas_call | solution.py:42
  42.8 1.0 %collective-permute-start.1 = (bf16[4,32,128]{2,1,0:T(8,128)(2,1)S(1)}, bf16[4,32,128]{2,1,0:T(8,128)(2,1)S(1)}, u32[]{:S(2)}, u32[]{:S(2)}) collective-permute-start(bf16[4,32,128]{2,1,0:T(8,128)(2,1)S(1)} %get-tuple-element.26), channel_id=1, source_target_pairs={{0,1},{1,0},{2,3},{3,2},{4,5},{5,4},{6,7},{7,6},{8,9},{9,8},{10,11... | collective-permute-start | bytes 98312 | tf_op jit(solution)/shard_map/ppermute | solution.py:443
  43.7 0.0 collective-permute-done.10
  43.7 1.7 %collective-permute-done.11 = f32[64,128]{1,0:T(8,128)S(1)} collective-permute-done((f32[64,128]{1,0:T(8,128)S(1)}, f32[64,128]{1,0:T(8,128)S(1)}, u32[]{:S(2)}, u32[]{:S(2)}) %collective-permute-start.11) | collective-permute-done | bytes 32800 | tf_op jit(solution)/shard_map/ppermute | solution.py:445
  45.5 0.0 collective-permute-done.9
  45.5 4.7 %collective-permute-start.12 = (f32[64,128]{1,0:T(8,128)S(1)}, f32[64,128]{1,0:T(8,128)S(1)}, u32[]{:S(2)}, u32[]{:S(2)}) collective-permute-start(f32[64,128]{1,0:T(8,128)S(1)} %add_add_fusion.mine_ref), channel_id=1, source_target_pairs={{0,8},{1,9},{2,10},{3,11},{4,12},{5,13},{6,14},{7,15},{8,0},{9,1},... | collective-permute-start | bytes 98312 | tf_op jit(solution)/shard_map/ppermute | solution.py:447
  50.2 0.0 collective-permute-done.1.recv_ref
  50.2 0.7 %tile.1 = bf16[4,8,8,128]{3,2,1,0:T(8,128)(2,1)} custom-call(bf16[4,32,128]{2,1,0:T(8,128)(2,1)S(1)} %get-tuple-element.25.own_ref, bf16[4,32,128]{2,1,0:T(8,128)(2,1)S(1)} %collective-permute-done.1.recv_ref), custom_call_target="tpu_custom_call" | custom-call | flops 1000000 | bytes 200000 | tf_op jit(solution)/shard_map/tile/pallas_call | solution.py:42
  50.9 0.1 collective-permute-done.12.rest_ref
  51.1 0.9 %unpack.1 = (f32[4,16,27]{2,1,0:T(8,128)}, f32[27,16,32]{2,1,0:T(8,128)}) custom-call(f32[64,128]{1,0:T(8,128)S(1)} %add_add_fusion.mine_ref, f32[64,128]{1,0:T(8,128)S(1)} %collective-permute-done.12.rest_ref), custom_call_target="tpu_custom_call" | custom-call | flops 1000000 | bytes 200000 | tf_op jit(solution)/shard_map/unpack/pallas_call | solution.py:42
  (4 shorter events, 0.0 us)
Async XLA Ops:
  0.6 10.1 %copy-start.1 = (bf16[27,16,32]{2,1,0:T(8,128)(2,1)S(1)}, bf16[27,16,32]{2,1,0:T(8,128)(2,1)}, u32[]{:S(2)}) copy-start(bf16[27,16,32]{2,1,0:T(8,128)(2,1)} %param.9) | copy-start | bytes 82948
  4.0 7.1 %copy-start = (bf16[10,72,128]{2,1,0:T(8,128)(2,1)S(1)}, bf16[10,72,128]{2,1,0:T(8,128)(2,1)}, u32[]{:S(2)}) copy-start(bf16[10,72,128]{2,1,0:T(8,128)(2,1)} %get-tuple-element.18.keep_ref) | copy-start | bytes 552964
  4.0 7.1 %collective-permute-start = (bf16[10,72,128]{2,1,0:T(8,128)(2,1)}, bf16[10,72,128]{2,1,0:T(8,128)(2,1)S(1)}, u32[]{:S(2)}, u32[]{:S(2)}) collective-permute-start(bf16[10,72,128]{2,1,0:T(8,128)(2,1)} %get-tuple-element.19), channel_id=1, source_target_pairs={{0,1},{1,0},{2,3},{3,2},{4,5},{5,4},{6,7},{7,6},{8,9},{9,8},{10,11... | collective-permute-start | bytes 552968 | tf_op jit(solution)/shard_map/ppermute | solution.py:417
  6.5 13.4 %all-to-all-start = ((bf16[8,72,512]{2,1,0:T(8,128)(2,1)}), bf16[8,72,512]{2,1,0:T(8,128)(2,1)S(1)}, u32[]{:S(2)}, u32[]{:S(2)}) async-start(bf16[8,72,512]{2,1,0:T(8,128)(2,1)} %get-tuple-element.17), calls=%async_computation | async-start | bytes 1179648 | tf_op jit(solution)/shard_map/all_to_all | solution.py:418
  19.9 15.9 %copy-start.2 = (bf16[27,4,16]{0,2,1:T(8,128)(2,1)S(1)}, bf16[27,4,16]{0,2,1:T(8,128)(2,1)}, u32[]{:S(2)}) copy-start(bf16[27,4,16]{0,2,1:T(8,128)(2,1)} %param.8) | copy-start | bytes 10372
  22.9 2.9 %collective-permute-start.2 = (f32[64,128]{1,0:T(8,128)S(1)}, f32[64,128]{1,0:T(8,128)S(1)}, u32[]{:S(2)}, u32[]{:S(2)}) collective-permute-start(f32[64,128]{1,0:T(8,128)S(1)} %get-tuple-element.28), channel_id=1, source_target_pairs={{0,8},{1,9},{2,10},{3,11},{4,12},{5,13},{6,14},{7,15},{8,0},{9,1},... | collective-permute-start | bytes 98312 | tf_op jit(solution)/shard_map/ppermute | solution.py:442
  25.8 4.0 %collective-permute-start.4 = (f32[64,128]{1,0:T(8,128)S(1)}, f32[64,128]{1,0:T(8,128)S(1)}, u32[]{:S(2)}, u32[]{:S(2)}) collective-permute-start(f32[64,128]{1,0:T(8,128)S(1)} %add.30), channel_id=1, source_target_pairs={{0,48},{1,49},{2,50},{3,51},{4,52},{5,53},{6,54},{7,55},{8,56},{9,... | collective-permute-start | bytes 98312 | tf_op jit(solution)/shard_map/ppermute | solution.py:445
  28.3 4.3 %collective-permute-start.5 = (f32[64,128]{1,0:T(8,128)S(1)}, f32[64,128]{1,0:T(8,128)S(1)}, u32[]{:S(2)}, u32[]{:S(2)}) collective-permute-start(f32[64,128]{1,0:T(8,128)S(1)} %add.30), channel_id=1, source_target_pairs={{0,32},{1,33},{2,34},{3,35},{4,36},{5,37},{6,38},{7,39},{8,40},{9,... | collective-permute-start | bytes 98312 | tf_op jit(solution)/shard_map/ppermute | solution.py:445
  28.8 3.8 %collective-permute-start.3 = (f32[64,128]{1,0:T(8,128)S(1)}, f32[64,128]{1,0:T(8,128)S(1)}, u32[]{:S(2)}, u32[]{:S(2)}) collective-permute-start(f32[64,128]{1,0:T(8,128)S(1)} %add.30), channel_id=1, source_target_pairs={{0,16},{1,17},{2,18},{3,19},{4,20},{5,21},{6,22},{7,23},{8,24},{9,... | collective-permute-start | bytes 98312 | tf_op jit(solution)/shard_map/ppermute | solution.py:445
  32.6 4.1 %collective-permute-start.7 = (f32[64,128]{1,0:T(8,128)S(1)}, f32[64,128]{1,0:T(8,128)S(1)}, u32[]{:S(2)}, u32[]{:S(2)}) collective-permute-start(f32[64,128]{1,0:T(8,128)S(1)} %add_add_fusion.2), channel_id=1, source_target_pairs={{0,6},{1,7},{2,4},{3,5},{4,2},{5,3},{6,0},{7,1},{8,14},{9,15},{10,... | collective-permute-start | bytes 98312 | tf_op jit(solution)/shard_map/ppermute | solution.py:445
  33.5 4.3 %collective-permute-start.8 = (f32[64,128]{1,0:T(8,128)S(1)}, f32[64,128]{1,0:T(8,128)S(1)}, u32[]{:S(2)}, u32[]{:S(2)}) collective-permute-start(f32[64,128]{1,0:T(8,128)S(1)} %add_add_fusion.2), channel_id=1, source_target_pairs={{0,4},{1,5},{2,6},{3,7},{4,0},{5,1},{6,2},{7,3},{8,12},{9,13},{10,... | collective-permute-start | bytes 98312 | tf_op jit(solution)/shard_map/ppermute | solution.py:445
  34.9 2.9 %collective-permute-start.6 = (f32[64,128]{1,0:T(8,128)S(1)}, f32[64,128]{1,0:T(8,128)S(1)}, u32[]{:S(2)}, u32[]{:S(2)}) collective-permute-start(f32[64,128]{1,0:T(8,128)S(1)} %add_add_fusion.2), channel_id=1, source_target_pairs={{0,2},{1,3},{2,0},{3,1},{4,6},{5,7},{6,4},{7,5},{8,10},{9,11},{10,... | collective-permute-start | bytes 98312 | tf_op jit(solution)/shard_map/ppermute | solution.py:445
  37.8 5.9 %collective-permute-start.10 = (f32[64,128]{1,0:T(8,128)S(1)}, f32[64,128]{1,0:T(8,128)S(1)}, u32[]{:S(2)}, u32[]{:S(2)}) collective-permute-start(f32[64,128]{1,0:T(8,128)S(1)} %add_add_fusion.1), channel_id=1, source_target_pairs={{0,65},{1,64},{2,67},{3,66},{4,69},{5,68},{6,71},{7,70},{8,73},{9,... | collective-permute-start | bytes 98312 | tf_op jit(solution)/shard_map/ppermute | solution.py:445
  41.2 4.3 %collective-permute-start.11 = (f32[64,128]{1,0:T(8,128)S(1)}, f32[64,128]{1,0:T(8,128)S(1)}, u32[]{:S(2)}, u32[]{:S(2)}) collective-permute-start(f32[64,128]{1,0:T(8,128)S(1)} %add_add_fusion.1), channel_id=1, source_target_pairs={{0,64},{1,65},{2,66},{3,67},{4,68},{5,69},{6,70},{7,71},{8,72},{9,... | collective-permute-start | bytes 98312 | tf_op jit(solution)/shard_map/ppermute | solution.py:445
  41.3 4.2 %collective-permute-start.9 = (f32[64,128]{1,0:T(8,128)S(1)}, f32[64,128]{1,0:T(8,128)S(1)}, u32[]{:S(2)}, u32[]{:S(2)}) collective-permute-start(f32[64,128]{1,0:T(8,128)S(1)} %add_add_fusion.1), channel_id=1, source_target_pairs={{0,1},{1,0},{2,3},{3,2},{4,5},{5,4},{6,7},{7,6},{8,9},{9,8},{10,11... | collective-permute-start | bytes 98312 | tf_op jit(solution)/shard_map/ppermute | solution.py:445
  42.8 7.4 %collective-permute-start.1 = (bf16[4,32,128]{2,1,0:T(8,128)(2,1)S(1)}, bf16[4,32,128]{2,1,0:T(8,128)(2,1)S(1)}, u32[]{:S(2)}, u32[]{:S(2)}) collective-permute-start(bf16[4,32,128]{2,1,0:T(8,128)(2,1)S(1)} %get-tuple-element.26), channel_id=1, source_target_pairs={{0,1},{1,0},{2,3},{3,2},{4,5},{5,4},{6,7},{7,6},{8,9},{9,8},{10,11... | collective-permute-start | bytes 98312 | tf_op jit(solution)/shard_map/ppermute | solution.py:443
  45.5 5.6 %collective-permute-start.12 = (f32[64,128]{1,0:T(8,128)S(1)}, f32[64,128]{1,0:T(8,128)S(1)}, u32[]{:S(2)}, u32[]{:S(2)}) collective-permute-start(f32[64,128]{1,0:T(8,128)S(1)} %add_add_fusion.mine_ref), channel_id=1, source_target_pairs={{0,8},{1,9},{2,10},{3,11},{4,12},{5,13},{6,14},{7,15},{8,0},{9,1},... | collective-permute-start | bytes 98312 | tf_op jit(solution)/shard_map/ppermute | solution.py:447

commit v11 on v9

--- a/solution.py
+++ b/solution.py
@@ -386,7 +386,7 @@
             z = (2 * d[0] + d[4]) ^ j
             pairs.append((number(*d), number(z // 2, d[1], d[2], d[3], z % 2)))
         along_z.append(pairs)
-    return cores, [along_x, along_y, along_z]
+    return cores, [along_z, along_y, along_x]
 
 
 def body(inputs, pre_act, out_grad, conv1_weight, conv2_weight):

time: 52.1 us -> 52.1 us (level)
  starting transfers between devices: 25.1 us -> 24.2 us
  waiting for transfers between devices: 16.1 us -> 17 us
    ppermute x1, starting transfers between devices: 0.97 us -> 0.09 us  [body(): got = lax.ppermute(give, 'space', swap)]
    ppermute x9, waiting for transfers between devices: 6.9 us -> 7.78 us  [body(): parts = [lax.ppermute(total, ALL, pairs) for pairs in stage]]
where the time goes in v11:
time: 52.1 us; the launch traced here: 51.9 us
  starting transfers between devices  24.2 us (46%)
  waiting for transfers between devices  17 us (33%)
  Pallas kernels  9.56 us (18%)
  between operations  0.72 us (1%)
    ppermute x9, starting transfers between devices, body(): parts = [lax.ppermute(total, ALL, pairs) for pairs in stage]  10.6 us
    pallas_call x6, Pallas kernels, call(): pl.pallas_call(kernel, name=name, out_shape=outs, in_specs=[spec(i in far...  9.56 us
    all_to_all x1, waiting for transfers between devices, body(): strips = lax.all_to_all(strips, 'space', 0, 0, tiled=True)  8.02 us
    ppermute x9, waiting for transfers between devices, body(): parts = [lax.ppermute(total, ALL, pairs) for pairs in stage]  7.78 us
    ppermute x1, starting transfers between devices, body(): other = lax.ppermute(total, ALL, cores)  4.72 us
    all_to_all x1, starting transfers between devices, body(): strips = lax.all_to_all(strips, 'space', 0, 0, tiled=True)  4.19 us
    ppermute x1, starting transfers between devices, body(): recv = lax.ppermute(send, 'space', swap)  2.55 us
    ppermute x1, starting transfers between devices, body(): total = mine + lax.ppermute(rest, ALL, cores)  2.01 us
  transfers between devices with their start and end apart: 14, of which 9 were waited for; matrix products, arithmetic and copies ran while one was open for 1% of the time, Pallas kernels for 5%

profile of v11, /device:TPU:1, one launch (start us, length us, event | category | flops | bytes accessed | tf_op | source)
XLA Modules:
  0.0 51.9 jit_solution(17129188216713694998)
XLA Ops:
  0.6 0.0 copy-start.1
  0.6 3.3 %cut.1 = (bf16[10,72,128]{2,1,0:T(8,128)(2,1)}, bf16[10,72,128]{2,1,0:T(8,128)(2,1)}, bf16[8,72,512]{2,1,0:T(8,128)(2,1)}) custom-call(bf16[32,16,512]{2,1,0:T(8,128)(2,1)} %bitcast.14, bf16[16,8,8,128]{3,2,1,0:T(8,128)(2,1)} %bitcast.15, bf16[4,8,8,128]{3,2,1,0:T(8,128)(2,1)} %bitcast.16), custom_call_target="tpu_custom_call" | custom-call | flops 400000000 | bytes 2000000 | tf_op jit(solution)/shard_map/cut/pallas_call | solution.py:42
  4.0 0.0 copy-start
  4.0 2.5 %collective-permute-start = (bf16[10,72,128]{2,1,0:T(8,128)(2,1)}, bf16[10,72,128]{2,1,0:T(8,128)(2,1)S(1)}, u32[]{:S(2)}, u32[]{:S(2)}) collective-permute-start(bf16[10,72,128]{2,1,0:T(8,128)(2,1)} %get-tuple-element.19), channel_id=1, source_target_pairs={{0,1},{1,0},{2,3},{3,2},{4,5},{5,4},{6,7},{7,6},{8,9},{9,8},{10,11... | collective-permute-start | bytes 552968 | tf_op jit(solution)/shard_map/ppermute | solution.py:407
  6.5 4.2 %all-to-all-start = ((bf16[8,72,512]{2,1,0:T(8,128)(2,1)}), bf16[8,72,512]{2,1,0:T(8,128)(2,1)S(1)}, u32[]{:S(2)}, u32[]{:S(2)}) async-start(bf16[8,72,512]{2,1,0:T(8,128)(2,1)} %get-tuple-element.17), calls=%async_computation | async-start | bytes 1179648 | tf_op jit(solution)/shard_map/all_to_all | solution.py:408
  10.7 0.0 copy-done.1
  10.7 0.2 copy.8
  10.9 0.2 collective-permute-done.recv_ref
  11.1 0.0 copy-done
  11.1 0.8 %ready.1 = (bf16[8,80,256]{2,1,0:T(8,128)(2,1)S(1)}, bf16[864,640]{1,0:T(8,128)(2,1)S(1)}, bf16[256,640]{1,0:T(8,128)(2,1)S(1)}, bf16[768,256]{1,0:T(8,128)(2,1)S(1)}) custom-call(bf16[10,72,128]{2,1,0:T(8,128)(2,1)S(1)} %copy-done, bf16[10,72,128]{2,1,0:T(8,128)(2,1)S(1)} %collective-permute-done.recv_ref, bf16[864,16]{1,0:T(8,128)(2,1)S(1)} %bitcast.9), custom_call_target="tpu_custom_call" | custom-call | flops 20000000000 | bytes 5000000 | tf_op jit(solution)/shard_map/ready/pallas_call | solution.py:42
  11.9 8.0 %all-to-all-done.grad_ref = bf16[8,72,512]{2,1,0:T(8,128)(2,1)S(1)} async-done(((bf16[8,72,512]{2,1,0:T(8,128)(2,1)}), bf16[8,72,512]{2,1,0:T(8,128)(2,1)S(1)}, u32[]{:S(2)}, u32[]{:S(2)}) %all-to-all-start) | async-done | bytes 589856 | tf_op jit(solution)/shard_map/all_to_all | solution.py:408
  19.9 0.0 copy-start.2
  19.9 3.0 %grads.1 = (bf16[800,256]{1,0:T(8,128)(2,1)S(1)}, f32[64,128]{1,0:T(8,128)S(1)}, f32[64,128]{1,0:T(8,128)S(1)}) custom-call(bf16[8,72,512]{2,1,0:T(8,128)(2,1)S(1)} %all-to-all-done.grad_ref, bf16[8,80,256]{2,1,0:T(8,128)(2,1)S(1)} %get-tuple-element.20.pre_ref, bf16[864,640]{1,0:T(8,128)(2,1)S(1)} %get-tuple-element.21.hid_ref, ...), custom_call_target="tpu_custom_call" | custom-call | flops 3000000000 | bytes 4000000 | tf_op jit(solution)/shard_map/grads/pallas_call | solution.py:42
  22.9 2.0 %collective-permute-start.2 = (f32[64,128]{1,0:T(8,128)S(1)}, f32[64,128]{1,0:T(8,128)S(1)}, u32[]{:S(2)}, u32[]{:S(2)}) collective-permute-start(f32[64,128]{1,0:T(8,128)S(1)} %get-tuple-element.28), channel_id=1, source_target_pairs={{0,8},{1,9},{2,10},{3,11},{4,12},{5,13},{6,14},{7,15},{8,0},{9,1},... | collective-permute-start | bytes 98312 | tf_op jit(solution)/shard_map/ppermute | solution.py:432
  24.9 0.9 %collective-permute-done.2 = f32[64,128]{1,0:T(8,128)S(1)} collective-permute-done((f32[64,128]{1,0:T(8,128)S(1)}, f32[64,128]{1,0:T(8,128)S(1)}, u32[]{:S(2)}, u32[]{:S(2)}) %collective-permute-start.2) | collective-permute-done | bytes 32800 | tf_op jit(solution)/shard_map/ppermute | solution.py:432
  25.8 3.3 %collective-permute-start.4 = (f32[64,128]{1,0:T(8,128)S(1)}, f32[64,128]{1,0:T(8,128)S(1)}, u32[]{:S(2)}, u32[]{:S(2)}) collective-permute-start(f32[64,128]{1,0:T(8,128)S(1)} %add.30), channel_id=1, source_target_pairs={{0,65},{1,64},{2,67},{3,66},{4,69},{5,68},{6,71},{7,70},{8,73},{9,... | collective-permute-start | bytes 98312 | tf_op jit(solution)/shard_map/ppermute | solution.py:435
  29.1 0.1 collective-permute-start.5
  29.1 0.6 %collective-permute-start.3 = (f32[64,128]{1,0:T(8,128)S(1)}, f32[64,128]{1,0:T(8,128)S(1)}, u32[]{:S(2)}, u32[]{:S(2)}) collective-permute-start(f32[64,128]{1,0:T(8,128)S(1)} %add.30), channel_id=1, source_target_pairs={{0,1},{1,0},{2,3},{3,2},{4,5},{5,4},{6,7},{7,6},{8,9},{9,8},{10,11... | collective-permute-start | bytes 98312 | tf_op jit(solution)/shard_map/ppermute | solution.py:435
  29.7 0.6 %collective-permute-done.4 = f32[64,128]{1,0:T(8,128)S(1)} collective-permute-done((f32[64,128]{1,0:T(8,128)S(1)}, f32[64,128]{1,0:T(8,128)S(1)}, u32[]{:S(2)}, u32[]{:S(2)}) %collective-permute-start.4) | collective-permute-done | bytes 32800 | tf_op jit(solution)/shard_map/ppermute | solution.py:435
  30.4 3.0 %collective-permute-done.5 = f32[64,128]{1,0:T(8,128)S(1)} collective-permute-done((f32[64,128]{1,0:T(8,128)S(1)}, f32[64,128]{1,0:T(8,128)S(1)}, u32[]{:S(2)}, u32[]{:S(2)}) %collective-permute-start.5) | collective-permute-done | bytes 32800 | tf_op jit(solution)/shard_map/ppermute | solution.py:435
  33.3 0.0 collective-permute-done.3
  33.4 1.0 %collective-permute-start.7 = (f32[64,128]{1,0:T(8,128)S(1)}, f32[64,128]{1,0:T(8,128)S(1)}, u32[]{:S(2)}, u32[]{:S(2)}) collective-permute-start(f32[64,128]{1,0:T(8,128)S(1)} %add_add_fusion.2), channel_id=1, source_target_pairs={{0,6},{1,7},{2,4},{3,5},{4,2},{5,3},{6,0},{7,1},{8,14},{9,15},{10,... | collective-permute-start | bytes 98312 | tf_op jit(solution)/shard_map/ppermute | solution.py:435
  34.3 1.2 %collective-permute-start.8 = (f32[64,128]{1,0:T(8,128)S(1)}, f32[64,128]{1,0:T(8,128)S(1)}, u32[]{:S(2)}, u32[]{:S(2)}) collective-permute-start(f32[64,128]{1,0:T(8,128)S(1)} %add_add_fusion.2), channel_id=1, source_target_pairs={{0,4},{1,5},{2,6},{3,7},{4,0},{5,1},{6,2},{7,3},{8,12},{9,13},{10,... | collective-permute-start | bytes 98312 | tf_op jit(solution)/shard_map/ppermute | solution.py:435
  35.5 1.2 %collective-permute-start.6 = (f32[64,128]{1,0:T(8,128)S(1)}, f32[64,128]{1,0:T(8,128)S(1)}, u32[]{:S(2)}, u32[]{:S(2)}) collective-permute-start(f32[64,128]{1,0:T(8,128)S(1)} %add_add_fusion.2), channel_id=1, source_target_pairs={{0,2},{1,3},{2,0},{3,1},{4,6},{5,7},{6,4},{7,5},{8,10},{9,11},{10,... | collective-permute-start | bytes 98312 | tf_op jit(solution)/shard_map/ppermute | solution.py:435
  36.7 0.0 copy-done.2
  36.7 0.2 copy.9
  36.9 0.5 collective-permute-done.7
  37.4 1.2 %collective-permute-done.8 = f32[64,128]{1,0:T(8,128)S(1)} collective-permute-done((f32[64,128]{1,0:T(8,128)S(1)}, f32[64,128]{1,0:T(8,128)S(1)}, u32[]{:S(2)}, u32[]{:S(2)}) %collective-permute-start.8) | collective-permute-done | bytes 32800 | tf_op jit(solution)/shard_map/ppermute | solution.py:435
  38.6 0.0 collective-permute-done.6
  38.6 2.6 %collective-permute-start.10 = (f32[64,128]{1,0:T(8,128)S(1)}, f32[64,128]{1,0:T(8,128)S(1)}, u32[]{:S(2)}, u32[]{:S(2)}) collective-permute-start(f32[64,128]{1,0:T(8,128)S(1)} %add_add_fusion.1), channel_id=1, source_target_pairs={{0,48},{1,49},{2,50},{3,51},{4,52},{5,53},{6,54},{7,55},{8,56},{9,... | collective-permute-start | bytes 98312 | tf_op jit(solution)/shard_map/ppermute | solution.py:435
  41.2 0.5 %collective-permute-start.11 = (f32[64,128]{1,0:T(8,128)S(1)}, f32[64,128]{1,0:T(8,128)S(1)}, u32[]{:S(2)}, u32[]{:S(2)}) collective-permute-start(f32[64,128]{1,0:T(8,128)S(1)} %add_add_fusion.1), channel_id=1, source_target_pairs={{0,32},{1,33},{2,34},{3,35},{4,36},{5,37},{6,38},{7,39},{8,40},{9,... | collective-permute-start | bytes 98312 | tf_op jit(solution)/shard_map/ppermute | solution.py:435
  41.7 0.3 collective-permute-start.9
  41.9 0.9 %back.1 = (bf16[4,32,128]{2,1,0:T(8,128)(2,1)S(1)}, bf16[4,32,128]{2,1,0:T(8,128)(2,1)S(1)}) custom-call(bf16[800,256]{1,0:T(8,128)(2,1)S(1)} %get-tuple-element.24.act_s, bf16[432,4]{1,0:T(8,128)(2,1)S(1)} %bitcast.10), custom_call_target="tpu_custom_call" | custom-call | flops 500000000 | bytes 1000000 | tf_op jit(solution)/shard_map/back/pallas_call | solution.py:42
  42.8 0.1 collective-permute-start.1
  42.9 0.0 collective-permute-done.10
  42.9 2.5 %collective-permute-done.11 = f32[64,128]{1,0:T(8,128)S(1)} collective-permute-done((f32[64,128]{1,0:T(8,128)S(1)}, f32[64,128]{1,0:T(8,128)S(1)}, u32[]{:S(2)}, u32[]{:S(2)}) %collective-permute-start.11) | collective-permute-done | bytes 32800 | tf_op jit(solution)/shard_map/ppermute | solution.py:435
  45.4 0.0 collective-permute-done.9
  45.4 4.7 %collective-permute-start.12 = (f32[64,128]{1,0:T(8,128)S(1)}, f32[64,128]{1,0:T(8,128)S(1)}, u32[]{:S(2)}, u32[]{:S(2)}) collective-permute-start(f32[64,128]{1,0:T(8,128)S(1)} %add_add_fusion.mine_ref), channel_id=1, source_target_pairs={{0,8},{1,9},{2,10},{3,11},{4,12},{5,13},{6,14},{7,15},{8,0},{9,1},... | collective-permute-start | bytes 98312 | tf_op jit(solution)/shard_map/ppermute | solution.py:437
  50.2 0.0 collective-permute-done.1.recv_ref
  50.2 0.7 %tile.1 = bf16[4,8,8,128]{3,2,1,0:T(8,128)(2,1)} custom-call(bf16[4,32,128]{2,1,0:T(8,128)(2,1)S(1)} %get-tuple-element.25.own_ref, bf16[4,32,128]{2,1,0:T(8,128)(2,1)S(1)} %collective-permute-done.1.recv_ref), custom_call_target="tpu_custom_call" | custom-call | flops 1000000 | bytes 200000 | tf_op jit(solution)/shard_map/tile/pallas_call | solution.py:42
  50.9 0.1 collective-permute-done.12.rest_ref
  51.0 0.9 %unpack.1 = (f32[4,16,27]{2,1,0:T(8,128)}, f32[27,16,32]{2,1,0:T(8,128)}) custom-call(f32[64,128]{1,0:T(8,128)S(1)} %add_add_fusion.mine_ref, f32[64,128]{1,0:T(8,128)S(1)} %collective-permute-done.12.rest_ref), custom_call_target="tpu_custom_call" | custom-call | flops 1000000 | bytes 200000 | tf_op jit(solution)/shard_map/unpack/pallas_call | solution.py:42
  (4 shorter events, 0.0 us)
Async XLA Ops:
  0.6 10.1 %copy-start.1 = (bf16[27,16,32]{2,1,0:T(8,128)(2,1)S(1)}, bf16[27,16,32]{2,1,0:T(8,128)(2,1)}, u32[]{:S(2)}) copy-start(bf16[27,16,32]{2,1,0:T(8,128)(2,1)} %param.9) | copy-start | bytes 82948
  4.0 7.1 %copy-start = (bf16[10,72,128]{2,1,0:T(8,128)(2,1)S(1)}, bf16[10,72,128]{2,1,0:T(8,128)(2,1)}, u32[]{:S(2)}) copy-start(bf16[10,72,128]{2,1,0:T(8,128)(2,1)} %get-tuple-element.18.keep_ref) | copy-start | bytes 552964
  4.0 7.1 %collective-permute-start = (bf16[10,72,128]{2,1,0:T(8,128)(2,1)}, bf16[10,72,128]{2,1,0:T(8,128)(2,1)S(1)}, u32[]{:S(2)}, u32[]{:S(2)}) collective-permute-start(bf16[10,72,128]{2,1,0:T(8,128)(2,1)} %get-tuple-element.19), channel_id=1, source_target_pairs={{0,1},{1,0},{2,3},{3,2},{4,5},{5,4},{6,7},{7,6},{8,9},{9,8},{10,11... | collective-permute-start | bytes 552968 | tf_op jit(solution)/shard_map/ppermute | solution.py:407
  6.5 13.4 %all-to-all-start = ((bf16[8,72,512]{2,1,0:T(8,128)(2,1)}), bf16[8,72,512]{2,1,0:T(8,128)(2,1)S(1)}, u32[]{:S(2)}, u32[]{:S(2)}) async-start(bf16[8,72,512]{2,1,0:T(8,128)(2,1)} %get-tuple-element.17), calls=%async_computation | async-start | bytes 1179648 | tf_op jit(solution)/shard_map/all_to_all | solution.py:408
  19.9 16.8 %copy-start.2 = (bf16[27,4,16]{0,2,1:T(8,128)(2,1)S(1)}, bf16[27,4,16]{0,2,1:T(8,128)(2,1)}, u32[]{:S(2)}) copy-start(bf16[27,4,16]{0,2,1:T(8,128)(2,1)} %param.8) | copy-start | bytes 10372
  22.9 2.9 %collective-permute-start.2 = (f32[64,128]{1,0:T(8,128)S(1)}, f32[64,128]{1,0:T(8,128)S(1)}, u32[]{:S(2)}, u32[]{:S(2)}) collective-permute-start(f32[64,128]{1,0:T(8,128)S(1)} %get-tuple-element.28), channel_id=1, source_target_pairs={{0,8},{1,9},{2,10},{3,11},{4,12},{5,13},{6,14},{7,15},{8,0},{9,1},... | collective-permute-start | bytes 98312 | tf_op jit(solution)/shard_map/ppermute | solution.py:432
  25.8 4.6 %collective-permute-start.4 = (f32[64,128]{1,0:T(8,128)S(1)}, f32[64,128]{1,0:T(8,128)S(1)}, u32[]{:S(2)}, u32[]{:S(2)}) collective-permute-start(f32[64,128]{1,0:T(8,128)S(1)} %add.30), channel_id=1, source_target_pairs={{0,65},{1,64},{2,67},{3,66},{4,69},{5,68},{6,71},{7,70},{8,73},{9,... | collective-permute-start | bytes 98312 | tf_op jit(solution)/shard_map/ppermute | solution.py:435
  29.1 4.3 %collective-permute-start.5 = (f32[64,128]{1,0:T(8,128)S(1)}, f32[64,128]{1,0:T(8,128)S(1)}, u32[]{:S(2)}, u32[]{:S(2)}) collective-permute-start(f32[64,128]{1,0:T(8,128)S(1)} %add.30), channel_id=1, source_target_pairs={{0,64},{1,65},{2,66},{3,67},{4,68},{5,69},{6,70},{7,71},{8,72},{9,... | collective-permute-start | bytes 98312 | tf_op jit(solution)/shard_map/ppermute | solution.py:435
  29.1 4.2 %collective-permute-start.3 = (f32[64,128]{1,0:T(8,128)S(1)}, f32[64,128]{1,0:T(8,128)S(1)}, u32[]{:S(2)}, u32[]{:S(2)}) collective-permute-start(f32[64,128]{1,0:T(8,128)S(1)} %add.30), channel_id=1, source_target_pairs={{0,1},{1,0},{2,3},{3,2},{4,5},{5,4},{6,7},{7,6},{8,9},{9,8},{10,11... | collective-permute-start | bytes 98312 | tf_op jit(solution)/shard_map/ppermute | solution.py:435
  33.4 4.1 %collective-permute-start.7 = (f32[64,128]{1,0:T(8,128)S(1)}, f32[64,128]{1,0:T(8,128)S(1)}, u32[]{:S(2)}, u32[]{:S(2)}) collective-permute-start(f32[64,128]{1,0:T(8,128)S(1)} %add_add_fusion.2), channel_id=1, source_target_pairs={{0,6},{1,7},{2,4},{3,5},{4,2},{5,3},{6,0},{7,1},{8,14},{9,15},{10,... | collective-permute-start | bytes 98312 | tf_op jit(solution)/shard_map/ppermute | solution.py:435
  34.3 4.3 %collective-permute-start.8 = (f32[64,128]{1,0:T(8,128)S(1)}, f32[64,128]{1,0:T(8,128)S(1)}, u32[]{:S(2)}, u32[]{:S(2)}) collective-permute-start(f32[64,128]{1,0:T(8,128)S(1)} %add_add_fusion.2), channel_id=1, source_target_pairs={{0,4},{1,5},{2,6},{3,7},{4,0},{5,1},{6,2},{7,3},{8,12},{9,13},{10,... | collective-permute-start | bytes 98312 | tf_op jit(solution)/shard_map/ppermute | solution.py:435
  35.5 3.1 %collective-permute-start.6 = (f32[64,128]{1,0:T(8,128)S(1)}, f32[64,128]{1,0:T(8,128)S(1)}, u32[]{:S(2)}, u32[]{:S(2)}) collective-permute-start(f32[64,128]{1,0:T(8,128)S(1)} %add_add_fusion.2), channel_id=1, source_target_pairs={{0,2},{1,3},{2,0},{3,1},{4,6},{5,7},{6,4},{7,5},{8,10},{9,11},{10,... | collective-permute-start | bytes 98312 | tf_op jit(solution)/shard_map/ppermute | solution.py:435
  38.6 4.3 %collective-permute-start.10 = (f32[64,128]{1,0:T(8,128)S(1)}, f32[64,128]{1,0:T(8,128)S(1)}, u32[]{:S(2)}, u32[]{:S(2)}) collective-permute-start(f32[64,128]{1,0:T(8,128)S(1)} %add_add_fusion.1), channel_id=1, source_target_pairs={{0,48},{1,49},{2,50},{3,51},{4,52},{5,53},{6,54},{7,55},{8,56},{9,... | collective-permute-start | bytes 98312 | tf_op jit(solution)/shard_map/ppermute | solution.py:435
  41.2 4.3 %collective-permute-start.11 = (f32[64,128]{1,0:T(8,128)S(1)}, f32[64,128]{1,0:T(8,128)S(1)}, u32[]{:S(2)}, u32[]{:S(2)}) collective-permute-start(f32[64,128]{1,0:T(8,128)S(1)} %add_add_fusion.1), channel_id=1, source_target_pairs={{0,32},{1,33},{2,34},{3,35},{4,36},{5,37},{6,38},{7,39},{8,40},{9,... | collective-permute-start | bytes 98312 | tf_op jit(solution)/shard_map/ppermute | solution.py:435
  41.7 3.8 %collective-permute-start.9 = (f32[64,128]{1,0:T(8,128)S(1)}, f32[64,128]{1,0:T(8,128)S(1)}, u32[]{:S(2)}, u32[]{:S(2)}) collective-permute-start(f32[64,128]{1,0:T(8,128)S(1)} %add_add_fusion.1), channel_id=1, source_target_pairs={{0,16},{1,17},{2,18},{3,19},{4,20},{5,21},{6,22},{7,23},{8,24},{9,... | collective-permute-start | bytes 98312 | tf_op jit(solution)/shard_map/ppermute | solution.py:435
  42.8 7.3 %collective-permute-start.1 = (bf16[4,32,128]{2,1,0:T(8,128)(2,1)S(1)}, bf16[4,32,128]{2,1,0:T(8,128)(2,1)S(1)}, u32[]{:S(2)}, u32[]{:S(2)}) collective-permute-start(bf16[4,32,128]{2,1,0:T(8,128)(2,1)S(1)} %get-tuple-element.26), channel_id=1, source_target_pairs={{0,1},{1,0},{2,3},{3,2},{4,5},{5,4},{6,7},{7,6},{8,9},{9,8},{10,11... | collective-permute-start | bytes 98312 | tf_op jit(solution)/shard_map/ppermute | solution.py:433
  45.4 5.6 %collective-permute-start.12 = (f32[64,128]{1,0:T(8,128)S(1)}, f32[64,128]{1,0:T(8,128)S(1)}, u32[]{:S(2)}, u32[]{:S(2)}) collective-permute-start(f32[64,128]{1,0:T(8,128)S(1)} %add_add_fusion.mine_ref), channel_id=1, source_target_pairs={{0,8},{1,9},{2,10},{3,11},{4,12},{5,13},{6,14},{7,15},{8,0},{9,1},... | collective-permute-start | bytes 98312 | tf_op jit(solution)/shard_map/ppermute | solution.py:437

commit v12 on v11

--- a/solution.py
+++ b/solution.py
@@ -430,10 +430,12 @@
         [act, conv1_weight.transpose(0, 2, 1).reshape(432, 4)], 5e8, 1e6,
     )
     total = mine + lax.ppermute(rest, ALL, cores)
-    got = lax.ppermute(give, "space", swap)
     for stage in stages:
         parts = [lax.ppermute(total, ALL, pairs) for pairs in stage]
         total = (total + parts[0]) + (parts[1] + parts[2])
+        if stage is stages[0]:
+            total, give = lax.optimization_barrier((total, give))
+    got = lax.ppermute(give, "space", swap)
     other = lax.ppermute(total, ALL, cores)
     (input_grad,) = call(tile_kernel, "tile", [shape((4, 8, 8, 128), BF16)], [], [own, got], 1e6, 2e5)
     first, second = call(

time: 52.1 us -> 52.1 us (level)
  no operation moved by 1% of the time
where the time goes in v12:
time: 52.1 us; the launch traced here: 51.9 us
  starting transfers between devices  24.1 us (46%)
  waiting for transfers between devices  17.1 us (33%)
  Pallas kernels  9.56 us (18%)
  between operations  0.72 us (1%)
    ppermute x9, starting transfers between devices, body(): parts = [lax.ppermute(total, ALL, pairs) for pairs in stage]  10.6 us
    pallas_call x6, Pallas kernels, call(): pl.pallas_call(kernel, name=name, out_shape=outs, in_specs=[spec(i in far...  9.56 us
    ppermute x9, waiting for transfers between devices, body(): parts = [lax.ppermute(total, ALL, pairs) for pairs in stage]  8.1 us
    all_to_all x1, waiting for transfers between devices, body(): strips = lax.all_to_all(strips, 'space', 0, 0, tiled=True)  8.02 us
    ppermute x1, starting transfers between devices, body(): other = lax.ppermute(total, ALL, cores)  4.72 us
    all_to_all x1, starting transfers between devices, body(): strips = lax.all_to_all(strips, 'space', 0, 0, tiled=True)  4.19 us
    ppermute x1, starting transfers between devices, body(): recv = lax.ppermute(send, 'space', swap)  2.55 us
    ppermute x1, starting transfers between devices, body(): total = mine + lax.ppermute(rest, ALL, cores)  2.01 us
  transfers between devices with their start and end apart: 14, of which 9 were waited for; matrix products, arithmetic and copies ran while one was open for 1% of the time, Pallas kernels for 5%

profile of v12, /device:TPU:1, one launch (start us, length us, event | category | flops | bytes accessed | tf_op | source)
XLA Modules:
  0.0 51.9 jit_solution(15333038432725005211)
XLA Ops:
  0.6 0.0 copy-start.1
  0.6 3.3 %cut.1 = (bf16[10,72,128]{2,1,0:T(8,128)(2,1)}, bf16[10,72,128]{2,1,0:T(8,128)(2,1)}, bf16[8,72,512]{2,1,0:T(8,128)(2,1)}) custom-call(bf16[32,16,512]{2,1,0:T(8,128)(2,1)} %bitcast.14, bf16[16,8,8,128]{3,2,1,0:T(8,128)(2,1)} %bitcast.15, bf16[4,8,8,128]{3,2,1,0:T(8,128)(2,1)} %bitcast.16), custom_call_target="tpu_custom_call" | custom-call | flops 400000000 | bytes 2000000 | tf_op jit(solution)/shard_map/cut/pallas_call | solution.py:42
  4.0 0.0 copy-start
  4.0 2.5 %collective-permute-start = (bf16[10,72,128]{2,1,0:T(8,128)(2,1)}, bf16[10,72,128]{2,1,0:T(8,128)(2,1)S(1)}, u32[]{:S(2)}, u32[]{:S(2)}) collective-permute-start(bf16[10,72,128]{2,1,0:T(8,128)(2,1)} %get-tuple-element.21), channel_id=1, source_target_pairs={{0,1},{1,0},{2,3},{3,2},{4,5},{5,4},{6,7},{7,6},{8,9},{9,8},{10,11... | collective-permute-start | bytes 552968 | tf_op jit(solution)/shard_map/ppermute | solution.py:407
  6.5 4.2 %all-to-all-start = ((bf16[8,72,512]{2,1,0:T(8,128)(2,1)}), bf16[8,72,512]{2,1,0:T(8,128)(2,1)S(1)}, u32[]{:S(2)}, u32[]{:S(2)}) async-start(bf16[8,72,512]{2,1,0:T(8,128)(2,1)} %get-tuple-element.19), calls=%async_computation | async-start | bytes 1179648 | tf_op jit(solution)/shard_map/all_to_all | solution.py:408
  10.7 0.0 copy-done.1
  10.7 0.2 copy.8
  10.9 0.2 collective-permute-done.recv_ref
  11.1 0.0 copy-done
  11.1 0.8 %ready.1 = (bf16[8,80,256]{2,1,0:T(8,128)(2,1)S(1)}, bf16[864,640]{1,0:T(8,128)(2,1)S(1)}, bf16[256,640]{1,0:T(8,128)(2,1)S(1)}, bf16[768,256]{1,0:T(8,128)(2,1)S(1)}) custom-call(bf16[10,72,128]{2,1,0:T(8,128)(2,1)S(1)} %copy-done, bf16[10,72,128]{2,1,0:T(8,128)(2,1)S(1)} %collective-permute-done.recv_ref, bf16[864,16]{1,0:T(8,128)(2,1)S(1)} %bitcast.9), custom_call_target="tpu_custom_call" | custom-call | flops 20000000000 | bytes 5000000 | tf_op jit(solution)/shard_map/ready/pallas_call | solution.py:42
  11.9 8.0 %all-to-all-done.grad_ref = bf16[8,72,512]{2,1,0:T(8,128)(2,1)S(1)} async-done(((bf16[8,72,512]{2,1,0:T(8,128)(2,1)}), bf16[8,72,512]{2,1,0:T(8,128)(2,1)S(1)}, u32[]{:S(2)}, u32[]{:S(2)}) %all-to-all-start) | async-done | bytes 589856 | tf_op jit(solution)/shard_map/all_to_all | solution.py:408
  19.9 0.0 copy-start.2
  19.9 3.0 %grads.1 = (bf16[800,256]{1,0:T(8,128)(2,1)S(1)}, f32[64,128]{1,0:T(8,128)S(1)}, f32[64,128]{1,0:T(8,128)S(1)}) custom-call(bf16[8,72,512]{2,1,0:T(8,128)(2,1)S(1)} %all-to-all-done.grad_ref, bf16[8,80,256]{2,1,0:T(8,128)(2,1)S(1)} %get-tuple-element.22.pre_ref, bf16[864,640]{1,0:T(8,128)(2,1)S(1)} %get-tuple-element.23.hid_ref, ...), custom_call_target="tpu_custom_call" | custom-call | flops 3000000000 | bytes 4000000 | tf_op jit(solution)/shard_map/grads/pallas_call | solution.py:42
  22.9 2.0 %collective-permute-start.1 = (f32[64,128]{1,0:T(8,128)S(1)}, f32[64,128]{1,0:T(8,128)S(1)}, u32[]{:S(2)}, u32[]{:S(2)}) collective-permute-start(f32[64,128]{1,0:T(8,128)S(1)} %get-tuple-element.29), channel_id=1, source_target_pairs={{0,8},{1,9},{2,10},{3,11},{4,12},{5,13},{6,14},{7,15},{8,0},{9,1},... | collective-permute-start | bytes 98312 | tf_op jit(solution)/shard_map/ppermute | solution.py:432
  24.9 0.0 copy-done.2
  24.9 0.2 copy.9
  25.1 0.6 %collective-permute-done.1 = f32[64,128]{1,0:T(8,128)S(1)} collective-permute-done((f32[64,128]{1,0:T(8,128)S(1)}, f32[64,128]{1,0:T(8,128)S(1)}, u32[]{:S(2)}, u32[]{:S(2)}) %collective-permute-start.1) | collective-permute-done | bytes 32800 | tf_op jit(solution)/shard_map/ppermute | solution.py:432
  25.8 3.3 %collective-permute-start.3 = (f32[64,128]{1,0:T(8,128)S(1)}, f32[64,128]{1,0:T(8,128)S(1)}, u32[]{:S(2)}, u32[]{:S(2)}) collective-permute-start(f32[64,128]{1,0:T(8,128)S(1)} %add.30), channel_id=1, source_target_pairs={{0,65},{1,64},{2,67},{3,66},{4,69},{5,68},{6,71},{7,70},{8,73},{9,... | collective-permute-start | bytes 98312 | tf_op jit(solution)/shard_map/ppermute | solution.py:434
  29.1 0.1 collective-permute-start.4
  29.1 0.6 %collective-permute-start.2 = (f32[64,128]{1,0:T(8,128)S(1)}, f32[64,128]{1,0:T(8,128)S(1)}, u32[]{:S(2)}, u32[]{:S(2)}) collective-permute-start(f32[64,128]{1,0:T(8,128)S(1)} %add.30), channel_id=1, source_target_pairs={{0,1},{1,0},{2,3},{3,2},{4,5},{5,4},{6,7},{7,6},{8,9},{9,8},{10,11... | collective-permute-start | bytes 98312 | tf_op jit(solution)/shard_map/ppermute | solution.py:434
  29.7 0.9 %back.1 = (bf16[4,32,128]{2,1,0:T(8,128)(2,1)S(1)}, bf16[4,32,128]{2,1,0:T(8,128)(2,1)S(1)}) custom-call(bf16[800,256]{1,0:T(8,128)(2,1)S(1)} %get-tuple-element.26.act_s, bf16[432,4]{1,0:T(8,128)(2,1)S(1)} %bitcast.10), custom_call_target="tpu_custom_call" | custom-call | flops 500000000 | bytes 1000000 | tf_op jit(solution)/shard_map/back/pallas_call | solution.py:42
  30.6 0.0 collective-permute-done.3
  30.6 2.7 %collective-permute-done.4 = f32[64,128]{1,0:T(8,128)S(1)} collective-permute-done((f32[64,128]{1,0:T(8,128)S(1)}, f32[64,128]{1,0:T(8,128)S(1)}, u32[]{:S(2)}, u32[]{:S(2)}) %collective-permute-start.4) | collective-permute-done | bytes 32800 | tf_op jit(solution)/shard_map/ppermute | solution.py:434
  33.3 0.0 collective-permute-done.2
  33.4 1.0 %collective-permute-start.7 = (f32[64,128]{1,0:T(8,128)S(1)}, f32[64,128]{1,0:T(8,128)S(1)}, u32[]{:S(2)}, u32[]{:S(2)}) collective-permute-start(f32[64,128]{1,0:T(8,128)S(1)} %add_add_fusion.2), channel_id=1, source_target_pairs={{0,6},{1,7},{2,4},{3,5},{4,2},{5,3},{6,0},{7,1},{8,14},{9,15},{10,... | collective-permute-start | bytes 98312 | tf_op jit(solution)/shard_map/ppermute | solution.py:434
  34.3 1.2 %collective-permute-start.8 = (f32[64,128]{1,0:T(8,128)S(1)}, f32[64,128]{1,0:T(8,128)S(1)}, u32[]{:S(2)}, u32[]{:S(2)}) collective-permute-start(f32[64,128]{1,0:T(8,128)S(1)} %add_add_fusion.2), channel_id=1, source_target_pairs={{0,4},{1,5},{2,6},{3,7},{4,0},{5,1},{6,2},{7,3},{8,12},{9,13},{10,... | collective-permute-start | bytes 98312 | tf_op jit(solution)/shard_map/ppermute | solution.py:434
  35.5 1.2 %collective-permute-start.6 = (f32[64,128]{1,0:T(8,128)S(1)}, f32[64,128]{1,0:T(8,128)S(1)}, u32[]{:S(2)}, u32[]{:S(2)}) collective-permute-start(f32[64,128]{1,0:T(8,128)S(1)} %add_add_fusion.2), channel_id=1, source_target_pairs={{0,2},{1,3},{2,0},{3,1},{4,6},{5,7},{6,4},{7,5},{8,10},{9,11},{10,... | collective-permute-start | bytes 98312 | tf_op jit(solution)/shard_map/ppermute | solution.py:434
  36.7 0.7 %collective-permute-done.7 = f32[64,128]{1,0:T(8,128)S(1)} collective-permute-done((f32[64,128]{1,0:T(8,128)S(1)}, f32[64,128]{1,0:T(8,128)S(1)}, u32[]{:S(2)}, u32[]{:S(2)}) %collective-permute-start.7) | collective-permute-done | bytes 32800 | tf_op jit(solution)/shard_map/ppermute | solution.py:434
  37.4 1.2 %collective-permute-done.8 = f32[64,128]{1,0:T(8,128)S(1)} collective-permute-done((f32[64,128]{1,0:T(8,128)S(1)}, f32[64,128]{1,0:T(8,128)S(1)}, u32[]{:S(2)}, u32[]{:S(2)}) %collective-permute-start.8) | collective-permute-done | bytes 32800 | tf_op jit(solution)/shard_map/ppermute | solution.py:434
  38.6 0.0 collective-permute-done.6
  38.6 2.6 %collective-permute-start.10 = (f32[64,128]{1,0:T(8,128)S(1)}, f32[64,128]{1,0:T(8,128)S(1)}, u32[]{:S(2)}, u32[]{:S(2)}) collective-permute-start(f32[64,128]{1,0:T(8,128)S(1)} %add_add_fusion.1), channel_id=1, source_target_pairs={{0,48},{1,49},{2,50},{3,51},{4,52},{5,53},{6,54},{7,55},{8,56},{9,... | collective-permute-start | bytes 98312 | tf_op jit(solution)/shard_map/ppermute | solution.py:434
  41.2 0.5 %collective-permute-start.11 = (f32[64,128]{1,0:T(8,128)S(1)}, f32[64,128]{1,0:T(8,128)S(1)}, u32[]{:S(2)}, u32[]{:S(2)}) collective-permute-start(f32[64,128]{1,0:T(8,128)S(1)} %add_add_fusion.1), channel_id=1, source_target_pairs={{0,32},{1,33},{2,34},{3,35},{4,36},{5,37},{6,38},{7,39},{8,40},{9,... | collective-permute-start | bytes 98312 | tf_op jit(solution)/shard_map/ppermute | solution.py:434
  41.7 0.3 collective-permute-start.9
  41.9 0.0 collective-permute-start.5
  41.9 0.7 %collective-permute-done.10 = f32[64,128]{1,0:T(8,128)S(1)} collective-permute-done((f32[64,128]{1,0:T(8,128)S(1)}, f32[64,128]{1,0:T(8,128)S(1)}, u32[]{:S(2)}, u32[]{:S(2)}) %collective-permute-start.10) | collective-permute-done | bytes 32800 | tf_op jit(solution)/shard_map/ppermute | solution.py:434
  42.7 2.8 %collective-permute-done.11 = f32[64,128]{1,0:T(8,128)S(1)} collective-permute-done((f32[64,128]{1,0:T(8,128)S(1)}, f32[64,128]{1,0:T(8,128)S(1)}, u32[]{:S(2)}, u32[]{:S(2)}) %collective-permute-start.11) | collective-permute-done | bytes 32800 | tf_op jit(solution)/shard_map/ppermute | solution.py:434
  45.4 0.0 collective-permute-done.9
  45.4 4.7 %collective-permute-start.12 = (f32[64,128]{1,0:T(8,128)S(1)}, f32[64,128]{1,0:T(8,128)S(1)}, u32[]{:S(2)}, u32[]{:S(2)}) collective-permute-start(f32[64,128]{1,0:T(8,128)S(1)} %add_add_fusion.mine_ref), channel_id=1, source_target_pairs={{0,8},{1,9},{2,10},{3,11},{4,12},{5,13},{6,14},{7,15},{8,0},{9,1},... | collective-permute-start | bytes 98312 | tf_op jit(solution)/shard_map/ppermute | solution.py:439
  50.2 0.0 collective-permute-done.5.recv_ref
  50.2 0.7 %tile.1 = bf16[4,8,8,128]{3,2,1,0:T(8,128)(2,1)} custom-call(bf16[4,32,128]{2,1,0:T(8,128)(2,1)S(1)} %get-tuple-element.27.own_ref, bf16[4,32,128]{2,1,0:T(8,128)(2,1)S(1)} %collective-permute-done.5.recv_ref), custom_call_target="tpu_custom_call" | custom-call | flops 1000000 | bytes 200000 | tf_op jit(solution)/shard_map/tile/pallas_call | solution.py:42
  50.9 0.1 collective-permute-done.12.rest_ref
  51.0 0.9 %unpack.1 = (f32[4,16,27]{2,1,0:T(8,128)}, f32[27,16,32]{2,1,0:T(8,128)}) custom-call(f32[64,128]{1,0:T(8,128)S(1)} %add_add_fusion.mine_ref, f32[64,128]{1,0:T(8,128)S(1)} %collective-permute-done.12.rest_ref), custom_call_target="tpu_custom_call" | custom-call | flops 1000000 | bytes 200000 | tf_op jit(solution)/shard_map/unpack/pallas_call | solution.py:42
  (4 shorter events, 0.0 us)
Async XLA Ops:
  0.6 10.1 %copy-start.1 = (bf16[27,16,32]{2,1,0:T(8,128)(2,1)S(1)}, bf16[27,16,32]{2,1,0:T(8,128)(2,1)}, u32[]{:S(2)}) copy-start(bf16[27,16,32]{2,1,0:T(8,128)(2,1)} %param.9) | copy-start | bytes 82948
  4.0 7.1 %copy-start = (bf16[10,72,128]{2,1,0:T(8,128)(2,1)S(1)}, bf16[10,72,128]{2,1,0:T(8,128)(2,1)}, u32[]{:S(2)}) copy-start(bf16[10,72,128]{2,1,0:T(8,128)(2,1)} %get-tuple-element.20.keep_ref) | copy-start | bytes 552964
  4.0 7.1 %collective-permute-start = (bf16[10,72,128]{2,1,0:T(8,128)(2,1)}, bf16[10,72,128]{2,1,0:T(8,128)(2,1)S(1)}, u32[]{:S(2)}, u32[]{:S(2)}) collective-permute-start(bf16[10,72,128]{2,1,0:T(8,128)(2,1)} %get-tuple-element.21), channel_id=1, source_target_pairs={{0,1},{1,0},{2,3},{3,2},{4,5},{5,4},{6,7},{7,6},{8,9},{9,8},{10,11... | collective-permute-start | bytes 552968 | tf_op jit(solution)/shard_map/ppermute | solution.py:407
  6.5 13.4 %all-to-all-start = ((bf16[8,72,512]{2,1,0:T(8,128)(2,1)}), bf16[8,72,512]{2,1,0:T(8,128)(2,1)S(1)}, u32[]{:S(2)}, u32[]{:S(2)}) async-start(bf16[8,72,512]{2,1,0:T(8,128)(2,1)} %get-tuple-element.19), calls=%async_computation | async-start | bytes 1179648 | tf_op jit(solution)/shard_map/all_to_all | solution.py:408
  19.9 5.0 %copy-start.2 = (bf16[27,4,16]{0,2,1:T(8,128)(2,1)S(1)}, bf16[27,4,16]{0,2,1:T(8,128)(2,1)}, u32[]{:S(2)}) copy-start(bf16[27,4,16]{0,2,1:T(8,128)(2,1)} %param.8) | copy-start | bytes 10372
  22.9 2.9 %collective-permute-start.1 = (f32[64,128]{1,0:T(8,128)S(1)}, f32[64,128]{1,0:T(8,128)S(1)}, u32[]{:S(2)}, u32[]{:S(2)}) collective-permute-start(f32[64,128]{1,0:T(8,128)S(1)} %get-tuple-element.29), channel_id=1, source_target_pairs={{0,8},{1,9},{2,10},{3,11},{4,12},{5,13},{6,14},{7,15},{8,0},{9,1},... | collective-permute-start | bytes 98312 | tf_op jit(solution)/shard_map/ppermute | solution.py:432
  25.8 4.9 %collective-permute-start.3 = (f32[64,128]{1,0:T(8,128)S(1)}, f32[64,128]{1,0:T(8,128)S(1)}, u32[]{:S(2)}, u32[]{:S(2)}) collective-permute-start(f32[64,128]{1,0:T(8,128)S(1)} %add.30), channel_id=1, source_target_pairs={{0,65},{1,64},{2,67},{3,66},{4,69},{5,68},{6,71},{7,70},{8,73},{9,... | collective-permute-start | bytes 98312 | tf_op jit(solution)/shard_map/ppermute | solution.py:434
  29.1 4.3 %collective-permute-start.4 = (f32[64,128]{1,0:T(8,128)S(1)}, f32[64,128]{1,0:T(8,128)S(1)}, u32[]{:S(2)}, u32[]{:S(2)}) collective-permute-start(f32[64,128]{1,0:T(8,128)S(1)} %add.30), channel_id=1, source_target_pairs={{0,64},{1,65},{2,66},{3,67},{4,68},{5,69},{6,70},{7,71},{8,72},{9,... | collective-permute-start | bytes 98312 | tf_op jit(solution)/shard_map/ppermute | solution.py:434
  29.1 4.2 %collective-permute-start.2 = (f32[64,128]{1,0:T(8,128)S(1)}, f32[64,128]{1,0:T(8,128)S(1)}, u32[]{:S(2)}, u32[]{:S(2)}) collective-permute-start(f32[64,128]{1,0:T(8,128)S(1)} %add.30), channel_id=1, source_target_pairs={{0,1},{1,0},{2,3},{3,2},{4,5},{5,4},{6,7},{7,6},{8,9},{9,8},{10,11... | collective-permute-start | bytes 98312 | tf_op jit(solution)/shard_map/ppermute | solution.py:434
  33.4 4.1 %collective-permute-start.7 = (f32[64,128]{1,0:T(8,128)S(1)}, f32[64,128]{1,0:T(8,128)S(1)}, u32[]{:S(2)}, u32[]{:S(2)}) collective-permute-start(f32[64,128]{1,0:T(8,128)S(1)} %add_add_fusion.2), channel_id=1, source_target_pairs={{0,6},{1,7},{2,4},{3,5},{4,2},{5,3},{6,0},{7,1},{8,14},{9,15},{10,... | collective-permute-start | bytes 98312 | tf_op jit(solution)/shard_map/ppermute | solution.py:434
  34.3 4.3 %collective-permute-start.8 = (f32[64,128]{1,0:T(8,128)S(1)}, f32[64,128]{1,0:T(8,128)S(1)}, u32[]{:S(2)}, u32[]{:S(2)}) collective-permute-start(f32[64,128]{1,0:T(8,128)S(1)} %add_add_fusion.2), channel_id=1, source_target_pairs={{0,4},{1,5},{2,6},{3,7},{4,0},{5,1},{6,2},{7,3},{8,12},{9,13},{10,... | collective-permute-start | bytes 98312 | tf_op jit(solution)/shard_map/ppermute | solution.py:434
  35.5 3.1 %collective-permute-start.6 = (f32[64,128]{1,0:T(8,128)S(1)}, f32[64,128]{1,0:T(8,128)S(1)}, u32[]{:S(2)}, u32[]{:S(2)}) collective-permute-start(f32[64,128]{1,0:T(8,128)S(1)} %add_add_fusion.2), channel_id=1, source_target_pairs={{0,2},{1,3},{2,0},{3,1},{4,6},{5,7},{6,4},{7,5},{8,10},{9,11},{10,... | collective-permute-start | bytes 98312 | tf_op jit(solution)/shard_map/ppermute | solution.py:434
  38.6 4.1 %collective-permute-start.10 = (f32[64,128]{1,0:T(8,128)S(1)}, f32[64,128]{1,0:T(8,128)S(1)}, u32[]{:S(2)}, u32[]{:S(2)}) collective-permute-start(f32[64,128]{1,0:T(8,128)S(1)} %add_add_fusion.1), channel_id=1, source_target_pairs={{0,48},{1,49},{2,50},{3,51},{4,52},{5,53},{6,54},{7,55},{8,56},{9,... | collective-permute-start | bytes 98312 | tf_op jit(solution)/shard_map/ppermute | solution.py:434
  41.2 4.3 %collective-permute-start.11 = (f32[64,128]{1,0:T(8,128)S(1)}, f32[64,128]{1,0:T(8,128)S(1)}, u32[]{:S(2)}, u32[]{:S(2)}) collective-permute-start(f32[64,128]{1,0:T(8,128)S(1)} %add_add_fusion.1), channel_id=1, source_target_pairs={{0,32},{1,33},{2,34},{3,35},{4,36},{5,37},{6,38},{7,39},{8,40},{9,... | collective-permute-start | bytes 98312 | tf_op jit(solution)/shard_map/ppermute | solution.py:434
  41.7 3.8 %collective-permute-start.9 = (f32[64,128]{1,0:T(8,128)S(1)}, f32[64,128]{1,0:T(8,128)S(1)}, u32[]{:S(2)}, u32[]{:S(2)}) collective-permute-start(f32[64,128]{1,0:T(8,128)S(1)} %add_add_fusion.1), channel_id=1, source_target_pairs={{0,16},{1,17},{2,18},{3,19},{4,20},{5,21},{6,22},{7,23},{8,24},{9,... | collective-permute-start | bytes 98312 | tf_op jit(solution)/shard_map/ppermute | solution.py:434
  41.9 8.2 %collective-permute-start.5 = (bf16[4,32,128]{2,1,0:T(8,128)(2,1)S(1)}, bf16[4,32,128]{2,1,0:T(8,128)(2,1)S(1)}, u32[]{:S(2)}, u32[]{:S(2)}) collective-permute-start(bf16[4,32,128]{2,1,0:T(8,128)(2,1)S(1)} %get-tuple-element.31), channel_id=1, source_target_pairs={{0,1},{1,0},{2,3},{3,2},{4,5},{5,4},{6,7},{7,6},{8,9},{9,8},{10,11... | collective-permute-start | bytes 98312 | tf_op jit(solution)/shard_map/ppermute | solution.py:438
  45.4 5.6 %collective-permute-start.12 = (f32[64,128]{1,0:T(8,128)S(1)}, f32[64,128]{1,0:T(8,128)S(1)}, u32[]{:S(2)}, u32[]{:S(2)}) collective-permute-start(f32[64,128]{1,0:T(8,128)S(1)} %add_add_fusion.mine_ref), channel_id=1, source_target_pairs={{0,8},{1,9},{2,10},{3,11},{4,12},{5,13},{6,14},{7,15},{8,0},{9,1},... | collective-permute-start | bytes 98312 | tf_op jit(solution)/shard_map/ppermute | solution.py:439

commit v13 on v11

--- a/solution.py
+++ b/solution.py
@@ -386,7 +386,7 @@
             z = (2 * d[0] + d[4]) ^ j
             pairs.append((number(*d), number(z // 2, d[1], d[2], d[3], z % 2)))
         along_z.append(pairs)
-    return cores, [along_z, along_y, along_x]
+    return cores, [along_y, along_z, along_x]
 
 
 def body(inputs, pre_act, out_grad, conv1_weight, conv2_weight):

time: 52.1 us -> 52.1 us (level)
  no operation moved by 1% of the time
where the time goes in v13:
time: 52.1 us; the launch traced here: 51.9 us
  starting transfers between devices  24.2 us (46%)
  waiting for transfers between devices  17 us (33%)
  Pallas kernels  9.56 us (18%)
  between operations  0.72 us (1%)
    ppermute x9, starting transfers between devices, body(): parts = [lax.ppermute(total, ALL, pairs) for pairs in stage]  10.6 us
    pallas_call x6, Pallas kernels, call(): pl.pallas_call(kernel, name=name, out_shape=outs, in_specs=[spec(i in far...  9.56 us
    all_to_all x1, waiting for transfers between devices, body(): strips = lax.all_to_all(strips, 'space', 0, 0, tiled=True)  8.02 us
    ppermute x9, waiting for transfers between devices, body(): parts = [lax.ppermute(total, ALL, pairs) for pairs in stage]  7.77 us
    ppermute x1, starting transfers between devices, body(): other = lax.ppermute(total, ALL, cores)  4.72 us
    all_to_all x1, starting transfers between devices, body(): strips = lax.all_to_all(strips, 'space', 0, 0, tiled=True)  4.19 us
    ppermute x1, starting transfers between devices, body(): recv = lax.ppermute(send, 'space', swap)  2.55 us
    ppermute x1, starting transfers between devices, body(): total = mine + lax.ppermute(rest, ALL, cores)  2.01 us
  transfers between devices with their start and end apart: 14, of which 9 were waited for; matrix products, arithmetic and copies ran while one was open for 1% of the time, Pallas kernels for 5%

profile of v13, /device:TPU:1, one launch (start us, length us, event | category | flops | bytes accessed | tf_op | source)
XLA Modules:
  0.0 51.9 jit_solution(8856107990937037927)
XLA Ops:
  0.6 0.0 copy-start.1
  0.6 3.3 %cut.1 = (bf16[10,72,128]{2,1,0:T(8,128)(2,1)}, bf16[10,72,128]{2,1,0:T(8,128)(2,1)}, bf16[8,72,512]{2,1,0:T(8,128)(2,1)}) custom-call(bf16[32,16,512]{2,1,0:T(8,128)(2,1)} %bitcast.14, bf16[16,8,8,128]{3,2,1,0:T(8,128)(2,1)} %bitcast.15, bf16[4,8,8,128]{3,2,1,0:T(8,128)(2,1)} %bitcast.16), custom_call_target="tpu_custom_call" | custom-call | flops 400000000 | bytes 2000000 | tf_op jit(solution)/shard_map/cut/pallas_call | solution.py:42
  4.0 0.0 copy-start
  4.0 2.5 %collective-permute-start = (bf16[10,72,128]{2,1,0:T(8,128)(2,1)}, bf16[10,72,128]{2,1,0:T(8,128)(2,1)S(1)}, u32[]{:S(2)}, u32[]{:S(2)}) collective-permute-start(bf16[10,72,128]{2,1,0:T(8,128)(2,1)} %get-tuple-element.19), channel_id=1, source_target_pairs={{0,1},{1,0},{2,3},{3,2},{4,5},{5,4},{6,7},{7,6},{8,9},{9,8},{10,11... | collective-permute-start | bytes 552968 | tf_op jit(solution)/shard_map/ppermute | solution.py:407
  6.5 4.2 %all-to-all-start = ((bf16[8,72,512]{2,1,0:T(8,128)(2,1)}), bf16[8,72,512]{2,1,0:T(8,128)(2,1)S(1)}, u32[]{:S(2)}, u32[]{:S(2)}) async-start(bf16[8,72,512]{2,1,0:T(8,128)(2,1)} %get-tuple-element.17), calls=%async_computation | async-start | bytes 1179648 | tf_op jit(solution)/shard_map/all_to_all | solution.py:408
  10.7 0.0 copy-done.1
  10.7 0.2 copy.8
  10.9 0.2 collective-permute-done.recv_ref
  11.1 0.0 copy-done
  11.1 0.8 %ready.1 = (bf16[8,80,256]{2,1,0:T(8,128)(2,1)S(1)}, bf16[864,640]{1,0:T(8,128)(2,1)S(1)}, bf16[256,640]{1,0:T(8,128)(2,1)S(1)}, bf16[768,256]{1,0:T(8,128)(2,1)S(1)}) custom-call(bf16[10,72,128]{2,1,0:T(8,128)(2,1)S(1)} %copy-done, bf16[10,72,128]{2,1,0:T(8,128)(2,1)S(1)} %collective-permute-done.recv_ref, bf16[864,16]{1,0:T(8,128)(2,1)S(1)} %bitcast.9), custom_call_target="tpu_custom_call" | custom-call | flops 20000000000 | bytes 5000000 | tf_op jit(solution)/shard_map/ready/pallas_call | solution.py:42
  11.9 8.0 %all-to-all-done.grad_ref = bf16[8,72,512]{2,1,0:T(8,128)(2,1)S(1)} async-done(((bf16[8,72,512]{2,1,0:T(8,128)(2,1)}), bf16[8,72,512]{2,1,0:T(8,128)(2,1)S(1)}, u32[]{:S(2)}, u32[]{:S(2)}) %all-to-all-start) | async-done | bytes 589856 | tf_op jit(solution)/shard_map/all_to_all | solution.py:408
  19.9 0.0 copy-start.2
  19.9 3.0 %grads.1 = (bf16[800,256]{1,0:T(8,128)(2,1)S(1)}, f32[64,128]{1,0:T(8,128)S(1)}, f32[64,128]{1,0:T(8,128)S(1)}) custom-call(bf16[8,72,512]{2,1,0:T(8,128)(2,1)S(1)} %all-to-all-done.grad_ref, bf16[8,80,256]{2,1,0:T(8,128)(2,1)S(1)} %get-tuple-element.20.pre_ref, bf16[864,640]{1,0:T(8,128)(2,1)S(1)} %get-tuple-element.21.hid_ref, ...), custom_call_target="tpu_custom_call" | custom-call | flops 3000000000 | bytes 4000000 | tf_op jit(solution)/shard_map/grads/pallas_call | solution.py:42
  22.9 2.0 %collective-permute-start.2 = (f32[64,128]{1,0:T(8,128)S(1)}, f32[64,128]{1,0:T(8,128)S(1)}, u32[]{:S(2)}, u32[]{:S(2)}) collective-permute-start(f32[64,128]{1,0:T(8,128)S(1)} %get-tuple-element.28), channel_id=1, source_target_pairs={{0,8},{1,9},{2,10},{3,11},{4,12},{5,13},{6,14},{7,15},{8,0},{9,1},... | collective-permute-start | bytes 98312 | tf_op jit(solution)/shard_map/ppermute | solution.py:432
  24.9 0.9 %collective-permute-done.2 = f32[64,128]{1,0:T(8,128)S(1)} collective-permute-done((f32[64,128]{1,0:T(8,128)S(1)}, f32[64,128]{1,0:T(8,128)S(1)}, u32[]{:S(2)}, u32[]{:S(2)}) %collective-permute-start.2) | collective-permute-done | bytes 32800 | tf_op jit(solution)/shard_map/ppermute | solution.py:432
  25.8 0.9 %collective-permute-start.4 = (f32[64,128]{1,0:T(8,128)S(1)}, f32[64,128]{1,0:T(8,128)S(1)}, u32[]{:S(2)}, u32[]{:S(2)}) collective-permute-start(f32[64,128]{1,0:T(8,128)S(1)} %add.30), channel_id=1, source_target_pairs={{0,6},{1,7},{2,4},{3,5},{4,2},{5,3},{6,0},{7,1},{8,14},{9,15},{10,... | collective-permute-start | bytes 98312 | tf_op jit(solution)/shard_map/ppermute | solution.py:435
  26.6 1.4 %collective-permute-start.5 = (f32[64,128]{1,0:T(8,128)S(1)}, f32[64,128]{1,0:T(8,128)S(1)}, u32[]{:S(2)}, u32[]{:S(2)}) collective-permute-start(f32[64,128]{1,0:T(8,128)S(1)} %add.30), channel_id=1, source_target_pairs={{0,4},{1,5},{2,6},{3,7},{4,0},{5,1},{6,2},{7,3},{8,12},{9,13},{10,... | collective-permute-start | bytes 98312 | tf_op jit(solution)/shard_map/ppermute | solution.py:435
  28.0 1.0 %collective-permute-start.3 = (f32[64,128]{1,0:T(8,128)S(1)}, f32[64,128]{1,0:T(8,128)S(1)}, u32[]{:S(2)}, u32[]{:S(2)}) collective-permute-start(f32[64,128]{1,0:T(8,128)S(1)} %add.30), channel_id=1, source_target_pairs={{0,2},{1,3},{2,0},{3,1},{4,6},{5,7},{6,4},{7,5},{8,10},{9,11},{10,... | collective-permute-start | bytes 98312 | tf_op jit(solution)/shard_map/ppermute | solution.py:435
  29.0 0.7 %collective-permute-done.4 = f32[64,128]{1,0:T(8,128)S(1)} collective-permute-done((f32[64,128]{1,0:T(8,128)S(1)}, f32[64,128]{1,0:T(8,128)S(1)}, u32[]{:S(2)}, u32[]{:S(2)}) %collective-permute-start.4) | collective-permute-done | bytes 32800 | tf_op jit(solution)/shard_map/ppermute | solution.py:435
  29.7 1.2 %collective-permute-done.5 = f32[64,128]{1,0:T(8,128)S(1)} collective-permute-done((f32[64,128]{1,0:T(8,128)S(1)}, f32[64,128]{1,0:T(8,128)S(1)}, u32[]{:S(2)}, u32[]{:S(2)}) %collective-permute-start.5) | collective-permute-done | bytes 32800 | tf_op jit(solution)/shard_map/ppermute | solution.py:435
  30.9 0.0 collective-permute-done.3
  30.9 3.4 %collective-permute-start.7 = (f32[64,128]{1,0:T(8,128)S(1)}, f32[64,128]{1,0:T(8,128)S(1)}, u32[]{:S(2)}, u32[]{:S(2)}) collective-permute-start(f32[64,128]{1,0:T(8,128)S(1)} %add_add_fusion.2), channel_id=1, source_target_pairs={{0,65},{1,64},{2,67},{3,66},{4,69},{5,68},{6,71},{7,70},{8,73},{9,... | collective-permute-start | bytes 98312 | tf_op jit(solution)/shard_map/ppermute | solution.py:435
  34.3 0.1 collective-permute-start.8
  34.4 0.6 %collective-permute-start.6 = (f32[64,128]{1,0:T(8,128)S(1)}, f32[64,128]{1,0:T(8,128)S(1)}, u32[]{:S(2)}, u32[]{:S(2)}) collective-permute-start(f32[64,128]{1,0:T(8,128)S(1)} %add_add_fusion.2), channel_id=1, source_target_pairs={{0,1},{1,0},{2,3},{3,2},{4,5},{5,4},{6,7},{7,6},{8,9},{9,8},{10,11... | collective-permute-start | bytes 98312 | tf_op jit(solution)/shard_map/ppermute | solution.py:435
  35.0 0.0 copy-done.2
  35.0 0.2 copy.9
  35.2 0.4 collective-permute-done.7
  35.6 3.0 %collective-permute-done.8 = f32[64,128]{1,0:T(8,128)S(1)} collective-permute-done((f32[64,128]{1,0:T(8,128)S(1)}, f32[64,128]{1,0:T(8,128)S(1)}, u32[]{:S(2)}, u32[]{:S(2)}) %collective-permute-start.8) | collective-permute-done | bytes 32800 | tf_op jit(solution)/shard_map/ppermute | solution.py:435
  38.6 0.0 collective-permute-done.6
  38.6 2.6 %collective-permute-start.10 = (f32[64,128]{1,0:T(8,128)S(1)}, f32[64,128]{1,0:T(8,128)S(1)}, u32[]{:S(2)}, u32[]{:S(2)}) collective-permute-start(f32[64,128]{1,0:T(8,128)S(1)} %add_add_fusion.1), channel_id=1, source_target_pairs={{0,48},{1,49},{2,50},{3,51},{4,52},{5,53},{6,54},{7,55},{8,56},{9,... | collective-permute-start | bytes 98312 | tf_op jit(solution)/shard_map/ppermute | solution.py:435
  41.2 0.5 %collective-permute-start.11 = (f32[64,128]{1,0:T(8,128)S(1)}, f32[64,128]{1,0:T(8,128)S(1)}, u32[]{:S(2)}, u32[]{:S(2)}) collective-permute-start(f32[64,128]{1,0:T(8,128)S(1)} %add_add_fusion.1), channel_id=1, source_target_pairs={{0,32},{1,33},{2,34},{3,35},{4,36},{5,37},{6,38},{7,39},{8,40},{9,... | collective-permute-start | bytes 98312 | tf_op jit(solution)/shard_map/ppermute | solution.py:435
  41.7 0.3 collective-permute-start.9
  41.9 0.9 %back.1 = (bf16[4,32,128]{2,1,0:T(8,128)(2,1)S(1)}, bf16[4,32,128]{2,1,0:T(8,128)(2,1)S(1)}) custom-call(bf16[800,256]{1,0:T(8,128)(2,1)S(1)} %get-tuple-element.24.act_s, bf16[432,4]{1,0:T(8,128)(2,1)S(1)} %bitcast.10), custom_call_target="tpu_custom_call" | custom-call | flops 500000000 | bytes 1000000 | tf_op jit(solution)/shard_map/back/pallas_call | solution.py:42
  42.8 0.1 collective-permute-start.1
  42.9 0.0 collective-permute-done.10
  42.9 2.5 %collective-permute-done.11 = f32[64,128]{1,0:T(8,128)S(1)} collective-permute-done((f32[64,128]{1,0:T(8,128)S(1)}, f32[64,128]{1,0:T(8,128)S(1)}, u32[]{:S(2)}, u32[]{:S(2)}) %collective-permute-start.11) | collective-permute-done | bytes 32800 | tf_op jit(solution)/shard_map/ppermute | solution.py:435
  45.4 0.0 collective-permute-done.9
  45.4 4.7 %collective-permute-start.12 = (f32[64,128]{1,0:T(8,128)S(1)}, f32[64,128]{1,0:T(8,128)S(1)}, u32[]{:S(2)}, u32[]{:S(2)}) collective-permute-start(f32[64,128]{1,0:T(8,128)S(1)} %add_add_fusion.mine_ref), channel_id=1, source_target_pairs={{0,8},{1,9},{2,10},{3,11},{4,12},{5,13},{6,14},{7,15},{8,0},{9,1},... | collective-permute-start | bytes 98312 | tf_op jit(solution)/shard_map/ppermute | solution.py:437
  50.2 0.0 collective-permute-done.1.recv_ref
  50.2 0.7 %tile.1 = bf16[4,8,8,128]{3,2,1,0:T(8,128)(2,1)} custom-call(bf16[4,32,128]{2,1,0:T(8,128)(2,1)S(1)} %get-tuple-element.25.own_ref, bf16[4,32,128]{2,1,0:T(8,128)(2,1)S(1)} %collective-permute-done.1.recv_ref), custom_call_target="tpu_custom_call" | custom-call | flops 1000000 | bytes 200000 | tf_op jit(solution)/shard_map/tile/pallas_call | solution.py:42
  50.9 0.1 collective-permute-done.12.rest_ref
  51.0 0.9 %unpack.1 = (f32[4,16,27]{2,1,0:T(8,128)}, f32[27,16,32]{2,1,0:T(8,128)}) custom-call(f32[64,128]{1,0:T(8,128)S(1)} %add_add_fusion.mine_ref, f32[64,128]{1,0:T(8,128)S(1)} %collective-permute-done.12.rest_ref), custom_call_target="tpu_custom_call" | custom-call | flops 1000000 | bytes 200000 | tf_op jit(solution)/shard_map/unpack/pallas_call | solution.py:42
  (4 shorter events, 0.0 us)
Async XLA Ops:
  0.6 10.1 %copy-start.1 = (bf16[27,16,32]{2,1,0:T(8,128)(2,1)S(1)}, bf16[27,16,32]{2,1,0:T(8,128)(2,1)}, u32[]{:S(2)}) copy-start(bf16[27,16,32]{2,1,0:T(8,128)(2,1)} %param.9) | copy-start | bytes 82948
  4.0 7.1 %copy-start = (bf16[10,72,128]{2,1,0:T(8,128)(2,1)S(1)}, bf16[10,72,128]{2,1,0:T(8,128)(2,1)}, u32[]{:S(2)}) copy-start(bf16[10,72,128]{2,1,0:T(8,128)(2,1)} %get-tuple-element.18.keep_ref) | copy-start | bytes 552964
  4.0 7.1 %collective-permute-start = (bf16[10,72,128]{2,1,0:T(8,128)(2,1)}, bf16[10,72,128]{2,1,0:T(8,128)(2,1)S(1)}, u32[]{:S(2)}, u32[]{:S(2)}) collective-permute-start(bf16[10,72,128]{2,1,0:T(8,128)(2,1)} %get-tuple-element.19), channel_id=1, source_target_pairs={{0,1},{1,0},{2,3},{3,2},{4,5},{5,4},{6,7},{7,6},{8,9},{9,8},{10,11... | collective-permute-start | bytes 552968 | tf_op jit(solution)/shard_map/ppermute | solution.py:407
  6.5 13.4 %all-to-all-start = ((bf16[8,72,512]{2,1,0:T(8,128)(2,1)}), bf16[8,72,512]{2,1,0:T(8,128)(2,1)S(1)}, u32[]{:S(2)}, u32[]{:S(2)}) async-start(bf16[8,72,512]{2,1,0:T(8,128)(2,1)} %get-tuple-element.17), calls=%async_computation | async-start | bytes 1179648 | tf_op jit(solution)/shard_map/all_to_all | solution.py:408
  19.9 15.1 %copy-start.2 = (bf16[27,4,16]{0,2,1:T(8,128)(2,1)S(1)}, bf16[27,4,16]{0,2,1:T(8,128)(2,1)}, u32[]{:S(2)}) copy-start(bf16[27,4,16]{0,2,1:T(8,128)(2,1)} %param.8) | copy-start | bytes 10372
  22.9 2.9 %collective-permute-start.2 = (f32[64,128]{1,0:T(8,128)S(1)}, f32[64,128]{1,0:T(8,128)S(1)}, u32[]{:S(2)}, u32[]{:S(2)}) collective-permute-start(f32[64,128]{1,0:T(8,128)S(1)} %get-tuple-element.28), channel_id=1, source_target_pairs={{0,8},{1,9},{2,10},{3,11},{4,12},{5,13},{6,14},{7,15},{8,0},{9,1},... | collective-permute-start | bytes 98312 | tf_op jit(solution)/shard_map/ppermute | solution.py:432
  25.8 4.0 %collective-permute-start.4 = (f32[64,128]{1,0:T(8,128)S(1)}, f32[64,128]{1,0:T(8,128)S(1)}, u32[]{:S(2)}, u32[]{:S(2)}) collective-permute-start(f32[64,128]{1,0:T(8,128)S(1)} %add.30), channel_id=1, source_target_pairs={{0,6},{1,7},{2,4},{3,5},{4,2},{5,3},{6,0},{7,1},{8,14},{9,15},{10,... | collective-permute-start | bytes 98312 | tf_op jit(solution)/shard_map/ppermute | solution.py:435
  26.6 4.3 %collective-permute-start.5 = (f32[64,128]{1,0:T(8,128)S(1)}, f32[64,128]{1,0:T(8,128)S(1)}, u32[]{:S(2)}, u32[]{:S(2)}) collective-permute-start(f32[64,128]{1,0:T(8,128)S(1)} %add.30), channel_id=1, source_target_pairs={{0,4},{1,5},{2,6},{3,7},{4,0},{5,1},{6,2},{7,3},{8,12},{9,13},{10,... | collective-permute-start | bytes 98312 | tf_op jit(solution)/shard_map/ppermute | solution.py:435
  28.0 2.9 %collective-permute-start.3 = (f32[64,128]{1,0:T(8,128)S(1)}, f32[64,128]{1,0:T(8,128)S(1)}, u32[]{:S(2)}, u32[]{:S(2)}) collective-permute-start(f32[64,128]{1,0:T(8,128)S(1)} %add.30), channel_id=1, source_target_pairs={{0,2},{1,3},{2,0},{3,1},{4,6},{5,7},{6,4},{7,5},{8,10},{9,11},{10,... | collective-permute-start | bytes 98312 | tf_op jit(solution)/shard_map/ppermute | solution.py:435
  30.9 4.7 %collective-permute-start.7 = (f32[64,128]{1,0:T(8,128)S(1)}, f32[64,128]{1,0:T(8,128)S(1)}, u32[]{:S(2)}, u32[]{:S(2)}) collective-permute-start(f32[64,128]{1,0:T(8,128)S(1)} %add_add_fusion.2), channel_id=1, source_target_pairs={{0,65},{1,64},{2,67},{3,66},{4,69},{5,68},{6,71},{7,70},{8,73},{9,... | collective-permute-start | bytes 98312 | tf_op jit(solution)/shard_map/ppermute | solution.py:435
  34.3 4.3 %collective-permute-start.8 = (f32[64,128]{1,0:T(8,128)S(1)}, f32[64,128]{1,0:T(8,128)S(1)}, u32[]{:S(2)}, u32[]{:S(2)}) collective-permute-start(f32[64,128]{1,0:T(8,128)S(1)} %add_add_fusion.2), channel_id=1, source_target_pairs={{0,64},{1,65},{2,66},{3,67},{4,68},{5,69},{6,70},{7,71},{8,72},{9,... | collective-permute-start | bytes 98312 | tf_op jit(solution)/shard_map/ppermute | solution.py:435
  34.4 4.2 %collective-permute-start.6 = (f32[64,128]{1,0:T(8,128)S(1)}, f32[64,128]{1,0:T(8,128)S(1)}, u32[]{:S(2)}, u32[]{:S(2)}) collective-permute-start(f32[64,128]{1,0:T(8,128)S(1)} %add_add_fusion.2), channel_id=1, source_target_pairs={{0,1},{1,0},{2,3},{3,2},{4,5},{5,4},{6,7},{7,6},{8,9},{9,8},{10,11... | collective-permute-start | bytes 98312 | tf_op jit(solution)/shard_map/ppermute | solution.py:435
  38.6 4.3 %collective-permute-start.10 = (f32[64,128]{1,0:T(8,128)S(1)}, f32[64,128]{1,0:T(8,128)S(1)}, u32[]{:S(2)}, u32[]{:S(2)}) collective-permute-start(f32[64,128]{1,0:T(8,128)S(1)} %add_add_fusion.1), channel_id=1, source_target_pairs={{0,48},{1,49},{2,50},{3,51},{4,52},{5,53},{6,54},{7,55},{8,56},{9,... | collective-permute-start | bytes 98312 | tf_op jit(solution)/shard_map/ppermute | solution.py:435
  41.2 4.3 %collective-permute-start.11 = (f32[64,128]{1,0:T(8,128)S(1)}, f32[64,128]{1,0:T(8,128)S(1)}, u32[]{:S(2)}, u32[]{:S(2)}) collective-permute-start(f32[64,128]{1,0:T(8,128)S(1)} %add_add_fusion.1), channel_id=1, source_target_pairs={{0,32},{1,33},{2,34},{3,35},{4,36},{5,37},{6,38},{7,39},{8,40},{9,... | collective-permute-start | bytes 98312 | tf_op jit(solution)/shard_map/ppermute | solution.py:435
  41.7 3.8 %collective-permute-start.9 = (f32[64,128]{1,0:T(8,128)S(1)}, f32[64,128]{1,0:T(8,128)S(1)}, u32[]{:S(2)}, u32[]{:S(2)}) collective-permute-start(f32[64,128]{1,0:T(8,128)S(1)} %add_add_fusion.1), channel_id=1, source_target_pairs={{0,16},{1,17},{2,18},{3,19},{4,20},{5,21},{6,22},{7,23},{8,24},{9,... | collective-permute-start | bytes 98312 | tf_op jit(solution)/shard_map/ppermute | solution.py:435
  42.8 7.3 %collective-permute-start.1 = (bf16[4,32,128]{2,1,0:T(8,128)(2,1)S(1)}, bf16[4,32,128]{2,1,0:T(8,128)(2,1)S(1)}, u32[]{:S(2)}, u32[]{:S(2)}) collective-permute-start(bf16[4,32,128]{2,1,0:T(8,128)(2,1)S(1)} %get-tuple-element.26), channel_id=1, source_target_pairs={{0,1},{1,0},{2,3},{3,2},{4,5},{5,4},{6,7},{7,6},{8,9},{9,8},{10,11... | collective-permute-start | bytes 98312 | tf_op jit(solution)/shard_map/ppermute | solution.py:433
  45.4 5.6 %collective-permute-start.12 = (f32[64,128]{1,0:T(8,128)S(1)}, f32[64,128]{1,0:T(8,128)S(1)}, u32[]{:S(2)}, u32[]{:S(2)}) collective-permute-start(f32[64,128]{1,0:T(8,128)S(1)} %add_add_fusion.mine_ref), channel_id=1, source_target_pairs={{0,8},{1,9},{2,10},{3,11},{4,12},{5,13},{6,14},{7,15},{8,0},{9,1},... | collective-permute-start | bytes 98312 | tf_op jit(solution)/shard_map/ppermute | solution.py:437
